TPU v7x, 32 devices: a whole 2x2x4 slice. The times are simulated.
32 devices in a mesh: depth: 4 (over x, core), scan: 8 (over z, y).
Axes of the slice: x: 2, y: 2, z: 4, core: 2. Of those that a mesh axis runs over, the one named last changes fastest.
Arguments:
- transmission: float32 [4, 2, 512, 3072], P('depth', None, 'scan'), may hold values from -5 to 5
- probe: float32 [2, 256, 256], replicated, may hold values from -6 to 6
- exit_adjoint: float32 [2, 16, 2, 256, 256], P(None, 'scan'), may hold values from -6 to 6
- scan_row: int32 [2, 16], P(None, 'scan'), may hold values from 0 to 511, as said below
- scan_col: int32 [2, 16], P(None, 'scan'), may hold values from 0 to 2816
Outputs:
- object_grad: float32 [4, 2, 512, 3072], P('depth', None, 'scan')
- probe_grad: float32 [2, 256, 256], P(None, 'depth')
Inputs may be any that keep to these rules, and one draw needn't show every extreme that they name: `scan_row`: entries 2 * j to 2 * (j + 1) - 1 of every batch lie in rows 64 * j to 64 * (j + 1) - 1: they are the positions of scan region j.
All inputs are finite; a program needn't handle non-finite values.
Results may differ from a plain program's by a relative error of at most 0.0075.
Values may be sent and summed in bfloat16 or wider, within the bound.
No kernel may reach another device: no remote copies, remote signals or barrier semaphores. Data moves between devices by JAX's collectives and lax.ppermute only.
A program may use at most 128 MiB of HBM per device.

v0:
```python
import math

import jax
import jax.numpy as jnp
from jax import lax
from jax.sharding import PartitionSpec as P

fresnel = 0.25


def from_behind(value, axis, by):
    length = lax.axis_size(axis)
    return lax.ppermute(value, axis, [(i, (i + by) % length) for i in range(length)])


def shifted(block, axis, distance):
    devices = range(lax.axis_size(axis))
    route = [(i - distance, i) for i in devices if i - distance in devices]
    return lax.ppermute(block, axis, route)


def tables(extent):
    highest = lax.Precision.HIGHEST
    indices = jnp.arange(extent)
    frequency = jnp.where(indices < extent // 2, indices, indices - extent).astype(jnp.float32)
    phases = -math.pi * fresnel / extent * frequency * frequency
    factor_real = jnp.cos(phases)
    factor_imag = jnp.sin(phases)
    turns = indices[:, None] * indices[None, :] % extent
    angles = 2.0 * math.pi / extent * turns.astype(jnp.float32)
    cos_table = jnp.cos(angles)
    sin_table = jnp.sin(angles)
    mixed_real = cos_table * factor_real[None, :] - sin_table * factor_imag[None, :]
    mixed_imag = cos_table * factor_imag[None, :] + sin_table * factor_real[None, :]
    prop_real = (
        jnp.dot(mixed_real, cos_table, precision=highest)
        + jnp.dot(mixed_imag, sin_table, precision=highest)
    ) / extent
    prop_imag = (
        jnp.dot(mixed_imag, cos_table, precision=highest)
        - jnp.dot(mixed_real, sin_table, precision=highest)
    ) / extent
    return (prop_real, prop_imag)


def apply_left(matrix, values):
    return jnp.einsum(
        "ma,kab->kmb",
        matrix,
        values,
        precision=lax.Precision.HIGHEST,
        preferred_element_type=jnp.float32,
    )


def apply_right(values, matrix):
    return jnp.einsum(
        "kab,nb->kan",
        values,
        matrix,
        precision=lax.Precision.HIGHEST,
        preferred_element_type=jnp.float32,
    )


def propagate(fields, prop_real, prop_imag):
    in_real = fields[:, 0]
    in_imag = fields[:, 1]
    mid_real = apply_left(prop_real, in_real) - apply_left(prop_imag, in_imag)
    mid_imag = apply_left(prop_real, in_imag) + apply_left(prop_imag, in_real)
    out_real = apply_right(mid_real, prop_real) - apply_right(mid_imag, prop_imag)
    out_imag = apply_right(mid_real, prop_imag) + apply_right(mid_imag, prop_real)
    return jnp.stack([out_real, out_imag], axis=1)


def multiply(first, second):
    real_part = first[:, 0] * second[:, 0] - first[:, 1] * second[:, 1]
    imag_part = first[:, 0] * second[:, 1] + first[:, 1] * second[:, 0]
    return jnp.stack([real_part, imag_part], axis=1)


def conj_multiply(first, second):
    real_part = first[:, 0] * second[:, 0] + first[:, 1] * second[:, 1]
    imag_part = first[:, 0] * second[:, 1] - first[:, 1] * second[:, 0]
    return jnp.stack([real_part, imag_part], axis=1)


def extract(extended, layer, row_block, col_block, patch_side):

    def cut_one(row_start, col_start):
        return lax.dynamic_slice(
            extended[layer], (0, row_start, col_start), (2, patch_side, patch_side)
        )

    return jax.vmap(cut_one)(row_block, col_block)


def deposit(gradient, layer, row_block, col_block, pieces):
    patch_side = pieces.shape[2]

    def place(position, buffer_now):
        anchor = (layer, 0, row_block[position], col_block[position])
        before = lax.dynamic_slice(buffer_now, anchor, (1, 2, patch_side, patch_side))
        return lax.dynamic_update_slice(buffer_now, before + pieces[position][None], anchor)

    return lax.fori_loop(0, pieces.shape[0], place, gradient)


def local(transmission, probe, exit_adjoint, scan_row, scan_col):
    layers = transmission.shape[0]
    strip_rows = transmission.shape[2]
    columns = transmission.shape[3]
    patch_side = probe.shape[1]
    rim_count = patch_side // strip_rows
    section_count = lax.axis_size("depth")
    section_index = lax.axis_index("depth")
    region_index = lax.axis_index("scan")
    following = []
    for region_step in range(1, rim_count + 1):
        following.append(from_behind(transmission, "scan", -region_step))
    extended = jnp.concatenate([transmission] + following, axis=2)
    prop_real, prop_imag = tables(patch_side)
    local_rows = scan_row - region_index * strip_rows
    batches, per_batch = scan_row.shape
    step_count = batches + section_count - 1
    probe_block = jnp.broadcast_to(probe, (per_batch, 2, patch_side, patch_side))

    def forward(step_index, state_pair):
        incoming, saved_waves = state_pair
        micro_index = step_index - section_index
        is_active = (micro_index >= 0) & (micro_index < batches)
        slot_index = jnp.clip(micro_index, 0, batches - 1)
        wave_now = jnp.where(section_index == 0, probe_block, incoming.astype(jnp.float32))
        row_block = local_rows[slot_index]
        col_block = scan_col[slot_index]
        incident = [wave_now]
        local_patch = extract(extended, 0, row_block, col_block, patch_side)
        wave_now = propagate(multiply(local_patch, wave_now), prop_real, prop_imag)
        new_entry = jnp.where(is_active, jnp.stack(incident), saved_waves[slot_index])
        saved_waves = lax.dynamic_update_index_in_dim(saved_waves, new_entry, slot_index, 0)
        incoming = shifted(wave_now.astype(jnp.bfloat16), "depth", 1)
        return (incoming, saved_waves)

    start_incoming = jnp.zeros((per_batch, 2, patch_side, patch_side), jnp.bfloat16)
    start_saved = jnp.zeros((batches, layers, per_batch, 2, patch_side, patch_side), jnp.float32)
    unused_wave, saved_waves = lax.fori_loop(0, step_count, forward, (start_incoming, start_saved))

    def backward(step_index, state_triple):
        incoming, gradient, probe_total = state_triple
        micro_index = step_index - (section_count - 1 - section_index)
        is_active = (micro_index >= 0) & (micro_index < batches)
        slot_index = jnp.clip(micro_index, 0, batches - 1)
        active_weight = is_active.astype(jnp.float32)
        adjoint_now = jnp.where(
            section_index == section_count - 1,
            exit_adjoint[slot_index],
            incoming.astype(jnp.float32),
        )
        row_block = local_rows[slot_index]
        col_block = scan_col[slot_index]
        for layer in reversed(range(layers)):
            spread_back = propagate(adjoint_now, prop_real, -prop_imag)
            local_patch = extract(extended, layer, row_block, col_block, patch_side)
            update_piece = (
                conj_multiply(saved_waves[slot_index, layer], spread_back) * active_weight
            )
            gradient = deposit(gradient, layer, row_block, col_block, update_piece)
            adjoint_now = conj_multiply(local_patch, spread_back)
        probe_total = probe_total + jnp.where(
            is_active & (section_index == 0), jnp.sum(adjoint_now, axis=0), 0.0
        )
        incoming = shifted(adjoint_now.astype(jnp.bfloat16), "depth", -1)
        return (incoming, gradient, probe_total)

    start_grad = jnp.zeros((layers, 2, strip_rows + patch_side, columns), jnp.float32)
    start_probe = jnp.zeros((2, patch_side, patch_side), jnp.float32)
    unused_adjoint, gradient, probe_total = lax.fori_loop(
        0, step_count, backward, (start_incoming, start_grad, start_probe)
    )
    object_grad = gradient[:, :, :strip_rows, :]
    for region_step in range(1, rim_count + 1):
        lower_piece = gradient[:, :, region_step * strip_rows : (region_step + 1) * strip_rows, :]
        object_grad = object_grad + from_behind(
            lower_piece.astype(jnp.bfloat16), "scan", region_step
        ).astype(lower_piece.dtype)
    partial_total = lax.psum(probe_total, "scan")
    probe_grad = lax.psum_scatter(
        partial_total.astype(jnp.bfloat16), "depth", scatter_dimension=1, tiled=True
    ).astype(jnp.float32)
    return (object_grad, probe_grad)


def solution(mesh):
    placed = (
        P("depth", None, "scan", None),
        P(),
        P(None, "scan", None, None, None),
        P(None, "scan"),
        P(None, "scan"),
    )
    return jax.shard_map(
        local,
        mesh=mesh,
        in_specs=placed,
        out_specs=(P("depth", None, "scan", None), P(None, "depth", None)),
        check_vma=False,
    )
```

profile of v0, /device:TPU:0, one launch (start us, length us, event | category | flops | bytes accessed | tf_op | source)
XLA Modules:
  0.0 822.7 jit_solution(2117557643805735677)
XLA Ops:
  7.2 5.0 collective-permute-start.4
  14.1 2.6 collective-permute-start.5
  22.8 92.0 %collective-permute-done.2 = f32[1,2,64,3072]{3,2,1,0:T(8,128)} collective-permute-done((f32[1,2,64,3072]{3,2,1,0:T(8,128)}, f32[1,2,64,3072]{3,2,1,0:T(8,128)}, u32[]{:S(2)}, u32[]{:S(2)}) %collective-permute-start.2) | collective-permute-done | bytes 1572896 | tf_op jit(solution)/shard_map/ppermute | solution.py:13
  119.4 96.2 %collective-permute-done.5 = f32[1,2,64,3072]{3,2,1,0:T(8,128)} collective-permute-done((f32[1,2,64,3072]{3,2,1,0:T(8,128)}, f32[1,2,64,3072]{3,2,1,0:T(8,128)}, u32[]{:S(2)}, u32[]{:S(2)}) %collective-permute-start.5) | collective-permute-done | bytes 1572896 | tf_op jit(solution)/shard_map/ppermute | solution.py:13
  220.8 137.5 %while.72 = (s32[]{:T(128)}, bf16[2,2,256,256]{3,2,0,1:T(8,128)(2,1)S(1)}, f32[2,1,2,2,256,256]{5,4,2,3,1,0:T(8,128)}, f32[1,2,320,3072]{3,2,1,0:T(8,128)}, s32[...) while((s32[]{:T(128)}, ...), condition=%wide.region_1.2_spmd.clone, body=%wide.region_0.1_spmd.clone.sunk | while | flops 3223846912 | bytes 25691188 | solution.py:146
  222.2 6.7 while.76
  222.9 2.7 bitcast_dynamic-update-slice_fusion.8
  226.3 2.7 bitcast_dynamic-update-slice_fusion.8
  243.7 6.6 while.76
  244.4 2.7 bitcast_dynamic-update-slice_fusion.8
  247.7 2.6 bitcast_dynamic-update-slice_fusion.8
  260.8 8.8 %collective-permute-start.1 = (bf16[2,2,256,256]{3,2,0,1:T(8,128)(2,1)S(1)}, bf16[2,2,256,256]{3,2,0,1:T(8,128)(2,1)S(1)}, u32[]{:S(2)}, u32[]{:S(2)}) collective-permute-start(bf16[2,2,256,256]{3,2,0,1:T(8,128)(2,1)S(1)} %pad_maximum_fusion.3), channel_id=1, source_target_pairs={{0,8},{8,16},{16,24},{1,9},{9,17},{17,25},{2,10},{10,18},{18,26},{... | collective-permute-start | bytes 1572872 | tf_op jit(solution)/shard_map/while/body/eval_jaxpr/ppermute | solution.py:19
  272.5 6.6 while.76
  273.2 2.7 bitcast_dynamic-update-slice_fusion.8
  276.6 2.6 bitcast_dynamic-update-slice_fusion.8
  289.7 9.0 %collective-permute-start.1 = (bf16[2,2,256,256]{3,2,0,1:T(8,128)(2,1)S(1)}, bf16[2,2,256,256]{3,2,0,1:T(8,128)(2,1)S(1)}, u32[]{:S(2)}, u32[]{:S(2)}) collective-permute-start(bf16[2,2,256,256]{3,2,0,1:T(8,128)(2,1)S(1)} %pad_maximum_fusion.3), channel_id=1, source_target_pairs={{0,8},{8,16},{16,24},{1,9},{9,17},{17,25},{2,10},{10,18},{18,26},{... | collective-permute-start | bytes 1572872 | tf_op jit(solution)/shard_map/while/body/eval_jaxpr/ppermute | solution.py:19
  301.6 6.6 while.76
  302.3 2.7 bitcast_dynamic-update-slice_fusion.8
  318.7 9.1 %collective-permute-start.1 = (bf16[2,2,256,256]{3,2,0,1:T(8,128)(2,1)S(1)}, bf16[2,2,256,256]{3,2,0,1:T(8,128)(2,1)S(1)}, u32[]{:S(2)}, u32[]{:S(2)}) collective-permute-start(bf16[2,2,256,256]{3,2,0,1:T(8,128)(2,1)S(1)} %pad_maximum_fusion.3), channel_id=1, source_target_pairs={{0,8},{8,16},{16,24},{1,9},{9,17},{17,25},{2,10},{10,18},{18,26},{... | collective-permute-start | bytes 1572872 | tf_op jit(solution)/shard_map/while/body/eval_jaxpr/ppermute | solution.py:19
  330.7 6.6 while.76
  331.4 2.7 bitcast_dynamic-update-slice_fusion.8
  347.8 9.0 %collective-permute-start.1 = (bf16[2,2,256,256]{3,2,0,1:T(8,128)(2,1)S(1)}, bf16[2,2,256,256]{3,2,0,1:T(8,128)(2,1)S(1)}, u32[]{:S(2)}, u32[]{:S(2)}) collective-permute-start(bf16[2,2,256,256]{3,2,0,1:T(8,128)(2,1)S(1)} %pad_maximum_fusion.3), channel_id=1, source_target_pairs={{0,8},{8,16},{16,24},{1,9},{9,17},{17,25},{2,10},{10,18},{18,26},{... | collective-permute-start | bytes 1572872 | tf_op jit(solution)/shard_map/while/body/eval_jaxpr/ppermute | solution.py:19
  359.2 4.1 broadcast_in_dim.53
  363.3 275.0 %while.75 = (s32[]{:T(128)}, bf16[2,2,256,256]{3,2,0,1:T(8,128)(2,1)}, f32[1,2,320,3072]{3,2,1,0:T(8,128)}, f32[2,256,256]{2,1,0:T(8,128)}, f32[1,2,320,3072]{3,...) while((s32[]{:T(128)}, ...), condition=%wide.region_6.7_spmd.clone, body=%wide.region_2.6_spmd.clone.sunk | while | flops 3225550848 | bytes 49809460 | solution.py:177
  375.9 8.4 %while.77 = (s32[]{:T(128)}, f32[2,320,3072]{2,1,0:T(8,128)}, s32[2,3]{1,0:T(2,128)S(1)}, f32[2,2,256,256]{3,2,0,1:T(8,128)}, s32[]{:T(128)}) while((s32[]{:T(128)}, f32[2,320,3072]{2,1,0:T(8,128)}, s32[2,3]{1,0:T(2,128)S(1)}, f32[2,2,256,256]{3,2,0,1:T(8,128)}, s32[]{:T(128)}) %tuple.191), condition=%wide.while_cond.1, body=%wide.while_body.1.sunk | while | flops 2 | bytes 1049717 | solution.py:91
  376.6 3.5 bitcast_dynamic-update-slice_fusion.7
  380.7 3.5 bitcast_dynamic-update-slice_fusion.7
  385.6 3.2 add_bitcast_fusion.2
  392.2 25.5 %while.78 = (s32[]{:T(128)}, f32[1,2,320,3072]{3,2,1,0:T(8,128)}, s32[2]{0:T(128)S(1)}, s32[2]{0:T(128)S(1)}, f32[2,2,256,256]{3,2,0,1:T(8,128)S(1)}, /*index=5*/s32[]{:T(128)}, s32[]{:T(128)}, s32[]{:T(128)}, s32[]{:T(128)}) while((s32[]{:T(128)}, f32[1,2,320,3072]{3,2,1,0:T(8,128)}, s32[2]{0:T(128)S(1)}, s32[2]{0:T(128)S(1)}, ...), condition=%wide.region_4.4_spmd, body=%wide.region_3.3_spmd.sunk | while | flops 131080 | bytes 2621649 | solution.py:106
  398.7 6.2 dynamic_update_slice.21
  411.4 6.3 dynamic_update_slice.21
  431.3 8.4 %while.77 = (s32[]{:T(128)}, f32[2,320,3072]{2,1,0:T(8,128)}, s32[2,3]{1,0:T(2,128)S(1)}, f32[2,2,256,256]{3,2,0,1:T(8,128)}, s32[]{:T(128)}) while((s32[]{:T(128)}, f32[2,320,3072]{2,1,0:T(8,128)}, s32[2,3]{1,0:T(2,128)S(1)}, f32[2,2,256,256]{3,2,0,1:T(8,128)}, s32[]{:T(128)}) %tuple.191), condition=%wide.while_cond.1, body=%wide.while_body.1.sunk | while | flops 2 | bytes 1049717 | solution.py:91
  432.0 3.5 bitcast_dynamic-update-slice_fusion.7
  436.2 3.5 bitcast_dynamic-update-slice_fusion.7
  441.0 3.2 add_bitcast_fusion.2
  447.7 25.5 %while.78 = (s32[]{:T(128)}, f32[1,2,320,3072]{3,2,1,0:T(8,128)}, s32[2]{0:T(128)S(1)}, s32[2]{0:T(128)S(1)}, f32[2,2,256,256]{3,2,0,1:T(8,128)S(1)}, /*index=5*/s32[]{:T(128)}, s32[]{:T(128)}, s32[]{:T(128)}, s32[]{:T(128)}) while((s32[]{:T(128)}, f32[1,2,320,3072]{3,2,1,0:T(8,128)}, s32[2]{0:T(128)S(1)}, s32[2]{0:T(128)S(1)}, ...), condition=%wide.region_4.4_spmd, body=%wide.region_3.3_spmd.sunk | while | flops 131080 | bytes 2621649 | solution.py:106
  454.1 6.2 dynamic_update_slice.21
  466.8 6.3 dynamic_update_slice.21
  486.7 8.4 %while.77 = (s32[]{:T(128)}, f32[2,320,3072]{2,1,0:T(8,128)}, s32[2,3]{1,0:T(2,128)S(1)}, f32[2,2,256,256]{3,2,0,1:T(8,128)}, s32[]{:T(128)}) while((s32[]{:T(128)}, f32[2,320,3072]{2,1,0:T(8,128)}, s32[2,3]{1,0:T(2,128)S(1)}, f32[2,2,256,256]{3,2,0,1:T(8,128)}, s32[]{:T(128)}) %tuple.191), condition=%wide.while_cond.1, body=%wide.while_body.1.sunk | while | flops 2 | bytes 1049717 | solution.py:91
  487.4 3.5 bitcast_dynamic-update-slice_fusion.7
  491.6 3.5 bitcast_dynamic-update-slice_fusion.7
  496.5 3.2 add_bitcast_fusion.2
  503.1 25.5 %while.78 = (s32[]{:T(128)}, f32[1,2,320,3072]{3,2,1,0:T(8,128)}, s32[2]{0:T(128)S(1)}, s32[2]{0:T(128)S(1)}, f32[2,2,256,256]{3,2,0,1:T(8,128)S(1)}, /*index=5*/s32[]{:T(128)}, s32[]{:T(128)}, s32[]{:T(128)}, s32[]{:T(128)}) while((s32[]{:T(128)}, f32[1,2,320,3072]{3,2,1,0:T(8,128)}, s32[2]{0:T(128)S(1)}, s32[2]{0:T(128)S(1)}, ...), condition=%wide.region_4.4_spmd, body=%wide.region_3.3_spmd.sunk | while | flops 131080 | bytes 2621649 | solution.py:106
  509.6 6.2 dynamic_update_slice.21
  522.2 6.3 dynamic_update_slice.21
  542.2 8.4 %while.77 = (s32[]{:T(128)}, f32[2,320,3072]{2,1,0:T(8,128)}, s32[2,3]{1,0:T(2,128)S(1)}, f32[2,2,256,256]{3,2,0,1:T(8,128)}, s32[]{:T(128)}) while((s32[]{:T(128)}, f32[2,320,3072]{2,1,0:T(8,128)}, s32[2,3]{1,0:T(2,128)S(1)}, f32[2,2,256,256]{3,2,0,1:T(8,128)}, s32[]{:T(128)}) %tuple.191), condition=%wide.while_cond.1, body=%wide.while_body.1.sunk | while | flops 2 | bytes 1049717 | solution.py:91
  542.9 3.5 bitcast_dynamic-update-slice_fusion.7
  547.0 3.5 bitcast_dynamic-update-slice_fusion.7
  551.9 3.2 add_bitcast_fusion.2
  558.5 25.5 %while.78 = (s32[]{:T(128)}, f32[1,2,320,3072]{3,2,1,0:T(8,128)}, s32[2]{0:T(128)S(1)}, s32[2]{0:T(128)S(1)}, f32[2,2,256,256]{3,2,0,1:T(8,128)S(1)}, /*index=5*/s32[]{:T(128)}, s32[]{:T(128)}, s32[]{:T(128)}, s32[]{:T(128)}) while((s32[]{:T(128)}, f32[1,2,320,3072]{3,2,1,0:T(8,128)}, s32[2]{0:T(128)S(1)}, s32[2]{0:T(128)S(1)}, ...), condition=%wide.region_4.4_spmd, body=%wide.region_3.3_spmd.sunk | while | flops 131080 | bytes 2621649 | solution.py:106
  565.0 6.2 dynamic_update_slice.21
  577.7 6.3 dynamic_update_slice.21
  597.6 8.3 %while.77 = (s32[]{:T(128)}, f32[2,320,3072]{2,1,0:T(8,128)}, s32[2,3]{1,0:T(2,128)S(1)}, f32[2,2,256,256]{3,2,0,1:T(8,128)}, s32[]{:T(128)}) while((s32[]{:T(128)}, f32[2,320,3072]{2,1,0:T(8,128)}, s32[2,3]{1,0:T(2,128)S(1)}, f32[2,2,256,256]{3,2,0,1:T(8,128)}, s32[]{:T(128)}) %tuple.191), condition=%wide.while_cond.1, body=%wide.while_body.1.sunk | while | flops 2 | bytes 1049717 | solution.py:91
  598.3 3.5 bitcast_dynamic-update-slice_fusion.7
  602.5 3.4 bitcast_dynamic-update-slice_fusion.7
  607.2 3.2 add_bitcast_fusion.2
  613.9 23.4 %while.78 = (s32[]{:T(128)}, f32[1,2,320,3072]{3,2,1,0:T(8,128)}, s32[2]{0:T(128)S(1)}, s32[2]{0:T(128)S(1)}, f32[2,2,256,256]{3,2,0,1:T(8,128)S(1)}, /*index=5*/s32[]{:T(128)}, s32[]{:T(128)}, s32[]{:T(128)}, s32[]{:T(128)}) while((s32[]{:T(128)}, f32[1,2,320,3072]{3,2,1,0:T(8,128)}, s32[2]{0:T(128)S(1)}, s32[2]{0:T(128)S(1)}, ...), condition=%wide.region_4.4_spmd, body=%wide.region_3.3_spmd.sunk | while | flops 131080 | bytes 2621649 | solution.py:106
  620.3 6.1 dynamic_update_slice.21
  632.8 4.5 dynamic_update_slice.21
  638.3 3.8 convert.14
  644.7 4.1 collective-permute-start.8
  650.5 120.5 %all-reduce.1 = bf16[2,256,256]{2,1,0:T(8,128)(2,1)} all-reduce(f32[2,256,256]{2,1,0:T(8,128)S(1)} %copy-done.5), channel_id=1, replica_groups=mesh['depth'=4,'scan'=8] {'scan'}, use_global_device_ids=true, to_apply=%region_7.8 | all-reduce | flops 131072 | bytes 786432 | tf_op jit(solution)/shard_map/psum | solution.py:186
  771.1 39.7 %reduce-scatter.2.cloned.1.call-done = bf16[2,64,256]{2,1,0:T(8,128)(2,1)} async-done(((bf16[2,256,256]{2,1,0:T(8,128)(2,1)}), bf16[2,64,256]{2,1,0:T(8,128)(2,1)}) %reduce-scatter.2.cloned.1.call-update) | async-done | bytes 65552 | tf_op jit(solution)/shard_map/reduce_scatter | solution.py:187
  812.3 3.6 convert_add_fusion
  (363 shorter events, 227.1 us)
Async XLA Ops:
  7.2 803.6 %reduce-scatter.2.cloned.1.call-start = ((), (), s32[]{:S(2)}) async-start(), calls=%async_computation.1 | async-start | bytes 327680 | tf_op jit(solution)/shard_map/reduce_scatter | solution.py:187
  7.2 110.7 %collective-permute-start.4 = (f32[1,2,64,3072]{3,2,1,0:T(8,128)}, f32[1,2,64,3072]{3,2,1,0:T(8,128)}, u32[]{:S(2)}, u32[]{:S(2)}) collective-permute-start(f32[1,2,64,3072]{3,2,1,0:T(8,128)} %param.11), channel_id=1, source_target_pairs={{0,5},{1,6},{2,7},{3,0},{4,1},{5,2},{6,3},{7,4},{8,13},{9,14},{10,... | collective-permute-start | bytes 4718600 | tf_op jit(solution)/shard_map/ppermute | solution.py:13
  12.3 104.1 %collective-permute-start.3 = (f32[1,2,64,3072]{3,2,1,0:T(8,128)}, f32[1,2,64,3072]{3,2,1,0:T(8,128)}, u32[]{:S(2)}, u32[]{:S(2)}) collective-permute-start(f32[1,2,64,3072]{3,2,1,0:T(8,128)} %param.11), channel_id=1, source_target_pairs={{0,6},{1,7},{2,0},{3,1},{4,2},{5,3},{6,4},{7,5},{8,14},{9,15},{10,... | collective-permute-start | bytes 4718600 | tf_op jit(solution)/shard_map/ppermute | solution.py:13
  13.6 101.2 %collective-permute-start.2 = (f32[1,2,64,3072]{3,2,1,0:T(8,128)}, f32[1,2,64,3072]{3,2,1,0:T(8,128)}, u32[]{:S(2)}, u32[]{:S(2)}) collective-permute-start(f32[1,2,64,3072]{3,2,1,0:T(8,128)} %param.11), channel_id=1, source_target_pairs={{0,7},{1,0},{2,1},{3,2},{4,3},{5,4},{6,5},{7,6},{8,15},{9,8},{10,9... | collective-permute-start | bytes 4718600 | tf_op jit(solution)/shard_map/ppermute | solution.py:13
  14.1 201.5 %collective-permute-start.5 = (f32[1,2,64,3072]{3,2,1,0:T(8,128)}, f32[1,2,64,3072]{3,2,1,0:T(8,128)}, u32[]{:S(2)}, u32[]{:S(2)}) collective-permute-start(f32[1,2,64,3072]{3,2,1,0:T(8,128)} %param.11), channel_id=1, source_target_pairs={{0,4},{1,5},{2,6},{3,7},{4,0},{5,1},{6,2},{7,3},{8,12},{9,13},{10,... | collective-permute-start | bytes 4718600 | tf_op jit(solution)/shard_map/ppermute | solution.py:13
  19.7 2.9 copy-start.8
  19.7 3.0 copy-start.6
  217.1 3.7 copy-start
  217.1 3.7 copy-start.7
  239.4 2.8 collective-permute-start.1
  260.8 10.3 %collective-permute-start.1 = (bf16[2,2,256,256]{3,2,0,1:T(8,128)(2,1)S(1)}, bf16[2,2,256,256]{3,2,0,1:T(8,128)(2,1)S(1)}, u32[]{:S(2)}, u32[]{:S(2)}) collective-permute-start(bf16[2,2,256,256]{3,2,0,1:T(8,128)(2,1)S(1)} %pad_maximum_fusion.3), channel_id=1, source_target_pairs={{0,8},{8,16},{16,24},{1,9},{9,17},{17,25},{2,10},{10,18},{18,26},{... | collective-permute-start | bytes 1572872 | tf_op jit(solution)/shard_map/while/body/eval_jaxpr/ppermute | solution.py:19
  289.7 10.5 %collective-permute-start.1 = (bf16[2,2,256,256]{3,2,0,1:T(8,128)(2,1)S(1)}, bf16[2,2,256,256]{3,2,0,1:T(8,128)(2,1)S(1)}, u32[]{:S(2)}, u32[]{:S(2)}) collective-permute-start(bf16[2,2,256,256]{3,2,0,1:T(8,128)(2,1)S(1)} %pad_maximum_fusion.3), channel_id=1, source_target_pairs={{0,8},{8,16},{16,24},{1,9},{9,17},{17,25},{2,10},{10,18},{18,26},{... | collective-permute-start | bytes 1572872 | tf_op jit(solution)/shard_map/while/body/eval_jaxpr/ppermute | solution.py:19
  318.7 10.6 %collective-permute-start.1 = (bf16[2,2,256,256]{3,2,0,1:T(8,128)(2,1)S(1)}, bf16[2,2,256,256]{3,2,0,1:T(8,128)(2,1)S(1)}, u32[]{:S(2)}, u32[]{:S(2)}) collective-permute-start(bf16[2,2,256,256]{3,2,0,1:T(8,128)(2,1)S(1)} %pad_maximum_fusion.3), channel_id=1, source_target_pairs={{0,8},{8,16},{16,24},{1,9},{9,17},{17,25},{2,10},{10,18},{18,26},{... | collective-permute-start | bytes 1572872 | tf_op jit(solution)/shard_map/while/body/eval_jaxpr/ppermute | solution.py:19
  347.8 10.5 %collective-permute-start.1 = (bf16[2,2,256,256]{3,2,0,1:T(8,128)(2,1)S(1)}, bf16[2,2,256,256]{3,2,0,1:T(8,128)(2,1)S(1)}, u32[]{:S(2)}, u32[]{:S(2)}) collective-permute-start(bf16[2,2,256,256]{3,2,0,1:T(8,128)(2,1)S(1)} %pad_maximum_fusion.3), channel_id=1, source_target_pairs={{0,8},{8,16},{16,24},{1,9},{9,17},{17,25},{2,10},{10,18},{18,26},{... | collective-permute-start | bytes 1572872 | tf_op jit(solution)/shard_map/while/body/eval_jaxpr/ppermute | solution.py:19
  384.2 1.2 copy-start.1
  384.2 1.4 copy-start.2
  389.7 28.2 %collective-permute-start = (bf16[2,2,256,256]{3,2,0,1:T(8,128)(2,1)}, bf16[2,2,256,256]{3,2,0,1:T(8,128)(2,1)}, u32[]{:S(2)}, u32[]{:S(2)}) collective-permute-start(bf16[2,2,256,256]{3,2,0,1:T(8,128)(2,1)} %fusion.198), channel_id=1, source_target_pairs={{8,0},{16,8},{24,16},{9,1},{17,9},{25,17},{10,2},{18,10},{26,18},{... | collective-permute-start | bytes 1572872 | tf_op jit(solution)/shard_map/while/body/eval_jaxpr/ppermute | solution.py:19
  392.2 25.5 %copy-start.3 = (f32[2,256,256]{2,1,0:T(8,128)S(1)}, f32[2,256,256]{2,1,0:T(8,128)}, u32[]{:S(2)}) copy-start(f32[2,256,256]{2,1,0:T(8,128)} %get-tuple-element.1269) | copy-start | bytes 1572868 | tf_op jit(solution)/shard_map/while
  417.9 0.8 copy-start.4
  439.7 1.2 copy-start.1
  439.7 1.4 copy-start.2
  445.1 28.2 %collective-permute-start = (bf16[2,2,256,256]{3,2,0,1:T(8,128)(2,1)}, bf16[2,2,256,256]{3,2,0,1:T(8,128)(2,1)}, u32[]{:S(2)}, u32[]{:S(2)}) collective-permute-start(bf16[2,2,256,256]{3,2,0,1:T(8,128)(2,1)} %fusion.198), channel_id=1, source_target_pairs={{8,0},{16,8},{24,16},{9,1},{17,9},{25,17},{10,2},{18,10},{26,18},{... | collective-permute-start | bytes 1572872 | tf_op jit(solution)/shard_map/while/body/eval_jaxpr/ppermute | solution.py:19
  447.7 25.5 %copy-start.3 = (f32[2,256,256]{2,1,0:T(8,128)S(1)}, f32[2,256,256]{2,1,0:T(8,128)}, u32[]{:S(2)}) copy-start(f32[2,256,256]{2,1,0:T(8,128)} %get-tuple-element.1269) | copy-start | bytes 1572868 | tf_op jit(solution)/shard_map/while
  473.3 0.8 copy-start.4
  495.1 1.2 copy-start.1
  495.1 1.4 copy-start.2
  500.6 28.2 %collective-permute-start = (bf16[2,2,256,256]{3,2,0,1:T(8,128)(2,1)}, bf16[2,2,256,256]{3,2,0,1:T(8,128)(2,1)}, u32[]{:S(2)}, u32[]{:S(2)}) collective-permute-start(bf16[2,2,256,256]{3,2,0,1:T(8,128)(2,1)} %fusion.198), channel_id=1, source_target_pairs={{8,0},{16,8},{24,16},{9,1},{17,9},{25,17},{10,2},{18,10},{26,18},{... | collective-permute-start | bytes 1572872 | tf_op jit(solution)/shard_map/while/body/eval_jaxpr/ppermute | solution.py:19
  503.1 25.5 %copy-start.3 = (f32[2,256,256]{2,1,0:T(8,128)S(1)}, f32[2,256,256]{2,1,0:T(8,128)}, u32[]{:S(2)}) copy-start(f32[2,256,256]{2,1,0:T(8,128)} %get-tuple-element.1269) | copy-start | bytes 1572868 | tf_op jit(solution)/shard_map/while
  528.7 0.8 copy-start.4
  550.5 1.2 copy-start.1
  550.5 1.4 copy-start.2
  556.0 28.2 %collective-permute-start = (bf16[2,2,256,256]{3,2,0,1:T(8,128)(2,1)}, bf16[2,2,256,256]{3,2,0,1:T(8,128)(2,1)}, u32[]{:S(2)}, u32[]{:S(2)}) collective-permute-start(bf16[2,2,256,256]{3,2,0,1:T(8,128)(2,1)} %fusion.198), channel_id=1, source_target_pairs={{8,0},{16,8},{24,16},{9,1},{17,9},{25,17},{10,2},{18,10},{26,18},{... | collective-permute-start | bytes 1572872 | tf_op jit(solution)/shard_map/while/body/eval_jaxpr/ppermute | solution.py:19
  558.5 25.5 %copy-start.3 = (f32[2,256,256]{2,1,0:T(8,128)S(1)}, f32[2,256,256]{2,1,0:T(8,128)}, u32[]{:S(2)}) copy-start(f32[2,256,256]{2,1,0:T(8,128)} %get-tuple-element.1269) | copy-start | bytes 1572868 | tf_op jit(solution)/shard_map/while
  584.2 0.8 copy-start.4
  605.9 1.2 copy-start.1
  605.9 1.4 copy-start.2
  611.3 26.1 %collective-permute-start = (bf16[2,2,256,256]{3,2,0,1:T(8,128)(2,1)}, bf16[2,2,256,256]{3,2,0,1:T(8,128)(2,1)}, u32[]{:S(2)}, u32[]{:S(2)}) collective-permute-start(bf16[2,2,256,256]{3,2,0,1:T(8,128)(2,1)} %fusion.198), channel_id=1, source_target_pairs={{8,0},{16,8},{24,16},{9,1},{17,9},{25,17},{10,2},{18,10},{26,18},{... | collective-permute-start | bytes 1572872 | tf_op jit(solution)/shard_map/while/body/eval_jaxpr/ppermute | solution.py:19
  613.9 23.4 %copy-start.3 = (f32[2,256,256]{2,1,0:T(8,128)S(1)}, f32[2,256,256]{2,1,0:T(8,128)}, u32[]{:S(2)}) copy-start(f32[2,256,256]{2,1,0:T(8,128)} %get-tuple-element.1269) | copy-start | bytes 1572868 | tf_op jit(solution)/shard_map/while
  637.5 0.8 copy-start.4
  642.1 8.4 %copy-start.5 = (f32[2,256,256]{2,1,0:T(8,128)S(1)}, f32[2,256,256]{2,1,0:T(8,128)}, u32[]{:S(2)}) copy-start(f32[2,256,256]{2,1,0:T(8,128)} %get-tuple-element.618) | copy-start | bytes 1572868
  643.5 168.8 %collective-permute-start.6 = (bf16[1,2,64,3072]{3,2,1,0:T(8,128)(2,1)}, bf16[1,2,64,3072]{3,2,1,0:T(8,128)(2,1)S(1)}, u32[]{:S(2)}, u32[]{:S(2)}) collective-permute-start(bf16[1,2,64,3072]{3,2,1,0:T(8,128)(2,1)} %get-tuple-element.831), channel_id=1, source_target_pairs={{0,1},{1,2},{2,3},{3,4},{4,5},{5,6},{6,7},{7,0},{8,9},{9,10},{10,1... | collective-permute-start | bytes 2359304 | tf_op jit(solution)/shard_map/ppermute | solution.py:13
  643.5 168.8 %collective-permute-start.9 = (bf16[1,2,64,3072]{3,2,1,0:T(8,128)(2,1)}, bf16[1,2,64,3072]{3,2,1,0:T(8,128)(2,1)S(1)}, u32[]{:S(2)}, u32[]{:S(2)}) collective-permute-start(bf16[1,2,64,3072]{3,2,1,0:T(8,128)(2,1)} %get-tuple-element.832), channel_id=1, source_target_pairs={{0,4},{1,5},{2,6},{3,7},{4,0},{5,1},{6,2},{7,3},{8,12},{9,13},{10,... | collective-permute-start | bytes 2359304 | tf_op jit(solution)/shard_map/ppermute | solution.py:13
  644.7 167.6 %collective-permute-start.8 = (bf16[1,2,64,3072]{3,2,1,0:T(8,128)(2,1)}, bf16[1,2,64,3072]{3,2,1,0:T(8,128)(2,1)}, u32[]{:S(2)}, u32[]{:S(2)}) collective-permute-start(bf16[1,2,64,3072]{3,2,1,0:T(8,128)(2,1)} %get-tuple-element.833), channel_id=1, source_target_pairs={{0,3},{1,4},{2,5},{3,6},{4,7},{5,0},{6,1},{7,2},{8,11},{9,12},{10,... | collective-permute-start | bytes 2359304 | tf_op jit(solution)/shard_map/ppermute | solution.py:13
  648.8 163.5 %collective-permute-start.7 = (bf16[1,2,64,3072]{3,2,1,0:T(8,128)(2,1)S(1)}, bf16[1,2,64,3072]{3,2,1,0:T(8,128)(2,1)}, u32[]{:S(2)}, u32[]{:S(2)}) collective-permute-start(bf16[1,2,64,3072]{3,2,1,0:T(8,128)(2,1)S(1)} %get-tuple-element.834), channel_id=1, source_target_pairs={{0,2},{1,3},{2,4},{3,5},{4,6},{5,7},{6,0},{7,1},{8,10},{9,11},{10,... | collective-permute-start | bytes 2359304 | tf_op jit(solution)/shard_map/ppermute | solution.py:13
Sparse Core Ops, SparseCore 0:
  771.2 39.5 reduce-scatter.1
where the time goes:
time: 830 us; the launch traced here: 823 us
  waiting for transfers between devices  235 us (28%)
  local copies, waits for them, and re-layouts  206 us (25%)
  blocking collectives  121 us (15%)
  matrix products  93.6 us (11%)
  starting transfers between devices  60.2 us (7%)
  other arithmetic  51.6 us (6%)
  loops' own time  40.9 us (5%)
  between operations  14.2 us (2%)
    ppermute x8, waiting for transfers between devices, from_behind(): lax.ppermute(value, axis, [(i, (i + by) % length) for i in range(length)])  188 us
    psum x1, blocking collectives, local(): partial_total = lax.psum(probe_total, 'scan')  121 us
    gather x60, local copies, waits for them, and re-layouts  74.4 us
    dynamic_update_slice x10, local copies, waits for them, and re-layouts, place(): lax.dynamic_update_slice(buffer_now, before + pieces[position][None], anc...  60.9 us
    dot_general x40, matrix products, apply_right(): jnp.einsum('kab,nb->kan', values, matrix, precision=lax.Precision.HIGHEST...  55.6 us
    ppermute x10, starting transfers between devices, shifted(): return lax.ppermute(block, axis, route)  43.7 us
    reduce_scatter x1, waiting for transfers between devices, local(): lax.psum_scatter(partial_total.astype(jnp.bfloat16), 'depth', scatter_dim...  39.7 us
    another operation x5, loops' own time, deposit(): return lax.fori_loop(0, pieces.shape[0], place, gradient)  39 us
  transfers between devices with their start and end apart: 19, of which 8 were waited for; matrix products, arithmetic and copies ran while one was open for 13% of the time, Pallas kernels for 0%

commit v1 on v0

v1 whole, which is shorter than its diff:
```python
import functools

import jax
import jax.numpy as jnp
import numpy as np
from jax import lax
from jax.experimental import pallas as pl
from jax.experimental.pallas import tpu as pltpu
from jax.sharding import PartitionSpec as P

fresnel = 0.25
LANES = 128
bf16 = jnp.bfloat16
f32 = jnp.float32


def propagator(extent):
    indices = np.arange(extent)
    frequency = np.where(indices < extent // 2, indices, indices - extent).astype(np.float64)
    factor = np.exp(-1j * np.pi * fresnel / extent * frequency * frequency)
    column = np.fft.ifft(factor)
    matrix = column[(indices[:, None] - indices[None, :]) % extent]
    return matrix.real, matrix.imag


def halves(matrix):
    high = matrix.astype(np.float32).astype(bf16)
    low = (matrix - high.astype(np.float64)).astype(np.float32).astype(bf16)
    return high, low


def tables(extent):
    real, imag = propagator(extent)
    left = halves(np.concatenate([real, imag], axis=0))
    right = halves(np.concatenate([real, imag], axis=1))
    left_table = np.concatenate([left[0], left[0], left[1]], axis=1)
    right_table = np.concatenate([right[0], right[0], right[1]], axis=0)
    return left_table, right_table


def split(values):
    high = values.astype(bf16)
    low = (values - high.astype(f32)).astype(bf16)
    return high, low


def propagate(fields, left, right):
    side = fields[0][0].shape[0]
    high, low = split(jnp.concatenate([part for field in fields for part in field], axis=1))
    middle = jnp.dot(left, jnp.concatenate([high, low, high], axis=0), preferred_element_type=f32)
    rows = []
    for index in range(len(fields)):
        by_real = middle[:side, 2 * index * side : 2 * (index + 1) * side]
        by_imag = middle[side:, 2 * index * side : 2 * (index + 1) * side]
        rows.append(by_real[:, :side] - by_imag[:, side:])
        rows.append(by_real[:, side:] + by_imag[:, :side])
    high, low = split(jnp.concatenate(rows, axis=0))
    result = jnp.dot(jnp.concatenate([high, low, high], axis=1), right, preferred_element_type=f32)
    results = []
    for index in range(len(fields)):
        real = result[2 * index * side : (2 * index + 1) * side]
        imag = result[(2 * index + 1) * side : 2 * (index + 1) * side]
        results.append((real[:, :side] - imag[:, side:], real[:, side:] + imag[:, :side]))
    return results


def multiply(first, second):
    return (
        first[0] * second[0] - first[1] * second[1],
        first[0] * second[1] + first[1] * second[0],
    )


def turned(values, down, across):
    return pltpu.roll(pltpu.roll(values, down, 0), across, 1)


def turned_back(values, down, across):
    rows, columns = values.shape
    return turned(values, lax.rem(rows - down, rows), lax.rem(columns - across, columns))


def stretch(column, side, width):
    base = pl.multiple_of(column // LANES * LANES, LANES)
    after = pl.multiple_of(jnp.minimum(base + side, width - LANES), LANES)
    return base, after, column - base


def this_place():
    section = lax.axis_index("depth")
    return section % 2, section // 2


def column_of(places, width, *index):
    return lax.rem(places[index], width)


def window_place(places, home, turn, strip, width, flip=0):
    core, _ = this_place()
    regions = lax.axis_size("scan")
    source = lax.rem(lax.axis_index("scan") - home + regions, regions)
    value = places[core ^ flip, turn]
    return value // width - source * strip, lax.rem(lax.rem(value, width), LANES)


def pick_kernel(waves, out, buffer, arrived):
    core, half = this_place()
    copy = pltpu.make_async_copy(waves.at[core, 1 - half], buffer, arrived)
    copy.start()
    copy.wait()
    out[...] = buffer[...].astype(bf16)


def extract_kernel(reach, *refs):
    places, (strip, *outs) = refs[:reach], refs[reach:]
    count, _, rows, side = outs[0].shape
    width = strip.shape[2]
    core, _ = this_place()
    lane = lax.broadcasted_iota(jnp.int32, (rows, LANES), 1)
    for flip in range(2):
        for step in range(reach):
            out = outs[flip * reach + step]
            for turn in range(count):
                column = column_of(places[step], width, core ^ flip, turn)
                base, after, begin = stretch(column, side, width)
                rest = pl.multiple_of(base + LANES, LANES)
                for plane in range(2):
                    first = strip[plane, :, pl.ds(base, LANES)]
                    again = strip[plane, :, pl.ds(after, LANES)]
                    out[turn, plane, :, :LANES] = jnp.where(lane < begin, again, first).astype(bf16)
                    out[turn, plane, :, LANES:] = strip[plane, :, pl.ds(rest, side - LANES)].astype(
                        bf16
                    )


def start_kernel(home, strip, width, places, probe, *refs):
    adjoints, (left, right, out) = refs[:-3], refs[-3:]
    _, half = this_place()

    @pl.when(half == 0)
    def _():
        for turn in range(len(adjoints)):
            down, across = window_place(places, home, turn, strip, width)
            for plane in range(2):
                out[turn, plane] = turned(probe[plane], down, across)

    @pl.when(half != 0)
    def _():
        fields = []
        for turn, adjoint in enumerate(adjoints):
            down, across = window_place(places, home, turn, strip, width)
            real, imag = (turned(adjoint[plane].astype(f32), down, across) for plane in range(2))
            fields.append((real, -imag))
        for turn, field in enumerate(propagate(fields, left[...], right[...])):
            out[turn, 0], out[turn, 1] = field


def pair(ref, *index):
    return ref[(*index, 0)].astype(f32), ref[(*index, 1)].astype(f32)


def own_first():
    core, half = this_place()
    return jnp.where(core == half, 0, 1)


def near_kernel(home, width, places, start, left, right, *refs):
    pieces, (frames, waves, sent) = refs[:-3], refs[-3:]
    reach = len(pieces) // 2
    count, _, strip, side = pieces[0].shape
    own = own_first()
    row = lax.broadcasted_iota(jnp.int32, (strip, side), 0)
    for flip in range(2):
        parts = pieces[flip * reach : (flip + 1) * reach]
        for turn in range(count):
            down, _ = window_place(places, home, turn, strip, width)
            for plane in range(2):
                first = parts[0][turn, plane].astype(f32)
                again = parts[-1][turn, plane].astype(f32)
                frames[own ^ flip, turn, plane, :strip] = jnp.where(
                    row < down, again, first
                ).astype(bf16)
                for step in range(1, reach - 1):
                    frames[own ^ flip, turn, plane, step * strip : (step + 1) * strip] = parts[step][
                        turn, plane
                    ]
    fields = [multiply(pair(frames, 0, turn), pair(start, turn)) for turn in range(count)]
    for turn, field in enumerate(propagate(fields, left[...], right[...])):
        waves[turn, 0], waves[turn, 1] = field
        real, imag = multiply(pair(frames, 1, turn), field)
        sent[turn, 0] = real.astype(bf16)
        sent[turn, 1] = imag.astype(bf16)


def far_kernel(start, left, right, frames, waves, arrived, kept, given, last):
    count = start.shape[0]
    own = own_first()
    fields = propagate([pair(arrived, turn) for turn in range(count)], left[...], right[...])
    outer, inner = [], []
    for turn, field in enumerate(fields):
        outer.append(multiply(pair(waves, turn), field))
        inner.append(multiply(pair(frames, 1, turn), field))
    for turn, field in enumerate(propagate(inner, left[...], right[...])):
        first = multiply(pair(start, turn), field)
        for plane, sign in ((0, 1.0), (1, -1.0)):
            mine = jnp.where(own == 0, first[plane], outer[turn][plane])
            other = jnp.where(own == 0, outer[turn][plane], first[plane])
            kept[turn, plane] = (mine * sign).astype(bf16)
            given[turn, plane] = (other * sign).astype(bf16)
        last[turn, 0], last[turn, 1] = multiply(pair(frames, 0, turn), field)


def part_kernel(home, width, places, kept, arrived, *outs):
    _, count, _, strip, side = outs[0].shape
    row = lax.broadcasted_iota(jnp.int32, (strip, side), 0)
    for flip, windows in enumerate((kept, arrived)):
        for turn in range(count):
            down, _ = window_place(places, home, turn, strip, width, flip)
            for plane in range(2):
                ends = windows[turn, plane, :strip].astype(f32)
                outs[0][flip, turn, plane] = jnp.where(row < down, 0.0, ends).astype(bf16)
                outs[-1][flip, turn, plane] = jnp.where(row < down, ends, 0.0).astype(bf16)
                for step in range(1, len(outs) - 1):
                    outs[step][flip, turn, plane] = windows[
                        turn, plane, step * strip : (step + 1) * strip
                    ]


def probe_kernel(home, strip, width, places, waves, near, away, sent, total):
    core, half = this_place()
    weight = jnp.where(half == 0, 1.0, 0.0)
    for plane, sign in ((0, weight), (1, -weight)):
        parts = []
        for turn in range(waves.shape[0]):
            down, across = window_place(places, home, turn, strip, width)
            parts.append(turned_back(waves[turn, plane], down, across))
        total[plane] = sum(parts) * sign
    height = near.shape[1]
    for index, out in enumerate((near, away)):
        for plane in range(2):
            mine = pl.multiple_of((2 * index + core) * height, height)
            other = pl.multiple_of((2 * index + (core ^ 1)) * height, height)
            out[plane] = total[plane, pl.ds(mine, height)]
            sent[index, plane] = total[plane, pl.ds(other, height)].astype(bf16)


def deposit_kernel(reach, *refs):
    places, pieces, (out, total, done) = refs[:reach], refs[reach : 2 * reach], refs[2 * reach :]
    _, count, _, strip, side = pieces[0].shape
    width = out.shape[2]
    core, _ = this_place()
    stretches = []
    for step in range(reach):
        for flip in range(2):
            for turn in range(count):
                column = column_of(places[step], width, core ^ flip, turn)
                stretches.append((pieces[step].at[flip, turn], *stretch(column, side, width)))
    height = strip // 4
    lane = lax.broadcasted_iota(jnp.int32, (height, LANES), 1)
    copies = []
    for plane in range(2):
        for start in range(0, strip, height):
            rows = pl.ds(start, height)
            total[plane, rows] = jnp.zeros((height, width), f32)
            for piece, base, after, begin in stretches:
                rest = pl.multiple_of(base + LANES, LANES)
                ends = piece[plane, rows, :LANES].astype(f32)
                total[plane, rows, pl.ds(base, LANES)] += jnp.where(lane < begin, 0.0, ends)
                total[plane, rows, pl.ds(rest, side - LANES)] += piece[plane, rows, LANES:].astype(
                    f32
                )
                total[plane, rows, pl.ds(after, LANES)] += jnp.where(lane < begin, ends, 0.0)
            copy = pltpu.make_async_copy(
                total.at[plane, rows], out.at[plane, rows], done.at[len(copies)]
            )
            copy.start()
            copies.append(copy)
    for copy in copies:
        copy.wait()


def local(transmission, probe, exit_adjoint, scan_row, scan_col):
    depth = lax.axis_size("depth")
    regions = lax.axis_size("scan")
    strip, width = transmission.shape[2:]
    side = probe.shape[1]
    reach = side // strip + 1
    home = reach // 2
    count = scan_row.shape[1]
    assert transmission.shape[0] == 1 and depth == 4 and scan_row.shape[0] == 2
    assert side == 2 * LANES and count == 2

    half = lax.axis_index("depth") // (depth // 2)
    once = lax.axis_index("depth") // depth + 1

    def along_scan(value, by):
        return lax.ppermute(value, "scan", [(i, (i + by) % regions) for i in range(regions)])

    def across(value, flip, by, sections=range(depth)):
        if flip == 0 and by == 0:
            return value
        route = [
            (d * regions + i, (d ^ flip) * regions + (i + by) % regions)
            for d in sections
            for i in range(regions)
        ]
        return lax.ppermute(value, ("depth", "scan"), route)

    smem = pl.BlockSpec(memory_space=pltpu.SMEM)
    vmem = pl.BlockSpec(memory_space=pltpu.VMEM)

    def call(kernel, out_shape, in_specs, flops, name, scratch=(), out_spec=vmem):
        return pl.pallas_call(
            kernel,
            out_shape=out_shape,
            in_specs=in_specs,
            out_specs=jax.tree.map(lambda _: out_spec, out_shape),
            scratch_shapes=scratch,
            compiler_params=pltpu.CompilerParams(vmem_limit_bytes=24 * 1024 * 1024),
            cost_estimate=pl.CostEstimate(flops=flops, bytes_accessed=4 << 20, transcendentals=0),
            name=name,
        )

    shape = jax.ShapeDtypeStruct
    piece = shape((count, 2, strip, side), bf16)
    wave = (2, side, side)
    field = (count,) + wave
    left, right = (jnp.asarray(table) for table in tables(side))
    lower = range(depth // 2)

    adjoint = call(
        pick_kernel,
        shape(wave, bf16),
        [pl.BlockSpec(memory_space=pltpu.HBM)],
        1 << 20,
        "pick",
        [pltpu.VMEM(wave, f32), pltpu.SemaphoreType.DMA],
    )(exit_adjoint)
    packed = scan_row * width + scan_col
    adjoint, packed = lax.optimization_barrier((adjoint, packed))
    adjoint = along_scan(adjoint, home)
    places = [packed] + [along_scan(packed, step) for step in range(1, reach)]

    order = [(flip, step) for flip in range(2) for step in range(reach)]
    far_first = sorted(order, key=lambda key: -abs(key[1] - home))
    pieces = call(
        functools.partial(extract_kernel, reach),
        [piece] * len(order),
        [smem] * reach + [vmem],
        1 << 26,
        "extract",
    )(*places, transmission[0])
    pieces = dict(zip(order, pieces))
    adjoint, pieces[0, home] = lax.optimization_barrier((adjoint, pieces[0, home]))
    flipped = lax.fori_loop(0, once, lambda _, held: across(held, 2, 0, lower), adjoint)
    adjoints = [adjoint, flipped]
    for flip, step in far_first:
        pieces[flip, step] = across(pieces[flip, step], flip, home - step)

    start = call(
        functools.partial(start_kernel, home, strip, width),
        shape(field, f32),
        [smem] + [vmem] * (3 + count),
        1 << 30,
        "start",
    )(places[home], probe, *adjoints, left, right)
    frames, waves, sent = call(
        functools.partial(near_kernel, home, width),
        [shape((2,) + field, bf16), shape(field, f32), shape(field, bf16)],
        [smem] + [vmem] * (3 + len(order)),
        1 << 31,
        "near",
    )(places[home], start, left, right, *(pieces[key] for key in order))
    arrived = across(sent, 2, 0)
    kept, given, last = call(
        far_kernel,
        [shape(field, bf16)] * 2 + [shape(field, f32)],
        [vmem] * 6,
        1 << 32,
        "far",
    )(start, left, right, frames, waves, arrived)
    parts = call(
        functools.partial(part_kernel, home, width),
        [shape((2,) + piece.shape, bf16)] * reach,
        [smem] + [vmem] * 2,
        1 << 26,
        "part",
    )(places[home], kept, across(given, 1, 0))
    parts = list(parts)

    height = side // depth
    near, away, probe_sent = call(
        functools.partial(probe_kernel, home, strip, width),
        [shape((2, height, side), f32)] * 2 + [shape((2, 2, height, side), bf16)],
        [smem, vmem],
        1 << 26,
        "probe",
        [pltpu.VMEM(wave, f32)],
    )(places[home], last)
    returned = [across(part, 0, step - home) for step, part in enumerate(parts)]

    def probe_rounds(_, held):
        near, away, given = held
        given = given.astype(f32)
        away = across((away + given[1]).astype(bf16), 2, 0, lower).astype(f32)
        total = jnp.where(half == 0, near + given[0], away)
        if regions & (regions - 1):
            total = lax.psum(total, "scan")
        else:
            span = 1
            while span < regions:
                rounded = total.astype(bf16)
                route = [(i, i ^ span) for i in range(regions)]
                total = rounded.astype(f32) + lax.ppermute(rounded, "scan", route).astype(f32)
                span *= 2
        return total, away, held[2]

    near, parts[home] = lax.optimization_barrier((near, parts[home]))
    probe_grad, *_ = lax.fori_loop(
        0, once, probe_rounds, (near, away, across(probe_sent, 1, 0))
    )
    probe_grad, returned[home] = lax.optimization_barrier((probe_grad, parts[home]))
    object_grad = call(
        functools.partial(deposit_kernel, reach),
        shape(transmission.shape[1:], f32),
        [smem] * reach + [vmem] * reach,
        1 << 26,
        "deposit",
        [pltpu.VMEM(transmission.shape[1:], f32), pltpu.SemaphoreType.DMA((8,))],
        pl.BlockSpec(memory_space=pltpu.HBM),
    )(*places, *returned)
    return object_grad[None], probe_grad


def solution(mesh):
    placed = (
        P("depth", None, "scan", None),
        P(),
        P(None, "scan", None, None, None),
        P(None, "scan"),
        P(None, "scan"),
    )
    return jax.shard_map(
        local,
        mesh=mesh,
        in_specs=placed,
        out_specs=(P("depth", None, "scan", None), P(None, "depth", None)),
        check_vma=False,
    )
```

time: 830 us -> 102 us (0.12)
  local copies, waits for them, and re-layouts: 206 us -> 4.51 us
  waiting for transfers between devices: 235 us -> 44.8 us
  blocking collectives: 121 us -> 0 us
  matrix products: 93.6 us -> 0 us
  other arithmetic: 51.6 us -> 0.12 us
  loops' own time: 40.9 us -> 0.06 us
  starting transfers between devices: 60.2 us -> 36 us
  Pallas kernels: 0 us -> 15.2 us
  between operations: 14.2 us -> 0.86 us
    ppermute x18 -> x26, waiting for transfers between devices: 196 us -> 44.8 us  [the longest x18 25.1 us: across(): return lax.ppermute(value, ('depth', 'scan'), route)]
    psum x1 -> x0, blocking collectives: 121 us -> none  [local(): partial_total = lax.psum(probe_total, 'scan')]
    dot_general x84 -> x0, matrix products: 93.6 us -> none  [the longest x40 55.6 us: apply_right(): jnp.einsum('kab,nb->kan', values, matrix, precision=lax.Precision.HIGHEST...]
    gather x60 -> x0, local copies, waits for them, and re-layouts: 74.4 us -> none
    dynamic_update_slice x10 -> x0, local copies, waits for them, and re-layouts: 60.9 us -> none  [place(): lax.dynamic_update_slice(buffer_now, before + pieces[position][None], anc...]
    another operation x17 -> x2, loops' own time: 40.9 us -> 0.06 us  [the longest x1 0.05 us: local(): lax.fori_loop(0, once, probe_rounds, (near, away, across(probe_sent, 1, 0)))]
    reduce_scatter x1 -> x0, waiting for transfers between devices: 39.7 us -> none  [local(): lax.psum_scatter(partial_total.astype(jnp.bfloat16), 'depth', scatter_dim...]
    dynamic_slice x35 -> x0, local copies, waits for them, and re-layouts: 26.4 us -> none  [the longest x20 11.7 us: place(): anchor = (layer, 0, row_block[position], col_block[position])]
  transfers between devices with their start and end apart: 19 -> 26, of which waited for: 8 -> 13; matrix products, arithmetic and copies ran while one was open for 13% -> 0% of each run, Pallas kernels for 0% -> 4%
where the time goes in v1:
time: 102 us
  waiting for transfers between devices  44.8 us (44%)
  starting transfers between devices  36 us (35%)
  Pallas kernels  15.2 us (15%)
  local copies, waits for them, and re-layouts  4.51 us (4%)
    ppermute x18, waiting for transfers between devices, across(): return lax.ppermute(value, ('depth', 'scan'), route)  25.1 us
    ppermute x18, starting transfers between devices, across(): return lax.ppermute(value, ('depth', 'scan'), route)  24.9 us
    ppermute x3, waiting for transfers between devices, probe_rounds(): lax.ppermute(rounded, 'scan', route).astype(f32)  15 us
    ppermute x5, starting transfers between devices, along_scan(): lax.ppermute(value, 'scan', [(i, (i + by) % regions) for i in range(regio...  8.99 us
    pallas_call x1, Pallas kernels, local(): call(far_kernel, [shape(field, bf16)] * 2 + [shape(field, f32)], [vmem] *...  5.51 us
    ppermute x5, waiting for transfers between devices, along_scan(): lax.ppermute(value, 'scan', [(i, (i + by) % regions) for i in range(regio...  4.75 us
    unnamed x19, local copies, waits for them, and re-layouts  4.49 us
    pallas_call x1, Pallas kernels, local(): call(functools.partial(deposit_kernel, reach), shape(transmission.shape[1...  3.03 us
  transfers between devices with their start and end apart: 26, of which 13 were waited for; matrix products, arithmetic and copies ran while one was open for 0% of the time, Pallas kernels for 4%

profile of v1, /device:TPU:0, one launch (start us, length us, event | category | flops | bytes accessed | tf_op | source)
XLA Modules:
  0.0 101.6 jit_solution(17886855447027459279)
XLA Ops:
  0.6 1.6 %copy-done = f32[2,2,2,256,256]{4,3,2,1,0:T(8,128)S(1)} copy-done((f32[2,2,2,256,256]{4,3,2,1,0:T(8,128)S(1)}, f32[2,2,2,256,256]{4,3,2,1,0:T(8,128)}, u32[]{:S(2)}) %copy-start) | copy-done | bytes 2097176
  2.2 0.1 pick.1
  2.3 0.6 copy-done.7
  2.9 0.0 copy-done.8
  2.9 3.0 %collective-permute-start.9 = (bf16[2,256,256]{2,1,0:T(8,128)(2,1)S(1)}, bf16[2,256,256]{2,1,0:T(8,128)(2,1)S(1)}, u32[]{:S(2)}, u32[]{:S(2)}) collective-permute-start(bf16[2,256,256]{2,1,0:T(8,128)(2,1)S(1)} %pick.1), channel_id=1, source_target_pairs={{0,2},{1,3},{2,4},{3,5},{4,6},{5,7},{6,0},{7,1},{8,10},{9,11},{10,... | collective-permute-start | bytes 786440 | tf_op jit(solution)/shard_map/ppermute | solution.py:297
  5.9 2.6 %collective-permute-start.8 = (s32[2,2]{1,0:T(2,128)S(1)}, s32[2,2]{1,0:T(2,128)S(1)}, u32[]{:S(2)}, u32[]{:S(2)}) collective-permute-start(s32[2,2]{1,0:T(2,128)S(1)} %multiply_add_fusion.refs_0_), channel_id=1, source_target_pairs={{0,4},{1,5},{2,6},{3,7},{4,0},{5,1},{6,2},{7,3},{8,12},{9,13},{10,... | collective-permute-start | bytes 56 | tf_op jit(solution)/shard_map/ppermute | solution.py:297
  8.5 1.2 %collective-permute-start.7 = (s32[2,2]{1,0:T(2,128)S(1)}, s32[2,2]{1,0:T(2,128)S(1)}, u32[]{:S(2)}, u32[]{:S(2)}) collective-permute-start(s32[2,2]{1,0:T(2,128)S(1)} %multiply_add_fusion.refs_0_), channel_id=1, source_target_pairs={{0,3},{1,4},{2,5},{3,6},{4,7},{5,0},{6,1},{7,2},{8,11},{9,12},{10,... | collective-permute-start | bytes 56 | tf_op jit(solution)/shard_map/ppermute | solution.py:297
  9.7 0.7 collective-permute-start.6
  10.4 1.5 %collective-permute-start.5 = (s32[2,2]{1,0:T(2,128)S(1)}, s32[2,2]{1,0:T(2,128)S(1)}, u32[]{:S(2)}, u32[]{:S(2)}) collective-permute-start(s32[2,2]{1,0:T(2,128)S(1)} %multiply_add_fusion.refs_0_), channel_id=1, source_target_pairs={{0,1},{1,2},{2,3},{3,4},{4,5},{5,6},{6,7},{7,0},{8,9},{9,10},{10,1... | collective-permute-start | bytes 56 | tf_op jit(solution)/shard_map/ppermute | solution.py:297
  11.9 0.0 collective-permute-done.8.refs_4_
  11.9 2.0 %collective-permute-done.7.refs_3_ = s32[2,2]{1,0:T(2,128)S(1)} collective-permute-done((s32[2,2]{1,0:T(2,128)S(1)}, s32[2,2]{1,0:T(2,128)S(1)}, u32[]{:S(2)}, u32[]{:S(2)}) %collective-permute-start.7) | collective-permute-done | bytes 48 | tf_op jit(solution)/shard_map/ppermute | solution.py:297
  14.0 1.1 %collective-permute-done.6.refs_2_.places = s32[2,2]{1,0:T(2,128)S(1)} collective-permute-done((s32[2,2]{1,0:T(2,128)S(1)}, s32[2,2]{1,0:T(2,128)S(1)}, u32[]{:S(2)}, u32[]{:S(2)}) %collective-permute-start.6) | collective-permute-done | bytes 48 | tf_op jit(solution)/shard_map/ppermute | solution.py:297
  15.1 1.6 %collective-permute-done.5.refs_1_ = s32[2,2]{1,0:T(2,128)S(1)} collective-permute-done((s32[2,2]{1,0:T(2,128)S(1)}, s32[2,2]{1,0:T(2,128)S(1)}, u32[]{:S(2)}, u32[]{:S(2)}) %collective-permute-start.5) | collective-permute-done | bytes 48 | tf_op jit(solution)/shard_map/ppermute | solution.py:297
  16.7 1.2 %extract.1 = (bf16[2,2,64,256]{3,2,1,0:T(8,128)(2,1)S(1)}, bf16[2,2,64,256]{3,2,1,0:T(8,128)(2,1)S(1)}, bf16[2,2,64,256]{3,2,1,0:T(8,128)(2,1)S(1)}, bf16[2,2,64...) custom-call(s32[2,2]{1,0:T(2,128)S(1)} %multiply_add_fusion.refs_0_,, ...), custom_call_target="tpu_custom_call" | custom-call | flops 67108864 | bytes 4194304 | tf_op jit(solution)/shard_map/extract/pallas_call | solution.py:346
  17.8 0.1 collective-permute-start.10
  17.9 0.5 collective-permute-start.11
  18.4 4.2 %collective-permute-start.12 = (bf16[2,2,64,256]{3,2,1,0:T(8,128)(2,1)S(1)}, bf16[2,2,64,256]{3,2,1,0:T(8,128)(2,1)S(1)}, u32[]{:S(2)}, u32[]{:S(2)}) collective-permute-start(bf16[2,2,64,256]{3,2,1,0:T(8,128)(2,1)S(1)} %get-tuple-element.135), channel_id=1, source_target_pairs={{0,7},{1,0},{2,1},{3,2},{4,3},{5,4},{6,5},{7,6},{8,15},{9,8},{10,9... | collective-permute-start | bytes 393224 | tf_op jit(solution)/shard_map/ppermute | solution.py:307
  22.7 2.0 %collective-permute-start.13 = (bf16[2,2,64,256]{3,2,1,0:T(8,128)(2,1)S(1)}, bf16[2,2,64,256]{3,2,1,0:T(8,128)(2,1)S(1)}, u32[]{:S(2)}, u32[]{:S(2)}) collective-permute-start(bf16[2,2,64,256]{3,2,1,0:T(8,128)(2,1)S(1)} %get-tuple-element.136), channel_id=1, source_target_pairs={{0,6},{1,7},{2,0},{3,1},{4,2},{5,3},{6,4},{7,5},{8,14},{9,15},{10,... | collective-permute-start | bytes 393224 | tf_op jit(solution)/shard_map/ppermute | solution.py:307
  24.6 0.0 collective-permute-done.9.refs_0_
  24.7 0.1 collective-permute-start.14
  24.7 1.3 %collective-permute-done.10.refs_0_ = bf16[2,2,64,256]{3,2,1,0:T(8,128)(2,1)S(1)} collective-permute-done((bf16[2,2,64,256]{3,2,1,0:T(8,128)(2,1)S(1)}, bf16[2,2,64,256]{3,2,1,0:T(8,128)(2,1)S(1)}, u32[]{:S(2)}, u32[]{:S(2)}) %collective-permute-start.10) | collective-permute-done | bytes 131104 | tf_op jit(solution)/shard_map/ppermute | solution.py:307
  26.0 0.0 collective-permute-start.15
  26.0 1.1 %collective-permute-done.11.refs_1_ = bf16[2,2,64,256]{3,2,1,0:T(8,128)(2,1)S(1)} collective-permute-done((bf16[2,2,64,256]{3,2,1,0:T(8,128)(2,1)S(1)}, bf16[2,2,64,256]{3,2,1,0:T(8,128)(2,1)S(1)}, u32[]{:S(2)}, u32[]{:S(2)}) %collective-permute-start.11) | collective-permute-done | bytes 131104 | tf_op jit(solution)/shard_map/ppermute | solution.py:307
  27.1 0.0 collective-permute-start.16
  27.1 3.4 %collective-permute-start.17 = (bf16[2,2,64,256]{3,2,1,0:T(8,128)(2,1)S(1)}, bf16[2,2,64,256]{3,2,1,0:T(8,128)(2,1)S(1)}, u32[]{:S(2)}, u32[]{:S(2)}) collective-permute-start(bf16[2,2,64,256]{3,2,1,0:T(8,128)(2,1)S(1)} %get-tuple-element.140), channel_id=1, source_target_pairs={{0,15},{1,8},{2,9},{3,10},{4,11},{5,12},{6,13},{7,14},{8,7},{9,0},... | collective-permute-start | bytes 393224 | tf_op jit(solution)/shard_map/ppermute | solution.py:307
  30.6 9.6 %while.24 = (s32[]{:T(128)}, bf16[2,256,256]{2,1,0:T(8,128)(2,1)S(1)}, s32[]{:T(128)}, s32[]{:T(128)}) while((s32[]{:T(128)}, bf16[2,256,256]{2,1,0:T(8,128)(2,1)S(1)}, s32[]{:T(128)}, s32[]{:T(128)}) %tuple.53), condition=%wide.region_1.2_spmd, body=%wide.region_0.1_spmd.sunk | while | flops 2 | bytes 1572957 | solution.py:355
  30.6 3.4 %collective-permute-start = (bf16[2,256,256]{2,1,0:T(8,128)(2,1)S(1)}, bf16[2,256,256]{2,1,0:T(8,128)(2,1)S(1)}, u32[]{:S(2)}, u32[]{:S(2)}) collective-permute-start(bf16[2,256,256]{2,1,0:T(8,128)(2,1)S(1)} %get-tuple-element.248), channel_id=1, source_target_pairs={{0,16},{1,17},{2,18},{3,19},{4,20},{5,21},{6,22},{7,23},{8,24},{9,... | collective-permute-start | bytes 786440 | tf_op jit(solution)/shard_map/while/body/ppermute | solution.py:307
  34.0 6.1 %collective-permute-done = bf16[2,256,256]{2,1,0:T(8,128)(2,1)S(1)} collective-permute-done((bf16[2,256,256]{2,1,0:T(8,128)(2,1)S(1)}, bf16[2,256,256]{2,1,0:T(8,128)(2,1)S(1)}, u32[]{:S(2)}, u32[]{:S(2)}) %collective-permute-start) | collective-permute-done | bytes 262176 | tf_op jit(solution)/shard_map/while/body/ppermute | solution.py:307
  40.1 0.1 collective-permute-start.18
  40.2 0.0 copy-start.3
  40.2 1.1 %copy-done.3 = bf16[768,512]{1,0:T(8,128)(2,1)S(1)} copy-done((bf16[768,512]{1,0:T(8,128)(2,1)S(1)}, bf16[768,512]{1,0:T(8,128)(2,1)}, u32[]{:S(2)}) %copy-start.3) | copy-done | bytes 786456
  41.4 1.1 %copy-done.5 = bf16[512,768]{1,0:T(8,128)(2,1)S(1)} copy-done((bf16[512,768]{1,0:T(8,128)(2,1)S(1)}, bf16[512,768]{1,0:T(8,128)(2,1)}, u32[]{:S(2)}) %copy-start.5) | copy-done | bytes 786456
  42.5 1.0 start.1
  43.5 0.0 collective-permute-done.15.refs_6_
  43.5 0.0 collective-permute-done.16.refs_7_
  43.5 2.3 %collective-permute-done.18.refs_9_ = bf16[2,2,64,256]{3,2,1,0:T(8,128)(2,1)S(1)} collective-permute-done((bf16[2,2,64,256]{3,2,1,0:T(8,128)(2,1)S(1)}, bf16[2,2,64,256]{3,2,1,0:T(8,128)(2,1)S(1)}, u32[]{:S(2)}, u32[]{:S(2)}) %collective-permute-start.18) | collective-permute-done | bytes 131104 | tf_op jit(solution)/shard_map/ppermute | solution.py:307
  45.8 2.7 %near.1 = (bf16[2,2,2,256,256]{4,3,2,1,0:T(8,128)(2,1)S(1)}, f32[2,2,256,256]{3,2,1,0:T(8,128)S(1)}, bf16[2,2,256,256]{3,2,1,0:T(8,128)(2,1)S(1)}) custom-call(s32[2,2]{1,0:T(2,128)S(1)} %collective-permute-done.6.refs_2_.places, f32[2,2,256,256]{3,2,1,0:T(8,128)S(1)} %start.1, bf16[512,768]{1,0:T(8,128)(2,1)S(1)} %copy-done.5, ...), custom_call_target="tpu_custom_call" | custom-call | flops 2147483648 | bytes 4194304 | tf_op jit(solution)/shard_map/near/pallas_call | solution.py:367
  48.6 2.5 %collective-permute-start.19 = (bf16[2,2,256,256]{3,2,1,0:T(8,128)(2,1)S(1)}, bf16[2,2,256,256]{3,2,1,0:T(8,128)(2,1)S(1)}, u32[]{:S(2)}, u32[]{:S(2)}) collective-permute-start(bf16[2,2,256,256]{3,2,1,0:T(8,128)(2,1)S(1)} %get-tuple-element.144), channel_id=1, source_target_pairs={{0,16},{1,17},{2,18},{3,19},{4,20},{5,21},{6,22},{7,23},{8,24},{9,... | collective-permute-start | bytes 1572872 | tf_op jit(solution)/shard_map/ppermute | solution.py:307
  51.1 12.0 %collective-permute-done.19.arrived = bf16[2,2,256,256]{3,2,1,0:T(8,128)(2,1)S(1)} collective-permute-done((bf16[2,2,256,256]{3,2,1,0:T(8,128)(2,1)S(1)}, bf16[2,2,256,256]{3,2,1,0:T(8,128)(2,1)S(1)}, u32[]{:S(2)}, u32[]{:S(2)}) %collective-permute-start.19) | collective-permute-done | bytes 524320 | tf_op jit(solution)/shard_map/ppermute | solution.py:307
  63.2 5.5 %far.1 = (bf16[2,2,256,256]{3,2,1,0:T(8,128)(2,1)S(1)}, bf16[2,2,256,256]{3,2,1,0:T(8,128)(2,1)S(1)}, f32[2,2,256,256]{3,2,1,0:T(8,128)S(1)}) custom-call(f32[2,2,256,256]{3,2,1,0:T(8,128)S(1)} %start.1, bf16[512,768]{1,0:T(8,128)(2,1)S(1)} %copy-done.5, bf16[768,512]{1,0:T(8,128)(2,1)S(1)} %copy-done.4, ...), custom_call_target="tpu_custom_call" | custom-call | flops 4294967296 | bytes 4194304 | tf_op jit(solution)/shard_map/far/pallas_call | solution.py:375
  68.7 0.1 collective-permute-start.20
  68.8 1.0 %probe.3 = (f32[2,64,256]{2,1,0:T(8,128)S(1)}, f32[2,64,256]{2,1,0:T(8,128)S(1)}, bf16[2,2,64,256]{3,2,1,0:T(8,128)(2,1)S(1)}) custom-call(s32[2,2]{1,0:T(2,128)S(1)} %collective-permute-done.6.refs_2_.places, f32[2,2,256,256]{3,2,1,0:T(8,128)S(1)} %get-tuple-element.149.waves), custom_call_target="tpu_custom_call" | custom-call | flops 67108864 | bytes 4194304 | tf_op jit(solution)/shard_map/probe/pallas_call | solution.py:392
  69.8 0.6 collective-permute-start.23
  70.4 0.3 collective-permute-done.20.arrived
  70.7 0.7 part.1
  71.4 2.3 %collective-permute-start.21 = (bf16[2,2,2,64,256]{4,3,2,1,0:T(8,128)(2,1)S(1)}, bf16[2,2,2,64,256]{4,3,2,1,0:T(8,128)(2,1)S(1)}, u32[]{:S(2)}, u32[]{:S(2)}) collective-permute-start(bf16[2,2,2,64,256]{4,3,2,1,0:T(8,128)(2,1)S(1)} %get-tuple-element.147), channel_id=1, source_target_pairs={{0,6},{1,7},{2,0},{3,1},{4,2},{5,3},{6,4},{7,5},{8,14},{9,15},{10,... | collective-permute-start | bytes 786440 | tf_op jit(solution)/shard_map/ppermute | solution.py:307
  73.7 0.0 collective-permute-start.22
  73.7 2.0 %collective-permute-start.24 = (bf16[2,2,2,64,256]{4,3,2,1,0:T(8,128)(2,1)S(1)}, bf16[2,2,2,64,256]{4,3,2,1,0:T(8,128)(2,1)S(1)}, u32[]{:S(2)}, u32[]{:S(2)}) collective-permute-start(bf16[2,2,2,64,256]{4,3,2,1,0:T(8,128)(2,1)S(1)} %get-tuple-element.158), channel_id=1, source_target_pairs={{0,1},{1,2},{2,3},{3,4},{4,5},{5,6},{6,7},{7,0},{8,9},{9,10},{10,1... | collective-permute-start | bytes 786440 | tf_op jit(solution)/shard_map/ppermute | solution.py:307
  75.7 0.0 collective-permute-start.25
  75.7 0.0 collective-permute-done.23
  75.7 22.8 %while.25 = (s32[]{:T(128)}, f32[2,64,256]{2,1,0:T(8,128)S(1)}, f32[2,64,256]{2,1,0:T(8,128)S(1)}, s32[]{:T(128)}, pred[]{:T(512)}, /*index=5*/bf16[2,2,64,256]{3,2,1,0:T(8,128)(2,1)S(1)}, s32[]{:T(128)}) while((s32[]{:T(128)}, f32[2,64,256]{2,1,0:T(8,128)S(1)}, f32[2,64,256]{2,1,0:T(8,128)S(1)}, s32[]{:T(128)}, pred[]{:T(512)}, ...), condition=%wide.region_3.4_spmd, body=%wide.region_2.3_spmd.sunk | while | flops 589826 | bytes 2949358 | solution.py:419
  75.7 3.6 %collective-permute-start.1 = (bf16[2,64,256]{2,1,0:T(8,128)(2,1)S(1)}, bf16[2,64,256]{2,1,0:T(8,128)(2,1)S(1)}, u32[]{:S(2)}, u32[]{:S(2)}) collective-permute-start(bf16[2,64,256]{2,1,0:T(8,128)(2,1)S(1)} %fusion.7), channel_id=1, source_target_pairs={{0,16},{1,17},{2,18},{3,19},{4,20},{5,21},{6,22},{7,23},{8,24},{9,... | collective-permute-start | bytes 196616 | tf_op jit(solution)/shard_map/while/body/ppermute | solution.py:307
  79.4 1.9 %collective-permute-done.1 = bf16[2,64,256]{2,1,0:T(8,128)(2,1)S(1)} collective-permute-done((bf16[2,64,256]{2,1,0:T(8,128)(2,1)S(1)}, bf16[2,64,256]{2,1,0:T(8,128)(2,1)S(1)}, u32[]{:S(2)}, u32[]{:S(2)}) %collective-permute-start.1) | collective-permute-done | bytes 65568 | tf_op jit(solution)/shard_map/while/body/ppermute | solution.py:307
  81.3 0.8 collective-permute-start.2
  82.1 6.6 %collective-permute-done.2 = bf16[2,64,256]{2,1,0:T(8,128)(2,1)S(1)} collective-permute-done((bf16[2,64,256]{2,1,0:T(8,128)(2,1)S(1)}, bf16[2,64,256]{2,1,0:T(8,128)(2,1)S(1)}, u32[]{:S(2)}, u32[]{:S(2)}) %collective-permute-start.2) | collective-permute-done | bytes 65568 | tf_op jit(solution)/shard_map/while/body/ppermute | solution.py:414
  88.8 0.1 collective-permute-start.3
  88.8 4.3 %collective-permute-done.3 = bf16[2,64,256]{2,1,0:T(8,128)(2,1)S(1)} collective-permute-done((bf16[2,64,256]{2,1,0:T(8,128)(2,1)S(1)}, bf16[2,64,256]{2,1,0:T(8,128)(2,1)S(1)}, u32[]{:S(2)}, u32[]{:S(2)}) %collective-permute-start.3) | collective-permute-done | bytes 65568 | tf_op jit(solution)/shard_map/while/body/ppermute | solution.py:414
  93.1 1.2 %collective-permute-start.4 = (bf16[2,64,256]{2,1,0:T(8,128)(2,1)S(1)}, bf16[2,64,256]{2,1,0:T(8,128)(2,1)S(1)}, u32[]{:S(2)}, u32[]{:S(2)}) collective-permute-start(bf16[2,64,256]{2,1,0:T(8,128)(2,1)S(1)} %add_convert_fusion.5), channel_id=1, source_target_pairs={{0,4},{1,5},{2,6},{3,7},{4,0},{5,1},{6,2},{7,3},{8,12},{9,13},{10,... | collective-permute-start | bytes 196616 | tf_op jit(solution)/shard_map/while/body/ppermute | solution.py:414
  94.3 4.1 %collective-permute-done.4 = bf16[2,64,256]{2,1,0:T(8,128)(2,1)S(1)} collective-permute-done((bf16[2,64,256]{2,1,0:T(8,128)(2,1)S(1)}, bf16[2,64,256]{2,1,0:T(8,128)(2,1)S(1)}, u32[]{:S(2)}, u32[]{:S(2)}) %collective-permute-start.4) | collective-permute-done | bytes 65568 | tf_op jit(solution)/shard_map/while/body/ppermute | solution.py:414
  98.5 0.0 copy-start.6
  98.5 0.0 collective-permute-done.21.refs_5_
  98.5 0.0 collective-permute-done.24.refs_8_
  98.5 0.0 collective-permute-done.25.refs_9_
  98.5 3.0 %deposit.1 = f32[2,64,3072]{2,1,0:T(8,128)} custom-call(s32[2,2]{1,0:T(2,128)S(1)} %multiply_add_fusion.refs_0_, s32[2,2]{1,0:T(2,128)S(1)} %collective-permute-done.5.refs_1_, s32[2,2]{1,0:T(2,128)S(1)} %collective-permute-done.6.refs_2_.places, s32[2,2]{1,0:T(2,128)S(1)} %collective-permute-done.7.refs_3_, s32[2,2]{1,0:T(2,128)S(1)} %collective-permute-done.8.refs_4_, ...), custom_call_target="tpu_custom_call" | custom-call | flops 67108864 | bytes 4194304 | tf_op jit(solution)/shard_map/deposit/pallas_call | solution.py:423
  (25 shorter events, 0.2 us)
Async XLA Ops:
  0.6 1.6 %copy-start = (f32[2,2,2,256,256]{4,3,2,1,0:T(8,128)S(1)}, f32[2,2,2,256,256]{4,3,2,1,0:T(8,128)}, u32[]{:S(2)}) copy-start(f32[2,2,2,256,256]{4,3,2,1,0:T(8,128)} %waves.1) | copy-start | bytes 6291460
  2.2 0.7 copy-start.7
  2.2 0.7 copy-start.8
  2.2 14.4 %copy-start.1 = (f32[1,2,64,3072]{3,2,1,0:T(8,128)S(1)}, f32[1,2,64,3072]{3,2,1,0:T(8,128)}, u32[]{:S(2)}) copy-start(f32[1,2,64,3072]{3,2,1,0:T(8,128)} %param.11) | copy-start | bytes 4718596
  2.9 21.7 %collective-permute-start.9 = (bf16[2,256,256]{2,1,0:T(8,128)(2,1)S(1)}, bf16[2,256,256]{2,1,0:T(8,128)(2,1)S(1)}, u32[]{:S(2)}, u32[]{:S(2)}) collective-permute-start(bf16[2,256,256]{2,1,0:T(8,128)(2,1)S(1)} %pick.1), channel_id=1, source_target_pairs={{0,2},{1,3},{2,4},{3,5},{4,6},{5,7},{6,0},{7,1},{8,10},{9,11},{10,... | collective-permute-start | bytes 786440 | tf_op jit(solution)/shard_map/ppermute | solution.py:297
  5.9 6.0 %collective-permute-start.8 = (s32[2,2]{1,0:T(2,128)S(1)}, s32[2,2]{1,0:T(2,128)S(1)}, u32[]{:S(2)}, u32[]{:S(2)}) collective-permute-start(s32[2,2]{1,0:T(2,128)S(1)} %multiply_add_fusion.refs_0_), channel_id=1, source_target_pairs={{0,4},{1,5},{2,6},{3,7},{4,0},{5,1},{6,2},{7,3},{8,12},{9,13},{10,... | collective-permute-start | bytes 56 | tf_op jit(solution)/shard_map/ppermute | solution.py:297
  8.5 5.4 %collective-permute-start.7 = (s32[2,2]{1,0:T(2,128)S(1)}, s32[2,2]{1,0:T(2,128)S(1)}, u32[]{:S(2)}, u32[]{:S(2)}) collective-permute-start(s32[2,2]{1,0:T(2,128)S(1)} %multiply_add_fusion.refs_0_), channel_id=1, source_target_pairs={{0,3},{1,4},{2,5},{3,6},{4,7},{5,0},{6,1},{7,2},{8,11},{9,12},{10,... | collective-permute-start | bytes 56 | tf_op jit(solution)/shard_map/ppermute | solution.py:297
  9.7 5.4 %collective-permute-start.6 = (s32[2,2]{1,0:T(2,128)S(1)}, s32[2,2]{1,0:T(2,128)S(1)}, u32[]{:S(2)}, u32[]{:S(2)}) collective-permute-start(s32[2,2]{1,0:T(2,128)S(1)} %multiply_add_fusion.refs_0_), channel_id=1, source_target_pairs={{0,2},{1,3},{2,4},{3,5},{4,6},{5,7},{6,0},{7,1},{8,10},{9,11},{10,... | collective-permute-start | bytes 56 | tf_op jit(solution)/shard_map/ppermute | solution.py:297
  10.4 6.3 %collective-permute-start.5 = (s32[2,2]{1,0:T(2,128)S(1)}, s32[2,2]{1,0:T(2,128)S(1)}, u32[]{:S(2)}, u32[]{:S(2)}) collective-permute-start(s32[2,2]{1,0:T(2,128)S(1)} %multiply_add_fusion.refs_0_), channel_id=1, source_target_pairs={{0,1},{1,2},{2,3},{3,4},{4,5},{5,6},{6,7},{7,0},{8,9},{9,10},{10,1... | collective-permute-start | bytes 56 | tf_op jit(solution)/shard_map/ppermute | solution.py:297
  17.8 8.2 %collective-permute-start.10 = (bf16[2,2,64,256]{3,2,1,0:T(8,128)(2,1)S(1)}, bf16[2,2,64,256]{3,2,1,0:T(8,128)(2,1)S(1)}, u32[]{:S(2)}, u32[]{:S(2)}) collective-permute-start(bf16[2,2,64,256]{3,2,1,0:T(8,128)(2,1)S(1)} %get-tuple-element.132), channel_id=1, source_target_pairs={{0,2},{1,3},{2,4},{3,5},{4,6},{5,7},{6,0},{7,1},{8,10},{9,11},{10,... | collective-permute-start | bytes 393224 | tf_op jit(solution)/shard_map/ppermute | solution.py:307
  17.9 9.2 %collective-permute-start.11 = (bf16[2,2,64,256]{3,2,1,0:T(8,128)(2,1)S(1)}, bf16[2,2,64,256]{3,2,1,0:T(8,128)(2,1)S(1)}, u32[]{:S(2)}, u32[]{:S(2)}) collective-permute-start(bf16[2,2,64,256]{3,2,1,0:T(8,128)(2,1)S(1)} %get-tuple-element.133), channel_id=1, source_target_pairs={{0,1},{1,2},{2,3},{3,4},{4,5},{5,6},{6,7},{7,0},{8,9},{9,10},{10,1... | collective-permute-start | bytes 393224 | tf_op jit(solution)/shard_map/ppermute | solution.py:307
  18.4 8.7 %collective-permute-start.12 = (bf16[2,2,64,256]{3,2,1,0:T(8,128)(2,1)S(1)}, bf16[2,2,64,256]{3,2,1,0:T(8,128)(2,1)S(1)}, u32[]{:S(2)}, u32[]{:S(2)}) collective-permute-start(bf16[2,2,64,256]{3,2,1,0:T(8,128)(2,1)S(1)} %get-tuple-element.135), channel_id=1, source_target_pairs={{0,7},{1,0},{2,1},{3,2},{4,3},{5,4},{6,5},{7,6},{8,15},{9,8},{10,9... | collective-permute-start | bytes 393224 | tf_op jit(solution)/shard_map/ppermute | solution.py:307
  22.7 7.9 %collective-permute-start.13 = (bf16[2,2,64,256]{3,2,1,0:T(8,128)(2,1)S(1)}, bf16[2,2,64,256]{3,2,1,0:T(8,128)(2,1)S(1)}, u32[]{:S(2)}, u32[]{:S(2)}) collective-permute-start(bf16[2,2,64,256]{3,2,1,0:T(8,128)(2,1)S(1)} %get-tuple-element.136), channel_id=1, source_target_pairs={{0,6},{1,7},{2,0},{3,1},{4,2},{5,3},{6,4},{7,5},{8,14},{9,15},{10,... | collective-permute-start | bytes 393224 | tf_op jit(solution)/shard_map/ppermute | solution.py:307
  24.6 15.6 %copy-start.2 = (f32[2,256,256]{2,1,0:T(8,128)S(1)}, f32[2,256,256]{2,1,0:T(8,128)}, u32[]{:S(2)}) copy-start(f32[2,256,256]{2,1,0:T(8,128)} %probe.2) | copy-start | bytes 1572868
  24.7 18.8 %collective-permute-start.14 = (bf16[2,2,64,256]{3,2,1,0:T(8,128)(2,1)S(1)}, bf16[2,2,64,256]{3,2,1,0:T(8,128)(2,1)S(1)}, u32[]{:S(2)}, u32[]{:S(2)}) collective-permute-start(bf16[2,2,64,256]{3,2,1,0:T(8,128)(2,1)S(1)} %get-tuple-element.137), channel_id=1, source_target_pairs={{0,10},{1,11},{2,12},{3,13},{4,14},{5,15},{6,8},{7,9},{8,2},{9,3},... | collective-permute-start | bytes 393224 | tf_op jit(solution)/shard_map/ppermute | solution.py:307
  26.0 17.5 %collective-permute-start.15 = (bf16[2,2,64,256]{3,2,1,0:T(8,128)(2,1)S(1)}, bf16[2,2,64,256]{3,2,1,0:T(8,128)(2,1)S(1)}, u32[]{:S(2)}, u32[]{:S(2)}) collective-permute-start(bf16[2,2,64,256]{3,2,1,0:T(8,128)(2,1)S(1)} %get-tuple-element.138), channel_id=1, source_target_pairs={{0,9},{1,10},{2,11},{3,12},{4,13},{5,14},{6,15},{7,8},{8,1},{9,2},... | collective-permute-start | bytes 393224 | tf_op jit(solution)/shard_map/ppermute | solution.py:307
  27.1 16.4 %collective-permute-start.16 = (bf16[2,2,64,256]{3,2,1,0:T(8,128)(2,1)S(1)}, bf16[2,2,64,256]{3,2,1,0:T(8,128)(2,1)S(1)}, u32[]{:S(2)}, u32[]{:S(2)}) collective-permute-start(bf16[2,2,64,256]{3,2,1,0:T(8,128)(2,1)S(1)} %get-tuple-element.139), channel_id=1, source_target_pairs={{0,8},{1,9},{2,10},{3,11},{4,12},{5,13},{6,14},{7,15},{8,0},{9,1},... | collective-permute-start | bytes 393224 | tf_op jit(solution)/shard_map/ppermute | solution.py:307
  27.1 16.4 %collective-permute-start.17 = (bf16[2,2,64,256]{3,2,1,0:T(8,128)(2,1)S(1)}, bf16[2,2,64,256]{3,2,1,0:T(8,128)(2,1)S(1)}, u32[]{:S(2)}, u32[]{:S(2)}) collective-permute-start(bf16[2,2,64,256]{3,2,1,0:T(8,128)(2,1)S(1)} %get-tuple-element.140), channel_id=1, source_target_pairs={{0,15},{1,8},{2,9},{3,10},{4,11},{5,12},{6,13},{7,14},{8,7},{9,0},... | collective-permute-start | bytes 393224 | tf_op jit(solution)/shard_map/ppermute | solution.py:307
  30.6 9.6 %collective-permute-start = (bf16[2,256,256]{2,1,0:T(8,128)(2,1)S(1)}, bf16[2,256,256]{2,1,0:T(8,128)(2,1)S(1)}, u32[]{:S(2)}, u32[]{:S(2)}) collective-permute-start(bf16[2,256,256]{2,1,0:T(8,128)(2,1)S(1)} %get-tuple-element.248), channel_id=1, source_target_pairs={{0,16},{1,17},{2,18},{3,19},{4,20},{5,21},{6,22},{7,23},{8,24},{9,... | collective-permute-start | bytes 786440 | tf_op jit(solution)/shard_map/while/body/ppermute | solution.py:307
  40.1 5.7 %collective-permute-start.18 = (bf16[2,2,64,256]{3,2,1,0:T(8,128)(2,1)S(1)}, bf16[2,2,64,256]{3,2,1,0:T(8,128)(2,1)S(1)}, u32[]{:S(2)}, u32[]{:S(2)}) collective-permute-start(bf16[2,2,64,256]{3,2,1,0:T(8,128)(2,1)S(1)} %get-tuple-element.141), channel_id=1, source_target_pairs={{0,14},{1,15},{2,8},{3,9},{4,10},{5,11},{6,12},{7,13},{8,6},{9,7},... | collective-permute-start | bytes 393224 | tf_op jit(solution)/shard_map/ppermute | solution.py:307
  40.2 1.1 %copy-start.3 = (bf16[768,512]{1,0:T(8,128)(2,1)S(1)}, bf16[768,512]{1,0:T(8,128)(2,1)}, u32[]{:S(2)}) copy-start(bf16[768,512]{1,0:T(8,128)(2,1)} %constant.49.clone.refs_3_.right) | copy-start | bytes 2359300
  41.4 1.1 %copy-start.5 = (bf16[512,768]{1,0:T(8,128)(2,1)S(1)}, bf16[512,768]{1,0:T(8,128)(2,1)}, u32[]{:S(2)}) copy-start(bf16[512,768]{1,0:T(8,128)(2,1)} %constant.48.clone.refs_2_.left) | copy-start | bytes 2359300
  42.5 3.4 %copy-start.4 = (bf16[768,512]{1,0:T(8,128)(2,1)S(1)}, bf16[768,512]{1,0:T(8,128)(2,1)}, u32[]{:S(2)}) copy-start(bf16[768,512]{1,0:T(8,128)(2,1)} %constant.49.clone.refs_3_.right) | copy-start | bytes 2359300
  48.6 14.6 %collective-permute-start.19 = (bf16[2,2,256,256]{3,2,1,0:T(8,128)(2,1)S(1)}, bf16[2,2,256,256]{3,2,1,0:T(8,128)(2,1)S(1)}, u32[]{:S(2)}, u32[]{:S(2)}) collective-permute-start(bf16[2,2,256,256]{3,2,1,0:T(8,128)(2,1)S(1)} %get-tuple-element.144), channel_id=1, source_target_pairs={{0,16},{1,17},{2,18},{3,19},{4,20},{5,21},{6,22},{7,23},{8,24},{9,... | collective-permute-start | bytes 1572872 | tf_op jit(solution)/shard_map/ppermute | solution.py:307
  68.7 2.0 %collective-permute-start.20 = (bf16[2,2,256,256]{3,2,1,0:T(8,128)(2,1)S(1)}, bf16[2,2,256,256]{3,2,1,0:T(8,128)(2,1)S(1)}, u32[]{:S(2)}, u32[]{:S(2)}) collective-permute-start(bf16[2,2,256,256]{3,2,1,0:T(8,128)(2,1)S(1)} %get-tuple-element.146), channel_id=1, source_target_pairs={{0,8},{1,9},{2,10},{3,11},{4,12},{5,13},{6,14},{7,15},{8,0},{9,1},... | collective-permute-start | bytes 1572872 | tf_op jit(solution)/shard_map/ppermute | solution.py:307
  69.8 5.9 %collective-permute-start.23 = (bf16[2,2,64,256]{3,2,1,0:T(8,128)(2,1)S(1)}, bf16[2,2,64,256]{3,2,1,0:T(8,128)(2,1)S(1)}, u32[]{:S(2)}, u32[]{:S(2)}) collective-permute-start(bf16[2,2,64,256]{3,2,1,0:T(8,128)(2,1)S(1)} %get-tuple-element.154), channel_id=1, source_target_pairs={{0,8},{1,9},{2,10},{3,11},{4,12},{5,13},{6,14},{7,15},{8,0},{9,1},... | collective-permute-start | bytes 393224 | tf_op jit(solution)/shard_map/ppermute | solution.py:307
  71.4 27.1 %collective-permute-start.21 = (bf16[2,2,2,64,256]{4,3,2,1,0:T(8,128)(2,1)S(1)}, bf16[2,2,2,64,256]{4,3,2,1,0:T(8,128)(2,1)S(1)}, u32[]{:S(2)}, u32[]{:S(2)}) collective-permute-start(bf16[2,2,2,64,256]{4,3,2,1,0:T(8,128)(2,1)S(1)} %get-tuple-element.147), channel_id=1, source_target_pairs={{0,6},{1,7},{2,0},{3,1},{4,2},{5,3},{6,4},{7,5},{8,14},{9,15},{10,... | collective-permute-start | bytes 786440 | tf_op jit(solution)/shard_map/ppermute | solution.py:307
  73.7 24.9 %collective-permute-start.22 = (bf16[2,2,2,64,256]{4,3,2,1,0:T(8,128)(2,1)S(1)}, bf16[2,2,2,64,256]{4,3,2,1,0:T(8,128)(2,1)S(1)}, u32[]{:S(2)}, u32[]{:S(2)}) collective-permute-start(bf16[2,2,2,64,256]{4,3,2,1,0:T(8,128)(2,1)S(1)} %get-tuple-element.148), channel_id=1, source_target_pairs={{0,7},{1,0},{2,1},{3,2},{4,3},{5,4},{6,5},{7,6},{8,15},{9,8},{10,9... | collective-permute-start | bytes 786440 | tf_op jit(solution)/shard_map/ppermute | solution.py:307
  73.7 24.9 %collective-permute-start.24 = (bf16[2,2,2,64,256]{4,3,2,1,0:T(8,128)(2,1)S(1)}, bf16[2,2,2,64,256]{4,3,2,1,0:T(8,128)(2,1)S(1)}, u32[]{:S(2)}, u32[]{:S(2)}) collective-permute-start(bf16[2,2,2,64,256]{4,3,2,1,0:T(8,128)(2,1)S(1)} %get-tuple-element.158), channel_id=1, source_target_pairs={{0,1},{1,2},{2,3},{3,4},{4,5},{5,6},{6,7},{7,0},{8,9},{9,10},{10,1... | collective-permute-start | bytes 786440 | tf_op jit(solution)/shard_map/ppermute | solution.py:307
  75.7 22.9 %collective-permute-start.25 = (bf16[2,2,2,64,256]{4,3,2,1,0:T(8,128)(2,1)S(1)}, bf16[2,2,2,64,256]{4,3,2,1,0:T(8,128)(2,1)S(1)}, u32[]{:S(2)}, u32[]{:S(2)}) collective-permute-start(bf16[2,2,2,64,256]{4,3,2,1,0:T(8,128)(2,1)S(1)} %get-tuple-element.159), channel_id=1, source_target_pairs={{0,2},{1,3},{2,4},{3,5},{4,6},{5,7},{6,0},{7,1},{8,10},{9,11},{10,... | collective-permute-start | bytes 786440 | tf_op jit(solution)/shard_map/ppermute | solution.py:307
  75.7 5.5 %collective-permute-start.1 = (bf16[2,64,256]{2,1,0:T(8,128)(2,1)S(1)}, bf16[2,64,256]{2,1,0:T(8,128)(2,1)S(1)}, u32[]{:S(2)}, u32[]{:S(2)}) collective-permute-start(bf16[2,64,256]{2,1,0:T(8,128)(2,1)S(1)} %fusion.7), channel_id=1, source_target_pairs={{0,16},{1,17},{2,18},{3,19},{4,20},{5,21},{6,22},{7,23},{8,24},{9,... | collective-permute-start | bytes 196616 | tf_op jit(solution)/shard_map/while/body/ppermute | solution.py:307
  81.3 7.5 %collective-permute-start.2 = (bf16[2,64,256]{2,1,0:T(8,128)(2,1)S(1)}, bf16[2,64,256]{2,1,0:T(8,128)(2,1)S(1)}, u32[]{:S(2)}, u32[]{:S(2)}) collective-permute-start(bf16[2,64,256]{2,1,0:T(8,128)(2,1)S(1)} %get-tuple-element.241), channel_id=1, source_target_pairs={{0,1},{1,0},{2,3},{3,2},{4,5},{5,4},{6,7},{7,6},{8,9},{9,8},{10,11... | collective-permute-start | bytes 196616 | tf_op jit(solution)/shard_map/while/body/ppermute | solution.py:414
  88.8 4.3 %collective-permute-start.3 = (bf16[2,64,256]{2,1,0:T(8,128)(2,1)S(1)}, bf16[2,64,256]{2,1,0:T(8,128)(2,1)S(1)}, u32[]{:S(2)}, u32[]{:S(2)}) collective-permute-start(bf16[2,64,256]{2,1,0:T(8,128)(2,1)S(1)} %add_convert_fusion.4), channel_id=1, source_target_pairs={{0,2},{1,3},{2,0},{3,1},{4,6},{5,7},{6,4},{7,5},{8,10},{9,11},{10,... | collective-permute-start | bytes 196616 | tf_op jit(solution)/shard_map/while/body/ppermute | solution.py:414
  93.1 5.3 %collective-permute-start.4 = (bf16[2,64,256]{2,1,0:T(8,128)(2,1)S(1)}, bf16[2,64,256]{2,1,0:T(8,128)(2,1)S(1)}, u32[]{:S(2)}, u32[]{:S(2)}) collective-permute-start(bf16[2,64,256]{2,1,0:T(8,128)(2,1)S(1)} %add_convert_fusion.5), channel_id=1, source_target_pairs={{0,4},{1,5},{2,6},{3,7},{4,0},{5,1},{6,2},{7,3},{8,12},{9,13},{10,... | collective-permute-start | bytes 196616 | tf_op jit(solution)/shard_map/while/body/ppermute | solution.py:414
  98.5 3.1 %copy-start.6 = (f32[2,64,256]{2,1,0:T(8,128)}, f32[2,64,256]{2,1,0:T(8,128)S(1)}, u32[]{:S(2)}) copy-start(f32[2,64,256]{2,1,0:T(8,128)S(1)} %get-tuple-element.126) | copy-start | bytes 393220

commit v2 on v1

--- a/solution.py
+++ b/solution.py
@@ -46,16 +46,22 @@
 
 def propagate(fields, left, right):
     side = fields[0][0].shape[0]
-    high, low = split(jnp.concatenate([part for field in fields for part in field], axis=1))
-    middle = jnp.dot(left, jnp.concatenate([high, low, high], axis=0), preferred_element_type=f32)
+
+    def parts(values, axis):
+        high, low = split(values)
+        if left.shape[1] == 3 * side:
+            return jnp.concatenate([high, low, high], axis=axis)
+        return jnp.concatenate([high, high], axis=axis)
+
+    columns = parts(jnp.concatenate([part for field in fields for part in field], axis=1), 0)
+    middle = jnp.dot(left, columns, preferred_element_type=f32)
     rows = []
     for index in range(len(fields)):
         by_real = middle[:side, 2 * index * side : 2 * (index + 1) * side]
         by_imag = middle[side:, 2 * index * side : 2 * (index + 1) * side]
         rows.append(by_real[:, :side] - by_imag[:, side:])
         rows.append(by_real[:, side:] + by_imag[:, :side])
-    high, low = split(jnp.concatenate(rows, axis=0))
-    result = jnp.dot(jnp.concatenate([high, low, high], axis=1), right, preferred_element_type=f32)
+    result = jnp.dot(parts(jnp.concatenate(rows, axis=0), 1), right, preferred_element_type=f32)
     results = []
     for index in range(len(fields)):
         real = result[2 * index * side : (2 * index + 1) * side]
@@ -164,76 +170,82 @@
     return jnp.where(core == half, 0, 1)
 
 
-def near_kernel(home, width, places, start, left, right, *refs):
-    pieces, (frames, waves, sent) = refs[:-3], refs[-3:]
+def near_kernel(home, turn, early, width, places, start, left, right, *refs):
+    pieces, (frames, wave, sent) = refs[:-3], refs[-3:]
     reach = len(pieces) // 2
-    count, _, strip, side = pieces[0].shape
+    _, _, strip, side = pieces[0].shape
     own = own_first()
     row = lax.broadcasted_iota(jnp.int32, (strip, side), 0)
+    down, _ = window_place(places, home, turn, strip, width)
     for flip in range(2):
         parts = pieces[flip * reach : (flip + 1) * reach]
+        for plane in range(2):
+            first = parts[0][turn, plane].astype(f32)
+            again = parts[-1][turn, plane].astype(f32)
+            frames[own ^ flip, plane, :strip] = jnp.where(row < down, again, first).astype(bf16)
+            for step in range(1, reach - 1):
+                frames[own ^ flip, plane, step * strip : (step + 1) * strip] = parts[step][
+                    turn, plane
+                ]
+    field = multiply(pair(frames, 0), pair(start, turn))
+    if early:
+        (field,) = propagate([field], left[:, side:], right[side:])
+        wave[0], wave[1] = field
+        real, imag = multiply(pair(frames, 1), field)
+    else:
+        (field,) = propagate([field], left[...], right[...])
+        wave[0], wave[1] = field
+        ((real, imag),) = propagate([multiply(pair(frames, 1), field)], left[...], right[...])
+    sent[0] = real.astype(bf16)
+    sent[1] = imag.astype(bf16)
+
+
+def far_kernel(turn, early, start, left, right, frames, wave, arrived, kept, given, last):
+    own = own_first()
+    side = start.shape[2]
+    field = pair(arrived)
+    if early:
+        (field,) = propagate([field], left[...], right[...])
+        outer = multiply(pair(wave), field)
+        (field,) = propagate([multiply(pair(frames, 1), field)], left[...], right[...])
+    else:
+        outer = multiply(pair(wave), field)
+        (field,) = propagate([multiply(pair(frames, 1), field)], left[:, side:], right[side:])
+    first = multiply(pair(start, turn), field)
+    for plane, sign in ((0, 1.0), (1, -1.0)):
+        kept[plane] = (jnp.where(own == 0, first[plane], outer[plane]) * sign).astype(bf16)
+        given[plane] = (jnp.where(own == 0, outer[plane], first[plane]) * sign).astype(bf16)
+    last[0], last[1] = multiply(pair(frames, 0), field)
+
+
+def part_kernel(home, width, places, *refs):
+    count = places.shape[1]
+    windows, outs = refs[: 2 * count], refs[2 * count :]
+    _, _, _, strip, side = outs[0].shape
+    row = lax.broadcasted_iota(jnp.int32, (strip, side), 0)
+    for flip in range(2):
         for turn in range(count):
-            down, _ = window_place(places, home, turn, strip, width)
-            for plane in range(2):
-                first = parts[0][turn, plane].astype(f32)
-                again = parts[-1][turn, plane].astype(f32)
-                frames[own ^ flip, turn, plane, :strip] = jnp.where(
-                    row < down, again, first
-                ).astype(bf16)
-                for step in range(1, reach - 1):
-                    frames[own ^ flip, turn, plane, step * strip : (step + 1) * strip] = parts[step][
-                        turn, plane
-                    ]
-    fields = [multiply(pair(frames, 0, turn), pair(start, turn)) for turn in range(count)]
-    for turn, field in enumerate(propagate(fields, left[...], right[...])):
-        waves[turn, 0], waves[turn, 1] = field
-        real, imag = multiply(pair(frames, 1, turn), field)
-        sent[turn, 0] = real.astype(bf16)
-        sent[turn, 1] = imag.astype(bf16)
-
-
-def far_kernel(start, left, right, frames, waves, arrived, kept, given, last):
-    count = start.shape[0]
-    own = own_first()
-    fields = propagate([pair(arrived, turn) for turn in range(count)], left[...], right[...])
-    outer, inner = [], []
-    for turn, field in enumerate(fields):
-        outer.append(multiply(pair(waves, turn), field))
-        inner.append(multiply(pair(frames, 1, turn), field))
-    for turn, field in enumerate(propagate(inner, left[...], right[...])):
-        first = multiply(pair(start, turn), field)
-        for plane, sign in ((0, 1.0), (1, -1.0)):
-            mine = jnp.where(own == 0, first[plane], outer[turn][plane])
-            other = jnp.where(own == 0, outer[turn][plane], first[plane])
-            kept[turn, plane] = (mine * sign).astype(bf16)
-            given[turn, plane] = (other * sign).astype(bf16)
-        last[turn, 0], last[turn, 1] = multiply(pair(frames, 0, turn), field)
-
-
-def part_kernel(home, width, places, kept, arrived, *outs):
-    _, count, _, strip, side = outs[0].shape
-    row = lax.broadcasted_iota(jnp.int32, (strip, side), 0)
-    for flip, windows in enumerate((kept, arrived)):
-        for turn in range(count):
+            window = windows[flip * count + turn]
             down, _ = window_place(places, home, turn, strip, width, flip)
             for plane in range(2):
-                ends = windows[turn, plane, :strip].astype(f32)
+                ends = window[plane, :strip].astype(f32)
                 outs[0][flip, turn, plane] = jnp.where(row < down, 0.0, ends).astype(bf16)
                 outs[-1][flip, turn, plane] = jnp.where(row < down, ends, 0.0).astype(bf16)
                 for step in range(1, len(outs) - 1):
-                    outs[step][flip, turn, plane] = windows[
-                        turn, plane, step * strip : (step + 1) * strip
+                    outs[step][flip, turn, plane] = window[
+                        plane, step * strip : (step + 1) * strip
                     ]
 
 
-def probe_kernel(home, strip, width, places, waves, near, away, sent, total):
+def probe_kernel(home, strip, width, places, *refs):
+    waves, (near, away, sent, total) = refs[:-4], refs[-4:]
     core, half = this_place()
     weight = jnp.where(half == 0, 1.0, 0.0)
     for plane, sign in ((0, weight), (1, -weight)):
         parts = []
-        for turn in range(waves.shape[0]):
+        for turn, wave in enumerate(waves):
             down, across = window_place(places, home, turn, strip, width)
-            parts.append(turned_back(waves[turn, plane], down, across))
+            parts.append(turned_back(wave[plane], down, across))
         total[plane] = sum(parts) * sign
     height = near.shape[1]
     for index, out in enumerate((near, away)):
@@ -245,38 +257,25 @@
 
 
 def deposit_kernel(reach, *refs):
-    places, pieces, (out, total, done) = refs[:reach], refs[reach : 2 * reach], refs[2 * reach :]
+    places, pieces, out = refs[:reach], refs[reach:-1], refs[-1]
     _, count, _, strip, side = pieces[0].shape
     width = out.shape[2]
     core, _ = this_place()
-    stretches = []
-    for step in range(reach):
+    lane = lax.broadcasted_iota(jnp.int32, (strip, LANES), 1)
+    out[...] = jnp.zeros(out.shape, f32)
+    for step, piece in enumerate(pieces):
         for flip in range(2):
             for turn in range(count):
                 column = column_of(places[step], width, core ^ flip, turn)
-                stretches.append((pieces[step].at[flip, turn], *stretch(column, side, width)))
-    height = strip // 4
-    lane = lax.broadcasted_iota(jnp.int32, (height, LANES), 1)
-    copies = []
-    for plane in range(2):
-        for start in range(0, strip, height):
-            rows = pl.ds(start, height)
-            total[plane, rows] = jnp.zeros((height, width), f32)
-            for piece, base, after, begin in stretches:
+                base, after, begin = stretch(column, side, width)
                 rest = pl.multiple_of(base + LANES, LANES)
-                ends = piece[plane, rows, :LANES].astype(f32)
-                total[plane, rows, pl.ds(base, LANES)] += jnp.where(lane < begin, 0.0, ends)
-                total[plane, rows, pl.ds(rest, side - LANES)] += piece[plane, rows, LANES:].astype(
-                    f32
-                )
-                total[plane, rows, pl.ds(after, LANES)] += jnp.where(lane < begin, ends, 0.0)
-            copy = pltpu.make_async_copy(
-                total.at[plane, rows], out.at[plane, rows], done.at[len(copies)]
-            )
-            copy.start()
-            copies.append(copy)
-    for copy in copies:
-        copy.wait()
+                for plane in range(2):
+                    ends = piece[flip, turn, plane, :, :LANES].astype(f32)
+                    out[plane, :, pl.ds(base, LANES)] += jnp.where(lane < begin, 0.0, ends)
+                    out[plane, :, pl.ds(rest, side - LANES)] += piece[
+                        flip, turn, plane, :, LANES:
+                    ].astype(f32)
+                    out[plane, :, pl.ds(after, LANES)] += jnp.where(lane < begin, ends, 0.0)
 
 
 def local(transmission, probe, exit_adjoint, scan_row, scan_col):
@@ -290,9 +289,6 @@
     assert transmission.shape[0] == 1 and depth == 4 and scan_row.shape[0] == 2
     assert side == 2 * LANES and count == 2
 
-    half = lax.axis_index("depth") // (depth // 2)
-    once = lax.axis_index("depth") // depth + 1
-
     def along_scan(value, by):
         return lax.ppermute(value, "scan", [(i, (i + by) % regions) for i in range(regions)])
 
@@ -309,12 +305,12 @@
     smem = pl.BlockSpec(memory_space=pltpu.SMEM)
     vmem = pl.BlockSpec(memory_space=pltpu.VMEM)
 
-    def call(kernel, out_shape, in_specs, flops, name, scratch=(), out_spec=vmem):
+    def call(kernel, out_shape, in_specs, flops, name, scratch=()):
         return pl.pallas_call(
             kernel,
             out_shape=out_shape,
             in_specs=in_specs,
-            out_specs=jax.tree.map(lambda _: out_spec, out_shape),
+            out_specs=jax.tree.map(lambda _: vmem, out_shape),
             scratch_shapes=scratch,
             compiler_params=pltpu.CompilerParams(vmem_limit_bytes=24 * 1024 * 1024),
             cost_estimate=pl.CostEstimate(flops=flops, bytes_accessed=4 << 20, transcendentals=0),
@@ -336,9 +332,9 @@
         "pick",
         [pltpu.VMEM(wave, f32), pltpu.SemaphoreType.DMA],
     )(exit_adjoint)
+    adjoint, scan_row = lax.optimization_barrier((adjoint, scan_row))
+    adjoint = along_scan(adjoint, home)
     packed = scan_row * width + scan_col
-    adjoint, packed = lax.optimization_barrier((adjoint, packed))
-    adjoint = along_scan(adjoint, home)
     places = [packed] + [along_scan(packed, step) for step in range(1, reach)]
 
     order = [(flip, step) for flip in range(2) for step in range(reach)]
@@ -352,8 +348,7 @@
     )(*places, transmission[0])
     pieces = dict(zip(order, pieces))
     adjoint, pieces[0, home] = lax.optimization_barrier((adjoint, pieces[0, home]))
-    flipped = lax.fori_loop(0, once, lambda _, held: across(held, 2, 0, lower), adjoint)
-    adjoints = [adjoint, flipped]
+    adjoints = [adjoint, across(adjoint, 2, 0, lower)]
     for flip, step in far_first:
         pieces[flip, step] = across(pieces[flip, step], flip, home - step)
 
@@ -364,70 +359,77 @@
         1 << 30,
         "start",
     )(places[home], probe, *adjoints, left, right)
-    frames, waves, sent = call(
-        functools.partial(near_kernel, home, width),
-        [shape((2,) + field, bf16), shape(field, f32), shape(field, bf16)],
-        [smem] + [vmem] * (3 + len(order)),
-        1 << 31,
-        "near",
-    )(places[home], start, left, right, *(pieces[key] for key in order))
-    arrived = across(sent, 2, 0)
-    kept, given, last = call(
-        far_kernel,
-        [shape(field, bf16)] * 2 + [shape(field, f32)],
-        [vmem] * 6,
-        1 << 32,
-        "far",
-    )(start, left, right, frames, waves, arrived)
+    chains = []
+    for turn in range(count):
+        frames, forward, sent = call(
+            functools.partial(near_kernel, home, turn, turn == count - 1, width),
+            [shape((2,) + wave, bf16), shape(wave, f32), shape(wave, bf16)],
+            [smem] + [vmem] * (3 + len(order)),
+            1 << 30,
+            "near",
+        )(places[home], start, left, right, *(pieces[key] for key in order))
+        chains.append((frames, forward, across(sent, 2, 0)))
+    kept, given, lasts = [], [], []
+    for turn, chain in enumerate(chains):
+        mine, other, last = call(
+            functools.partial(far_kernel, turn, turn == count - 1),
+            [shape(wave, bf16)] * 2 + [shape(wave, f32)],
+            [vmem] * 6,
+            1 << 31,
+            "far",
+        )(start, left, right, *chain)
+        kept.append(mine)
+        given.append(across(other, 1, 0))
+        lasts.append(last)
     parts = call(
         functools.partial(part_kernel, home, width),
         [shape((2,) + piece.shape, bf16)] * reach,
-        [smem] + [vmem] * 2,
+        [smem] + [vmem] * (2 * count),
         1 << 26,
         "part",
-    )(places[home], kept, across(given, 1, 0))
+    )(places[home], *kept, *given)
     parts = list(parts)
 
     height = side // depth
     near, away, probe_sent = call(
         functools.partial(probe_kernel, home, strip, width),
         [shape((2, height, side), f32)] * 2 + [shape((2, 2, height, side), bf16)],
-        [smem, vmem],
+        [smem] + [vmem] * count,
         1 << 26,
         "probe",
         [pltpu.VMEM(wave, f32)],
-    )(places[home], last)
+    )(places[home], *lasts)
     returned = [across(part, 0, step - home) for step, part in enumerate(parts)]
+
+    def scan_round(total, span):
+        rounded = total.astype(bf16)
+        route = [(i, i ^ span) for i in range(regions)]
+        return rounded.astype(f32) + lax.ppermute(rounded, "scan", route).astype(f32)
 
     def probe_rounds(_, held):
         near, away, given = held
-        given = given.astype(f32)
-        away = across((away + given[1]).astype(bf16), 2, 0, lower).astype(f32)
-        total = jnp.where(half == 0, near + given[0], away)
-        if regions & (regions - 1):
-            total = lax.psum(total, "scan")
-        else:
-            span = 1
-            while span < regions:
-                rounded = total.astype(bf16)
-                route = [(i, i ^ span) for i in range(regions)]
-                total = rounded.astype(f32) + lax.ppermute(rounded, "scan", route).astype(f32)
-                span *= 2
-        return total, away, held[2]
-
+        away = across((away + given[1].astype(f32)).astype(bf16), 2, 0, lower).astype(f32)
+        total = jnp.where(half == 0, near + given[0].astype(f32), away)
+        for span in spans[:-1]:
+            total = scan_round(total, span)
+        return total, away, given
+
+    half = lax.axis_index("depth") // (depth // 2)
+    once = lax.axis_index("depth") // depth + 1
+    assert regions & (regions - 1) == 0
+    spans = [1 << level for level in range(regions.bit_length() - 1)]
     near, parts[home] = lax.optimization_barrier((near, parts[home]))
     probe_grad, *_ = lax.fori_loop(
         0, once, probe_rounds, (near, away, across(probe_sent, 1, 0))
     )
-    probe_grad, returned[home] = lax.optimization_barrier((probe_grad, parts[home]))
+    probe_grad, returned = lax.optimization_barrier((probe_grad, returned))
+    probe_grad = scan_round(probe_grad, spans[-1])
     object_grad = call(
         functools.partial(deposit_kernel, reach),
         shape(transmission.shape[1:], f32),
         [smem] * reach + [vmem] * reach,
         1 << 26,
         "deposit",
-        [pltpu.VMEM(transmission.shape[1:], f32), pltpu.SemaphoreType.DMA((8,))],
-        pl.BlockSpec(memory_space=pltpu.HBM),
     )(*places, *returned)
     return object_grad[None], probe_grad
 

time: 102 us -> 91.8 us (0.900)
  waiting for transfers between devices: 44.8 us -> 32.7 us
  Pallas kernels: 15.2 us -> 18.5 us
  local copies, waits for them, and re-layouts: 4.51 us -> 1.6 us
  other arithmetic: 0.12 us -> 1.45 us
    ppermute x18 -> x20, waiting for transfers between devices: 25.1 us -> 16.6 us  [across(): return lax.ppermute(value, ('depth', 'scan'), route)]
    pallas_call x2 -> x4, Pallas kernels: 8.25 us -> 11.8 us  [the longest x2 6.36 us: local(): call(functools.partial(near_kernel, home, turn, turn == count - 1, width)...]
    ppermute x5, waiting for transfers between devices: 4.75 us -> 1.82 us  [along_scan(): lax.ppermute(value, 'scan', [(i, (i + by) % regions) for i in range(regio...]
    unnamed x19 -> x10, local copies, waits for them, and re-layouts: 4.49 us -> 1.6 us
    ppermute x18 -> x20, starting transfers between devices: 24.9 us -> 25.1 us  [across(): return lax.ppermute(value, ('depth', 'scan'), route)]
  transfers between devices with their start and end apart: 26 -> 28, of which waited for: 13 -> 15; matrix products, arithmetic and copies ran while one was open for 0% -> 1% of each run, Pallas kernels for 4% -> 18%
where the time goes in v2:
time: 91.8 us; the launch traced here: 91.6 us
  starting transfers between devices  36.5 us (40%)
  waiting for transfers between devices  32.7 us (36%)
  Pallas kernels  18.5 us (20%)
  local copies, waits for them, and re-layouts  1.6 us (2%)
  other arithmetic  1.45 us (2%)
    ppermute x20, starting transfers between devices, across(): return lax.ppermute(value, ('depth', 'scan'), route)  25.1 us
    ppermute x20, waiting for transfers between devices, across(): return lax.ppermute(value, ('depth', 'scan'), route)  16.6 us
    ppermute x3, waiting for transfers between devices, scan_round(): lax.ppermute(rounded, 'scan', route).astype(f32)  14.3 us
    ppermute x5, starting transfers between devices, along_scan(): lax.ppermute(value, 'scan', [(i, (i + by) % regions) for i in range(regio...  9.94 us
    pallas_call x2, Pallas kernels, local(): call(functools.partial(near_kernel, home, turn, turn == count - 1, width)...  6.36 us
    pallas_call x2, Pallas kernels, local(): call(functools.partial(far_kernel, turn, turn == count - 1), [shape(wave,...  5.45 us
    pallas_call x1, Pallas kernels, local(): call(functools.partial(deposit_kernel, reach), shape(transmission.shape[1...  2.68 us
  transfers between devices with their start and end apart: 28, of which 15 were waited for; matrix products, arithmetic and copies ran while one was open for 1% of the time, Pallas kernels for 18%

profile of v2, /device:TPU:0, one launch (start us, length us, event | category | flops | bytes accessed | tf_op | source)
XLA Modules:
  0.0 91.6 jit_solution(1506602780021377462)
XLA Ops:
  0.6 1.6 %copy-done = f32[2,2,2,256,256]{4,3,2,1,0:T(8,128)S(1)} copy-done((f32[2,2,2,256,256]{4,3,2,1,0:T(8,128)S(1)}, f32[2,2,2,256,256]{4,3,2,1,0:T(8,128)}, u32[]{:S(2)}) %copy-start) | copy-done | bytes 2097176
  2.2 0.1 pick.1
  2.3 3.1 %collective-permute-start.7 = (bf16[2,256,256]{2,1,0:T(8,128)(2,1)S(1)}, bf16[2,256,256]{2,1,0:T(8,128)(2,1)S(1)}, u32[]{:S(2)}, u32[]{:S(2)}) collective-permute-start(bf16[2,256,256]{2,1,0:T(8,128)(2,1)S(1)} %pick.1), channel_id=1, source_target_pairs={{0,2},{1,3},{2,4},{3,5},{4,6},{5,7},{6,0},{7,1},{8,10},{9,11},{10,... | collective-permute-start | bytes 786440 | tf_op jit(solution)/shard_map/ppermute | solution.py:293
  5.4 0.7 multiply_add_fusion.refs_0_
  6.1 1.6 %collective-permute-start.4 = (s32[2,2]{1,0:T(2,128)S(1)}, s32[2,2]{1,0:T(2,128)S(1)}, u32[]{:S(2)}, u32[]{:S(2)}) collective-permute-start(s32[2,2]{1,0:T(2,128)S(1)} %multiply_add_fusion.refs_0_), channel_id=1, source_target_pairs={{0,2},{1,3},{2,4},{3,5},{4,6},{5,7},{6,0},{7,1},{8,10},{9,11},{10,... | collective-permute-start | bytes 56 | tf_op jit(solution)/shard_map/ppermute | solution.py:293
  7.7 1.5 %collective-permute-start.3 = (s32[2,2]{1,0:T(2,128)S(1)}, s32[2,2]{1,0:T(2,128)S(1)}, u32[]{:S(2)}, u32[]{:S(2)}) collective-permute-start(s32[2,2]{1,0:T(2,128)S(1)} %multiply_add_fusion.refs_0_), channel_id=1, source_target_pairs={{0,1},{1,2},{2,3},{3,4},{4,5},{5,6},{6,7},{7,0},{8,9},{9,10},{10,1... | collective-permute-start | bytes 56 | tf_op jit(solution)/shard_map/ppermute | solution.py:293
  9.2 1.1 %collective-permute-start.5 = (s32[2,2]{1,0:T(2,128)S(1)}, s32[2,2]{1,0:T(2,128)S(1)}, u32[]{:S(2)}, u32[]{:S(2)}) collective-permute-start(s32[2,2]{1,0:T(2,128)S(1)} %multiply_add_fusion.refs_0_), channel_id=1, source_target_pairs={{0,3},{1,4},{2,5},{3,6},{4,7},{5,0},{6,1},{7,2},{8,11},{9,12},{10,... | collective-permute-start | bytes 56 | tf_op jit(solution)/shard_map/ppermute | solution.py:293
  10.3 2.6 %collective-permute-start.6 = (s32[2,2]{1,0:T(2,128)S(1)}, s32[2,2]{1,0:T(2,128)S(1)}, u32[]{:S(2)}, u32[]{:S(2)}) collective-permute-start(s32[2,2]{1,0:T(2,128)S(1)} %multiply_add_fusion.refs_0_), channel_id=1, source_target_pairs={{0,4},{1,5},{2,6},{3,7},{4,0},{5,1},{6,2},{7,3},{8,12},{9,13},{10,... | collective-permute-start | bytes 56 | tf_op jit(solution)/shard_map/ppermute | solution.py:293
  13.0 0.9 collective-permute-done.4.refs_2_.places
  13.8 1.0 %collective-permute-done.3.refs_1_ = s32[2,2]{1,0:T(2,128)S(1)} collective-permute-done((s32[2,2]{1,0:T(2,128)S(1)}, s32[2,2]{1,0:T(2,128)S(1)}, u32[]{:S(2)}, u32[]{:S(2)}) %collective-permute-start.3) | collective-permute-done | bytes 48 | tf_op jit(solution)/shard_map/ppermute | solution.py:293
  14.8 0.0 collective-permute-done.5.refs_3_
  14.8 0.0 collective-permute-done.6.refs_4_
  14.8 1.2 %extract.1 = (bf16[2,2,64,256]{3,2,1,0:T(8,128)(2,1)S(1)}, bf16[2,2,64,256]{3,2,1,0:T(8,128)(2,1)S(1)}, bf16[2,2,64,256]{3,2,1,0:T(8,128)(2,1)S(1)}, bf16[2,2,64...) custom-call(s32[2,2]{1,0:T(2,128)S(1)} %multiply_add_fusion.refs_0_,, ...), custom_call_target="tpu_custom_call" | custom-call | flops 67108864 | bytes 4194304 | tf_op jit(solution)/shard_map/extract/pallas_call | solution.py:342
  16.0 0.0 collective-permute-done.7.refs_0_
  16.0 3.6 %collective-permute-start.8 = (bf16[2,256,256]{2,1,0:T(8,128)(2,1)S(1)}, bf16[2,256,256]{2,1,0:T(8,128)(2,1)S(1)}, u32[]{:S(2)}, u32[]{:S(2)}) collective-permute-start(bf16[2,256,256]{2,1,0:T(8,128)(2,1)S(1)} %collective-permute-done.7.refs_0_), channel_id=1, source_target_pairs={{0,16},{1,17},{2,18},{3,19},{4,20},{5,21},{6,22},{7,23},{8,24},{9,... | collective-permute-start | bytes 786440 | tf_op jit(solution)/shard_map/ppermute | solution.py:303
  19.6 2.0 %collective-permute-start.10 = (bf16[2,2,64,256]{3,2,1,0:T(8,128)(2,1)S(1)}, bf16[2,2,64,256]{3,2,1,0:T(8,128)(2,1)S(1)}, u32[]{:S(2)}, u32[]{:S(2)}) collective-permute-start(bf16[2,2,64,256]{3,2,1,0:T(8,128)(2,1)S(1)} %get-tuple-element.123), channel_id=1, source_target_pairs={{0,1},{1,2},{2,3},{3,4},{4,5},{5,6},{6,7},{7,0},{8,9},{9,10},{10,1... | collective-permute-start | bytes 393224 | tf_op jit(solution)/shard_map/ppermute | solution.py:303
  21.6 2.8 %collective-permute-start.11 = (bf16[2,2,64,256]{3,2,1,0:T(8,128)(2,1)S(1)}, bf16[2,2,64,256]{3,2,1,0:T(8,128)(2,1)S(1)}, u32[]{:S(2)}, u32[]{:S(2)}) collective-permute-start(bf16[2,2,64,256]{3,2,1,0:T(8,128)(2,1)S(1)} %get-tuple-element.125), channel_id=1, source_target_pairs={{0,7},{1,0},{2,1},{3,2},{4,3},{5,4},{6,5},{7,6},{8,15},{9,8},{10,9... | collective-permute-start | bytes 393224 | tf_op jit(solution)/shard_map/ppermute | solution.py:303
  24.4 1.6 %collective-permute-start.12 = (bf16[2,2,64,256]{3,2,1,0:T(8,128)(2,1)S(1)}, bf16[2,2,64,256]{3,2,1,0:T(8,128)(2,1)S(1)}, u32[]{:S(2)}, u32[]{:S(2)}) collective-permute-start(bf16[2,2,64,256]{3,2,1,0:T(8,128)(2,1)S(1)} %get-tuple-element.126), channel_id=1, source_target_pairs={{0,6},{1,7},{2,0},{3,1},{4,2},{5,3},{6,4},{7,5},{8,14},{9,15},{10,... | collective-permute-start | bytes 393224 | tf_op jit(solution)/shard_map/ppermute | solution.py:303
  26.0 0.0 collective-permute-start.13
  26.0 1.5 %collective-permute-done.10.refs_1_ = bf16[2,2,64,256]{3,2,1,0:T(8,128)(2,1)S(1)} collective-permute-done((bf16[2,2,64,256]{3,2,1,0:T(8,128)(2,1)S(1)}, bf16[2,2,64,256]{3,2,1,0:T(8,128)(2,1)S(1)}, u32[]{:S(2)}, u32[]{:S(2)}) %collective-permute-start.10) | collective-permute-done | bytes 131104 | tf_op jit(solution)/shard_map/ppermute | solution.py:303
  27.6 0.0 collective-permute-start.14
  27.6 0.4 collective-permute-done.11.refs_3_
  28.0 0.0 collective-permute-start.15
  28.0 1.7 %collective-permute-done.12.refs_4_ = bf16[2,2,64,256]{3,2,1,0:T(8,128)(2,1)S(1)} collective-permute-done((bf16[2,2,64,256]{3,2,1,0:T(8,128)(2,1)S(1)}, bf16[2,2,64,256]{3,2,1,0:T(8,128)(2,1)S(1)}, u32[]{:S(2)}, u32[]{:S(2)}) %collective-permute-start.12) | collective-permute-done | bytes 131104 | tf_op jit(solution)/shard_map/ppermute | solution.py:303
  29.8 2.5 %collective-permute-start.16 = (bf16[2,2,64,256]{3,2,1,0:T(8,128)(2,1)S(1)}, bf16[2,2,64,256]{3,2,1,0:T(8,128)(2,1)S(1)}, u32[]{:S(2)}, u32[]{:S(2)}) collective-permute-start(bf16[2,2,64,256]{3,2,1,0:T(8,128)(2,1)S(1)} %get-tuple-element.130), channel_id=1, source_target_pairs={{0,15},{1,8},{2,9},{3,10},{4,11},{5,12},{6,13},{7,14},{8,7},{9,0},... | collective-permute-start | bytes 393224 | tf_op jit(solution)/shard_map/ppermute | solution.py:303
  32.3 1.0 %collective-permute-done.13.refs_5_ = bf16[2,2,64,256]{3,2,1,0:T(8,128)(2,1)S(1)} collective-permute-done((bf16[2,2,64,256]{3,2,1,0:T(8,128)(2,1)S(1)}, bf16[2,2,64,256]{3,2,1,0:T(8,128)(2,1)S(1)}, u32[]{:S(2)}, u32[]{:S(2)}) %collective-permute-start.13) | collective-permute-done | bytes 131104 | tf_op jit(solution)/shard_map/ppermute | solution.py:303
  33.3 1.5 %collective-permute-start.17 = (bf16[2,2,64,256]{3,2,1,0:T(8,128)(2,1)S(1)}, bf16[2,2,64,256]{3,2,1,0:T(8,128)(2,1)S(1)}, u32[]{:S(2)}, u32[]{:S(2)}) collective-permute-start(bf16[2,2,64,256]{3,2,1,0:T(8,128)(2,1)S(1)} %get-tuple-element.131), channel_id=1, source_target_pairs={{0,14},{1,15},{2,8},{3,9},{4,10},{5,11},{6,12},{7,13},{8,6},{9,7},... | collective-permute-start | bytes 393224 | tf_op jit(solution)/shard_map/ppermute | solution.py:303
  34.8 0.0 collective-permute-done.8.refs_1_
  34.8 1.0 %start.1 = f32[2,2,256,256]{3,2,1,0:T(8,128)S(1)} custom-call(s32[2,2]{1,0:T(2,128)S(1)} %collective-permute-done.4.refs_2_.places, f32[2,256,256]{2,1,0:T(8,128)S(1)} %copy-done.2, bf16[2,256,256]{2,1,0:T(8,128)(2,1)S(1)} %collective-permute-done.7.refs_0_, bf16[2,256,256]{2,1,0:T(8,128)(2,1)S(1)} %collective-permute-done.8.refs_1_, ...), custom_call_target="tpu_custom_call" | custom-call | flops 1073741824 | bytes 4194304 | tf_op jit(solution)/shard_map/start/pallas_call | solution.py:355
  35.8 0.0 collective-permute-done.14.refs_6_
  35.9 1.5 %collective-permute-done.16.refs_8_ = bf16[2,2,64,256]{3,2,1,0:T(8,128)(2,1)S(1)} collective-permute-done((bf16[2,2,64,256]{3,2,1,0:T(8,128)(2,1)S(1)}, bf16[2,2,64,256]{3,2,1,0:T(8,128)(2,1)S(1)}, u32[]{:S(2)}, u32[]{:S(2)}) %collective-permute-start.16) | collective-permute-done | bytes 131104 | tf_op jit(solution)/shard_map/ppermute | solution.py:303
  37.3 1.7 %collective-permute-done.17.refs_9_ = bf16[2,2,64,256]{3,2,1,0:T(8,128)(2,1)S(1)} collective-permute-done((bf16[2,2,64,256]{3,2,1,0:T(8,128)(2,1)S(1)}, bf16[2,2,64,256]{3,2,1,0:T(8,128)(2,1)S(1)}, u32[]{:S(2)}, u32[]{:S(2)}) %collective-permute-start.17) | collective-permute-done | bytes 131104 | tf_op jit(solution)/shard_map/ppermute | solution.py:303
  39.0 3.6 %collective-permute-done.9.refs_0_ = bf16[2,2,64,256]{3,2,1,0:T(8,128)(2,1)S(1)} collective-permute-done((bf16[2,2,64,256]{3,2,1,0:T(8,128)(2,1)S(1)}, bf16[2,2,64,256]{3,2,1,0:T(8,128)(2,1)S(1)}, u32[]{:S(2)}, u32[]{:S(2)}) %collective-permute-start.9) | collective-permute-done | bytes 131104 | tf_op jit(solution)/shard_map/ppermute | solution.py:303
  42.7 2.0 %near.3 = (bf16[2,2,256,256]{3,2,1,0:T(8,128)(2,1)S(1)}, f32[2,256,256]{2,1,0:T(8,128)S(1)}, bf16[2,256,256]{2,1,0:T(8,128)(2,1)S(1)}) custom-call(s32[2,2]{1,0:T(2,128)S(1)} %collective-permute-done.4.refs_2_.places, f32[2,2,256,256]{3,2,1,0:T(8,128)S(1)} %start.1, bf16[512,768]{1,0:T(8,128)(2,1)S(1)} %copy-done.3, bf16[768,512]{1,0:T(8,128)(2,1)S(1)} %copy-done.4, ...), custom_call_target="tpu_custom_call" | custom-call | flops 1073741824 | bytes 4194304 | tf_op jit(solution)/shard_map/near/pallas_call | solution.py:364
  44.7 0.1 collective-permute-start.19
  44.7 4.4 %near.2 = (bf16[2,2,256,256]{3,2,1,0:T(8,128)(2,1)S(1)}, f32[2,256,256]{2,1,0:T(8,128)S(1)}, bf16[2,256,256]{2,1,0:T(8,128)(2,1)S(1)}) custom-call(s32[2,2]{1,0:T(2,128)S(1)} %collective-permute-done.4.refs_2_.places, f32[2,2,256,256]{3,2,1,0:T(8,128)S(1)} %start.1, bf16[512,768]{1,0:T(8,128)(2,1)S(1)} %copy-done.3, bf16[768,512]{1,0:T(8,128)(2,1)S(1)} %copy-done.4, ...), custom_call_target="tpu_custom_call" | custom-call | flops 1073741824 | bytes 4194304 | tf_op jit(solution)/shard_map/near/pallas_call | solution.py:364
  49.1 2.1 %collective-permute-start.18 = (bf16[2,256,256]{2,1,0:T(8,128)(2,1)S(1)}, bf16[2,256,256]{2,1,0:T(8,128)(2,1)S(1)}, u32[]{:S(2)}, u32[]{:S(2)}) collective-permute-start(bf16[2,256,256]{2,1,0:T(8,128)(2,1)S(1)} %get-tuple-element.134), channel_id=1, source_target_pairs={{0,16},{1,17},{2,18},{3,19},{4,20},{5,21},{6,22},{7,23},{8,24},{9,... | collective-permute-start | bytes 786440 | tf_op jit(solution)/shard_map/ppermute | solution.py:303
  51.2 2.6 %collective-permute-done.19.arrived = bf16[2,256,256]{2,1,0:T(8,128)(2,1)S(1)} collective-permute-done((bf16[2,256,256]{2,1,0:T(8,128)(2,1)S(1)}, bf16[2,256,256]{2,1,0:T(8,128)(2,1)S(1)}, u32[]{:S(2)}, u32[]{:S(2)}) %collective-permute-start.19) | collective-permute-done | bytes 262176 | tf_op jit(solution)/shard_map/ppermute | solution.py:303
  53.8 3.9 %far.3 = (bf16[2,256,256]{2,1,0:T(8,128)(2,1)S(1)}, bf16[2,256,256]{2,1,0:T(8,128)(2,1)S(1)}, f32[2,256,256]{2,1,0:T(8,128)S(1)}) custom-call(f32[2,2,256,256]{3,2,1,0:T(8,128)S(1)} %start.1, bf16[512,768]{1,0:T(8,128)(2,1)S(1)} %copy-done.3, bf16[768,512]{1,0:T(8,128)(2,1)S(1)} %copy-done.4, bf16[2,2,256,256]{3,2,1,0:T(8,128)(2,1)S(1)} %get-tuple-element.136.frames, ...), custom_call_target="tpu_custom_call" | custom-call | flops 2147483648 | bytes 4194304 | tf_op jit(solution)/shard_map/far/pallas_call | solution.py:374
  57.8 0.1 collective-permute-start.21
  57.9 0.5 collective-permute-done.18.arrived
  58.4 1.5 %far.2 = (bf16[2,256,256]{2,1,0:T(8,128)(2,1)S(1)}, bf16[2,256,256]{2,1,0:T(8,128)(2,1)S(1)}, f32[2,256,256]{2,1,0:T(8,128)S(1)}) custom-call(f32[2,2,256,256]{3,2,1,0:T(8,128)S(1)} %start.1, bf16[512,768]{1,0:T(8,128)(2,1)S(1)} %copy-done.3, bf16[768,512]{1,0:T(8,128)(2,1)S(1)} %copy-done.4, bf16[2,2,256,256]{3,2,1,0:T(8,128)(2,1)S(1)} %get-tuple-element.132.frames, ...), custom_call_target="tpu_custom_call" | custom-call | flops 2147483648 | bytes 4194304 | tf_op jit(solution)/shard_map/far/pallas_call | solution.py:374
  59.9 0.1 collective-permute-start.20
  60.0 1.0 %probe.3 = (f32[2,64,256]{2,1,0:T(8,128)S(1)}, f32[2,64,256]{2,1,0:T(8,128)S(1)}, bf16[2,2,64,256]{3,2,1,0:T(8,128)(2,1)S(1)}) custom-call(s32[2,2]{1,0:T(2,128)S(1)} %collective-permute-done.4.refs_2_.places, f32[2,256,256]{2,1,0:T(8,128)S(1)} %get-tuple-element.135.refs_0_, f32[2,256,256]{2,1,0:T(8,128)S(1)} %get-tuple-element.139.refs_1_), custom_call_target="tpu_custom_call" | custom-call | flops 67108864 | bytes 4194304 | tf_op jit(solution)/shard_map/probe/pallas_call | solution.py:394
  61.0 0.6 collective-permute-start.22
  61.6 0.0 collective-permute-done.21.refs_3_
  61.6 0.0 collective-permute-done.20.refs_2_
  61.6 0.7 part.1
  62.3 3.6 %collective-permute-start.23 = (bf16[2,2,2,64,256]{4,3,2,1,0:T(8,128)(2,1)S(1)}, bf16[2,2,2,64,256]{4,3,2,1,0:T(8,128)(2,1)S(1)}, u32[]{:S(2)}, u32[]{:S(2)}) collective-permute-start(bf16[2,2,2,64,256]{4,3,2,1,0:T(8,128)(2,1)S(1)} %get-tuple-element.150), channel_id=1, source_target_pairs={{0,6},{1,7},{2,0},{3,1},{4,2},{5,3},{6,4},{7,5},{8,14},{9,15},{10,... | collective-permute-start | bytes 786440 | tf_op jit(solution)/shard_map/ppermute | solution.py:303
  65.9 2.0 %collective-permute-start.25 = (bf16[2,2,2,64,256]{4,3,2,1,0:T(8,128)(2,1)S(1)}, bf16[2,2,2,64,256]{4,3,2,1,0:T(8,128)(2,1)S(1)}, u32[]{:S(2)}, u32[]{:S(2)}) collective-permute-start(bf16[2,2,2,64,256]{4,3,2,1,0:T(8,128)(2,1)S(1)} %get-tuple-element.152), channel_id=1, source_target_pairs={{0,1},{1,2},{2,3},{3,4},{4,5},{5,6},{6,7},{7,0},{8,9},{9,10},{10,1... | collective-permute-start | bytes 786440 | tf_op jit(solution)/shard_map/ppermute | solution.py:303
  67.9 17.5 %while.14 = (s32[]{:T(128)}, f32[2,64,256]{2,1,0:T(8,128)S(1)}, f32[2,64,256]{2,1,0:T(8,128)S(1)}, s32[]{:T(128)}, pred[]{:T(512)}, /*index=5*/bf16[2,2,64,256]{3,2,1,0:T(8,128)(2,1)S(1)}, s32[]{:T(128)}) while((s32[]{:T(128)}, f32[2,64,256]{2,1,0:T(8,128)S(1)}, f32[2,64,256]{2,1,0:T(8,128)S(1)}, s32[]{:T(128)}, pred[]{:T(512)}, ...), condition=%wide.region_1.2_spmd, body=%wide.region_0.1_spmd.sunk | while | flops 458754 | bytes 1966278 | solution.py:422
  67.9 2.5 %collective-permute-start = (bf16[2,64,256]{2,1,0:T(8,128)(2,1)S(1)}, bf16[2,64,256]{2,1,0:T(8,128)(2,1)S(1)}, u32[]{:S(2)}, u32[]{:S(2)}) collective-permute-start(bf16[2,64,256]{2,1,0:T(8,128)(2,1)S(1)} %fusion.5), channel_id=1, source_target_pairs={{0,16},{1,17},{2,18},{3,19},{4,20},{5,21},{6,22},{7,23},{8,24},{9,... | collective-permute-start | bytes 196616 | tf_op jit(solution)/shard_map/while/body/ppermute | solution.py:303
  70.4 1.9 %collective-permute-done = bf16[2,64,256]{2,1,0:T(8,128)(2,1)S(1)} collective-permute-done((bf16[2,64,256]{2,1,0:T(8,128)(2,1)S(1)}, bf16[2,64,256]{2,1,0:T(8,128)(2,1)S(1)}, u32[]{:S(2)}, u32[]{:S(2)}) %collective-permute-start) | collective-permute-done | bytes 65568 | tf_op jit(solution)/shard_map/while/body/ppermute | solution.py:303
  72.3 0.1 collective-permute-start.1
  72.4 8.5 %collective-permute-done.1 = bf16[2,64,256]{2,1,0:T(8,128)(2,1)S(1)} collective-permute-done((bf16[2,64,256]{2,1,0:T(8,128)(2,1)S(1)}, bf16[2,64,256]{2,1,0:T(8,128)(2,1)S(1)}, u32[]{:S(2)}, u32[]{:S(2)}) %collective-permute-start.1) | collective-permute-done | bytes 65568 | tf_op jit(solution)/shard_map/while/body/ppermute | solution.py:407
  80.9 0.1 collective-permute-start.2
  81.0 4.4 %collective-permute-done.2 = bf16[2,64,256]{2,1,0:T(8,128)(2,1)S(1)} collective-permute-done((bf16[2,64,256]{2,1,0:T(8,128)(2,1)S(1)}, bf16[2,64,256]{2,1,0:T(8,128)(2,1)S(1)}, u32[]{:S(2)}, u32[]{:S(2)}) %collective-permute-start.2) | collective-permute-done | bytes 65568 | tf_op jit(solution)/shard_map/while/body/ppermute | solution.py:407
  85.4 0.0 collective-permute-done.23.refs_5_
  85.4 0.0 collective-permute-done.25.refs_8_
  85.5 0.0 collective-permute-done.26.refs_9_
  85.5 1.3 %collective-permute-start.27 = (bf16[2,64,256]{2,1,0:T(8,128)(2,1)S(1)}, bf16[2,64,256]{2,1,0:T(8,128)(2,1)S(1)}, u32[]{:S(2)}, u32[]{:S(2)}) collective-permute-start(bf16[2,64,256]{2,1,0:T(8,128)(2,1)S(1)} %convert_element_type.65), channel_id=1, source_target_pairs={{0,4},{1,5},{2,6},{3,7},{4,0},{5,1},{6,2},{7,3},{8,12},{9,13},{10,... | collective-permute-start | bytes 196616 | tf_op jit(solution)/shard_map/ppermute | solution.py:407
  86.8 2.7 %deposit.1 = f32[2,64,3072]{2,1,0:T(8,128)} custom-call(s32[2,2]{1,0:T(2,128)S(1)} %multiply_add_fusion.refs_0_, s32[2,2]{1,0:T(2,128)S(1)} %collective-permute-done.3.refs_1_, s32[2,2]{1,0:T(2,128)S(1)} %collective-permute-done.4.refs_2_.places, s32[2,2]{1,0:T(2,128)S(1)} %collective-permute-done.5.refs_3_, s32[2,2]{1,0:T(2,128)S(1)} %collective-permute-done.6.refs_4_, ...), custom_call_target="tpu_custom_call" | custom-call | flops 67108864 | bytes 4194304 | tf_op jit(solution)/shard_map/deposit/pallas_call | solution.py:427
  89.5 1.5 %collective-permute-done.27 = bf16[2,64,256]{2,1,0:T(8,128)(2,1)S(1)} collective-permute-done((bf16[2,64,256]{2,1,0:T(8,128)(2,1)S(1)}, bf16[2,64,256]{2,1,0:T(8,128)(2,1)S(1)}, u32[]{:S(2)}, u32[]{:S(2)}) %collective-permute-start.27) | collective-permute-done | bytes 65568 | tf_op jit(solution)/shard_map/ppermute | solution.py:407
  90.9 0.7 convert_add_fusion.3
  (20 shorter events, 0.1 us)
Async XLA Ops:
  0.6 1.6 %copy-start = (f32[2,2,2,256,256]{4,3,2,1,0:T(8,128)S(1)}, f32[2,2,2,256,256]{4,3,2,1,0:T(8,128)}, u32[]{:S(2)}) copy-start(f32[2,2,2,256,256]{4,3,2,1,0:T(8,128)} %waves.1) | copy-start | bytes 6291460
  2.2 12.6 %copy-start.1 = (f32[1,2,64,3072]{3,2,1,0:T(8,128)S(1)}, f32[1,2,64,3072]{3,2,1,0:T(8,128)}, u32[]{:S(2)}) copy-start(f32[1,2,64,3072]{3,2,1,0:T(8,128)} %param.9) | copy-start | bytes 4718596
  2.2 32.6 %copy-start.2 = (f32[2,256,256]{2,1,0:T(8,128)S(1)}, f32[2,256,256]{2,1,0:T(8,128)}, u32[]{:S(2)}) copy-start(f32[2,256,256]{2,1,0:T(8,128)} %probe.2) | copy-start | bytes 1572868
  2.2 32.6 %copy-start.3 = (bf16[512,768]{1,0:T(8,128)(2,1)S(1)}, bf16[512,768]{1,0:T(8,128)(2,1)}, u32[]{:S(2)}) copy-start(bf16[512,768]{1,0:T(8,128)(2,1)} %constant.46.clone.refs_2_.left) | copy-start | bytes 2359300
  2.2 32.6 %copy-start.4 = (bf16[768,512]{1,0:T(8,128)(2,1)S(1)}, bf16[768,512]{1,0:T(8,128)(2,1)}, u32[]{:S(2)}) copy-start(bf16[768,512]{1,0:T(8,128)(2,1)} %constant.47.clone.refs_3_.right) | copy-start | bytes 2359300
  2.3 13.6 %collective-permute-start.7 = (bf16[2,256,256]{2,1,0:T(8,128)(2,1)S(1)}, bf16[2,256,256]{2,1,0:T(8,128)(2,1)S(1)}, u32[]{:S(2)}, u32[]{:S(2)}) collective-permute-start(bf16[2,256,256]{2,1,0:T(8,128)(2,1)S(1)} %pick.1), channel_id=1, source_target_pairs={{0,2},{1,3},{2,4},{3,5},{4,6},{5,7},{6,0},{7,1},{8,10},{9,11},{10,... | collective-permute-start | bytes 786440 | tf_op jit(solution)/shard_map/ppermute | solution.py:293
  6.1 7.7 %collective-permute-start.4 = (s32[2,2]{1,0:T(2,128)S(1)}, s32[2,2]{1,0:T(2,128)S(1)}, u32[]{:S(2)}, u32[]{:S(2)}) collective-permute-start(s32[2,2]{1,0:T(2,128)S(1)} %multiply_add_fusion.refs_0_), channel_id=1, source_target_pairs={{0,2},{1,3},{2,4},{3,5},{4,6},{5,7},{6,0},{7,1},{8,10},{9,11},{10,... | collective-permute-start | bytes 56 | tf_op jit(solution)/shard_map/ppermute | solution.py:293
  7.7 7.1 %collective-permute-start.3 = (s32[2,2]{1,0:T(2,128)S(1)}, s32[2,2]{1,0:T(2,128)S(1)}, u32[]{:S(2)}, u32[]{:S(2)}) collective-permute-start(s32[2,2]{1,0:T(2,128)S(1)} %multiply_add_fusion.refs_0_), channel_id=1, source_target_pairs={{0,1},{1,2},{2,3},{3,4},{4,5},{5,6},{6,7},{7,0},{8,9},{9,10},{10,1... | collective-permute-start | bytes 56 | tf_op jit(solution)/shard_map/ppermute | solution.py:293
  9.2 5.6 %collective-permute-start.5 = (s32[2,2]{1,0:T(2,128)S(1)}, s32[2,2]{1,0:T(2,128)S(1)}, u32[]{:S(2)}, u32[]{:S(2)}) collective-permute-start(s32[2,2]{1,0:T(2,128)S(1)} %multiply_add_fusion.refs_0_), channel_id=1, source_target_pairs={{0,3},{1,4},{2,5},{3,6},{4,7},{5,0},{6,1},{7,2},{8,11},{9,12},{10,... | collective-permute-start | bytes 56 | tf_op jit(solution)/shard_map/ppermute | solution.py:293
  10.3 4.5 %collective-permute-start.6 = (s32[2,2]{1,0:T(2,128)S(1)}, s32[2,2]{1,0:T(2,128)S(1)}, u32[]{:S(2)}, u32[]{:S(2)}) collective-permute-start(s32[2,2]{1,0:T(2,128)S(1)} %multiply_add_fusion.refs_0_), channel_id=1, source_target_pairs={{0,4},{1,5},{2,6},{3,7},{4,0},{5,1},{6,2},{7,3},{8,12},{9,13},{10,... | collective-permute-start | bytes 56 | tf_op jit(solution)/shard_map/ppermute | solution.py:293
  16.0 18.8 %collective-permute-start.8 = (bf16[2,256,256]{2,1,0:T(8,128)(2,1)S(1)}, bf16[2,256,256]{2,1,0:T(8,128)(2,1)S(1)}, u32[]{:S(2)}, u32[]{:S(2)}) collective-permute-start(bf16[2,256,256]{2,1,0:T(8,128)(2,1)S(1)} %collective-permute-done.7.refs_0_), channel_id=1, source_target_pairs={{0,16},{1,17},{2,18},{3,19},{4,20},{5,21},{6,22},{7,23},{8,24},{9,... | collective-permute-start | bytes 786440 | tf_op jit(solution)/shard_map/ppermute | solution.py:303
  19.6 7.9 %collective-permute-start.10 = (bf16[2,2,64,256]{3,2,1,0:T(8,128)(2,1)S(1)}, bf16[2,2,64,256]{3,2,1,0:T(8,128)(2,1)S(1)}, u32[]{:S(2)}, u32[]{:S(2)}) collective-permute-start(bf16[2,2,64,256]{3,2,1,0:T(8,128)(2,1)S(1)} %get-tuple-element.123), channel_id=1, source_target_pairs={{0,1},{1,2},{2,3},{3,4},{4,5},{5,6},{6,7},{7,0},{8,9},{9,10},{10,1... | collective-permute-start | bytes 393224 | tf_op jit(solution)/shard_map/ppermute | solution.py:303
  21.6 6.4 %collective-permute-start.11 = (bf16[2,2,64,256]{3,2,1,0:T(8,128)(2,1)S(1)}, bf16[2,2,64,256]{3,2,1,0:T(8,128)(2,1)S(1)}, u32[]{:S(2)}, u32[]{:S(2)}) collective-permute-start(bf16[2,2,64,256]{3,2,1,0:T(8,128)(2,1)S(1)} %get-tuple-element.125), channel_id=1, source_target_pairs={{0,7},{1,0},{2,1},{3,2},{4,3},{5,4},{6,5},{7,6},{8,15},{9,8},{10,9... | collective-permute-start | bytes 393224 | tf_op jit(solution)/shard_map/ppermute | solution.py:303
  24.4 5.3 %collective-permute-start.12 = (bf16[2,2,64,256]{3,2,1,0:T(8,128)(2,1)S(1)}, bf16[2,2,64,256]{3,2,1,0:T(8,128)(2,1)S(1)}, u32[]{:S(2)}, u32[]{:S(2)}) collective-permute-start(bf16[2,2,64,256]{3,2,1,0:T(8,128)(2,1)S(1)} %get-tuple-element.126), channel_id=1, source_target_pairs={{0,6},{1,7},{2,0},{3,1},{4,2},{5,3},{6,4},{7,5},{8,14},{9,15},{10,... | collective-permute-start | bytes 393224 | tf_op jit(solution)/shard_map/ppermute | solution.py:303
  26.0 7.3 %collective-permute-start.13 = (bf16[2,2,64,256]{3,2,1,0:T(8,128)(2,1)S(1)}, bf16[2,2,64,256]{3,2,1,0:T(8,128)(2,1)S(1)}, u32[]{:S(2)}, u32[]{:S(2)}) collective-permute-start(bf16[2,2,64,256]{3,2,1,0:T(8,128)(2,1)S(1)} %get-tuple-element.127), channel_id=1, source_target_pairs={{0,10},{1,11},{2,12},{3,13},{4,14},{5,15},{6,8},{7,9},{8,2},{9,3},... | collective-permute-start | bytes 393224 | tf_op jit(solution)/shard_map/ppermute | solution.py:303
  27.6 8.3 %collective-permute-start.14 = (bf16[2,2,64,256]{3,2,1,0:T(8,128)(2,1)S(1)}, bf16[2,2,64,256]{3,2,1,0:T(8,128)(2,1)S(1)}, u32[]{:S(2)}, u32[]{:S(2)}) collective-permute-start(bf16[2,2,64,256]{3,2,1,0:T(8,128)(2,1)S(1)} %get-tuple-element.128), channel_id=1, source_target_pairs={{0,9},{1,10},{2,11},{3,12},{4,13},{5,14},{6,15},{7,8},{8,1},{9,2},... | collective-permute-start | bytes 393224 | tf_op jit(solution)/shard_map/ppermute | solution.py:303
  28.0 7.8 %collective-permute-start.15 = (bf16[2,2,64,256]{3,2,1,0:T(8,128)(2,1)S(1)}, bf16[2,2,64,256]{3,2,1,0:T(8,128)(2,1)S(1)}, u32[]{:S(2)}, u32[]{:S(2)}) collective-permute-start(bf16[2,2,64,256]{3,2,1,0:T(8,128)(2,1)S(1)} %get-tuple-element.129), channel_id=1, source_target_pairs={{0,8},{1,9},{2,10},{3,11},{4,12},{5,13},{6,14},{7,15},{8,0},{9,1},... | collective-permute-start | bytes 393224 | tf_op jit(solution)/shard_map/ppermute | solution.py:303
  29.8 7.6 %collective-permute-start.16 = (bf16[2,2,64,256]{3,2,1,0:T(8,128)(2,1)S(1)}, bf16[2,2,64,256]{3,2,1,0:T(8,128)(2,1)S(1)}, u32[]{:S(2)}, u32[]{:S(2)}) collective-permute-start(bf16[2,2,64,256]{3,2,1,0:T(8,128)(2,1)S(1)} %get-tuple-element.130), channel_id=1, source_target_pairs={{0,15},{1,8},{2,9},{3,10},{4,11},{5,12},{6,13},{7,14},{8,7},{9,0},... | collective-permute-start | bytes 393224 | tf_op jit(solution)/shard_map/ppermute | solution.py:303
  33.3 5.8 %collective-permute-start.17 = (bf16[2,2,64,256]{3,2,1,0:T(8,128)(2,1)S(1)}, bf16[2,2,64,256]{3,2,1,0:T(8,128)(2,1)S(1)}, u32[]{:S(2)}, u32[]{:S(2)}) collective-permute-start(bf16[2,2,64,256]{3,2,1,0:T(8,128)(2,1)S(1)} %get-tuple-element.131), channel_id=1, source_target_pairs={{0,14},{1,15},{2,8},{3,9},{4,10},{5,11},{6,12},{7,13},{8,6},{9,7},... | collective-permute-start | bytes 393224 | tf_op jit(solution)/shard_map/ppermute | solution.py:303
  34.8 7.9 %collective-permute-start.9 = (bf16[2,2,64,256]{3,2,1,0:T(8,128)(2,1)S(1)}, bf16[2,2,64,256]{3,2,1,0:T(8,128)(2,1)S(1)}, u32[]{:S(2)}, u32[]{:S(2)}) collective-permute-start(bf16[2,2,64,256]{3,2,1,0:T(8,128)(2,1)S(1)} %get-tuple-element.122), channel_id=1, source_target_pairs={{0,2},{1,3},{2,4},{3,5},{4,6},{5,7},{6,0},{7,1},{8,10},{9,11},{10,... | collective-permute-start | bytes 393224 | tf_op jit(solution)/shard_map/ppermute | solution.py:303
  44.7 9.2 %collective-permute-start.19 = (bf16[2,256,256]{2,1,0:T(8,128)(2,1)S(1)}, bf16[2,256,256]{2,1,0:T(8,128)(2,1)S(1)}, u32[]{:S(2)}, u32[]{:S(2)}) collective-permute-start(bf16[2,256,256]{2,1,0:T(8,128)(2,1)S(1)} %get-tuple-element.138), channel_id=1, source_target_pairs={{0,16},{1,17},{2,18},{3,19},{4,20},{5,21},{6,22},{7,23},{8,24},{9,... | collective-permute-start | bytes 786440 | tf_op jit(solution)/shard_map/ppermute | solution.py:303
  49.1 9.2 %collective-permute-start.18 = (bf16[2,256,256]{2,1,0:T(8,128)(2,1)S(1)}, bf16[2,256,256]{2,1,0:T(8,128)(2,1)S(1)}, u32[]{:S(2)}, u32[]{:S(2)}) collective-permute-start(bf16[2,256,256]{2,1,0:T(8,128)(2,1)S(1)} %get-tuple-element.134), channel_id=1, source_target_pairs={{0,16},{1,17},{2,18},{3,19},{4,20},{5,21},{6,22},{7,23},{8,24},{9,... | collective-permute-start | bytes 786440 | tf_op jit(solution)/shard_map/ppermute | solution.py:303
  57.8 3.8 %collective-permute-start.21 = (bf16[2,256,256]{2,1,0:T(8,128)(2,1)S(1)}, bf16[2,256,256]{2,1,0:T(8,128)(2,1)S(1)}, u32[]{:S(2)}, u32[]{:S(2)}) collective-permute-start(bf16[2,256,256]{2,1,0:T(8,128)(2,1)S(1)} %get-tuple-element.144), channel_id=1, source_target_pairs={{0,8},{1,9},{2,10},{3,11},{4,12},{5,13},{6,14},{7,15},{8,0},{9,1},... | collective-permute-start | bytes 786440 | tf_op jit(solution)/shard_map/ppermute | solution.py:303
  59.9 1.7 %collective-permute-start.20 = (bf16[2,256,256]{2,1,0:T(8,128)(2,1)S(1)}, bf16[2,256,256]{2,1,0:T(8,128)(2,1)S(1)}, u32[]{:S(2)}, u32[]{:S(2)}) collective-permute-start(bf16[2,256,256]{2,1,0:T(8,128)(2,1)S(1)} %get-tuple-element.143), channel_id=1, source_target_pairs={{0,8},{1,9},{2,10},{3,11},{4,12},{5,13},{6,14},{7,15},{8,0},{9,1},... | collective-permute-start | bytes 786440 | tf_op jit(solution)/shard_map/ppermute | solution.py:303
  61.0 6.9 %collective-permute-start.22 = (bf16[2,2,64,256]{3,2,1,0:T(8,128)(2,1)S(1)}, bf16[2,2,64,256]{3,2,1,0:T(8,128)(2,1)S(1)}, u32[]{:S(2)}, u32[]{:S(2)}) collective-permute-start(bf16[2,2,64,256]{3,2,1,0:T(8,128)(2,1)S(1)} %get-tuple-element.148), channel_id=1, source_target_pairs={{0,8},{1,9},{2,10},{3,11},{4,12},{5,13},{6,14},{7,15},{8,0},{9,1},... | collective-permute-start | bytes 393224 | tf_op jit(solution)/shard_map/ppermute | solution.py:303
  62.3 23.1 %collective-permute-start.23 = (bf16[2,2,2,64,256]{4,3,2,1,0:T(8,128)(2,1)S(1)}, bf16[2,2,2,64,256]{4,3,2,1,0:T(8,128)(2,1)S(1)}, u32[]{:S(2)}, u32[]{:S(2)}) collective-permute-start(bf16[2,2,2,64,256]{4,3,2,1,0:T(8,128)(2,1)S(1)} %get-tuple-element.150), channel_id=1, source_target_pairs={{0,6},{1,7},{2,0},{3,1},{4,2},{5,3},{6,4},{7,5},{8,14},{9,15},{10,... | collective-permute-start | bytes 786440 | tf_op jit(solution)/shard_map/ppermute | solution.py:303
  65.9 19.6 %collective-permute-start.24 = (bf16[2,2,2,64,256]{4,3,2,1,0:T(8,128)(2,1)S(1)}, bf16[2,2,2,64,256]{4,3,2,1,0:T(8,128)(2,1)S(1)}, u32[]{:S(2)}, u32[]{:S(2)}) collective-permute-start(bf16[2,2,2,64,256]{4,3,2,1,0:T(8,128)(2,1)S(1)} %get-tuple-element.151), channel_id=1, source_target_pairs={{0,7},{1,0},{2,1},{3,2},{4,3},{5,4},{6,5},{7,6},{8,15},{9,8},{10,9... | collective-permute-start | bytes 786440 | tf_op jit(solution)/shard_map/ppermute | solution.py:303
  65.9 19.6 %collective-permute-start.25 = (bf16[2,2,2,64,256]{4,3,2,1,0:T(8,128)(2,1)S(1)}, bf16[2,2,2,64,256]{4,3,2,1,0:T(8,128)(2,1)S(1)}, u32[]{:S(2)}, u32[]{:S(2)}) collective-permute-start(bf16[2,2,2,64,256]{4,3,2,1,0:T(8,128)(2,1)S(1)} %get-tuple-element.152), channel_id=1, source_target_pairs={{0,1},{1,2},{2,3},{3,4},{4,5},{5,6},{6,7},{7,0},{8,9},{9,10},{10,1... | collective-permute-start | bytes 786440 | tf_op jit(solution)/shard_map/ppermute | solution.py:303
  67.9 17.5 %collective-permute-start.26 = (bf16[2,2,2,64,256]{4,3,2,1,0:T(8,128)(2,1)S(1)}, bf16[2,2,2,64,256]{4,3,2,1,0:T(8,128)(2,1)S(1)}, u32[]{:S(2)}, u32[]{:S(2)}) collective-permute-start(bf16[2,2,2,64,256]{4,3,2,1,0:T(8,128)(2,1)S(1)} %get-tuple-element.153), channel_id=1, source_target_pairs={{0,2},{1,3},{2,4},{3,5},{4,6},{5,7},{6,0},{7,1},{8,10},{9,11},{10,... | collective-permute-start | bytes 786440 | tf_op jit(solution)/shard_map/ppermute | solution.py:303
  67.9 4.4 %collective-permute-start = (bf16[2,64,256]{2,1,0:T(8,128)(2,1)S(1)}, bf16[2,64,256]{2,1,0:T(8,128)(2,1)S(1)}, u32[]{:S(2)}, u32[]{:S(2)}) collective-permute-start(bf16[2,64,256]{2,1,0:T(8,128)(2,1)S(1)} %fusion.5), channel_id=1, source_target_pairs={{0,16},{1,17},{2,18},{3,19},{4,20},{5,21},{6,22},{7,23},{8,24},{9,... | collective-permute-start | bytes 196616 | tf_op jit(solution)/shard_map/while/body/ppermute | solution.py:303
  72.3 8.6 %collective-permute-start.1 = (bf16[2,64,256]{2,1,0:T(8,128)(2,1)S(1)}, bf16[2,64,256]{2,1,0:T(8,128)(2,1)S(1)}, u32[]{:S(2)}, u32[]{:S(2)}) collective-permute-start(bf16[2,64,256]{2,1,0:T(8,128)(2,1)S(1)} %get-tuple-element.214), channel_id=1, source_target_pairs={{0,1},{1,0},{2,3},{3,2},{4,5},{5,4},{6,7},{7,6},{8,9},{9,8},{10,11... | collective-permute-start | bytes 196616 | tf_op jit(solution)/shard_map/while/body/ppermute | solution.py:407
  80.9 4.5 %collective-permute-start.2 = (bf16[2,64,256]{2,1,0:T(8,128)(2,1)S(1)}, bf16[2,64,256]{2,1,0:T(8,128)(2,1)S(1)}, u32[]{:S(2)}, u32[]{:S(2)}) collective-permute-start(bf16[2,64,256]{2,1,0:T(8,128)(2,1)S(1)} %add_convert_fusion.2), channel_id=1, source_target_pairs={{0,2},{1,3},{2,0},{3,1},{4,6},{5,7},{6,4},{7,5},{8,10},{9,11},{10,... | collective-permute-start | bytes 196616 | tf_op jit(solution)/shard_map/while/body/ppermute | solution.py:407
  85.5 5.4 %collective-permute-start.27 = (bf16[2,64,256]{2,1,0:T(8,128)(2,1)S(1)}, bf16[2,64,256]{2,1,0:T(8,128)(2,1)S(1)}, u32[]{:S(2)}, u32[]{:S(2)}) collective-permute-start(bf16[2,64,256]{2,1,0:T(8,128)(2,1)S(1)} %convert_element_type.65), channel_id=1, source_target_pairs={{0,4},{1,5},{2,6},{3,7},{4,0},{5,1},{6,2},{7,3},{8,12},{9,13},{10,... | collective-permute-start | bytes 196616 | tf_op jit(solution)/shard_map/ppermute | solution.py:407

commit v3 on v2

--- a/solution.py
+++ b/solution.py
@@ -350,6 +350,8 @@
     adjoint, pieces[0, home] = lax.optimization_barrier((adjoint, pieces[0, home]))
     adjoints = [adjoint, across(adjoint, 2, 0, lower)]
     for flip, step in far_first:
+        if (flip, step) == (1, home):
+            pieces[1, home], pieces[0, 0] = lax.optimization_barrier((pieces[1, home], pieces[0, 0]))
         pieces[flip, step] = across(pieces[flip, step], flip, home - step)
 
     start = call(
@@ -406,21 +408,23 @@
         route = [(i, i ^ span) for i in range(regions)]
         return rounded.astype(f32) + lax.ppermute(rounded, "scan", route).astype(f32)
 
-    def probe_rounds(_, held):
-        near, away, given = held
-        away = across((away + given[1].astype(f32)).astype(bf16), 2, 0, lower).astype(f32)
-        total = jnp.where(half == 0, near + given[0].astype(f32), away)
-        for span in spans[:-1]:
-            total = scan_round(total, span)
-        return total, away, given
-
     half = lax.axis_index("depth") // (depth // 2)
     once = lax.axis_index("depth") // depth + 1
     assert regions & (regions - 1) == 0
     spans = [1 << level for level in range(regions.bit_length() - 1)]
-    near, parts[home] = lax.optimization_barrier((near, parts[home]))
+    given = across(probe_sent, 1, 0)
+    away = (away + given[1].astype(f32)).astype(bf16)
+    away, parts[home] = lax.optimization_barrier((away, parts[home]))
+
+    def probe_rounds(_, held):
+        near, given, away = held
+        total = jnp.where(half == 0, near + given[0].astype(f32), away.astype(f32))
+        for span in spans[:-1]:
+            total = scan_round(total, span)
+        return total, given, away
+
     probe_grad, *_ = lax.fori_loop(
-        0, once, probe_rounds, (near, away, across(probe_sent, 1, 0))
+        0, once, probe_rounds, (near, given, across(away, 2, 0, lower))
     )
     probe_grad, returned = lax.optimization_barrier((probe_grad, returned))
     probe_grad = scan_round(probe_grad, spans[-1])

time: 91.8 us -> 93.1 us (1.014)
  starting transfers between devices: 36.5 us -> 39.8 us
  waiting for transfers between devices: 32.7 us -> 30.8 us
    ppermute x20, waiting for transfers between devices: 16.6 us -> 12.7 us  [across(): return lax.ppermute(value, ('depth', 'scan'), route)]
    ppermute x3, waiting for transfers between devices: 14.3 us -> 16.3 us  [scan_round(): lax.ppermute(rounded, 'scan', route).astype(f32)]
    ppermute x20, starting transfers between devices: 25.1 us -> 26.9 us  [across(): return lax.ppermute(value, ('depth', 'scan'), route)]
    ppermute x3, starting transfers between devices: 1.48 us -> 2.96 us  [scan_round(): lax.ppermute(rounded, 'scan', route).astype(f32)]
  transfers between devices with their start and end apart: 28 -> 28, of which waited for: 15 -> 15; matrix products, arithmetic and copies ran while one was open for 1% -> 1% of each run, Pallas kernels for 18% -> 14%
where the time goes in v3:
time: 93.1 us; the launch traced here: 92.9 us
  starting transfers between devices  39.8 us (43%)
  waiting for transfers between devices  30.8 us (33%)
  Pallas kernels  18.3 us (20%)
  local copies, waits for them, and re-layouts  1.6 us (2%)
  other arithmetic  1.45 us (2%)
    ppermute x20, starting transfers between devices, across(): return lax.ppermute(value, ('depth', 'scan'), route)  26.9 us
    ppermute x3, waiting for transfers between devices, scan_round(): lax.ppermute(rounded, 'scan', route).astype(f32)  16.3 us
    ppermute x20, waiting for transfers between devices, across(): return lax.ppermute(value, ('depth', 'scan'), route)  12.7 us
    ppermute x5, starting transfers between devices, along_scan(): lax.ppermute(value, 'scan', [(i, (i + by) % regions) for i in range(regio...  9.94 us
    pallas_call x2, Pallas kernels, local(): call(functools.partial(near_kernel, home, turn, turn == count - 1, width)...  6.31 us
    pallas_call x2, Pallas kernels, local(): call(functools.partial(far_kernel, turn, turn == count - 1), [shape(wave,...  5.37 us
    ppermute x3, starting transfers between devices, scan_round(): lax.ppermute(rounded, 'scan', route).astype(f32)  2.96 us
    pallas_call x1, Pallas kernels, local(): call(functools.partial(deposit_kernel, reach), shape(transmission.shape[1...  2.68 us
  transfers between devices with their start and end apart: 28, of which 15 were waited for; matrix products, arithmetic and copies ran while one was open for 1% of the time, Pallas kernels for 14%

profile of v3, /device:TPU:0, one launch (start us, length us, event | category | flops | bytes accessed | tf_op | source)
XLA Modules:
  0.0 92.9 jit_solution(13247407428885552359)
XLA Ops:
  0.6 1.6 %copy-done = f32[2,2,2,256,256]{4,3,2,1,0:T(8,128)S(1)} copy-done((f32[2,2,2,256,256]{4,3,2,1,0:T(8,128)S(1)}, f32[2,2,2,256,256]{4,3,2,1,0:T(8,128)}, u32[]{:S(2)}) %copy-start) | copy-done | bytes 2097176
  2.2 0.1 pick.1
  2.3 3.1 %collective-permute-start.6 = (bf16[2,256,256]{2,1,0:T(8,128)(2,1)S(1)}, bf16[2,256,256]{2,1,0:T(8,128)(2,1)S(1)}, u32[]{:S(2)}, u32[]{:S(2)}) collective-permute-start(bf16[2,256,256]{2,1,0:T(8,128)(2,1)S(1)} %pick.1), channel_id=1, source_target_pairs={{0,2},{1,3},{2,4},{3,5},{4,6},{5,7},{6,0},{7,1},{8,10},{9,11},{10,... | collective-permute-start | bytes 786440 | tf_op jit(solution)/shard_map/ppermute | solution.py:293
  5.4 0.7 multiply_add_fusion.refs_0_
  6.1 1.6 %collective-permute-start.3 = (s32[2,2]{1,0:T(2,128)S(1)}, s32[2,2]{1,0:T(2,128)S(1)}, u32[]{:S(2)}, u32[]{:S(2)}) collective-permute-start(s32[2,2]{1,0:T(2,128)S(1)} %multiply_add_fusion.refs_0_), channel_id=1, source_target_pairs={{0,2},{1,3},{2,4},{3,5},{4,6},{5,7},{6,0},{7,1},{8,10},{9,11},{10,... | collective-permute-start | bytes 56 | tf_op jit(solution)/shard_map/ppermute | solution.py:293
  7.7 1.5 %collective-permute-start.2 = (s32[2,2]{1,0:T(2,128)S(1)}, s32[2,2]{1,0:T(2,128)S(1)}, u32[]{:S(2)}, u32[]{:S(2)}) collective-permute-start(s32[2,2]{1,0:T(2,128)S(1)} %multiply_add_fusion.refs_0_), channel_id=1, source_target_pairs={{0,1},{1,2},{2,3},{3,4},{4,5},{5,6},{6,7},{7,0},{8,9},{9,10},{10,1... | collective-permute-start | bytes 56 | tf_op jit(solution)/shard_map/ppermute | solution.py:293
  9.2 1.1 %collective-permute-start.4 = (s32[2,2]{1,0:T(2,128)S(1)}, s32[2,2]{1,0:T(2,128)S(1)}, u32[]{:S(2)}, u32[]{:S(2)}) collective-permute-start(s32[2,2]{1,0:T(2,128)S(1)} %multiply_add_fusion.refs_0_), channel_id=1, source_target_pairs={{0,3},{1,4},{2,5},{3,6},{4,7},{5,0},{6,1},{7,2},{8,11},{9,12},{10,... | collective-permute-start | bytes 56 | tf_op jit(solution)/shard_map/ppermute | solution.py:293
  10.3 2.6 %collective-permute-start.5 = (s32[2,2]{1,0:T(2,128)S(1)}, s32[2,2]{1,0:T(2,128)S(1)}, u32[]{:S(2)}, u32[]{:S(2)}) collective-permute-start(s32[2,2]{1,0:T(2,128)S(1)} %multiply_add_fusion.refs_0_), channel_id=1, source_target_pairs={{0,4},{1,5},{2,6},{3,7},{4,0},{5,1},{6,2},{7,3},{8,12},{9,13},{10,... | collective-permute-start | bytes 56 | tf_op jit(solution)/shard_map/ppermute | solution.py:293
  13.0 0.9 collective-permute-done.3.refs_2_.places
  13.8 1.0 %collective-permute-done.2.refs_1_ = s32[2,2]{1,0:T(2,128)S(1)} collective-permute-done((s32[2,2]{1,0:T(2,128)S(1)}, s32[2,2]{1,0:T(2,128)S(1)}, u32[]{:S(2)}, u32[]{:S(2)}) %collective-permute-start.2) | collective-permute-done | bytes 48 | tf_op jit(solution)/shard_map/ppermute | solution.py:293
  14.8 0.0 collective-permute-done.4.refs_3_
  14.8 0.0 collective-permute-done.5.refs_4_
  14.8 1.2 %extract.1 = (bf16[2,2,64,256]{3,2,1,0:T(8,128)(2,1)S(1)}, bf16[2,2,64,256]{3,2,1,0:T(8,128)(2,1)S(1)}, bf16[2,2,64,256]{3,2,1,0:T(8,128)(2,1)S(1)}, bf16[2,2,64...) custom-call(s32[2,2]{1,0:T(2,128)S(1)} %multiply_add_fusion.refs_0_,, ...), custom_call_target="tpu_custom_call" | custom-call | flops 67108864 | bytes 4194304 | tf_op jit(solution)/shard_map/extract/pallas_call | solution.py:342
  16.0 0.0 collective-permute-done.6.refs_0_
  16.0 3.6 %collective-permute-start.7 = (bf16[2,256,256]{2,1,0:T(8,128)(2,1)S(1)}, bf16[2,256,256]{2,1,0:T(8,128)(2,1)S(1)}, u32[]{:S(2)}, u32[]{:S(2)}) collective-permute-start(bf16[2,256,256]{2,1,0:T(8,128)(2,1)S(1)} %collective-permute-done.6.refs_0_), channel_id=1, source_target_pairs={{0,16},{1,17},{2,18},{3,19},{4,20},{5,21},{6,22},{7,23},{8,24},{9,... | collective-permute-start | bytes 786440 | tf_op jit(solution)/shard_map/ppermute | solution.py:303
  19.6 1.4 %collective-permute-start.8 = (bf16[2,2,64,256]{3,2,1,0:T(8,128)(2,1)S(1)}, bf16[2,2,64,256]{3,2,1,0:T(8,128)(2,1)S(1)}, u32[]{:S(2)}, u32[]{:S(2)}) collective-permute-start(bf16[2,2,64,256]{3,2,1,0:T(8,128)(2,1)S(1)} %get-tuple-element.125), channel_id=1, source_target_pairs={{0,2},{1,3},{2,4},{3,5},{4,6},{5,7},{6,0},{7,1},{8,10},{9,11},{10,... | collective-permute-start | bytes 393224 | tf_op jit(solution)/shard_map/ppermute | solution.py:303
  21.1 3.8 %collective-permute-start.10 = (bf16[2,2,64,256]{3,2,1,0:T(8,128)(2,1)S(1)}, bf16[2,2,64,256]{3,2,1,0:T(8,128)(2,1)S(1)}, u32[]{:S(2)}, u32[]{:S(2)}) collective-permute-start(bf16[2,2,64,256]{3,2,1,0:T(8,128)(2,1)S(1)} %get-tuple-element.129), channel_id=1, source_target_pairs={{0,7},{1,0},{2,1},{3,2},{4,3},{5,4},{6,5},{7,6},{8,15},{9,8},{10,9... | collective-permute-start | bytes 393224 | tf_op jit(solution)/shard_map/ppermute | solution.py:303
  24.9 0.3 collective-permute-start.11
  25.2 0.0 collective-permute-start.12
  25.2 2.7 %collective-permute-done.8.refs_0_ = bf16[2,2,64,256]{3,2,1,0:T(8,128)(2,1)S(1)} collective-permute-done((bf16[2,2,64,256]{3,2,1,0:T(8,128)(2,1)S(1)}, bf16[2,2,64,256]{3,2,1,0:T(8,128)(2,1)S(1)}, u32[]{:S(2)}, u32[]{:S(2)}) %collective-permute-start.8) | collective-permute-done | bytes 131104 | tf_op jit(solution)/shard_map/ppermute | solution.py:303
  27.9 0.0 collective-permute-start.13
  27.9 0.2 collective-permute-done.10.refs_3_
  28.1 4.2 %collective-permute-start.15 = (bf16[2,2,64,256]{3,2,1,0:T(8,128)(2,1)S(1)}, bf16[2,2,64,256]{3,2,1,0:T(8,128)(2,1)S(1)}, u32[]{:S(2)}, u32[]{:S(2)}) collective-permute-start(bf16[2,2,64,256]{3,2,1,0:T(8,128)(2,1)S(1)} %get-tuple-element.134), channel_id=1, source_target_pairs={{0,15},{1,8},{2,9},{3,10},{4,11},{5,12},{6,13},{7,14},{8,7},{9,0},... | collective-permute-start | bytes 393224 | tf_op jit(solution)/shard_map/ppermute | solution.py:303
  32.4 0.5 collective-permute-done.12.refs_5_
  32.9 1.7 %collective-permute-start.9 = (bf16[2,2,64,256]{3,2,1,0:T(8,128)(2,1)S(1)}, bf16[2,2,64,256]{3,2,1,0:T(8,128)(2,1)S(1)}, u32[]{:S(2)}, u32[]{:S(2)}) collective-permute-start(bf16[2,2,64,256]{3,2,1,0:T(8,128)(2,1)S(1)} %get-tuple-element.127), channel_id=1, source_target_pairs={{0,1},{1,2},{2,3},{3,4},{4,5},{5,6},{6,7},{7,0},{8,9},{9,10},{10,1... | collective-permute-start | bytes 393224 | tf_op jit(solution)/shard_map/ppermute | solution.py:303
  34.6 0.0 collective-permute-done.7.refs_1_
  34.6 1.1 %collective-permute-start.14 = (bf16[2,2,64,256]{3,2,1,0:T(8,128)(2,1)S(1)}, bf16[2,2,64,256]{3,2,1,0:T(8,128)(2,1)S(1)}, u32[]{:S(2)}, u32[]{:S(2)}) collective-permute-start(bf16[2,2,64,256]{3,2,1,0:T(8,128)(2,1)S(1)} %get-tuple-element.133), channel_id=1, source_target_pairs={{0,8},{1,9},{2,10},{3,11},{4,12},{5,13},{6,14},{7,15},{8,0},{9,1},... | collective-permute-start | bytes 393224 | tf_op jit(solution)/shard_map/ppermute | solution.py:303
  35.7 1.0 %start.1 = f32[2,2,256,256]{3,2,1,0:T(8,128)S(1)} custom-call(s32[2,2]{1,0:T(2,128)S(1)} %collective-permute-done.3.refs_2_.places, f32[2,256,256]{2,1,0:T(8,128)S(1)} %copy-done.2, bf16[2,256,256]{2,1,0:T(8,128)(2,1)S(1)} %collective-permute-done.6.refs_0_, bf16[2,256,256]{2,1,0:T(8,128)(2,1)S(1)} %collective-permute-done.7.refs_1_, ...), custom_call_target="tpu_custom_call" | custom-call | flops 1073741824 | bytes 4194304 | tf_op jit(solution)/shard_map/start/pallas_call | solution.py:357
  36.7 0.0 collective-permute-done.15.refs_8_
  36.7 2.1 %collective-permute-done.16.refs_9_ = bf16[2,2,64,256]{3,2,1,0:T(8,128)(2,1)S(1)} collective-permute-done((bf16[2,2,64,256]{3,2,1,0:T(8,128)(2,1)S(1)}, bf16[2,2,64,256]{3,2,1,0:T(8,128)(2,1)S(1)}, u32[]{:S(2)}, u32[]{:S(2)}) %collective-permute-start.16) | collective-permute-done | bytes 131104 | tf_op jit(solution)/shard_map/ppermute | solution.py:303
  38.8 1.8 %collective-permute-done.9.refs_1_ = bf16[2,2,64,256]{3,2,1,0:T(8,128)(2,1)S(1)} collective-permute-done((bf16[2,2,64,256]{3,2,1,0:T(8,128)(2,1)S(1)}, bf16[2,2,64,256]{3,2,1,0:T(8,128)(2,1)S(1)}, u32[]{:S(2)}, u32[]{:S(2)}) %collective-permute-start.9) | collective-permute-done | bytes 131104 | tf_op jit(solution)/shard_map/ppermute | solution.py:303
  40.6 2.0 %near.3 = (bf16[2,2,256,256]{3,2,1,0:T(8,128)(2,1)S(1)}, f32[2,256,256]{2,1,0:T(8,128)S(1)}, bf16[2,256,256]{2,1,0:T(8,128)(2,1)S(1)}) custom-call(s32[2,2]{1,0:T(2,128)S(1)} %collective-permute-done.3.refs_2_.places, f32[2,2,256,256]{3,2,1,0:T(8,128)S(1)} %start.1, bf16[512,768]{1,0:T(8,128)(2,1)S(1)} %copy-done.3, bf16[768,512]{1,0:T(8,128)(2,1)S(1)} %copy-done.4, ...), custom_call_target="tpu_custom_call" | custom-call | flops 1073741824 | bytes 4194304 | tf_op jit(solution)/shard_map/near/pallas_call | solution.py:366
  42.6 0.1 collective-permute-start.18
  42.6 4.3 %near.2 = (bf16[2,2,256,256]{3,2,1,0:T(8,128)(2,1)S(1)}, f32[2,256,256]{2,1,0:T(8,128)S(1)}, bf16[2,256,256]{2,1,0:T(8,128)(2,1)S(1)}) custom-call(s32[2,2]{1,0:T(2,128)S(1)} %collective-permute-done.3.refs_2_.places, f32[2,2,256,256]{3,2,1,0:T(8,128)S(1)} %start.1, bf16[512,768]{1,0:T(8,128)(2,1)S(1)} %copy-done.3, bf16[768,512]{1,0:T(8,128)(2,1)S(1)} %copy-done.4, ...), custom_call_target="tpu_custom_call" | custom-call | flops 1073741824 | bytes 4194304 | tf_op jit(solution)/shard_map/near/pallas_call | solution.py:366
  47.0 2.1 %collective-permute-start.17 = (bf16[2,256,256]{2,1,0:T(8,128)(2,1)S(1)}, bf16[2,256,256]{2,1,0:T(8,128)(2,1)S(1)}, u32[]{:S(2)}, u32[]{:S(2)}) collective-permute-start(bf16[2,256,256]{2,1,0:T(8,128)(2,1)S(1)} %get-tuple-element.138), channel_id=1, source_target_pairs={{0,16},{1,17},{2,18},{3,19},{4,20},{5,21},{6,22},{7,23},{8,24},{9,... | collective-permute-start | bytes 786440 | tf_op jit(solution)/shard_map/ppermute | solution.py:303
  49.1 2.2 %collective-permute-done.18.arrived = bf16[2,256,256]{2,1,0:T(8,128)(2,1)S(1)} collective-permute-done((bf16[2,256,256]{2,1,0:T(8,128)(2,1)S(1)}, bf16[2,256,256]{2,1,0:T(8,128)(2,1)S(1)}, u32[]{:S(2)}, u32[]{:S(2)}) %collective-permute-start.18) | collective-permute-done | bytes 262176 | tf_op jit(solution)/shard_map/ppermute | solution.py:303
  51.3 3.9 %far.3 = (bf16[2,256,256]{2,1,0:T(8,128)(2,1)S(1)}, bf16[2,256,256]{2,1,0:T(8,128)(2,1)S(1)}, f32[2,256,256]{2,1,0:T(8,128)S(1)}) custom-call(f32[2,2,256,256]{3,2,1,0:T(8,128)S(1)} %start.1, bf16[512,768]{1,0:T(8,128)(2,1)S(1)} %copy-done.3, bf16[768,512]{1,0:T(8,128)(2,1)S(1)} %copy-done.4, bf16[2,2,256,256]{3,2,1,0:T(8,128)(2,1)S(1)} %get-tuple-element.140.frames, ...), custom_call_target="tpu_custom_call" | custom-call | flops 2147483648 | bytes 4194304 | tf_op jit(solution)/shard_map/far/pallas_call | solution.py:376
  55.2 1.7 %collective-permute-done.17.arrived = bf16[2,256,256]{2,1,0:T(8,128)(2,1)S(1)} collective-permute-done((bf16[2,256,256]{2,1,0:T(8,128)(2,1)S(1)}, bf16[2,256,256]{2,1,0:T(8,128)(2,1)S(1)}, u32[]{:S(2)}, u32[]{:S(2)}) %collective-permute-start.17) | collective-permute-done | bytes 262176 | tf_op jit(solution)/shard_map/ppermute | solution.py:303
  56.9 1.5 %far.2 = (bf16[2,256,256]{2,1,0:T(8,128)(2,1)S(1)}, bf16[2,256,256]{2,1,0:T(8,128)(2,1)S(1)}, f32[2,256,256]{2,1,0:T(8,128)S(1)}) custom-call(f32[2,2,256,256]{3,2,1,0:T(8,128)S(1)} %start.1, bf16[512,768]{1,0:T(8,128)(2,1)S(1)} %copy-done.3, bf16[768,512]{1,0:T(8,128)(2,1)S(1)} %copy-done.4, bf16[2,2,256,256]{3,2,1,0:T(8,128)(2,1)S(1)} %get-tuple-element.136.frames, ...), custom_call_target="tpu_custom_call" | custom-call | flops 2147483648 | bytes 4194304 | tf_op jit(solution)/shard_map/far/pallas_call | solution.py:376
  58.4 1.0 %probe.3 = (f32[2,64,256]{2,1,0:T(8,128)S(1)}, f32[2,64,256]{2,1,0:T(8,128)S(1)}, bf16[2,2,64,256]{3,2,1,0:T(8,128)(2,1)S(1)}) custom-call(s32[2,2]{1,0:T(2,128)S(1)} %collective-permute-done.3.refs_2_.places, f32[2,256,256]{2,1,0:T(8,128)S(1)} %get-tuple-element.139.refs_0_, f32[2,256,256]{2,1,0:T(8,128)S(1)} %get-tuple-element.143.refs_1_), custom_call_target="tpu_custom_call" | custom-call | flops 67108864 | bytes 4194304 | tf_op jit(solution)/shard_map/probe/pallas_call | solution.py:396
  59.4 0.4 collective-permute-start.19
  59.9 0.2 collective-permute-start.21
  60.0 0.3 collective-permute-start.20
  60.4 0.5 collective-permute-done.19
  60.9 0.5 collective-permute-done.21.refs_3_
  61.4 0.4 collective-permute-done.20.refs_2_
  61.8 0.7 part.1
  62.4 2.8 %collective-permute-start.22 = (bf16[2,64,256]{2,1,0:T(8,128)(2,1)S(1)}, bf16[2,64,256]{2,1,0:T(8,128)(2,1)S(1)}, u32[]{:S(2)}, u32[]{:S(2)}) collective-permute-start(bf16[2,64,256]{2,1,0:T(8,128)(2,1)S(1)} %fusion.2), channel_id=1, source_target_pairs={{0,16},{1,17},{2,18},{3,19},{4,20},{5,21},{6,22},{7,23},{8,24},{9,... | collective-permute-start | bytes 196616 | tf_op jit(solution)/shard_map/ppermute | solution.py:303
  65.3 2.3 %collective-permute-start.23 = (bf16[2,2,2,64,256]{4,3,2,1,0:T(8,128)(2,1)S(1)}, bf16[2,2,2,64,256]{4,3,2,1,0:T(8,128)(2,1)S(1)}, u32[]{:S(2)}, u32[]{:S(2)}) collective-permute-start(bf16[2,2,2,64,256]{4,3,2,1,0:T(8,128)(2,1)S(1)} %get-tuple-element.154), channel_id=1, source_target_pairs={{0,6},{1,7},{2,0},{3,1},{4,2},{5,3},{6,4},{7,5},{8,14},{9,15},{10,... | collective-permute-start | bytes 786440 | tf_op jit(solution)/shard_map/ppermute | solution.py:303
  67.5 0.7 collective-permute-start.24
  68.2 1.4 %collective-permute-start.25 = (bf16[2,2,2,64,256]{4,3,2,1,0:T(8,128)(2,1)S(1)}, bf16[2,2,2,64,256]{4,3,2,1,0:T(8,128)(2,1)S(1)}, u32[]{:S(2)}, u32[]{:S(2)}) collective-permute-start(bf16[2,2,2,64,256]{4,3,2,1,0:T(8,128)(2,1)S(1)} %get-tuple-element.156), channel_id=1, source_target_pairs={{0,1},{1,2},{2,3},{3,4},{4,5},{5,6},{6,7},{7,0},{8,9},{9,10},{10,1... | collective-permute-start | bytes 786440 | tf_op jit(solution)/shard_map/ppermute | solution.py:303
  69.6 0.6 collective-permute-start.26
  70.2 0.0 collective-permute-done.22
  70.2 16.7 %while.12 = (s32[]{:T(128)}, f32[2,64,256]{2,1,0:T(8,128)S(1)}, s32[]{:T(128)}, pred[]{:T(512)}, bf16[2,2,64,256]{3,2,1,0:T(8,128)(2,1)S(1)}, /*index=5*/bf16[2,64,256]{2,1,0:T(8,128)(2,1)S(1)}, s32[]{:T(128)}) while((s32[]{:T(128)}, f32[2,64,256]{2,1,0:T(8,128)S(1)}, s32[]{:T(128)}, pred[]{:T(512)}, bf16[2,2,64,256]{3,2,1,0:T(8,128)(2,1)S(1)}, ...), condition=%wide.region_1.2_spmd, body=%wide.region_0.1_spmd.sunk | while | flops 393218 | bytes 1310878 | solution.py:426
  70.2 1.5 %collective-permute-start = (bf16[2,64,256]{2,1,0:T(8,128)(2,1)S(1)}, bf16[2,64,256]{2,1,0:T(8,128)(2,1)S(1)}, u32[]{:S(2)}, u32[]{:S(2)}) collective-permute-start(bf16[2,64,256]{2,1,0:T(8,128)(2,1)S(1)} %fusion.4), channel_id=1, source_target_pairs={{0,1},{1,0},{2,3},{3,2},{4,5},{5,4},{6,7},{7,6},{8,9},{9,8},{10,11... | collective-permute-start | bytes 196616 | tf_op jit(solution)/shard_map/while/body/ppermute | solution.py:409
  71.7 10.8 %collective-permute-done = bf16[2,64,256]{2,1,0:T(8,128)(2,1)S(1)} collective-permute-done((bf16[2,64,256]{2,1,0:T(8,128)(2,1)S(1)}, bf16[2,64,256]{2,1,0:T(8,128)(2,1)S(1)}, u32[]{:S(2)}, u32[]{:S(2)}) %collective-permute-start) | collective-permute-done | bytes 65568 | tf_op jit(solution)/shard_map/while/body/ppermute | solution.py:409
  82.6 0.2 collective-permute-start.1
  82.8 4.1 %collective-permute-done.1 = bf16[2,64,256]{2,1,0:T(8,128)(2,1)S(1)} collective-permute-done((bf16[2,64,256]{2,1,0:T(8,128)(2,1)S(1)}, bf16[2,64,256]{2,1,0:T(8,128)(2,1)S(1)}, u32[]{:S(2)}, u32[]{:S(2)}) %collective-permute-start.1) | collective-permute-done | bytes 65568 | tf_op jit(solution)/shard_map/while/body/ppermute | solution.py:409
  86.9 0.0 collective-permute-done.24.refs_6_
  86.9 0.0 collective-permute-done.25.refs_8_
  87.0 1.2 %collective-permute-start.27 = (bf16[2,64,256]{2,1,0:T(8,128)(2,1)S(1)}, bf16[2,64,256]{2,1,0:T(8,128)(2,1)S(1)}, u32[]{:S(2)}, u32[]{:S(2)}) collective-permute-start(bf16[2,64,256]{2,1,0:T(8,128)(2,1)S(1)} %convert_element_type.64), channel_id=1, source_target_pairs={{0,4},{1,5},{2,6},{3,7},{4,0},{5,1},{6,2},{7,3},{8,12},{9,13},{10,... | collective-permute-start | bytes 196616 | tf_op jit(solution)/shard_map/ppermute | solution.py:409
  88.2 2.7 %deposit.1 = f32[2,64,3072]{2,1,0:T(8,128)} custom-call(s32[2,2]{1,0:T(2,128)S(1)} %multiply_add_fusion.refs_0_, s32[2,2]{1,0:T(2,128)S(1)} %collective-permute-done.2.refs_1_, s32[2,2]{1,0:T(2,128)S(1)} %collective-permute-done.3.refs_2_.places, s32[2,2]{1,0:T(2,128)S(1)} %collective-permute-done.4.refs_3_, s32[2,2]{1,0:T(2,128)S(1)} %collective-permute-done.5.refs_4_, ...), custom_call_target="tpu_custom_call" | custom-call | flops 67108864 | bytes 4194304 | tf_op jit(solution)/shard_map/deposit/pallas_call | solution.py:431
  90.9 1.3 %collective-permute-done.27 = bf16[2,64,256]{2,1,0:T(8,128)(2,1)S(1)} collective-permute-done((bf16[2,64,256]{2,1,0:T(8,128)(2,1)S(1)}, bf16[2,64,256]{2,1,0:T(8,128)(2,1)S(1)}, u32[]{:S(2)}, u32[]{:S(2)}) %collective-permute-start.27) | collective-permute-done | bytes 65568 | tf_op jit(solution)/shard_map/ppermute | solution.py:409
  92.2 0.7 convert_add_fusion.3
  (20 shorter events, 0.1 us)
Async XLA Ops:
  0.6 1.6 %copy-start = (f32[2,2,2,256,256]{4,3,2,1,0:T(8,128)S(1)}, f32[2,2,2,256,256]{4,3,2,1,0:T(8,128)}, u32[]{:S(2)}) copy-start(f32[2,2,2,256,256]{4,3,2,1,0:T(8,128)} %waves.1) | copy-start | bytes 6291460
  2.2 12.6 %copy-start.1 = (f32[1,2,64,3072]{3,2,1,0:T(8,128)S(1)}, f32[1,2,64,3072]{3,2,1,0:T(8,128)}, u32[]{:S(2)}) copy-start(f32[1,2,64,3072]{3,2,1,0:T(8,128)} %param.9) | copy-start | bytes 4718596
  2.2 33.5 %copy-start.2 = (f32[2,256,256]{2,1,0:T(8,128)S(1)}, f32[2,256,256]{2,1,0:T(8,128)}, u32[]{:S(2)}) copy-start(f32[2,256,256]{2,1,0:T(8,128)} %probe.2) | copy-start | bytes 1572868
  2.2 33.5 %copy-start.3 = (bf16[512,768]{1,0:T(8,128)(2,1)S(1)}, bf16[512,768]{1,0:T(8,128)(2,1)}, u32[]{:S(2)}) copy-start(bf16[512,768]{1,0:T(8,128)(2,1)} %constant.46.clone.refs_2_.left) | copy-start | bytes 2359300
  2.2 33.5 %copy-start.4 = (bf16[768,512]{1,0:T(8,128)(2,1)S(1)}, bf16[768,512]{1,0:T(8,128)(2,1)}, u32[]{:S(2)}) copy-start(bf16[768,512]{1,0:T(8,128)(2,1)} %constant.47.clone.refs_3_.right) | copy-start | bytes 2359300
  2.3 13.6 %collective-permute-start.6 = (bf16[2,256,256]{2,1,0:T(8,128)(2,1)S(1)}, bf16[2,256,256]{2,1,0:T(8,128)(2,1)S(1)}, u32[]{:S(2)}, u32[]{:S(2)}) collective-permute-start(bf16[2,256,256]{2,1,0:T(8,128)(2,1)S(1)} %pick.1), channel_id=1, source_target_pairs={{0,2},{1,3},{2,4},{3,5},{4,6},{5,7},{6,0},{7,1},{8,10},{9,11},{10,... | collective-permute-start | bytes 786440 | tf_op jit(solution)/shard_map/ppermute | solution.py:293
  6.1 7.7 %collective-permute-start.3 = (s32[2,2]{1,0:T(2,128)S(1)}, s32[2,2]{1,0:T(2,128)S(1)}, u32[]{:S(2)}, u32[]{:S(2)}) collective-permute-start(s32[2,2]{1,0:T(2,128)S(1)} %multiply_add_fusion.refs_0_), channel_id=1, source_target_pairs={{0,2},{1,3},{2,4},{3,5},{4,6},{5,7},{6,0},{7,1},{8,10},{9,11},{10,... | collective-permute-start | bytes 56 | tf_op jit(solution)/shard_map/ppermute | solution.py:293
  7.7 7.1 %collective-permute-start.2 = (s32[2,2]{1,0:T(2,128)S(1)}, s32[2,2]{1,0:T(2,128)S(1)}, u32[]{:S(2)}, u32[]{:S(2)}) collective-permute-start(s32[2,2]{1,0:T(2,128)S(1)} %multiply_add_fusion.refs_0_), channel_id=1, source_target_pairs={{0,1},{1,2},{2,3},{3,4},{4,5},{5,6},{6,7},{7,0},{8,9},{9,10},{10,1... | collective-permute-start | bytes 56 | tf_op jit(solution)/shard_map/ppermute | solution.py:293
  9.2 5.6 %collective-permute-start.4 = (s32[2,2]{1,0:T(2,128)S(1)}, s32[2,2]{1,0:T(2,128)S(1)}, u32[]{:S(2)}, u32[]{:S(2)}) collective-permute-start(s32[2,2]{1,0:T(2,128)S(1)} %multiply_add_fusion.refs_0_), channel_id=1, source_target_pairs={{0,3},{1,4},{2,5},{3,6},{4,7},{5,0},{6,1},{7,2},{8,11},{9,12},{10,... | collective-permute-start | bytes 56 | tf_op jit(solution)/shard_map/ppermute | solution.py:293
  10.3 4.5 %collective-permute-start.5 = (s32[2,2]{1,0:T(2,128)S(1)}, s32[2,2]{1,0:T(2,128)S(1)}, u32[]{:S(2)}, u32[]{:S(2)}) collective-permute-start(s32[2,2]{1,0:T(2,128)S(1)} %multiply_add_fusion.refs_0_), channel_id=1, source_target_pairs={{0,4},{1,5},{2,6},{3,7},{4,0},{5,1},{6,2},{7,3},{8,12},{9,13},{10,... | collective-permute-start | bytes 56 | tf_op jit(solution)/shard_map/ppermute | solution.py:293
  16.0 18.6 %collective-permute-start.7 = (bf16[2,256,256]{2,1,0:T(8,128)(2,1)S(1)}, bf16[2,256,256]{2,1,0:T(8,128)(2,1)S(1)}, u32[]{:S(2)}, u32[]{:S(2)}) collective-permute-start(bf16[2,256,256]{2,1,0:T(8,128)(2,1)S(1)} %collective-permute-done.6.refs_0_), channel_id=1, source_target_pairs={{0,16},{1,17},{2,18},{3,19},{4,20},{5,21},{6,22},{7,23},{8,24},{9,... | collective-permute-start | bytes 786440 | tf_op jit(solution)/shard_map/ppermute | solution.py:303
  19.6 8.3 %collective-permute-start.8 = (bf16[2,2,64,256]{3,2,1,0:T(8,128)(2,1)S(1)}, bf16[2,2,64,256]{3,2,1,0:T(8,128)(2,1)S(1)}, u32[]{:S(2)}, u32[]{:S(2)}) collective-permute-start(bf16[2,2,64,256]{3,2,1,0:T(8,128)(2,1)S(1)} %get-tuple-element.125), channel_id=1, source_target_pairs={{0,2},{1,3},{2,4},{3,5},{4,6},{5,7},{6,0},{7,1},{8,10},{9,11},{10,... | collective-permute-start | bytes 393224 | tf_op jit(solution)/shard_map/ppermute | solution.py:303
  21.1 7.1 %collective-permute-start.10 = (bf16[2,2,64,256]{3,2,1,0:T(8,128)(2,1)S(1)}, bf16[2,2,64,256]{3,2,1,0:T(8,128)(2,1)S(1)}, u32[]{:S(2)}, u32[]{:S(2)}) collective-permute-start(bf16[2,2,64,256]{3,2,1,0:T(8,128)(2,1)S(1)} %get-tuple-element.129), channel_id=1, source_target_pairs={{0,7},{1,0},{2,1},{3,2},{4,3},{5,4},{6,5},{7,6},{8,15},{9,8},{10,9... | collective-permute-start | bytes 393224 | tf_op jit(solution)/shard_map/ppermute | solution.py:303
  24.9 7.5 %collective-permute-start.11 = (bf16[2,2,64,256]{3,2,1,0:T(8,128)(2,1)S(1)}, bf16[2,2,64,256]{3,2,1,0:T(8,128)(2,1)S(1)}, u32[]{:S(2)}, u32[]{:S(2)}) collective-permute-start(bf16[2,2,64,256]{3,2,1,0:T(8,128)(2,1)S(1)} %get-tuple-element.130), channel_id=1, source_target_pairs={{0,6},{1,7},{2,0},{3,1},{4,2},{5,3},{6,4},{7,5},{8,14},{9,15},{10,... | collective-permute-start | bytes 393224 | tf_op jit(solution)/shard_map/ppermute | solution.py:303
  25.2 7.7 %collective-permute-start.12 = (bf16[2,2,64,256]{3,2,1,0:T(8,128)(2,1)S(1)}, bf16[2,2,64,256]{3,2,1,0:T(8,128)(2,1)S(1)}, u32[]{:S(2)}, u32[]{:S(2)}) collective-permute-start(bf16[2,2,64,256]{3,2,1,0:T(8,128)(2,1)S(1)} %get-tuple-element.131), channel_id=1, source_target_pairs={{0,10},{1,11},{2,12},{3,13},{4,14},{5,15},{6,8},{7,9},{8,2},{9,3},... | collective-permute-start | bytes 393224 | tf_op jit(solution)/shard_map/ppermute | solution.py:303
  27.9 8.8 %collective-permute-start.13 = (bf16[2,2,64,256]{3,2,1,0:T(8,128)(2,1)S(1)}, bf16[2,2,64,256]{3,2,1,0:T(8,128)(2,1)S(1)}, u32[]{:S(2)}, u32[]{:S(2)}) collective-permute-start(bf16[2,2,64,256]{3,2,1,0:T(8,128)(2,1)S(1)} %get-tuple-element.132), channel_id=1, source_target_pairs={{0,9},{1,10},{2,11},{3,12},{4,13},{5,14},{6,15},{7,8},{8,1},{9,2},... | collective-permute-start | bytes 393224 | tf_op jit(solution)/shard_map/ppermute | solution.py:303
  28.1 8.6 %collective-permute-start.15 = (bf16[2,2,64,256]{3,2,1,0:T(8,128)(2,1)S(1)}, bf16[2,2,64,256]{3,2,1,0:T(8,128)(2,1)S(1)}, u32[]{:S(2)}, u32[]{:S(2)}) collective-permute-start(bf16[2,2,64,256]{3,2,1,0:T(8,128)(2,1)S(1)} %get-tuple-element.134), channel_id=1, source_target_pairs={{0,15},{1,8},{2,9},{3,10},{4,11},{5,12},{6,13},{7,14},{8,7},{9,0},... | collective-permute-start | bytes 393224 | tf_op jit(solution)/shard_map/ppermute | solution.py:303
  32.4 6.4 %collective-permute-start.16 = (bf16[2,2,64,256]{3,2,1,0:T(8,128)(2,1)S(1)}, bf16[2,2,64,256]{3,2,1,0:T(8,128)(2,1)S(1)}, u32[]{:S(2)}, u32[]{:S(2)}) collective-permute-start(bf16[2,2,64,256]{3,2,1,0:T(8,128)(2,1)S(1)} %get-tuple-element.135), channel_id=1, source_target_pairs={{0,14},{1,15},{2,8},{3,9},{4,10},{5,11},{6,12},{7,13},{8,6},{9,7},... | collective-permute-start | bytes 393224 | tf_op jit(solution)/shard_map/ppermute | solution.py:303
  32.9 7.7 %collective-permute-start.9 = (bf16[2,2,64,256]{3,2,1,0:T(8,128)(2,1)S(1)}, bf16[2,2,64,256]{3,2,1,0:T(8,128)(2,1)S(1)}, u32[]{:S(2)}, u32[]{:S(2)}) collective-permute-start(bf16[2,2,64,256]{3,2,1,0:T(8,128)(2,1)S(1)} %get-tuple-element.127), channel_id=1, source_target_pairs={{0,1},{1,2},{2,3},{3,4},{4,5},{5,6},{6,7},{7,0},{8,9},{9,10},{10,1... | collective-permute-start | bytes 393224 | tf_op jit(solution)/shard_map/ppermute | solution.py:303
  34.6 6.0 %collective-permute-start.14 = (bf16[2,2,64,256]{3,2,1,0:T(8,128)(2,1)S(1)}, bf16[2,2,64,256]{3,2,1,0:T(8,128)(2,1)S(1)}, u32[]{:S(2)}, u32[]{:S(2)}) collective-permute-start(bf16[2,2,64,256]{3,2,1,0:T(8,128)(2,1)S(1)} %get-tuple-element.133), channel_id=1, source_target_pairs={{0,8},{1,9},{2,10},{3,11},{4,12},{5,13},{6,14},{7,15},{8,0},{9,1},... | collective-permute-start | bytes 393224 | tf_op jit(solution)/shard_map/ppermute | solution.py:303
  42.6 8.7 %collective-permute-start.18 = (bf16[2,256,256]{2,1,0:T(8,128)(2,1)S(1)}, bf16[2,256,256]{2,1,0:T(8,128)(2,1)S(1)}, u32[]{:S(2)}, u32[]{:S(2)}) collective-permute-start(bf16[2,256,256]{2,1,0:T(8,128)(2,1)S(1)} %get-tuple-element.142), channel_id=1, source_target_pairs={{0,16},{1,17},{2,18},{3,19},{4,20},{5,21},{6,22},{7,23},{8,24},{9,... | collective-permute-start | bytes 786440 | tf_op jit(solution)/shard_map/ppermute | solution.py:303
  47.0 9.9 %collective-permute-start.17 = (bf16[2,256,256]{2,1,0:T(8,128)(2,1)S(1)}, bf16[2,256,256]{2,1,0:T(8,128)(2,1)S(1)}, u32[]{:S(2)}, u32[]{:S(2)}) collective-permute-start(bf16[2,256,256]{2,1,0:T(8,128)(2,1)S(1)} %get-tuple-element.138), channel_id=1, source_target_pairs={{0,16},{1,17},{2,18},{3,19},{4,20},{5,21},{6,22},{7,23},{8,24},{9,... | collective-permute-start | bytes 786440 | tf_op jit(solution)/shard_map/ppermute | solution.py:303
  59.4 1.4 %collective-permute-start.19 = (bf16[2,2,64,256]{3,2,1,0:T(8,128)(2,1)S(1)}, bf16[2,2,64,256]{3,2,1,0:T(8,128)(2,1)S(1)}, u32[]{:S(2)}, u32[]{:S(2)}) collective-permute-start(bf16[2,2,64,256]{3,2,1,0:T(8,128)(2,1)S(1)} %get-tuple-element.145), channel_id=1, source_target_pairs={{0,8},{1,9},{2,10},{3,11},{4,12},{5,13},{6,14},{7,15},{8,0},{9,1},... | collective-permute-start | bytes 393224 | tf_op jit(solution)/shard_map/ppermute | solution.py:303
  59.9 1.5 %collective-permute-start.21 = (bf16[2,256,256]{2,1,0:T(8,128)(2,1)S(1)}, bf16[2,256,256]{2,1,0:T(8,128)(2,1)S(1)}, u32[]{:S(2)}, u32[]{:S(2)}) collective-permute-start(bf16[2,256,256]{2,1,0:T(8,128)(2,1)S(1)} %get-tuple-element.150), channel_id=1, source_target_pairs={{0,8},{1,9},{2,10},{3,11},{4,12},{5,13},{6,14},{7,15},{8,0},{9,1},... | collective-permute-start | bytes 786440 | tf_op jit(solution)/shard_map/ppermute | solution.py:303
  60.0 1.7 %collective-permute-start.20 = (bf16[2,256,256]{2,1,0:T(8,128)(2,1)S(1)}, bf16[2,256,256]{2,1,0:T(8,128)(2,1)S(1)}, u32[]{:S(2)}, u32[]{:S(2)}) collective-permute-start(bf16[2,256,256]{2,1,0:T(8,128)(2,1)S(1)} %get-tuple-element.149), channel_id=1, source_target_pairs={{0,8},{1,9},{2,10},{3,11},{4,12},{5,13},{6,14},{7,15},{8,0},{9,1},... | collective-permute-start | bytes 786440 | tf_op jit(solution)/shard_map/ppermute | solution.py:303
  62.4 7.7 %collective-permute-start.22 = (bf16[2,64,256]{2,1,0:T(8,128)(2,1)S(1)}, bf16[2,64,256]{2,1,0:T(8,128)(2,1)S(1)}, u32[]{:S(2)}, u32[]{:S(2)}) collective-permute-start(bf16[2,64,256]{2,1,0:T(8,128)(2,1)S(1)} %fusion.2), channel_id=1, source_target_pairs={{0,16},{1,17},{2,18},{3,19},{4,20},{5,21},{6,22},{7,23},{8,24},{9,... | collective-permute-start | bytes 196616 | tf_op jit(solution)/shard_map/ppermute | solution.py:303
  65.3 21.6 %collective-permute-start.23 = (bf16[2,2,2,64,256]{4,3,2,1,0:T(8,128)(2,1)S(1)}, bf16[2,2,2,64,256]{4,3,2,1,0:T(8,128)(2,1)S(1)}, u32[]{:S(2)}, u32[]{:S(2)}) collective-permute-start(bf16[2,2,2,64,256]{4,3,2,1,0:T(8,128)(2,1)S(1)} %get-tuple-element.154), channel_id=1, source_target_pairs={{0,6},{1,7},{2,0},{3,1},{4,2},{5,3},{6,4},{7,5},{8,14},{9,15},{10,... | collective-permute-start | bytes 786440 | tf_op jit(solution)/shard_map/ppermute | solution.py:303
  67.5 19.4 %collective-permute-start.24 = (bf16[2,2,2,64,256]{4,3,2,1,0:T(8,128)(2,1)S(1)}, bf16[2,2,2,64,256]{4,3,2,1,0:T(8,128)(2,1)S(1)}, u32[]{:S(2)}, u32[]{:S(2)}) collective-permute-start(bf16[2,2,2,64,256]{4,3,2,1,0:T(8,128)(2,1)S(1)} %get-tuple-element.155), channel_id=1, source_target_pairs={{0,7},{1,0},{2,1},{3,2},{4,3},{5,4},{6,5},{7,6},{8,15},{9,8},{10,9... | collective-permute-start | bytes 786440 | tf_op jit(solution)/shard_map/ppermute | solution.py:303
  68.2 18.7 %collective-permute-start.25 = (bf16[2,2,2,64,256]{4,3,2,1,0:T(8,128)(2,1)S(1)}, bf16[2,2,2,64,256]{4,3,2,1,0:T(8,128)(2,1)S(1)}, u32[]{:S(2)}, u32[]{:S(2)}) collective-permute-start(bf16[2,2,2,64,256]{4,3,2,1,0:T(8,128)(2,1)S(1)} %get-tuple-element.156), channel_id=1, source_target_pairs={{0,1},{1,2},{2,3},{3,4},{4,5},{5,6},{6,7},{7,0},{8,9},{9,10},{10,1... | collective-permute-start | bytes 786440 | tf_op jit(solution)/shard_map/ppermute | solution.py:303
  69.6 17.4 %collective-permute-start.26 = (bf16[2,2,2,64,256]{4,3,2,1,0:T(8,128)(2,1)S(1)}, bf16[2,2,2,64,256]{4,3,2,1,0:T(8,128)(2,1)S(1)}, u32[]{:S(2)}, u32[]{:S(2)}) collective-permute-start(bf16[2,2,2,64,256]{4,3,2,1,0:T(8,128)(2,1)S(1)} %get-tuple-element.157), channel_id=1, source_target_pairs={{0,2},{1,3},{2,4},{3,5},{4,6},{5,7},{6,0},{7,1},{8,10},{9,11},{10,... | collective-permute-start | bytes 786440 | tf_op jit(solution)/shard_map/ppermute | solution.py:303
  70.2 12.3 %collective-permute-start = (bf16[2,64,256]{2,1,0:T(8,128)(2,1)S(1)}, bf16[2,64,256]{2,1,0:T(8,128)(2,1)S(1)}, u32[]{:S(2)}, u32[]{:S(2)}) collective-permute-start(bf16[2,64,256]{2,1,0:T(8,128)(2,1)S(1)} %fusion.4), channel_id=1, source_target_pairs={{0,1},{1,0},{2,3},{3,2},{4,5},{5,4},{6,7},{7,6},{8,9},{9,8},{10,11... | collective-permute-start | bytes 196616 | tf_op jit(solution)/shard_map/while/body/ppermute | solution.py:409
  82.6 4.3 %collective-permute-start.1 = (bf16[2,64,256]{2,1,0:T(8,128)(2,1)S(1)}, bf16[2,64,256]{2,1,0:T(8,128)(2,1)S(1)}, u32[]{:S(2)}, u32[]{:S(2)}) collective-permute-start(bf16[2,64,256]{2,1,0:T(8,128)(2,1)S(1)} %add_convert_fusion.2), channel_id=1, source_target_pairs={{0,2},{1,3},{2,0},{3,1},{4,6},{5,7},{6,4},{7,5},{8,10},{9,11},{10,... | collective-permute-start | bytes 196616 | tf_op jit(solution)/shard_map/while/body/ppermute | solution.py:409
  87.0 5.2 %collective-permute-start.27 = (bf16[2,64,256]{2,1,0:T(8,128)(2,1)S(1)}, bf16[2,64,256]{2,1,0:T(8,128)(2,1)S(1)}, u32[]{:S(2)}, u32[]{:S(2)}) collective-permute-start(bf16[2,64,256]{2,1,0:T(8,128)(2,1)S(1)} %convert_element_type.64), channel_id=1, source_target_pairs={{0,4},{1,5},{2,6},{3,7},{4,0},{5,1},{6,2},{7,3},{8,12},{9,13},{10,... | collective-permute-start | bytes 196616 | tf_op jit(solution)/shard_map/ppermute | solution.py:409

commit v4 on v2

--- a/solution.py
+++ b/solution.py
@@ -305,14 +305,14 @@
     smem = pl.BlockSpec(memory_space=pltpu.SMEM)
     vmem = pl.BlockSpec(memory_space=pltpu.VMEM)
 
-    def call(kernel, out_shape, in_specs, flops, name, scratch=()):
+    def call(kernel, out_shape, in_specs, flops, name, scratch=(), limit=24):
         return pl.pallas_call(
             kernel,
             out_shape=out_shape,
             in_specs=in_specs,
             out_specs=jax.tree.map(lambda _: vmem, out_shape),
             scratch_shapes=scratch,
-            compiler_params=pltpu.CompilerParams(vmem_limit_bytes=24 * 1024 * 1024),
+            compiler_params=pltpu.CompilerParams(vmem_limit_bytes=limit << 20),
             cost_estimate=pl.CostEstimate(flops=flops, bytes_accessed=4 << 20, transcendentals=0),
             name=name,
         )
@@ -331,6 +331,7 @@
         1 << 20,
         "pick",
         [pltpu.VMEM(wave, f32), pltpu.SemaphoreType.DMA],
+        62,
     )(exit_adjoint)
     adjoint, scan_row = lax.optimization_barrier((adjoint, scan_row))
     adjoint = along_scan(adjoint, home)
@@ -350,6 +351,8 @@
     adjoint, pieces[0, home] = lax.optimization_barrier((adjoint, pieces[0, home]))
     adjoints = [adjoint, across(adjoint, 2, 0, lower)]
     for flip, step in far_first:
+        if (flip, step) == (1, home):
+            pieces[1, home], pieces[0, 0] = lax.optimization_barrier((pieces[1, home], pieces[0, 0]))
         pieces[flip, step] = across(pieces[flip, step], flip, home - step)
 
     start = call(

time: 91.8 us -> 88.7 us (0.966)
  waiting for transfers between devices: 32.7 us -> 27.7 us
  Pallas kernels: 18.5 us -> 20.3 us
  starting transfers between devices: 36.5 us -> 37.6 us
    ppermute x20, waiting for transfers between devices: 16.6 us -> 12.2 us  [across(): return lax.ppermute(value, ('depth', 'scan'), route)]
    pallas_call x1, Pallas kernels: 0.09 us -> 1.91 us  [local(): call(pick_kernel, shape(wave, bf16), [pl.BlockSpec(memory_space=pltpu.HBM...]
    ppermute x3, waiting for transfers between devices: 14.3 us -> 12.8 us  [scan_round(): lax.ppermute(rounded, 'scan', route).astype(f32)]
    ppermute x3, starting transfers between devices: 1.48 us -> 2.72 us  [scan_round(): lax.ppermute(rounded, 'scan', route).astype(f32)]
  transfers between devices with their start and end apart: 28 -> 28, of which waited for: 15 -> 12; matrix products, arithmetic and copies ran while one was open for 1% -> 0% of each run, Pallas kernels for 18% -> 19%
where the time goes in v4:
time: 88.7 us; the launch traced here: 88.5 us
  starting transfers between devices  37.6 us (42%)
  waiting for transfers between devices  27.7 us (31%)
  Pallas kernels  20.3 us (23%)
  local copies, waits for them, and re-layouts  1.16 us (1%)
    ppermute x20, starting transfers between devices, across(): return lax.ppermute(value, ('depth', 'scan'), route)  24.9 us
    ppermute x3, waiting for transfers between devices, scan_round(): lax.ppermute(rounded, 'scan', route).astype(f32)  12.8 us
    ppermute x20, waiting for transfers between devices, across(): return lax.ppermute(value, ('depth', 'scan'), route)  12.2 us
    ppermute x5, starting transfers between devices, along_scan(): lax.ppermute(value, 'scan', [(i, (i + by) % regions) for i in range(regio...  9.99 us
    pallas_call x2, Pallas kernels, local(): call(functools.partial(near_kernel, home, turn, turn == count - 1, width)...  6.36 us
    pallas_call x2, Pallas kernels, local(): call(functools.partial(far_kernel, turn, turn == count - 1), [shape(wave,...  5.47 us
    ppermute x3, starting transfers between devices, scan_round(): lax.ppermute(rounded, 'scan', route).astype(f32)  2.72 us
    pallas_call x1, Pallas kernels, local(): call(functools.partial(deposit_kernel, reach), shape(transmission.shape[1...  2.68 us
  transfers between devices with their start and end apart: 28, of which 12 were waited for; matrix products, arithmetic and copies ran while one was open for 0% of the time, Pallas kernels for 19%

profile of v4, /device:TPU:0, one launch (start us, length us, event | category | flops | bytes accessed | tf_op | source)
XLA Modules:
  0.0 88.5 jit_solution(16123319077947408149)
XLA Ops:
  0.7 1.9 %pick.1 = bf16[2,256,256]{2,1,0:T(8,128)(2,1)} custom-call(f32[2,2,2,256,256]{4,3,2,1,0:T(8,128)} %waves.1), custom_call_target="tpu_custom_call" | custom-call | flops 1048576 | bytes 4194304 | tf_op jit(solution)/shard_map/pick/pallas_call | solution.py:327
  2.6 0.0 copy-start.1
  2.6 0.0 copy-start.2
  2.6 3.1 %collective-permute-start.7 = (bf16[2,256,256]{2,1,0:T(8,128)(2,1)}, bf16[2,256,256]{2,1,0:T(8,128)(2,1)S(1)}, u32[]{:S(2)}, u32[]{:S(2)}) collective-permute-start(bf16[2,256,256]{2,1,0:T(8,128)(2,1)} %pick.1), channel_id=1, source_target_pairs={{0,2},{1,3},{2,4},{3,5},{4,6},{5,7},{6,0},{7,1},{8,10},{9,11},{10,... | collective-permute-start | bytes 786440 | tf_op jit(solution)/shard_map/ppermute | solution.py:293
  5.7 1.6 %collective-permute-start.4 = (s32[2,2]{1,0:T(2,128)S(1)}, s32[2,2]{1,0:T(2,128)S(1)}, u32[]{:S(2)}, u32[]{:S(2)}) collective-permute-start(s32[2,2]{1,0:T(2,128)S(1)} %multiply_add_fusion.refs_0_), channel_id=1, source_target_pairs={{0,2},{1,3},{2,4},{3,5},{4,6},{5,7},{6,0},{7,1},{8,10},{9,11},{10,... | collective-permute-start | bytes 56 | tf_op jit(solution)/shard_map/ppermute | solution.py:293
  7.3 1.5 %collective-permute-start.3 = (s32[2,2]{1,0:T(2,128)S(1)}, s32[2,2]{1,0:T(2,128)S(1)}, u32[]{:S(2)}, u32[]{:S(2)}) collective-permute-start(s32[2,2]{1,0:T(2,128)S(1)} %multiply_add_fusion.refs_0_), channel_id=1, source_target_pairs={{0,1},{1,2},{2,3},{3,4},{4,5},{5,6},{6,7},{7,0},{8,9},{9,10},{10,1... | collective-permute-start | bytes 56 | tf_op jit(solution)/shard_map/ppermute | solution.py:293
  8.8 1.0 %collective-permute-start.5 = (s32[2,2]{1,0:T(2,128)S(1)}, s32[2,2]{1,0:T(2,128)S(1)}, u32[]{:S(2)}, u32[]{:S(2)}) collective-permute-start(s32[2,2]{1,0:T(2,128)S(1)} %multiply_add_fusion.refs_0_), channel_id=1, source_target_pairs={{0,3},{1,4},{2,5},{3,6},{4,7},{5,0},{6,1},{7,2},{8,11},{9,12},{10,... | collective-permute-start | bytes 56 | tf_op jit(solution)/shard_map/ppermute | solution.py:293
  9.9 2.7 %collective-permute-start.6 = (s32[2,2]{1,0:T(2,128)S(1)}, s32[2,2]{1,0:T(2,128)S(1)}, u32[]{:S(2)}, u32[]{:S(2)}) collective-permute-start(s32[2,2]{1,0:T(2,128)S(1)} %multiply_add_fusion.refs_0_), channel_id=1, source_target_pairs={{0,4},{1,5},{2,6},{3,7},{4,0},{5,1},{6,2},{7,3},{8,12},{9,13},{10,... | collective-permute-start | bytes 56 | tf_op jit(solution)/shard_map/ppermute | solution.py:293
  12.6 1.7 %collective-permute-done.4.refs_2_.places = s32[2,2]{1,0:T(2,128)S(1)} collective-permute-done((s32[2,2]{1,0:T(2,128)S(1)}, s32[2,2]{1,0:T(2,128)S(1)}, u32[]{:S(2)}, u32[]{:S(2)}) %collective-permute-start.4) | collective-permute-done | bytes 48 | tf_op jit(solution)/shard_map/ppermute | solution.py:293
  14.3 1.0 %collective-permute-done.3.refs_1_ = s32[2,2]{1,0:T(2,128)S(1)} collective-permute-done((s32[2,2]{1,0:T(2,128)S(1)}, s32[2,2]{1,0:T(2,128)S(1)}, u32[]{:S(2)}, u32[]{:S(2)}) %collective-permute-start.3) | collective-permute-done | bytes 48 | tf_op jit(solution)/shard_map/ppermute | solution.py:293
  15.3 1.2 %extract.1 = (bf16[2,2,64,256]{3,2,1,0:T(8,128)(2,1)S(1)}, bf16[2,2,64,256]{3,2,1,0:T(8,128)(2,1)S(1)}, bf16[2,2,64,256]{3,2,1,0:T(8,128)(2,1)S(1)}, bf16[2,2,64...) custom-call(s32[2,2]{1,0:T(2,128)S(1)} %multiply_add_fusion.refs_0_,, ...), custom_call_target="tpu_custom_call" | custom-call | flops 67108864 | bytes 4194304 | tf_op jit(solution)/shard_map/extract/pallas_call | solution.py:343
  16.5 0.0 collective-permute-done.7.refs_0_
  16.5 3.4 %collective-permute-start.8 = (bf16[2,256,256]{2,1,0:T(8,128)(2,1)S(1)}, bf16[2,256,256]{2,1,0:T(8,128)(2,1)S(1)}, u32[]{:S(2)}, u32[]{:S(2)}) collective-permute-start(bf16[2,256,256]{2,1,0:T(8,128)(2,1)S(1)} %collective-permute-done.7.refs_0_), channel_id=1, source_target_pairs={{0,16},{1,17},{2,18},{3,19},{4,20},{5,21},{6,22},{7,23},{8,24},{9,... | collective-permute-start | bytes 786440 | tf_op jit(solution)/shard_map/ppermute | solution.py:303
  19.9 0.8 collective-permute-start.9
  20.7 1.5 %collective-permute-start.10 = (bf16[2,2,64,256]{3,2,1,0:T(8,128)(2,1)S(1)}, bf16[2,2,64,256]{3,2,1,0:T(8,128)(2,1)S(1)}, u32[]{:S(2)}, u32[]{:S(2)}) collective-permute-start(bf16[2,2,64,256]{3,2,1,0:T(8,128)(2,1)S(1)} %get-tuple-element.127), channel_id=1, source_target_pairs={{0,1},{1,2},{2,3},{3,4},{4,5},{5,6},{6,7},{7,0},{8,9},{9,10},{10,1... | collective-permute-start | bytes 393224 | tf_op jit(solution)/shard_map/ppermute | solution.py:303
  22.2 3.2 %collective-permute-start.11 = (bf16[2,2,64,256]{3,2,1,0:T(8,128)(2,1)S(1)}, bf16[2,2,64,256]{3,2,1,0:T(8,128)(2,1)S(1)}, u32[]{:S(2)}, u32[]{:S(2)}) collective-permute-start(bf16[2,2,64,256]{3,2,1,0:T(8,128)(2,1)S(1)} %get-tuple-element.129), channel_id=1, source_target_pairs={{0,7},{1,0},{2,1},{3,2},{4,3},{5,4},{6,5},{7,6},{8,15},{9,8},{10,9... | collective-permute-start | bytes 393224 | tf_op jit(solution)/shard_map/ppermute | solution.py:303
  25.4 1.2 %collective-permute-start.12 = (bf16[2,2,64,256]{3,2,1,0:T(8,128)(2,1)S(1)}, bf16[2,2,64,256]{3,2,1,0:T(8,128)(2,1)S(1)}, u32[]{:S(2)}, u32[]{:S(2)}) collective-permute-start(bf16[2,2,64,256]{3,2,1,0:T(8,128)(2,1)S(1)} %get-tuple-element.130), channel_id=1, source_target_pairs={{0,6},{1,7},{2,0},{3,1},{4,2},{5,3},{6,4},{7,5},{8,14},{9,15},{10,... | collective-permute-start | bytes 393224 | tf_op jit(solution)/shard_map/ppermute | solution.py:303
  26.7 1.4 %collective-permute-done.9.refs_0_ = bf16[2,2,64,256]{3,2,1,0:T(8,128)(2,1)S(1)} collective-permute-done((bf16[2,2,64,256]{3,2,1,0:T(8,128)(2,1)S(1)}, bf16[2,2,64,256]{3,2,1,0:T(8,128)(2,1)S(1)}, u32[]{:S(2)}, u32[]{:S(2)}) %collective-permute-start.9) | collective-permute-done | bytes 131104 | tf_op jit(solution)/shard_map/ppermute | solution.py:303
  28.1 0.0 collective-permute-start.13
  28.1 2.1 %collective-permute-done.10.refs_1_ = bf16[2,2,64,256]{3,2,1,0:T(8,128)(2,1)S(1)} collective-permute-done((bf16[2,2,64,256]{3,2,1,0:T(8,128)(2,1)S(1)}, bf16[2,2,64,256]{3,2,1,0:T(8,128)(2,1)S(1)}, u32[]{:S(2)}, u32[]{:S(2)}) %collective-permute-start.10) | collective-permute-done | bytes 131104 | tf_op jit(solution)/shard_map/ppermute | solution.py:303
  30.2 0.0 collective-permute-start.14
  30.2 0.0 collective-permute-done.11.refs_3_
  30.2 4.4 %collective-permute-start.16 = (bf16[2,2,64,256]{3,2,1,0:T(8,128)(2,1)S(1)}, bf16[2,2,64,256]{3,2,1,0:T(8,128)(2,1)S(1)}, u32[]{:S(2)}, u32[]{:S(2)}) collective-permute-start(bf16[2,2,64,256]{3,2,1,0:T(8,128)(2,1)S(1)} %get-tuple-element.134), channel_id=1, source_target_pairs={{0,15},{1,8},{2,9},{3,10},{4,11},{5,12},{6,13},{7,14},{8,7},{9,0},... | collective-permute-start | bytes 393224 | tf_op jit(solution)/shard_map/ppermute | solution.py:303
  34.6 0.0 collective-permute-start.17
  34.6 0.0 collective-permute-done.8.refs_1_
  34.7 0.4 collective-permute-start.15
  35.0 1.1 %copy-done.3 = bf16[768,512]{1,0:T(8,128)(2,1)S(1)} copy-done((bf16[768,512]{1,0:T(8,128)(2,1)S(1)}, bf16[768,512]{1,0:T(8,128)(2,1)}, u32[]{:S(2)}) %copy-start.3) | copy-done | bytes 786456
  36.2 1.0 %start.1 = f32[2,2,256,256]{3,2,1,0:T(8,128)S(1)} custom-call(s32[2,2]{1,0:T(2,128)S(1)} %collective-permute-done.4.refs_2_.places, f32[2,256,256]{2,1,0:T(8,128)S(1)} %copy-done.1, bf16[2,256,256]{2,1,0:T(8,128)(2,1)S(1)} %collective-permute-done.7.refs_0_, bf16[2,256,256]{2,1,0:T(8,128)(2,1)S(1)} %collective-permute-done.8.refs_1_, ...), custom_call_target="tpu_custom_call" | custom-call | flops 1073741824 | bytes 4194304 | tf_op jit(solution)/shard_map/start/pallas_call | solution.py:358
  37.2 1.8 %collective-permute-done.14.refs_6_ = bf16[2,2,64,256]{3,2,1,0:T(8,128)(2,1)S(1)} collective-permute-done((bf16[2,2,64,256]{3,2,1,0:T(8,128)(2,1)S(1)}, bf16[2,2,64,256]{3,2,1,0:T(8,128)(2,1)S(1)}, u32[]{:S(2)}, u32[]{:S(2)}) %collective-permute-start.14) | collective-permute-done | bytes 131104 | tf_op jit(solution)/shard_map/ppermute | solution.py:303
  39.0 0.0 collective-permute-done.16.refs_8_
  39.0 1.6 %collective-permute-done.17.refs_9_ = bf16[2,2,64,256]{3,2,1,0:T(8,128)(2,1)S(1)} collective-permute-done((bf16[2,2,64,256]{3,2,1,0:T(8,128)(2,1)S(1)}, bf16[2,2,64,256]{3,2,1,0:T(8,128)(2,1)S(1)}, u32[]{:S(2)}, u32[]{:S(2)}) %collective-permute-start.17) | collective-permute-done | bytes 131104 | tf_op jit(solution)/shard_map/ppermute | solution.py:303
  40.5 0.0 collective-permute-done.15.refs_7_
  40.6 2.0 %near.3 = (bf16[2,2,256,256]{3,2,1,0:T(8,128)(2,1)S(1)}, f32[2,256,256]{2,1,0:T(8,128)S(1)}, bf16[2,256,256]{2,1,0:T(8,128)(2,1)S(1)}) custom-call(s32[2,2]{1,0:T(2,128)S(1)} %collective-permute-done.4.refs_2_.places, f32[2,2,256,256]{3,2,1,0:T(8,128)S(1)} %start.1, bf16[512,768]{1,0:T(8,128)(2,1)S(1)} %copy-done.2, bf16[768,512]{1,0:T(8,128)(2,1)S(1)} %copy-done.4, ...), custom_call_target="tpu_custom_call" | custom-call | flops 1073741824 | bytes 4194304 | tf_op jit(solution)/shard_map/near/pallas_call | solution.py:367
  42.5 0.1 collective-permute-start.19
  42.6 4.4 %near.2 = (bf16[2,2,256,256]{3,2,1,0:T(8,128)(2,1)S(1)}, f32[2,256,256]{2,1,0:T(8,128)S(1)}, bf16[2,256,256]{2,1,0:T(8,128)(2,1)S(1)}) custom-call(s32[2,2]{1,0:T(2,128)S(1)} %collective-permute-done.4.refs_2_.places, f32[2,2,256,256]{3,2,1,0:T(8,128)S(1)} %start.1, bf16[512,768]{1,0:T(8,128)(2,1)S(1)} %copy-done.2, bf16[768,512]{1,0:T(8,128)(2,1)S(1)} %copy-done.4, ...), custom_call_target="tpu_custom_call" | custom-call | flops 1073741824 | bytes 4194304 | tf_op jit(solution)/shard_map/near/pallas_call | solution.py:367
  47.0 2.1 %collective-permute-start.18 = (bf16[2,256,256]{2,1,0:T(8,128)(2,1)S(1)}, bf16[2,256,256]{2,1,0:T(8,128)(2,1)S(1)}, u32[]{:S(2)}, u32[]{:S(2)}) collective-permute-start(bf16[2,256,256]{2,1,0:T(8,128)(2,1)S(1)} %get-tuple-element.138), channel_id=1, source_target_pairs={{0,16},{1,17},{2,18},{3,19},{4,20},{5,21},{6,22},{7,23},{8,24},{9,... | collective-permute-start | bytes 786440 | tf_op jit(solution)/shard_map/ppermute | solution.py:303
  49.1 2.7 %collective-permute-done.19.arrived = bf16[2,256,256]{2,1,0:T(8,128)(2,1)S(1)} collective-permute-done((bf16[2,256,256]{2,1,0:T(8,128)(2,1)S(1)}, bf16[2,256,256]{2,1,0:T(8,128)(2,1)S(1)}, u32[]{:S(2)}, u32[]{:S(2)}) %collective-permute-start.19) | collective-permute-done | bytes 262176 | tf_op jit(solution)/shard_map/ppermute | solution.py:303
  51.8 3.9 %far.3 = (bf16[2,256,256]{2,1,0:T(8,128)(2,1)S(1)}, bf16[2,256,256]{2,1,0:T(8,128)(2,1)S(1)}, f32[2,256,256]{2,1,0:T(8,128)S(1)}) custom-call(f32[2,2,256,256]{3,2,1,0:T(8,128)S(1)} %start.1, bf16[512,768]{1,0:T(8,128)(2,1)S(1)} %copy-done.2, bf16[768,512]{1,0:T(8,128)(2,1)S(1)} %copy-done.4, bf16[2,2,256,256]{3,2,1,0:T(8,128)(2,1)S(1)} %get-tuple-element.140.frames, ...), custom_call_target="tpu_custom_call" | custom-call | flops 2147483648 | bytes 4194304 | tf_op jit(solution)/shard_map/far/pallas_call | solution.py:377
  55.7 0.1 collective-permute-start.21
  55.8 0.8 collective-permute-done.18.arrived
  56.6 1.5 %far.2 = (bf16[2,256,256]{2,1,0:T(8,128)(2,1)S(1)}, bf16[2,256,256]{2,1,0:T(8,128)(2,1)S(1)}, f32[2,256,256]{2,1,0:T(8,128)S(1)}) custom-call(f32[2,2,256,256]{3,2,1,0:T(8,128)S(1)} %start.1, bf16[512,768]{1,0:T(8,128)(2,1)S(1)} %copy-done.2, bf16[768,512]{1,0:T(8,128)(2,1)S(1)} %copy-done.4, bf16[2,2,256,256]{3,2,1,0:T(8,128)(2,1)S(1)} %get-tuple-element.136.frames, ...), custom_call_target="tpu_custom_call" | custom-call | flops 2147483648 | bytes 4194304 | tf_op jit(solution)/shard_map/far/pallas_call | solution.py:377
  58.1 0.1 collective-permute-start.20
  58.2 1.1 %probe.3 = (f32[2,64,256]{2,1,0:T(8,128)S(1)}, f32[2,64,256]{2,1,0:T(8,128)S(1)}, bf16[2,2,64,256]{3,2,1,0:T(8,128)(2,1)S(1)}) custom-call(s32[2,2]{1,0:T(2,128)S(1)} %collective-permute-done.4.refs_2_.places, f32[2,256,256]{2,1,0:T(8,128)S(1)} %get-tuple-element.139.refs_0_, f32[2,256,256]{2,1,0:T(8,128)S(1)} %get-tuple-element.143.refs_1_), custom_call_target="tpu_custom_call" | custom-call | flops 67108864 | bytes 4194304 | tf_op jit(solution)/shard_map/probe/pallas_call | solution.py:397
  59.2 0.6 collective-permute-start.22
  59.8 0.0 collective-permute-done.21.refs_3_
  59.8 0.7 part.1
  60.5 2.0 %collective-permute-start.23 = (bf16[2,2,2,64,256]{4,3,2,1,0:T(8,128)(2,1)S(1)}, bf16[2,2,2,64,256]{4,3,2,1,0:T(8,128)(2,1)S(1)}, u32[]{:S(2)}, u32[]{:S(2)}) collective-permute-start(bf16[2,2,2,64,256]{4,3,2,1,0:T(8,128)(2,1)S(1)} %get-tuple-element.154), channel_id=1, source_target_pairs={{0,6},{1,7},{2,0},{3,1},{4,2},{5,3},{6,4},{7,5},{8,14},{9,15},{10,... | collective-permute-start | bytes 786440 | tf_op jit(solution)/shard_map/ppermute | solution.py:303
  62.5 0.0 collective-permute-start.24
  62.5 2.0 %collective-permute-start.25 = (bf16[2,2,2,64,256]{4,3,2,1,0:T(8,128)(2,1)S(1)}, bf16[2,2,2,64,256]{4,3,2,1,0:T(8,128)(2,1)S(1)}, u32[]{:S(2)}, u32[]{:S(2)}) collective-permute-start(bf16[2,2,2,64,256]{4,3,2,1,0:T(8,128)(2,1)S(1)} %get-tuple-element.156), channel_id=1, source_target_pairs={{0,1},{1,2},{2,3},{3,4},{4,5},{5,6},{6,7},{7,0},{8,9},{9,10},{10,1... | collective-permute-start | bytes 786440 | tf_op jit(solution)/shard_map/ppermute | solution.py:303
  64.5 0.0 collective-permute-start.26
  64.6 17.6 %while.14 = (s32[]{:T(128)}, f32[2,64,256]{2,1,0:T(8,128)S(1)}, f32[2,64,256]{2,1,0:T(8,128)S(1)}, s32[]{:T(128)}, pred[]{:T(512)}, /*index=5*/bf16[2,2,64,256]{3,2,1,0:T(8,128)(2,1)S(1)}, s32[]{:T(128)}) while((s32[]{:T(128)}, f32[2,64,256]{2,1,0:T(8,128)S(1)}, f32[2,64,256]{2,1,0:T(8,128)S(1)}, s32[]{:T(128)}, pred[]{:T(512)}, ...), condition=%wide.region_1.2_spmd, body=%wide.region_0.1_spmd.sunk | while | flops 458754 | bytes 1966278 | solution.py:425
  64.6 2.9 %collective-permute-start = (bf16[2,64,256]{2,1,0:T(8,128)(2,1)S(1)}, bf16[2,64,256]{2,1,0:T(8,128)(2,1)S(1)}, u32[]{:S(2)}, u32[]{:S(2)}) collective-permute-start(bf16[2,64,256]{2,1,0:T(8,128)(2,1)S(1)} %fusion.5), channel_id=1, source_target_pairs={{0,16},{1,17},{2,18},{3,19},{4,20},{5,21},{6,22},{7,23},{8,24},{9,... | collective-permute-start | bytes 196616 | tf_op jit(solution)/shard_map/while/body/ppermute | solution.py:303
  67.6 1.9 %collective-permute-done = bf16[2,64,256]{2,1,0:T(8,128)(2,1)S(1)} collective-permute-done((bf16[2,64,256]{2,1,0:T(8,128)(2,1)S(1)}, bf16[2,64,256]{2,1,0:T(8,128)(2,1)S(1)}, u32[]{:S(2)}, u32[]{:S(2)}) %collective-permute-start) | collective-permute-done | bytes 65568 | tf_op jit(solution)/shard_map/while/body/ppermute | solution.py:303
  69.5 1.4 %collective-permute-start.1 = (bf16[2,64,256]{2,1,0:T(8,128)(2,1)S(1)}, bf16[2,64,256]{2,1,0:T(8,128)(2,1)S(1)}, u32[]{:S(2)}, u32[]{:S(2)}) collective-permute-start(bf16[2,64,256]{2,1,0:T(8,128)(2,1)S(1)} %get-tuple-element.218), channel_id=1, source_target_pairs={{0,1},{1,0},{2,3},{3,2},{4,5},{5,4},{6,7},{7,6},{8,9},{9,8},{10,11... | collective-permute-start | bytes 196616 | tf_op jit(solution)/shard_map/while/body/ppermute | solution.py:410
  70.9 6.9 %collective-permute-done.1 = bf16[2,64,256]{2,1,0:T(8,128)(2,1)S(1)} collective-permute-done((bf16[2,64,256]{2,1,0:T(8,128)(2,1)S(1)}, bf16[2,64,256]{2,1,0:T(8,128)(2,1)S(1)}, u32[]{:S(2)}, u32[]{:S(2)}) %collective-permute-start.1) | collective-permute-done | bytes 65568 | tf_op jit(solution)/shard_map/while/body/ppermute | solution.py:410
  77.8 0.1 collective-permute-start.2
  77.9 4.3 %collective-permute-done.2 = bf16[2,64,256]{2,1,0:T(8,128)(2,1)S(1)} collective-permute-done((bf16[2,64,256]{2,1,0:T(8,128)(2,1)S(1)}, bf16[2,64,256]{2,1,0:T(8,128)(2,1)S(1)}, u32[]{:S(2)}, u32[]{:S(2)}) %collective-permute-start.2) | collective-permute-done | bytes 65568 | tf_op jit(solution)/shard_map/while/body/ppermute | solution.py:410
  82.2 0.0 collective-permute-done.23.refs_5_
  82.2 0.0 collective-permute-done.25.refs_8_
  82.2 0.0 collective-permute-done.26.refs_9_
  82.2 1.2 %collective-permute-start.27 = (bf16[2,64,256]{2,1,0:T(8,128)(2,1)S(1)}, bf16[2,64,256]{2,1,0:T(8,128)(2,1)S(1)}, u32[]{:S(2)}, u32[]{:S(2)}) collective-permute-start(bf16[2,64,256]{2,1,0:T(8,128)(2,1)S(1)} %convert_element_type.65), channel_id=1, source_target_pairs={{0,4},{1,5},{2,6},{3,7},{4,0},{5,1},{6,2},{7,3},{8,12},{9,13},{10,... | collective-permute-start | bytes 196616 | tf_op jit(solution)/shard_map/ppermute | solution.py:410
  83.5 2.7 %deposit.1 = f32[2,64,3072]{2,1,0:T(8,128)} custom-call(s32[2,2]{1,0:T(2,128)S(1)} %multiply_add_fusion.refs_0_, s32[2,2]{1,0:T(2,128)S(1)} %collective-permute-done.3.refs_1_, s32[2,2]{1,0:T(2,128)S(1)} %collective-permute-done.4.refs_2_.places, s32[2,2]{1,0:T(2,128)S(1)} %collective-permute-done.5.refs_3_, s32[2,2]{1,0:T(2,128)S(1)} %collective-permute-done.6.refs_4_, ...), custom_call_target="tpu_custom_call" | custom-call | flops 67108864 | bytes 4194304 | tf_op jit(solution)/shard_map/deposit/pallas_call | solution.py:430
  86.1 1.7 %collective-permute-done.27 = bf16[2,64,256]{2,1,0:T(8,128)(2,1)S(1)} collective-permute-done((bf16[2,64,256]{2,1,0:T(8,128)(2,1)S(1)}, bf16[2,64,256]{2,1,0:T(8,128)(2,1)S(1)}, u32[]{:S(2)}, u32[]{:S(2)}) %collective-permute-start.27) | collective-permute-done | bytes 65568 | tf_op jit(solution)/shard_map/ppermute | solution.py:410
  87.8 0.7 convert_add_fusion.3
  (24 shorter events, 0.1 us)
Async XLA Ops:
  0.6 5.1 %copy-start.6 = (s32[2,2]{1,0:T(2,128)S(1)}, s32[2,2]{1,0:T(2,128)}, u32[]{:S(2)}) copy-start(s32[2,2]{1,0:T(2,128)} %param.12) | copy-start | bytes 52
  0.6 5.0 %copy-start.5 = (s32[2,2]{1,0:T(2,128)S(1)}, s32[2,2]{1,0:T(2,128)}, u32[]{:S(2)}) copy-start(s32[2,2]{1,0:T(2,128)} %param.13) | copy-start | bytes 52
  0.7 14.6 %copy-start = (f32[1,2,64,3072]{3,2,1,0:T(8,128)S(1)}, f32[1,2,64,3072]{3,2,1,0:T(8,128)}, u32[]{:S(2)}) copy-start(f32[1,2,64,3072]{3,2,1,0:T(8,128)} %param.9) | copy-start | bytes 4718596
  2.6 32.4 %copy-start.1 = (f32[2,256,256]{2,1,0:T(8,128)S(1)}, f32[2,256,256]{2,1,0:T(8,128)}, u32[]{:S(2)}) copy-start(f32[2,256,256]{2,1,0:T(8,128)} %probe.2) | copy-start | bytes 1572868
  2.6 32.4 %copy-start.2 = (bf16[512,768]{1,0:T(8,128)(2,1)S(1)}, bf16[512,768]{1,0:T(8,128)(2,1)}, u32[]{:S(2)}) copy-start(bf16[512,768]{1,0:T(8,128)(2,1)} %constant.46.clone.refs_2_.left) | copy-start | bytes 2359300
  2.6 13.9 %collective-permute-start.7 = (bf16[2,256,256]{2,1,0:T(8,128)(2,1)}, bf16[2,256,256]{2,1,0:T(8,128)(2,1)S(1)}, u32[]{:S(2)}, u32[]{:S(2)}) collective-permute-start(bf16[2,256,256]{2,1,0:T(8,128)(2,1)} %pick.1), channel_id=1, source_target_pairs={{0,2},{1,3},{2,4},{3,5},{4,6},{5,7},{6,0},{7,1},{8,10},{9,11},{10,... | collective-permute-start | bytes 786440 | tf_op jit(solution)/shard_map/ppermute | solution.py:293
  5.7 8.6 %collective-permute-start.4 = (s32[2,2]{1,0:T(2,128)S(1)}, s32[2,2]{1,0:T(2,128)S(1)}, u32[]{:S(2)}, u32[]{:S(2)}) collective-permute-start(s32[2,2]{1,0:T(2,128)S(1)} %multiply_add_fusion.refs_0_), channel_id=1, source_target_pairs={{0,2},{1,3},{2,4},{3,5},{4,6},{5,7},{6,0},{7,1},{8,10},{9,11},{10,... | collective-permute-start | bytes 56 | tf_op jit(solution)/shard_map/ppermute | solution.py:293
  7.3 7.9 %collective-permute-start.3 = (s32[2,2]{1,0:T(2,128)S(1)}, s32[2,2]{1,0:T(2,128)S(1)}, u32[]{:S(2)}, u32[]{:S(2)}) collective-permute-start(s32[2,2]{1,0:T(2,128)S(1)} %multiply_add_fusion.refs_0_), channel_id=1, source_target_pairs={{0,1},{1,2},{2,3},{3,4},{4,5},{5,6},{6,7},{7,0},{8,9},{9,10},{10,1... | collective-permute-start | bytes 56 | tf_op jit(solution)/shard_map/ppermute | solution.py:293
  8.8 6.4 %collective-permute-start.5 = (s32[2,2]{1,0:T(2,128)S(1)}, s32[2,2]{1,0:T(2,128)S(1)}, u32[]{:S(2)}, u32[]{:S(2)}) collective-permute-start(s32[2,2]{1,0:T(2,128)S(1)} %multiply_add_fusion.refs_0_), channel_id=1, source_target_pairs={{0,3},{1,4},{2,5},{3,6},{4,7},{5,0},{6,1},{7,2},{8,11},{9,12},{10,... | collective-permute-start | bytes 56 | tf_op jit(solution)/shard_map/ppermute | solution.py:293
  9.9 5.4 %collective-permute-start.6 = (s32[2,2]{1,0:T(2,128)S(1)}, s32[2,2]{1,0:T(2,128)S(1)}, u32[]{:S(2)}, u32[]{:S(2)}) collective-permute-start(s32[2,2]{1,0:T(2,128)S(1)} %multiply_add_fusion.refs_0_), channel_id=1, source_target_pairs={{0,4},{1,5},{2,6},{3,7},{4,0},{5,1},{6,2},{7,3},{8,12},{9,13},{10,... | collective-permute-start | bytes 56 | tf_op jit(solution)/shard_map/ppermute | solution.py:293
  16.5 18.2 %collective-permute-start.8 = (bf16[2,256,256]{2,1,0:T(8,128)(2,1)S(1)}, bf16[2,256,256]{2,1,0:T(8,128)(2,1)S(1)}, u32[]{:S(2)}, u32[]{:S(2)}) collective-permute-start(bf16[2,256,256]{2,1,0:T(8,128)(2,1)S(1)} %collective-permute-done.7.refs_0_), channel_id=1, source_target_pairs={{0,16},{1,17},{2,18},{3,19},{4,20},{5,21},{6,22},{7,23},{8,24},{9,... | collective-permute-start | bytes 786440 | tf_op jit(solution)/shard_map/ppermute | solution.py:303
  19.9 8.2 %collective-permute-start.9 = (bf16[2,2,64,256]{3,2,1,0:T(8,128)(2,1)S(1)}, bf16[2,2,64,256]{3,2,1,0:T(8,128)(2,1)S(1)}, u32[]{:S(2)}, u32[]{:S(2)}) collective-permute-start(bf16[2,2,64,256]{3,2,1,0:T(8,128)(2,1)S(1)} %get-tuple-element.125), channel_id=1, source_target_pairs={{0,2},{1,3},{2,4},{3,5},{4,6},{5,7},{6,0},{7,1},{8,10},{9,11},{10,... | collective-permute-start | bytes 393224 | tf_op jit(solution)/shard_map/ppermute | solution.py:303
  20.7 9.5 %collective-permute-start.10 = (bf16[2,2,64,256]{3,2,1,0:T(8,128)(2,1)S(1)}, bf16[2,2,64,256]{3,2,1,0:T(8,128)(2,1)S(1)}, u32[]{:S(2)}, u32[]{:S(2)}) collective-permute-start(bf16[2,2,64,256]{3,2,1,0:T(8,128)(2,1)S(1)} %get-tuple-element.127), channel_id=1, source_target_pairs={{0,1},{1,2},{2,3},{3,4},{4,5},{5,6},{6,7},{7,0},{8,9},{9,10},{10,1... | collective-permute-start | bytes 393224 | tf_op jit(solution)/shard_map/ppermute | solution.py:303
  22.2 8.0 %collective-permute-start.11 = (bf16[2,2,64,256]{3,2,1,0:T(8,128)(2,1)S(1)}, bf16[2,2,64,256]{3,2,1,0:T(8,128)(2,1)S(1)}, u32[]{:S(2)}, u32[]{:S(2)}) collective-permute-start(bf16[2,2,64,256]{3,2,1,0:T(8,128)(2,1)S(1)} %get-tuple-element.129), channel_id=1, source_target_pairs={{0,7},{1,0},{2,1},{3,2},{4,3},{5,4},{6,5},{7,6},{8,15},{9,8},{10,9... | collective-permute-start | bytes 393224 | tf_op jit(solution)/shard_map/ppermute | solution.py:303
  25.4 9.2 %collective-permute-start.12 = (bf16[2,2,64,256]{3,2,1,0:T(8,128)(2,1)S(1)}, bf16[2,2,64,256]{3,2,1,0:T(8,128)(2,1)S(1)}, u32[]{:S(2)}, u32[]{:S(2)}) collective-permute-start(bf16[2,2,64,256]{3,2,1,0:T(8,128)(2,1)S(1)} %get-tuple-element.130), channel_id=1, source_target_pairs={{0,6},{1,7},{2,0},{3,1},{4,2},{5,3},{6,4},{7,5},{8,14},{9,15},{10,... | collective-permute-start | bytes 393224 | tf_op jit(solution)/shard_map/ppermute | solution.py:303
  28.1 9.1 %collective-permute-start.13 = (bf16[2,2,64,256]{3,2,1,0:T(8,128)(2,1)S(1)}, bf16[2,2,64,256]{3,2,1,0:T(8,128)(2,1)S(1)}, u32[]{:S(2)}, u32[]{:S(2)}) collective-permute-start(bf16[2,2,64,256]{3,2,1,0:T(8,128)(2,1)S(1)} %get-tuple-element.131), channel_id=1, source_target_pairs={{0,10},{1,11},{2,12},{3,13},{4,14},{5,15},{6,8},{7,9},{8,2},{9,3},... | collective-permute-start | bytes 393224 | tf_op jit(solution)/shard_map/ppermute | solution.py:303
  30.2 8.8 %collective-permute-start.14 = (bf16[2,2,64,256]{3,2,1,0:T(8,128)(2,1)S(1)}, bf16[2,2,64,256]{3,2,1,0:T(8,128)(2,1)S(1)}, u32[]{:S(2)}, u32[]{:S(2)}) collective-permute-start(bf16[2,2,64,256]{3,2,1,0:T(8,128)(2,1)S(1)} %get-tuple-element.132), channel_id=1, source_target_pairs={{0,9},{1,10},{2,11},{3,12},{4,13},{5,14},{6,15},{7,8},{8,1},{9,2},... | collective-permute-start | bytes 393224 | tf_op jit(solution)/shard_map/ppermute | solution.py:303
  30.2 8.8 %collective-permute-start.16 = (bf16[2,2,64,256]{3,2,1,0:T(8,128)(2,1)S(1)}, bf16[2,2,64,256]{3,2,1,0:T(8,128)(2,1)S(1)}, u32[]{:S(2)}, u32[]{:S(2)}) collective-permute-start(bf16[2,2,64,256]{3,2,1,0:T(8,128)(2,1)S(1)} %get-tuple-element.134), channel_id=1, source_target_pairs={{0,15},{1,8},{2,9},{3,10},{4,11},{5,12},{6,13},{7,14},{8,7},{9,0},... | collective-permute-start | bytes 393224 | tf_op jit(solution)/shard_map/ppermute | solution.py:303
  34.6 5.9 %collective-permute-start.17 = (bf16[2,2,64,256]{3,2,1,0:T(8,128)(2,1)S(1)}, bf16[2,2,64,256]{3,2,1,0:T(8,128)(2,1)S(1)}, u32[]{:S(2)}, u32[]{:S(2)}) collective-permute-start(bf16[2,2,64,256]{3,2,1,0:T(8,128)(2,1)S(1)} %get-tuple-element.135), channel_id=1, source_target_pairs={{0,14},{1,15},{2,8},{3,9},{4,10},{5,11},{6,12},{7,13},{8,6},{9,7},... | collective-permute-start | bytes 393224 | tf_op jit(solution)/shard_map/ppermute | solution.py:303
  34.7 5.9 %collective-permute-start.15 = (bf16[2,2,64,256]{3,2,1,0:T(8,128)(2,1)S(1)}, bf16[2,2,64,256]{3,2,1,0:T(8,128)(2,1)S(1)}, u32[]{:S(2)}, u32[]{:S(2)}) collective-permute-start(bf16[2,2,64,256]{3,2,1,0:T(8,128)(2,1)S(1)} %get-tuple-element.133), channel_id=1, source_target_pairs={{0,8},{1,9},{2,10},{3,11},{4,12},{5,13},{6,14},{7,15},{8,0},{9,1},... | collective-permute-start | bytes 393224 | tf_op jit(solution)/shard_map/ppermute | solution.py:303
  35.0 1.1 %copy-start.3 = (bf16[768,512]{1,0:T(8,128)(2,1)S(1)}, bf16[768,512]{1,0:T(8,128)(2,1)}, u32[]{:S(2)}) copy-start(bf16[768,512]{1,0:T(8,128)(2,1)} %constant.47.clone.refs_3_.right) | copy-start | bytes 2359300
  36.2 4.4 %copy-start.4 = (bf16[768,512]{1,0:T(8,128)(2,1)S(1)}, bf16[768,512]{1,0:T(8,128)(2,1)}, u32[]{:S(2)}) copy-start(bf16[768,512]{1,0:T(8,128)(2,1)} %constant.47.clone.refs_3_.right) | copy-start | bytes 2359300
  42.5 9.2 %collective-permute-start.19 = (bf16[2,256,256]{2,1,0:T(8,128)(2,1)S(1)}, bf16[2,256,256]{2,1,0:T(8,128)(2,1)S(1)}, u32[]{:S(2)}, u32[]{:S(2)}) collective-permute-start(bf16[2,256,256]{2,1,0:T(8,128)(2,1)S(1)} %get-tuple-element.142), channel_id=1, source_target_pairs={{0,16},{1,17},{2,18},{3,19},{4,20},{5,21},{6,22},{7,23},{8,24},{9,... | collective-permute-start | bytes 786440 | tf_op jit(solution)/shard_map/ppermute | solution.py:303
  47.0 9.6 %collective-permute-start.18 = (bf16[2,256,256]{2,1,0:T(8,128)(2,1)S(1)}, bf16[2,256,256]{2,1,0:T(8,128)(2,1)S(1)}, u32[]{:S(2)}, u32[]{:S(2)}) collective-permute-start(bf16[2,256,256]{2,1,0:T(8,128)(2,1)S(1)} %get-tuple-element.138), channel_id=1, source_target_pairs={{0,16},{1,17},{2,18},{3,19},{4,20},{5,21},{6,22},{7,23},{8,24},{9,... | collective-permute-start | bytes 786440 | tf_op jit(solution)/shard_map/ppermute | solution.py:303
  55.7 4.1 %collective-permute-start.21 = (bf16[2,256,256]{2,1,0:T(8,128)(2,1)S(1)}, bf16[2,256,256]{2,1,0:T(8,128)(2,1)S(1)}, u32[]{:S(2)}, u32[]{:S(2)}) collective-permute-start(bf16[2,256,256]{2,1,0:T(8,128)(2,1)S(1)} %get-tuple-element.148), channel_id=1, source_target_pairs={{0,8},{1,9},{2,10},{3,11},{4,12},{5,13},{6,14},{7,15},{8,0},{9,1},... | collective-permute-start | bytes 786440 | tf_op jit(solution)/shard_map/ppermute | solution.py:303
  58.1 1.7 %collective-permute-start.20 = (bf16[2,256,256]{2,1,0:T(8,128)(2,1)S(1)}, bf16[2,256,256]{2,1,0:T(8,128)(2,1)S(1)}, u32[]{:S(2)}, u32[]{:S(2)}) collective-permute-start(bf16[2,256,256]{2,1,0:T(8,128)(2,1)S(1)} %get-tuple-element.147), channel_id=1, source_target_pairs={{0,8},{1,9},{2,10},{3,11},{4,12},{5,13},{6,14},{7,15},{8,0},{9,1},... | collective-permute-start | bytes 786440 | tf_op jit(solution)/shard_map/ppermute | solution.py:303
  59.2 5.4 %collective-permute-start.22 = (bf16[2,2,64,256]{3,2,1,0:T(8,128)(2,1)S(1)}, bf16[2,2,64,256]{3,2,1,0:T(8,128)(2,1)S(1)}, u32[]{:S(2)}, u32[]{:S(2)}) collective-permute-start(bf16[2,2,64,256]{3,2,1,0:T(8,128)(2,1)S(1)} %get-tuple-element.152), channel_id=1, source_target_pairs={{0,8},{1,9},{2,10},{3,11},{4,12},{5,13},{6,14},{7,15},{8,0},{9,1},... | collective-permute-start | bytes 393224 | tf_op jit(solution)/shard_map/ppermute | solution.py:303
  60.5 21.7 %collective-permute-start.23 = (bf16[2,2,2,64,256]{4,3,2,1,0:T(8,128)(2,1)S(1)}, bf16[2,2,2,64,256]{4,3,2,1,0:T(8,128)(2,1)S(1)}, u32[]{:S(2)}, u32[]{:S(2)}) collective-permute-start(bf16[2,2,2,64,256]{4,3,2,1,0:T(8,128)(2,1)S(1)} %get-tuple-element.154), channel_id=1, source_target_pairs={{0,6},{1,7},{2,0},{3,1},{4,2},{5,3},{6,4},{7,5},{8,14},{9,15},{10,... | collective-permute-start | bytes 786440 | tf_op jit(solution)/shard_map/ppermute | solution.py:303
  62.5 19.7 %collective-permute-start.24 = (bf16[2,2,2,64,256]{4,3,2,1,0:T(8,128)(2,1)S(1)}, bf16[2,2,2,64,256]{4,3,2,1,0:T(8,128)(2,1)S(1)}, u32[]{:S(2)}, u32[]{:S(2)}) collective-permute-start(bf16[2,2,2,64,256]{4,3,2,1,0:T(8,128)(2,1)S(1)} %get-tuple-element.155), channel_id=1, source_target_pairs={{0,7},{1,0},{2,1},{3,2},{4,3},{5,4},{6,5},{7,6},{8,15},{9,8},{10,9... | collective-permute-start | bytes 786440 | tf_op jit(solution)/shard_map/ppermute | solution.py:303
  62.5 19.7 %collective-permute-start.25 = (bf16[2,2,2,64,256]{4,3,2,1,0:T(8,128)(2,1)S(1)}, bf16[2,2,2,64,256]{4,3,2,1,0:T(8,128)(2,1)S(1)}, u32[]{:S(2)}, u32[]{:S(2)}) collective-permute-start(bf16[2,2,2,64,256]{4,3,2,1,0:T(8,128)(2,1)S(1)} %get-tuple-element.156), channel_id=1, source_target_pairs={{0,1},{1,2},{2,3},{3,4},{4,5},{5,6},{6,7},{7,0},{8,9},{9,10},{10,1... | collective-permute-start | bytes 786440 | tf_op jit(solution)/shard_map/ppermute | solution.py:303
  64.5 17.7 %collective-permute-start.26 = (bf16[2,2,2,64,256]{4,3,2,1,0:T(8,128)(2,1)S(1)}, bf16[2,2,2,64,256]{4,3,2,1,0:T(8,128)(2,1)S(1)}, u32[]{:S(2)}, u32[]{:S(2)}) collective-permute-start(bf16[2,2,2,64,256]{4,3,2,1,0:T(8,128)(2,1)S(1)} %get-tuple-element.157), channel_id=1, source_target_pairs={{0,2},{1,3},{2,4},{3,5},{4,6},{5,7},{6,0},{7,1},{8,10},{9,11},{10,... | collective-permute-start | bytes 786440 | tf_op jit(solution)/shard_map/ppermute | solution.py:303
  64.6 4.8 %collective-permute-start = (bf16[2,64,256]{2,1,0:T(8,128)(2,1)S(1)}, bf16[2,64,256]{2,1,0:T(8,128)(2,1)S(1)}, u32[]{:S(2)}, u32[]{:S(2)}) collective-permute-start(bf16[2,64,256]{2,1,0:T(8,128)(2,1)S(1)} %fusion.5), channel_id=1, source_target_pairs={{0,16},{1,17},{2,18},{3,19},{4,20},{5,21},{6,22},{7,23},{8,24},{9,... | collective-permute-start | bytes 196616 | tf_op jit(solution)/shard_map/while/body/ppermute | solution.py:303
  69.5 8.3 %collective-permute-start.1 = (bf16[2,64,256]{2,1,0:T(8,128)(2,1)S(1)}, bf16[2,64,256]{2,1,0:T(8,128)(2,1)S(1)}, u32[]{:S(2)}, u32[]{:S(2)}) collective-permute-start(bf16[2,64,256]{2,1,0:T(8,128)(2,1)S(1)} %get-tuple-element.218), channel_id=1, source_target_pairs={{0,1},{1,0},{2,3},{3,2},{4,5},{5,4},{6,7},{7,6},{8,9},{9,8},{10,11... | collective-permute-start | bytes 196616 | tf_op jit(solution)/shard_map/while/body/ppermute | solution.py:410
  77.8 4.3 %collective-permute-start.2 = (bf16[2,64,256]{2,1,0:T(8,128)(2,1)S(1)}, bf16[2,64,256]{2,1,0:T(8,128)(2,1)S(1)}, u32[]{:S(2)}, u32[]{:S(2)}) collective-permute-start(bf16[2,64,256]{2,1,0:T(8,128)(2,1)S(1)} %add_convert_fusion.2), channel_id=1, source_target_pairs={{0,2},{1,3},{2,0},{3,1},{4,6},{5,7},{6,4},{7,5},{8,10},{9,11},{10,... | collective-permute-start | bytes 196616 | tf_op jit(solution)/shard_map/while/body/ppermute | solution.py:410
  82.2 5.6 %collective-permute-start.27 = (bf16[2,64,256]{2,1,0:T(8,128)(2,1)S(1)}, bf16[2,64,256]{2,1,0:T(8,128)(2,1)S(1)}, u32[]{:S(2)}, u32[]{:S(2)}) collective-permute-start(bf16[2,64,256]{2,1,0:T(8,128)(2,1)S(1)} %convert_element_type.65), channel_id=1, source_target_pairs={{0,4},{1,5},{2,6},{3,7},{4,0},{5,1},{6,2},{7,3},{8,12},{9,13},{10,... | collective-permute-start | bytes 196616 | tf_op jit(solution)/shard_map/ppermute | solution.py:410

commit v5 on v4

--- a/solution.py
+++ b/solution.py
@@ -111,10 +111,20 @@
 
 def pick_kernel(waves, out, buffer, arrived):
     core, half = this_place()
-    copy = pltpu.make_async_copy(waves.at[core, 1 - half], buffer, arrived)
-    copy.start()
-    copy.wait()
-    out[...] = buffer[...].astype(bf16)
+    planes, rows, _ = out.shape
+    height = rows // 2
+    copies = []
+    for plane in range(planes):
+        for start in range(0, rows, height):
+            part = (plane, pl.ds(start, height))
+            copy = pltpu.make_async_copy(
+                waves.at[(core, 1 - half, *part)], buffer.at[part], arrived.at[len(copies)]
+            )
+            copy.start()
+            copies.append((part, copy))
+    for part, copy in copies:
+        copy.wait()
+        out[part] = buffer[part].astype(bf16)
 
 
 def extract_kernel(reach, *refs):
@@ -330,7 +340,7 @@
         [pl.BlockSpec(memory_space=pltpu.HBM)],
         1 << 20,
         "pick",
-        [pltpu.VMEM(wave, f32), pltpu.SemaphoreType.DMA],
+        [pltpu.VMEM(wave, f32), pltpu.SemaphoreType.DMA((4,))],
         62,
     )(exit_adjoint)
     adjoint, scan_row = lax.optimization_barrier((adjoint, scan_row))
@@ -340,14 +350,17 @@
 
     order = [(flip, step) for flip in range(2) for step in range(reach)]
     far_first = sorted(order, key=lambda key: -abs(key[1] - home))
-    pieces = call(
-        functools.partial(extract_kernel, reach),
-        [piece] * len(order),
-        [smem] * reach + [vmem],
-        1 << 26,
-        "extract",
-    )(*places, transmission[0])
-    pieces = dict(zip(order, pieces))
+    pieces = {}
+    for steps in (range(home + 1), range(home + 1, reach)):
+        keys = [(flip, step) for flip in range(2) for step in steps]
+        cut = call(
+            functools.partial(extract_kernel, len(steps)),
+            [piece] * len(keys),
+            [smem] * len(steps) + [vmem],
+            1 << 26,
+            "extract",
+        )(*(places[step] for step in steps), transmission[0])
+        pieces.update(zip(keys, cut))
     adjoint, pieces[0, home] = lax.optimization_barrier((adjoint, pieces[0, home]))
     adjoints = [adjoint, across(adjoint, 2, 0, lower)]
     for flip, step in far_first:

time: 88.7 us -> 93 us (1.048)
  waiting for transfers between devices: 27.7 us -> 35.7 us
  starting transfers between devices: 37.6 us -> 34.3 us
  local copies, waits for them, and re-layouts: 1.16 us -> 0.02 us
    ppermute x5, waiting for transfers between devices: 2.67 us -> 8.01 us  [along_scan(): lax.ppermute(value, 'scan', [(i, (i + by) % regions) for i in range(regio...]
    ppermute x20, starting transfers between devices: 24.9 us -> 22.3 us  [across(): return lax.ppermute(value, ('depth', 'scan'), route)]
    ppermute x20, waiting for transfers between devices: 12.2 us -> 13.7 us  [across(): return lax.ppermute(value, ('depth', 'scan'), route)]
    ppermute x3, starting transfers between devices: 2.72 us -> 1.39 us  [scan_round(): lax.ppermute(rounded, 'scan', route).astype(f32)]
    ppermute x3, waiting for transfers between devices: 12.8 us -> 14 us  [scan_round(): lax.ppermute(rounded, 'scan', route).astype(f32)]
    unnamed x14 -> x12, local copies, waits for them, and re-layouts: 1.16 us -> 0.02 us
  transfers between devices with their start and end apart: 28 -> 28, of which waited for: 12 -> 13; matrix products, arithmetic and copies ran while one was open for 0% -> 0% of each run, Pallas kernels for 19% -> 18%
where the time goes in v5:
time: 93 us; the launch traced here: 92.8 us
  waiting for transfers between devices  35.7 us (38%)
  starting transfers between devices  34.3 us (37%)
  Pallas kernels  21.1 us (23%)
    ppermute x20, starting transfers between devices, across(): return lax.ppermute(value, ('depth', 'scan'), route)  22.3 us
    ppermute x3, waiting for transfers between devices, scan_round(): lax.ppermute(rounded, 'scan', route).astype(f32)  14 us
    ppermute x20, waiting for transfers between devices, across(): return lax.ppermute(value, ('depth', 'scan'), route)  13.7 us
    ppermute x5, starting transfers between devices, along_scan(): lax.ppermute(value, 'scan', [(i, (i + by) % regions) for i in range(regio...  10.7 us
    ppermute x5, waiting for transfers between devices, along_scan(): lax.ppermute(value, 'scan', [(i, (i + by) % regions) for i in range(regio...  8.01 us
    pallas_call x2, Pallas kernels, local(): call(functools.partial(near_kernel, home, turn, turn == count - 1, width)...  6.36 us
    pallas_call x2, Pallas kernels, local(): call(functools.partial(far_kernel, turn, turn == count - 1), [shape(wave,...  5.47 us
    pallas_call x1, Pallas kernels, local(): call(functools.partial(deposit_kernel, reach), shape(transmission.shape[1...  2.68 us
  transfers between devices with their start and end apart: 28, of which 13 were waited for; matrix products, arithmetic and copies ran while one was open for 0% of the time, Pallas kernels for 18%

profile of v5, /device:TPU:0, one launch (start us, length us, event | category | flops | bytes accessed | tf_op | source)
XLA Modules:
  0.0 92.8 jit_solution(7729943287502880881)
XLA Ops:
  0.7 2.0 %pick.1 = bf16[2,256,256]{2,1,0:T(8,128)(2,1)} custom-call(f32[2,2,2,256,256]{4,3,2,1,0:T(8,128)} %waves.1), custom_call_target="tpu_custom_call" | custom-call | flops 1048576 | bytes 4194304 | tf_op jit(solution)/shard_map/pick/pallas_call | solution.py:337
  2.6 3.1 %collective-permute-start.7 = (bf16[2,256,256]{2,1,0:T(8,128)(2,1)}, bf16[2,256,256]{2,1,0:T(8,128)(2,1)S(1)}, u32[]{:S(2)}, u32[]{:S(2)}) collective-permute-start(bf16[2,256,256]{2,1,0:T(8,128)(2,1)} %pick.1), channel_id=1, source_target_pairs={{0,2},{1,3},{2,4},{3,5},{4,6},{5,7},{6,0},{7,1},{8,10},{9,11},{10,... | collective-permute-start | bytes 786440 | tf_op jit(solution)/shard_map/ppermute | solution.py:303
  5.7 1.6 %collective-permute-start.4 = (s32[2,2]{1,0:T(2,128)S(1)}, s32[2,2]{1,0:T(2,128)S(1)}, u32[]{:S(2)}, u32[]{:S(2)}) collective-permute-start(s32[2,2]{1,0:T(2,128)S(1)} %multiply_add_fusion.refs_0_), channel_id=1, source_target_pairs={{0,2},{1,3},{2,4},{3,5},{4,6},{5,7},{6,0},{7,1},{8,10},{9,11},{10,... | collective-permute-start | bytes 56 | tf_op jit(solution)/shard_map/ppermute | solution.py:303
  7.4 1.5 %collective-permute-start.3 = (s32[2,2]{1,0:T(2,128)S(1)}, s32[2,2]{1,0:T(2,128)S(1)}, u32[]{:S(2)}, u32[]{:S(2)}) collective-permute-start(s32[2,2]{1,0:T(2,128)S(1)} %multiply_add_fusion.refs_0_), channel_id=1, source_target_pairs={{0,1},{1,2},{2,3},{3,4},{4,5},{5,6},{6,7},{7,0},{8,9},{9,10},{10,1... | collective-permute-start | bytes 56 | tf_op jit(solution)/shard_map/ppermute | solution.py:303
  8.9 5.4 %collective-permute-done.4.refs_2_.places = s32[2,2]{1,0:T(2,128)S(1)} collective-permute-done((s32[2,2]{1,0:T(2,128)S(1)}, s32[2,2]{1,0:T(2,128)S(1)}, u32[]{:S(2)}, u32[]{:S(2)}) %collective-permute-start.4) | collective-permute-done | bytes 48 | tf_op jit(solution)/shard_map/ppermute | solution.py:303
  14.3 0.9 %collective-permute-done.3.refs_1_ = s32[2,2]{1,0:T(2,128)S(1)} collective-permute-done((s32[2,2]{1,0:T(2,128)S(1)}, s32[2,2]{1,0:T(2,128)S(1)}, u32[]{:S(2)}, u32[]{:S(2)}) %collective-permute-start.3) | collective-permute-done | bytes 48 | tf_op jit(solution)/shard_map/ppermute | solution.py:303
  15.3 0.9 extract.2
  16.2 0.0 collective-permute-done.7.refs_0_
  16.2 3.4 %collective-permute-start.8 = (bf16[2,256,256]{2,1,0:T(8,128)(2,1)S(1)}, bf16[2,256,256]{2,1,0:T(8,128)(2,1)S(1)}, u32[]{:S(2)}, u32[]{:S(2)}) collective-permute-start(bf16[2,256,256]{2,1,0:T(8,128)(2,1)S(1)} %collective-permute-done.7.refs_0_), channel_id=1, source_target_pairs={{0,16},{1,17},{2,18},{3,19},{4,20},{5,21},{6,22},{7,23},{8,24},{9,... | collective-permute-start | bytes 786440 | tf_op jit(solution)/shard_map/ppermute | solution.py:313
  19.6 0.1 collective-permute-start.9
  19.7 1.3 %collective-permute-start.5 = (s32[2,2]{1,0:T(2,128)S(1)}, s32[2,2]{1,0:T(2,128)S(1)}, u32[]{:S(2)}, u32[]{:S(2)}) collective-permute-start(s32[2,2]{1,0:T(2,128)S(1)} %multiply_add_fusion.refs_0_), channel_id=1, source_target_pairs={{0,3},{1,4},{2,5},{3,6},{4,7},{5,0},{6,1},{7,2},{8,11},{9,12},{10,... | collective-permute-start | bytes 56 | tf_op jit(solution)/shard_map/ppermute | solution.py:303
  21.0 3.1 %collective-permute-start.6 = (s32[2,2]{1,0:T(2,128)S(1)}, s32[2,2]{1,0:T(2,128)S(1)}, u32[]{:S(2)}, u32[]{:S(2)}) collective-permute-start(s32[2,2]{1,0:T(2,128)S(1)} %multiply_add_fusion.refs_0_), channel_id=1, source_target_pairs={{0,4},{1,5},{2,6},{3,7},{4,0},{5,1},{6,2},{7,3},{8,12},{9,13},{10,... | collective-permute-start | bytes 56 | tf_op jit(solution)/shard_map/ppermute | solution.py:303
  24.1 0.0 collective-permute-start.10
  24.1 1.1 %collective-permute-done.5.refs_0_.refs_3_ = s32[2,2]{1,0:T(2,128)S(1)} collective-permute-done((s32[2,2]{1,0:T(2,128)S(1)}, s32[2,2]{1,0:T(2,128)S(1)}, u32[]{:S(2)}, u32[]{:S(2)}) %collective-permute-start.5) | collective-permute-done | bytes 48 | tf_op jit(solution)/shard_map/ppermute | solution.py:303
  25.2 0.0 collective-permute-start.13
  25.2 0.5 collective-permute-done.6.refs_1_.refs_4_
  25.8 0.8 collective-permute-start.14
  26.6 0.8 extract.3
  27.4 0.0 collective-permute-done.9.refs_0_
  27.4 5.0 %collective-permute-start.11 = (bf16[2,2,64,256]{3,2,1,0:T(8,128)(2,1)S(1)}, bf16[2,2,64,256]{3,2,1,0:T(8,128)(2,1)S(1)}, u32[]{:S(2)}, u32[]{:S(2)}) collective-permute-start(bf16[2,2,64,256]{3,2,1,0:T(8,128)(2,1)S(1)} %get-tuple-element.129), channel_id=1, source_target_pairs={{0,7},{1,0},{2,1},{3,2},{4,3},{5,4},{6,5},{7,6},{8,15},{9,8},{10,9... | collective-permute-start | bytes 393224 | tf_op jit(solution)/shard_map/ppermute | solution.py:313
  32.4 0.0 collective-permute-done.10.refs_1_
  32.4 0.2 collective-permute-start.12
  32.6 0.0 collective-permute-done.13.refs_5_
  32.6 1.7 %collective-permute-start.16 = (bf16[2,2,64,256]{3,2,1,0:T(8,128)(2,1)S(1)}, bf16[2,2,64,256]{3,2,1,0:T(8,128)(2,1)S(1)}, u32[]{:S(2)}, u32[]{:S(2)}) collective-permute-start(bf16[2,2,64,256]{3,2,1,0:T(8,128)(2,1)S(1)} %get-tuple-element.134), channel_id=1, source_target_pairs={{0,15},{1,8},{2,9},{3,10},{4,11},{5,12},{6,13},{7,14},{8,7},{9,0},... | collective-permute-start | bytes 393224 | tf_op jit(solution)/shard_map/ppermute | solution.py:313
  34.3 3.6 %collective-permute-done.14.refs_6_ = bf16[2,2,64,256]{3,2,1,0:T(8,128)(2,1)S(1)} collective-permute-done((bf16[2,2,64,256]{3,2,1,0:T(8,128)(2,1)S(1)}, bf16[2,2,64,256]{3,2,1,0:T(8,128)(2,1)S(1)}, u32[]{:S(2)}, u32[]{:S(2)}) %collective-permute-start.14) | collective-permute-done | bytes 131104 | tf_op jit(solution)/shard_map/ppermute | solution.py:313
  37.9 1.2 %start.1 = f32[2,2,256,256]{3,2,1,0:T(8,128)S(1)} custom-call(s32[2,2]{1,0:T(2,128)S(1)} %collective-permute-done.4.refs_2_.places, f32[2,256,256]{2,1,0:T(8,128)S(1)} %copy-done.1, bf16[2,256,256]{2,1,0:T(8,128)(2,1)S(1)} %collective-permute-done.7.refs_0_, bf16[2,256,256]{2,1,0:T(8,128)(2,1)S(1)} %collective-permute-done.8.refs_1_, ...), custom_call_target="tpu_custom_call" | custom-call | flops 1073741824 | bytes 4194304 | tf_op jit(solution)/shard_map/start/pallas_call | solution.py:371
  39.1 0.0 collective-permute-done.11.refs_3_
  39.1 0.0 collective-permute-done.12.refs_4_
  39.1 2.8 %collective-permute-done.16.refs_8_ = bf16[2,2,64,256]{3,2,1,0:T(8,128)(2,1)S(1)} collective-permute-done((bf16[2,2,64,256]{3,2,1,0:T(8,128)(2,1)S(1)}, bf16[2,2,64,256]{3,2,1,0:T(8,128)(2,1)S(1)}, u32[]{:S(2)}, u32[]{:S(2)}) %collective-permute-start.16) | collective-permute-done | bytes 131104 | tf_op jit(solution)/shard_map/ppermute | solution.py:313
  41.9 1.9 %collective-permute-done.17.refs_9_ = bf16[2,2,64,256]{3,2,1,0:T(8,128)(2,1)S(1)} collective-permute-done((bf16[2,2,64,256]{3,2,1,0:T(8,128)(2,1)S(1)}, bf16[2,2,64,256]{3,2,1,0:T(8,128)(2,1)S(1)}, u32[]{:S(2)}, u32[]{:S(2)}) %collective-permute-start.17) | collective-permute-done | bytes 131104 | tf_op jit(solution)/shard_map/ppermute | solution.py:313
  43.8 0.0 collective-permute-done.15.refs_7_
  43.8 2.0 %near.3 = (bf16[2,2,256,256]{3,2,1,0:T(8,128)(2,1)S(1)}, f32[2,256,256]{2,1,0:T(8,128)S(1)}, bf16[2,256,256]{2,1,0:T(8,128)(2,1)S(1)}) custom-call(s32[2,2]{1,0:T(2,128)S(1)} %collective-permute-done.4.refs_2_.places, f32[2,2,256,256]{3,2,1,0:T(8,128)S(1)} %start.1, bf16[512,768]{1,0:T(8,128)(2,1)S(1)} %copy-done.2, bf16[768,512]{1,0:T(8,128)(2,1)S(1)} %copy-done.3, ...), custom_call_target="tpu_custom_call" | custom-call | flops 1073741824 | bytes 4194304 | tf_op jit(solution)/shard_map/near/pallas_call | solution.py:380
  45.8 0.1 collective-permute-start.19
  45.9 4.4 %near.2 = (bf16[2,2,256,256]{3,2,1,0:T(8,128)(2,1)S(1)}, f32[2,256,256]{2,1,0:T(8,128)S(1)}, bf16[2,256,256]{2,1,0:T(8,128)(2,1)S(1)}) custom-call(s32[2,2]{1,0:T(2,128)S(1)} %collective-permute-done.4.refs_2_.places, f32[2,2,256,256]{3,2,1,0:T(8,128)S(1)} %start.1, bf16[512,768]{1,0:T(8,128)(2,1)S(1)} %copy-done.2, bf16[768,512]{1,0:T(8,128)(2,1)S(1)} %copy-done.3, ...), custom_call_target="tpu_custom_call" | custom-call | flops 1073741824 | bytes 4194304 | tf_op jit(solution)/shard_map/near/pallas_call | solution.py:380
  50.3 2.1 %collective-permute-start.18 = (bf16[2,256,256]{2,1,0:T(8,128)(2,1)S(1)}, bf16[2,256,256]{2,1,0:T(8,128)(2,1)S(1)}, u32[]{:S(2)}, u32[]{:S(2)}) collective-permute-start(bf16[2,256,256]{2,1,0:T(8,128)(2,1)S(1)} %get-tuple-element.138), channel_id=1, source_target_pairs={{0,16},{1,17},{2,18},{3,19},{4,20},{5,21},{6,22},{7,23},{8,24},{9,... | collective-permute-start | bytes 786440 | tf_op jit(solution)/shard_map/ppermute | solution.py:313
  52.4 2.7 %collective-permute-done.19.arrived = bf16[2,256,256]{2,1,0:T(8,128)(2,1)S(1)} collective-permute-done((bf16[2,256,256]{2,1,0:T(8,128)(2,1)S(1)}, bf16[2,256,256]{2,1,0:T(8,128)(2,1)S(1)}, u32[]{:S(2)}, u32[]{:S(2)}) %collective-permute-start.19) | collective-permute-done | bytes 262176 | tf_op jit(solution)/shard_map/ppermute | solution.py:313
  55.0 3.9 %far.3 = (bf16[2,256,256]{2,1,0:T(8,128)(2,1)S(1)}, bf16[2,256,256]{2,1,0:T(8,128)(2,1)S(1)}, f32[2,256,256]{2,1,0:T(8,128)S(1)}) custom-call(f32[2,2,256,256]{3,2,1,0:T(8,128)S(1)} %start.1, bf16[512,768]{1,0:T(8,128)(2,1)S(1)} %copy-done.2, bf16[768,512]{1,0:T(8,128)(2,1)S(1)} %copy-done.3, bf16[2,2,256,256]{3,2,1,0:T(8,128)(2,1)S(1)} %get-tuple-element.140.frames, ...), custom_call_target="tpu_custom_call" | custom-call | flops 2147483648 | bytes 4194304 | tf_op jit(solution)/shard_map/far/pallas_call | solution.py:390
  59.0 0.1 collective-permute-start.21
  59.1 0.8 collective-permute-done.18.arrived
  59.8 1.5 %far.2 = (bf16[2,256,256]{2,1,0:T(8,128)(2,1)S(1)}, bf16[2,256,256]{2,1,0:T(8,128)(2,1)S(1)}, f32[2,256,256]{2,1,0:T(8,128)S(1)}) custom-call(f32[2,2,256,256]{3,2,1,0:T(8,128)S(1)} %start.1, bf16[512,768]{1,0:T(8,128)(2,1)S(1)} %copy-done.2, bf16[768,512]{1,0:T(8,128)(2,1)S(1)} %copy-done.3, bf16[2,2,256,256]{3,2,1,0:T(8,128)(2,1)S(1)} %get-tuple-element.136.frames, ...), custom_call_target="tpu_custom_call" | custom-call | flops 2147483648 | bytes 4194304 | tf_op jit(solution)/shard_map/far/pallas_call | solution.py:390
  61.4 0.1 collective-permute-start.20
  61.5 1.1 %probe.3 = (f32[2,64,256]{2,1,0:T(8,128)S(1)}, f32[2,64,256]{2,1,0:T(8,128)S(1)}, bf16[2,2,64,256]{3,2,1,0:T(8,128)(2,1)S(1)}) custom-call(s32[2,2]{1,0:T(2,128)S(1)} %collective-permute-done.4.refs_2_.places, f32[2,256,256]{2,1,0:T(8,128)S(1)} %get-tuple-element.139.refs_0_, f32[2,256,256]{2,1,0:T(8,128)S(1)} %get-tuple-element.143.refs_1_), custom_call_target="tpu_custom_call" | custom-call | flops 67108864 | bytes 4194304 | tf_op jit(solution)/shard_map/probe/pallas_call | solution.py:410
  62.5 0.6 collective-permute-start.22
  63.1 0.0 collective-permute-done.21.refs_3_
  63.1 0.0 collective-permute-done.20.refs_2_
  63.1 0.7 part.1
  63.8 3.6 %collective-permute-start.23 = (bf16[2,2,2,64,256]{4,3,2,1,0:T(8,128)(2,1)S(1)}, bf16[2,2,2,64,256]{4,3,2,1,0:T(8,128)(2,1)S(1)}, u32[]{:S(2)}, u32[]{:S(2)}) collective-permute-start(bf16[2,2,2,64,256]{4,3,2,1,0:T(8,128)(2,1)S(1)} %get-tuple-element.154), channel_id=1, source_target_pairs={{0,6},{1,7},{2,0},{3,1},{4,2},{5,3},{6,4},{7,5},{8,14},{9,15},{10,... | collective-permute-start | bytes 786440 | tf_op jit(solution)/shard_map/ppermute | solution.py:313
  67.3 0.0 collective-permute-start.24
  67.3 2.0 %collective-permute-start.25 = (bf16[2,2,2,64,256]{4,3,2,1,0:T(8,128)(2,1)S(1)}, bf16[2,2,2,64,256]{4,3,2,1,0:T(8,128)(2,1)S(1)}, u32[]{:S(2)}, u32[]{:S(2)}) collective-permute-start(bf16[2,2,2,64,256]{4,3,2,1,0:T(8,128)(2,1)S(1)} %get-tuple-element.156), channel_id=1, source_target_pairs={{0,1},{1,2},{2,3},{3,4},{4,5},{5,6},{6,7},{7,0},{8,9},{9,10},{10,1... | collective-permute-start | bytes 786440 | tf_op jit(solution)/shard_map/ppermute | solution.py:313
  69.4 0.0 collective-permute-done.22
  69.4 17.4 %while.14 = (s32[]{:T(128)}, f32[2,64,256]{2,1,0:T(8,128)S(1)}, f32[2,64,256]{2,1,0:T(8,128)S(1)}, s32[]{:T(128)}, pred[]{:T(512)}, /*index=5*/bf16[2,2,64,256]{3,2,1,0:T(8,128)(2,1)S(1)}, s32[]{:T(128)}) while((s32[]{:T(128)}, f32[2,64,256]{2,1,0:T(8,128)S(1)}, f32[2,64,256]{2,1,0:T(8,128)S(1)}, s32[]{:T(128)}, pred[]{:T(512)}, ...), condition=%wide.region_1.2_spmd, body=%wide.region_0.1_spmd.sunk | while | flops 458754 | bytes 1966278 | solution.py:438
  69.4 2.6 %collective-permute-start = (bf16[2,64,256]{2,1,0:T(8,128)(2,1)S(1)}, bf16[2,64,256]{2,1,0:T(8,128)(2,1)S(1)}, u32[]{:S(2)}, u32[]{:S(2)}) collective-permute-start(bf16[2,64,256]{2,1,0:T(8,128)(2,1)S(1)} %fusion.5), channel_id=1, source_target_pairs={{0,16},{1,17},{2,18},{3,19},{4,20},{5,21},{6,22},{7,23},{8,24},{9,... | collective-permute-start | bytes 196616 | tf_op jit(solution)/shard_map/while/body/ppermute | solution.py:313
  72.0 1.9 %collective-permute-done = bf16[2,64,256]{2,1,0:T(8,128)(2,1)S(1)} collective-permute-done((bf16[2,64,256]{2,1,0:T(8,128)(2,1)S(1)}, bf16[2,64,256]{2,1,0:T(8,128)(2,1)S(1)}, u32[]{:S(2)}, u32[]{:S(2)}) %collective-permute-start) | collective-permute-done | bytes 65568 | tf_op jit(solution)/shard_map/while/body/ppermute | solution.py:313
  73.9 0.1 collective-permute-start.1
  74.0 8.4 %collective-permute-done.1 = bf16[2,64,256]{2,1,0:T(8,128)(2,1)S(1)} collective-permute-done((bf16[2,64,256]{2,1,0:T(8,128)(2,1)S(1)}, bf16[2,64,256]{2,1,0:T(8,128)(2,1)S(1)}, u32[]{:S(2)}, u32[]{:S(2)}) %collective-permute-start.1) | collective-permute-done | bytes 65568 | tf_op jit(solution)/shard_map/while/body/ppermute | solution.py:423
  82.4 0.1 collective-permute-start.2
  82.5 4.3 %collective-permute-done.2 = bf16[2,64,256]{2,1,0:T(8,128)(2,1)S(1)} collective-permute-done((bf16[2,64,256]{2,1,0:T(8,128)(2,1)S(1)}, bf16[2,64,256]{2,1,0:T(8,128)(2,1)S(1)}, u32[]{:S(2)}, u32[]{:S(2)}) %collective-permute-start.2) | collective-permute-done | bytes 65568 | tf_op jit(solution)/shard_map/while/body/ppermute | solution.py:423
  86.8 0.0 collective-permute-done.23.refs_5_
  86.8 0.0 collective-permute-done.24.refs_6_
  86.8 0.0 collective-permute-done.26.refs_9_
  86.8 1.2 %collective-permute-start.27 = (bf16[2,64,256]{2,1,0:T(8,128)(2,1)S(1)}, bf16[2,64,256]{2,1,0:T(8,128)(2,1)S(1)}, u32[]{:S(2)}, u32[]{:S(2)}) collective-permute-start(bf16[2,64,256]{2,1,0:T(8,128)(2,1)S(1)} %convert_element_type.65), channel_id=1, source_target_pairs={{0,4},{1,5},{2,6},{3,7},{4,0},{5,1},{6,2},{7,3},{8,12},{9,13},{10,... | collective-permute-start | bytes 196616 | tf_op jit(solution)/shard_map/ppermute | solution.py:423
  88.1 2.7 %deposit.1 = f32[2,64,3072]{2,1,0:T(8,128)} custom-call(s32[2,2]{1,0:T(2,128)S(1)} %multiply_add_fusion.refs_0_, s32[2,2]{1,0:T(2,128)S(1)} %collective-permute-done.3.refs_1_, s32[2,2]{1,0:T(2,128)S(1)} %collective-permute-done.4.refs_2_.places, s32[2,2]{1,0:T(2,128)S(1)} %collective-permute-done.5.refs_0_.refs_3_, ...), custom_call_target="tpu_custom_call" | custom-call | flops 67108864 | bytes 4194304 | tf_op jit(solution)/shard_map/deposit/pallas_call | solution.py:443
  90.7 1.4 %collective-permute-done.27 = bf16[2,64,256]{2,1,0:T(8,128)(2,1)S(1)} collective-permute-done((bf16[2,64,256]{2,1,0:T(8,128)(2,1)S(1)}, bf16[2,64,256]{2,1,0:T(8,128)(2,1)S(1)}, u32[]{:S(2)}, u32[]{:S(2)}) %collective-permute-start.27) | collective-permute-done | bytes 65568 | tf_op jit(solution)/shard_map/ppermute | solution.py:423
  92.1 0.7 convert_add_fusion.3
  (23 shorter events, 0.1 us)
Async XLA Ops:
  0.6 5.1 %copy-start.5 = (s32[2,2]{1,0:T(2,128)S(1)}, s32[2,2]{1,0:T(2,128)}, u32[]{:S(2)}) copy-start(s32[2,2]{1,0:T(2,128)} %param.12) | copy-start | bytes 52
  0.6 5.1 %copy-start.4 = (s32[2,2]{1,0:T(2,128)S(1)}, s32[2,2]{1,0:T(2,128)}, u32[]{:S(2)}) copy-start(s32[2,2]{1,0:T(2,128)} %param.13) | copy-start | bytes 52
  0.7 14.6 %copy-start = (f32[1,2,64,3072]{3,2,1,0:T(8,128)S(1)}, f32[1,2,64,3072]{3,2,1,0:T(8,128)}, u32[]{:S(2)}) copy-start(f32[1,2,64,3072]{3,2,1,0:T(8,128)} %param.9) | copy-start | bytes 4718596
  2.6 13.6 %collective-permute-start.7 = (bf16[2,256,256]{2,1,0:T(8,128)(2,1)}, bf16[2,256,256]{2,1,0:T(8,128)(2,1)S(1)}, u32[]{:S(2)}, u32[]{:S(2)}) collective-permute-start(bf16[2,256,256]{2,1,0:T(8,128)(2,1)} %pick.1), channel_id=1, source_target_pairs={{0,2},{1,3},{2,4},{3,5},{4,6},{5,7},{6,0},{7,1},{8,10},{9,11},{10,... | collective-permute-start | bytes 786440 | tf_op jit(solution)/shard_map/ppermute | solution.py:303
  5.7 8.6 %collective-permute-start.4 = (s32[2,2]{1,0:T(2,128)S(1)}, s32[2,2]{1,0:T(2,128)S(1)}, u32[]{:S(2)}, u32[]{:S(2)}) collective-permute-start(s32[2,2]{1,0:T(2,128)S(1)} %multiply_add_fusion.refs_0_), channel_id=1, source_target_pairs={{0,2},{1,3},{2,4},{3,5},{4,6},{5,7},{6,0},{7,1},{8,10},{9,11},{10,... | collective-permute-start | bytes 56 | tf_op jit(solution)/shard_map/ppermute | solution.py:303
  7.4 7.9 %collective-permute-start.3 = (s32[2,2]{1,0:T(2,128)S(1)}, s32[2,2]{1,0:T(2,128)S(1)}, u32[]{:S(2)}, u32[]{:S(2)}) collective-permute-start(s32[2,2]{1,0:T(2,128)S(1)} %multiply_add_fusion.refs_0_), channel_id=1, source_target_pairs={{0,1},{1,2},{2,3},{3,4},{4,5},{5,6},{6,7},{7,0},{8,9},{9,10},{10,1... | collective-permute-start | bytes 56 | tf_op jit(solution)/shard_map/ppermute | solution.py:303
  15.3 22.6 %copy-start.1 = (f32[2,256,256]{2,1,0:T(8,128)S(1)}, f32[2,256,256]{2,1,0:T(8,128)}, u32[]{:S(2)}) copy-start(f32[2,256,256]{2,1,0:T(8,128)} %probe.2) | copy-start | bytes 1572868
  15.3 22.6 %copy-start.2 = (bf16[512,768]{1,0:T(8,128)(2,1)S(1)}, bf16[512,768]{1,0:T(8,128)(2,1)}, u32[]{:S(2)}) copy-start(bf16[512,768]{1,0:T(8,128)(2,1)} %constant.46.clone.refs_2_.left) | copy-start | bytes 2359300
  15.3 22.7 %copy-start.3 = (bf16[768,512]{1,0:T(8,128)(2,1)S(1)}, bf16[768,512]{1,0:T(8,128)(2,1)}, u32[]{:S(2)}) copy-start(bf16[768,512]{1,0:T(8,128)(2,1)} %constant.47.clone.refs_3_.right) | copy-start | bytes 2359300
  16.2 21.7 %collective-permute-start.8 = (bf16[2,256,256]{2,1,0:T(8,128)(2,1)S(1)}, bf16[2,256,256]{2,1,0:T(8,128)(2,1)S(1)}, u32[]{:S(2)}, u32[]{:S(2)}) collective-permute-start(bf16[2,256,256]{2,1,0:T(8,128)(2,1)S(1)} %collective-permute-done.7.refs_0_), channel_id=1, source_target_pairs={{0,16},{1,17},{2,18},{3,19},{4,20},{5,21},{6,22},{7,23},{8,24},{9,... | collective-permute-start | bytes 786440 | tf_op jit(solution)/shard_map/ppermute | solution.py:313
  19.6 7.7 %collective-permute-start.9 = (bf16[2,2,64,256]{3,2,1,0:T(8,128)(2,1)S(1)}, bf16[2,2,64,256]{3,2,1,0:T(8,128)(2,1)S(1)}, u32[]{:S(2)}, u32[]{:S(2)}) collective-permute-start(bf16[2,2,64,256]{3,2,1,0:T(8,128)(2,1)S(1)} %get-tuple-element.125), channel_id=1, source_target_pairs={{0,2},{1,3},{2,4},{3,5},{4,6},{5,7},{6,0},{7,1},{8,10},{9,11},{10,... | collective-permute-start | bytes 393224 | tf_op jit(solution)/shard_map/ppermute | solution.py:313
  19.7 5.5 %collective-permute-start.5 = (s32[2,2]{1,0:T(2,128)S(1)}, s32[2,2]{1,0:T(2,128)S(1)}, u32[]{:S(2)}, u32[]{:S(2)}) collective-permute-start(s32[2,2]{1,0:T(2,128)S(1)} %multiply_add_fusion.refs_0_), channel_id=1, source_target_pairs={{0,3},{1,4},{2,5},{3,6},{4,7},{5,0},{6,1},{7,2},{8,11},{9,12},{10,... | collective-permute-start | bytes 56 | tf_op jit(solution)/shard_map/ppermute | solution.py:303
  21.0 4.7 %collective-permute-start.6 = (s32[2,2]{1,0:T(2,128)S(1)}, s32[2,2]{1,0:T(2,128)S(1)}, u32[]{:S(2)}, u32[]{:S(2)}) collective-permute-start(s32[2,2]{1,0:T(2,128)S(1)} %multiply_add_fusion.refs_0_), channel_id=1, source_target_pairs={{0,4},{1,5},{2,6},{3,7},{4,0},{5,1},{6,2},{7,3},{8,12},{9,13},{10,... | collective-permute-start | bytes 56 | tf_op jit(solution)/shard_map/ppermute | solution.py:303
  24.1 8.3 %collective-permute-start.10 = (bf16[2,2,64,256]{3,2,1,0:T(8,128)(2,1)S(1)}, bf16[2,2,64,256]{3,2,1,0:T(8,128)(2,1)S(1)}, u32[]{:S(2)}, u32[]{:S(2)}) collective-permute-start(bf16[2,2,64,256]{3,2,1,0:T(8,128)(2,1)S(1)} %get-tuple-element.127), channel_id=1, source_target_pairs={{0,1},{1,2},{2,3},{3,4},{4,5},{5,6},{6,7},{7,0},{8,9},{9,10},{10,1... | collective-permute-start | bytes 393224 | tf_op jit(solution)/shard_map/ppermute | solution.py:313
  25.2 7.3 %collective-permute-start.13 = (bf16[2,2,64,256]{3,2,1,0:T(8,128)(2,1)S(1)}, bf16[2,2,64,256]{3,2,1,0:T(8,128)(2,1)S(1)}, u32[]{:S(2)}, u32[]{:S(2)}) collective-permute-start(bf16[2,2,64,256]{3,2,1,0:T(8,128)(2,1)S(1)} %get-tuple-element.131), channel_id=1, source_target_pairs={{0,10},{1,11},{2,12},{3,13},{4,14},{5,15},{6,8},{7,9},{8,2},{9,3},... | collective-permute-start | bytes 393224 | tf_op jit(solution)/shard_map/ppermute | solution.py:313
  25.8 12.1 %collective-permute-start.14 = (bf16[2,2,64,256]{3,2,1,0:T(8,128)(2,1)S(1)}, bf16[2,2,64,256]{3,2,1,0:T(8,128)(2,1)S(1)}, u32[]{:S(2)}, u32[]{:S(2)}) collective-permute-start(bf16[2,2,64,256]{3,2,1,0:T(8,128)(2,1)S(1)} %get-tuple-element.132), channel_id=1, source_target_pairs={{0,9},{1,10},{2,11},{3,12},{4,13},{5,14},{6,15},{7,8},{8,1},{9,2},... | collective-permute-start | bytes 393224 | tf_op jit(solution)/shard_map/ppermute | solution.py:313
  27.4 11.7 %collective-permute-start.11 = (bf16[2,2,64,256]{3,2,1,0:T(8,128)(2,1)S(1)}, bf16[2,2,64,256]{3,2,1,0:T(8,128)(2,1)S(1)}, u32[]{:S(2)}, u32[]{:S(2)}) collective-permute-start(bf16[2,2,64,256]{3,2,1,0:T(8,128)(2,1)S(1)} %get-tuple-element.129), channel_id=1, source_target_pairs={{0,7},{1,0},{2,1},{3,2},{4,3},{5,4},{6,5},{7,6},{8,15},{9,8},{10,9... | collective-permute-start | bytes 393224 | tf_op jit(solution)/shard_map/ppermute | solution.py:313
  32.4 6.7 %collective-permute-start.12 = (bf16[2,2,64,256]{3,2,1,0:T(8,128)(2,1)S(1)}, bf16[2,2,64,256]{3,2,1,0:T(8,128)(2,1)S(1)}, u32[]{:S(2)}, u32[]{:S(2)}) collective-permute-start(bf16[2,2,64,256]{3,2,1,0:T(8,128)(2,1)S(1)} %get-tuple-element.130), channel_id=1, source_target_pairs={{0,6},{1,7},{2,0},{3,1},{4,2},{5,3},{6,4},{7,5},{8,14},{9,15},{10,... | collective-permute-start | bytes 393224 | tf_op jit(solution)/shard_map/ppermute | solution.py:313
  32.6 9.4 %collective-permute-start.16 = (bf16[2,2,64,256]{3,2,1,0:T(8,128)(2,1)S(1)}, bf16[2,2,64,256]{3,2,1,0:T(8,128)(2,1)S(1)}, u32[]{:S(2)}, u32[]{:S(2)}) collective-permute-start(bf16[2,2,64,256]{3,2,1,0:T(8,128)(2,1)S(1)} %get-tuple-element.134), channel_id=1, source_target_pairs={{0,15},{1,8},{2,9},{3,10},{4,11},{5,12},{6,13},{7,14},{8,7},{9,0},... | collective-permute-start | bytes 393224 | tf_op jit(solution)/shard_map/ppermute | solution.py:313
  37.9 6.0 %collective-permute-start.17 = (bf16[2,2,64,256]{3,2,1,0:T(8,128)(2,1)S(1)}, bf16[2,2,64,256]{3,2,1,0:T(8,128)(2,1)S(1)}, u32[]{:S(2)}, u32[]{:S(2)}) collective-permute-start(bf16[2,2,64,256]{3,2,1,0:T(8,128)(2,1)S(1)} %get-tuple-element.135), channel_id=1, source_target_pairs={{0,14},{1,15},{2,8},{3,9},{4,10},{5,11},{6,12},{7,13},{8,6},{9,7},... | collective-permute-start | bytes 393224 | tf_op jit(solution)/shard_map/ppermute | solution.py:313
  37.9 6.0 %collective-permute-start.15 = (bf16[2,2,64,256]{3,2,1,0:T(8,128)(2,1)S(1)}, bf16[2,2,64,256]{3,2,1,0:T(8,128)(2,1)S(1)}, u32[]{:S(2)}, u32[]{:S(2)}) collective-permute-start(bf16[2,2,64,256]{3,2,1,0:T(8,128)(2,1)S(1)} %get-tuple-element.133), channel_id=1, source_target_pairs={{0,8},{1,9},{2,10},{3,11},{4,12},{5,13},{6,14},{7,15},{8,0},{9,1},... | collective-permute-start | bytes 393224 | tf_op jit(solution)/shard_map/ppermute | solution.py:313
  45.8 9.2 %collective-permute-start.19 = (bf16[2,256,256]{2,1,0:T(8,128)(2,1)S(1)}, bf16[2,256,256]{2,1,0:T(8,128)(2,1)S(1)}, u32[]{:S(2)}, u32[]{:S(2)}) collective-permute-start(bf16[2,256,256]{2,1,0:T(8,128)(2,1)S(1)} %get-tuple-element.142), channel_id=1, source_target_pairs={{0,16},{1,17},{2,18},{3,19},{4,20},{5,21},{6,22},{7,23},{8,24},{9,... | collective-permute-start | bytes 786440 | tf_op jit(solution)/shard_map/ppermute | solution.py:313
  50.3 9.6 %collective-permute-start.18 = (bf16[2,256,256]{2,1,0:T(8,128)(2,1)S(1)}, bf16[2,256,256]{2,1,0:T(8,128)(2,1)S(1)}, u32[]{:S(2)}, u32[]{:S(2)}) collective-permute-start(bf16[2,256,256]{2,1,0:T(8,128)(2,1)S(1)} %get-tuple-element.138), channel_id=1, source_target_pairs={{0,16},{1,17},{2,18},{3,19},{4,20},{5,21},{6,22},{7,23},{8,24},{9,... | collective-permute-start | bytes 786440 | tf_op jit(solution)/shard_map/ppermute | solution.py:313
  59.0 4.1 %collective-permute-start.21 = (bf16[2,256,256]{2,1,0:T(8,128)(2,1)S(1)}, bf16[2,256,256]{2,1,0:T(8,128)(2,1)S(1)}, u32[]{:S(2)}, u32[]{:S(2)}) collective-permute-start(bf16[2,256,256]{2,1,0:T(8,128)(2,1)S(1)} %get-tuple-element.148), channel_id=1, source_target_pairs={{0,8},{1,9},{2,10},{3,11},{4,12},{5,13},{6,14},{7,15},{8,0},{9,1},... | collective-permute-start | bytes 786440 | tf_op jit(solution)/shard_map/ppermute | solution.py:313
  61.4 1.7 %collective-permute-start.20 = (bf16[2,256,256]{2,1,0:T(8,128)(2,1)S(1)}, bf16[2,256,256]{2,1,0:T(8,128)(2,1)S(1)}, u32[]{:S(2)}, u32[]{:S(2)}) collective-permute-start(bf16[2,256,256]{2,1,0:T(8,128)(2,1)S(1)} %get-tuple-element.147), channel_id=1, source_target_pairs={{0,8},{1,9},{2,10},{3,11},{4,12},{5,13},{6,14},{7,15},{8,0},{9,1},... | collective-permute-start | bytes 786440 | tf_op jit(solution)/shard_map/ppermute | solution.py:313
  62.5 6.9 %collective-permute-start.22 = (bf16[2,2,64,256]{3,2,1,0:T(8,128)(2,1)S(1)}, bf16[2,2,64,256]{3,2,1,0:T(8,128)(2,1)S(1)}, u32[]{:S(2)}, u32[]{:S(2)}) collective-permute-start(bf16[2,2,64,256]{3,2,1,0:T(8,128)(2,1)S(1)} %get-tuple-element.152), channel_id=1, source_target_pairs={{0,8},{1,9},{2,10},{3,11},{4,12},{5,13},{6,14},{7,15},{8,0},{9,1},... | collective-permute-start | bytes 393224 | tf_op jit(solution)/shard_map/ppermute | solution.py:313
  63.8 23.0 %collective-permute-start.23 = (bf16[2,2,2,64,256]{4,3,2,1,0:T(8,128)(2,1)S(1)}, bf16[2,2,2,64,256]{4,3,2,1,0:T(8,128)(2,1)S(1)}, u32[]{:S(2)}, u32[]{:S(2)}) collective-permute-start(bf16[2,2,2,64,256]{4,3,2,1,0:T(8,128)(2,1)S(1)} %get-tuple-element.154), channel_id=1, source_target_pairs={{0,6},{1,7},{2,0},{3,1},{4,2},{5,3},{6,4},{7,5},{8,14},{9,15},{10,... | collective-permute-start | bytes 786440 | tf_op jit(solution)/shard_map/ppermute | solution.py:313
  67.3 19.5 %collective-permute-start.24 = (bf16[2,2,2,64,256]{4,3,2,1,0:T(8,128)(2,1)S(1)}, bf16[2,2,2,64,256]{4,3,2,1,0:T(8,128)(2,1)S(1)}, u32[]{:S(2)}, u32[]{:S(2)}) collective-permute-start(bf16[2,2,2,64,256]{4,3,2,1,0:T(8,128)(2,1)S(1)} %get-tuple-element.155), channel_id=1, source_target_pairs={{0,7},{1,0},{2,1},{3,2},{4,3},{5,4},{6,5},{7,6},{8,15},{9,8},{10,9... | collective-permute-start | bytes 786440 | tf_op jit(solution)/shard_map/ppermute | solution.py:313
  67.3 19.5 %collective-permute-start.25 = (bf16[2,2,2,64,256]{4,3,2,1,0:T(8,128)(2,1)S(1)}, bf16[2,2,2,64,256]{4,3,2,1,0:T(8,128)(2,1)S(1)}, u32[]{:S(2)}, u32[]{:S(2)}) collective-permute-start(bf16[2,2,2,64,256]{4,3,2,1,0:T(8,128)(2,1)S(1)} %get-tuple-element.156), channel_id=1, source_target_pairs={{0,1},{1,2},{2,3},{3,4},{4,5},{5,6},{6,7},{7,0},{8,9},{9,10},{10,1... | collective-permute-start | bytes 786440 | tf_op jit(solution)/shard_map/ppermute | solution.py:313
  69.4 17.5 %collective-permute-start.26 = (bf16[2,2,2,64,256]{4,3,2,1,0:T(8,128)(2,1)S(1)}, bf16[2,2,2,64,256]{4,3,2,1,0:T(8,128)(2,1)S(1)}, u32[]{:S(2)}, u32[]{:S(2)}) collective-permute-start(bf16[2,2,2,64,256]{4,3,2,1,0:T(8,128)(2,1)S(1)} %get-tuple-element.157), channel_id=1, source_target_pairs={{0,2},{1,3},{2,4},{3,5},{4,6},{5,7},{6,0},{7,1},{8,10},{9,11},{10,... | collective-permute-start | bytes 786440 | tf_op jit(solution)/shard_map/ppermute | solution.py:313
  69.4 4.5 %collective-permute-start = (bf16[2,64,256]{2,1,0:T(8,128)(2,1)S(1)}, bf16[2,64,256]{2,1,0:T(8,128)(2,1)S(1)}, u32[]{:S(2)}, u32[]{:S(2)}) collective-permute-start(bf16[2,64,256]{2,1,0:T(8,128)(2,1)S(1)} %fusion.5), channel_id=1, source_target_pairs={{0,16},{1,17},{2,18},{3,19},{4,20},{5,21},{6,22},{7,23},{8,24},{9,... | collective-permute-start | bytes 196616 | tf_op jit(solution)/shard_map/while/body/ppermute | solution.py:313
  73.9 8.5 %collective-permute-start.1 = (bf16[2,64,256]{2,1,0:T(8,128)(2,1)S(1)}, bf16[2,64,256]{2,1,0:T(8,128)(2,1)S(1)}, u32[]{:S(2)}, u32[]{:S(2)}) collective-permute-start(bf16[2,64,256]{2,1,0:T(8,128)(2,1)S(1)} %get-tuple-element.218), channel_id=1, source_target_pairs={{0,1},{1,0},{2,3},{3,2},{4,5},{5,4},{6,7},{7,6},{8,9},{9,8},{10,11... | collective-permute-start | bytes 196616 | tf_op jit(solution)/shard_map/while/body/ppermute | solution.py:423
  82.4 4.3 %collective-permute-start.2 = (bf16[2,64,256]{2,1,0:T(8,128)(2,1)S(1)}, bf16[2,64,256]{2,1,0:T(8,128)(2,1)S(1)}, u32[]{:S(2)}, u32[]{:S(2)}) collective-permute-start(bf16[2,64,256]{2,1,0:T(8,128)(2,1)S(1)} %add_convert_fusion.2), channel_id=1, source_target_pairs={{0,2},{1,3},{2,0},{3,1},{4,6},{5,7},{6,4},{7,5},{8,10},{9,11},{10,... | collective-permute-start | bytes 196616 | tf_op jit(solution)/shard_map/while/body/ppermute | solution.py:423
  86.8 5.3 %collective-permute-start.27 = (bf16[2,64,256]{2,1,0:T(8,128)(2,1)S(1)}, bf16[2,64,256]{2,1,0:T(8,128)(2,1)S(1)}, u32[]{:S(2)}, u32[]{:S(2)}) collective-permute-start(bf16[2,64,256]{2,1,0:T(8,128)(2,1)S(1)} %convert_element_type.65), channel_id=1, source_target_pairs={{0,4},{1,5},{2,6},{3,7},{4,0},{5,1},{6,2},{7,3},{8,12},{9,13},{10,... | collective-permute-start | bytes 196616 | tf_op jit(solution)/shard_map/ppermute | solution.py:423

commit v6 on v4

--- a/solution.py
+++ b/solution.py
@@ -256,14 +256,15 @@
             sent[index, plane] = total[plane, pl.ds(other, height)].astype(bf16)
 
 
-def deposit_kernel(reach, *refs):
+def deposit_kernel(steps, *refs):
+    reach = len(steps)
     places, pieces, out = refs[:reach], refs[reach:-1], refs[-1]
     _, count, _, strip, side = pieces[0].shape
     width = out.shape[2]
     core, _ = this_place()
     lane = lax.broadcasted_iota(jnp.int32, (strip, LANES), 1)
     out[...] = jnp.zeros(out.shape, f32)
-    for step, piece in enumerate(pieces):
+    for step, piece in zip(steps, pieces):
         for flip in range(2):
             for turn in range(count):
                 column = column_of(places[step], width, core ^ flip, turn)
@@ -421,19 +422,21 @@
     once = lax.axis_index("depth") // depth + 1
     assert regions & (regions - 1) == 0
     spans = [1 << level for level in range(regions.bit_length() - 1)]
+    spans = spans[-1:] + spans[:-1]
     near, parts[home] = lax.optimization_barrier((near, parts[home]))
     probe_grad, *_ = lax.fori_loop(
         0, once, probe_rounds, (near, away, across(probe_sent, 1, 0))
     )
     probe_grad, returned = lax.optimization_barrier((probe_grad, returned))
     probe_grad = scan_round(probe_grad, spans[-1])
+    far_steps = sorted(range(reach), key=lambda step: -abs(step - home))
     object_grad = call(
-        functools.partial(deposit_kernel, reach),
+        functools.partial(deposit_kernel, far_steps),
         shape(transmission.shape[1:], f32),
         [smem] * reach + [vmem] * reach,
         1 << 26,
         "deposit",
-    )(*places, *returned)
+    )(*places, *(returned[step] for step in far_steps))
     return object_grad[None], probe_grad
 
 

time: 88.7 us -> 92.6 us (1.044)
  waiting for transfers between devices: 27.7 us -> 31.6 us
    ppermute x3, waiting for transfers between devices: 12.8 us -> 16.7 us  [scan_round(): lax.ppermute(rounded, 'scan', route).astype(f32)]
  transfers between devices with their start and end apart: 28 -> 28, of which waited for: 12 -> 12; matrix products, arithmetic and copies ran while one was open for 0% -> 0% of each run, Pallas kernels for 19% -> 18%
where the time goes in v6:
time: 92.6 us; the launch traced here: 92.3 us
  starting transfers between devices  37.6 us (41%)
  waiting for transfers between devices  31.6 us (34%)
  Pallas kernels  20.3 us (22%)
  local copies, waits for them, and re-layouts  1.16 us (1%)
    ppermute x20, starting transfers between devices, across(): return lax.ppermute(value, ('depth', 'scan'), route)  24.9 us
    ppermute x3, waiting for transfers between devices, scan_round(): lax.ppermute(rounded, 'scan', route).astype(f32)  16.7 us
    ppermute x20, waiting for transfers between devices, across(): return lax.ppermute(value, ('depth', 'scan'), route)  12.2 us
    ppermute x5, starting transfers between devices, along_scan(): lax.ppermute(value, 'scan', [(i, (i + by) % regions) for i in range(regio...  9.99 us
    pallas_call x2, Pallas kernels, local(): call(functools.partial(near_kernel, home, turn, turn == count - 1, width)...  6.36 us
    pallas_call x2, Pallas kernels, local(): call(functools.partial(far_kernel, turn, turn == count - 1), [shape(wave,...  5.47 us
    ppermute x3, starting transfers between devices, scan_round(): lax.ppermute(rounded, 'scan', route).astype(f32)  2.73 us
    pallas_call x1, Pallas kernels, local(): call(functools.partial(deposit_kernel, far_steps), shape(transmission.sha...  2.68 us
  transfers between devices with their start and end apart: 28, of which 12 were waited for; matrix products, arithmetic and copies ran while one was open for 0% of the time, Pallas kernels for 18%

profile of v6, /device:TPU:0, one launch (start us, length us, event | category | flops | bytes accessed | tf_op | source)
XLA Modules:
  0.0 92.3 jit_solution(6065110210916458273)
XLA Ops:
  0.7 1.9 %pick.1 = bf16[2,256,256]{2,1,0:T(8,128)(2,1)} custom-call(f32[2,2,2,256,256]{4,3,2,1,0:T(8,128)} %waves.1), custom_call_target="tpu_custom_call" | custom-call | flops 1048576 | bytes 4194304 | tf_op jit(solution)/shard_map/pick/pallas_call | solution.py:328
  2.6 0.0 copy-start.1
  2.6 0.0 copy-start.2
  2.6 3.1 %collective-permute-start.7 = (bf16[2,256,256]{2,1,0:T(8,128)(2,1)}, bf16[2,256,256]{2,1,0:T(8,128)(2,1)S(1)}, u32[]{:S(2)}, u32[]{:S(2)}) collective-permute-start(bf16[2,256,256]{2,1,0:T(8,128)(2,1)} %pick.1), channel_id=1, source_target_pairs={{0,2},{1,3},{2,4},{3,5},{4,6},{5,7},{6,0},{7,1},{8,10},{9,11},{10,... | collective-permute-start | bytes 786440 | tf_op jit(solution)/shard_map/ppermute | solution.py:294
  5.7 1.6 %collective-permute-start.4 = (s32[2,2]{1,0:T(2,128)S(1)}, s32[2,2]{1,0:T(2,128)S(1)}, u32[]{:S(2)}, u32[]{:S(2)}) collective-permute-start(s32[2,2]{1,0:T(2,128)S(1)} %multiply_add_fusion.refs_0_), channel_id=1, source_target_pairs={{0,2},{1,3},{2,4},{3,5},{4,6},{5,7},{6,0},{7,1},{8,10},{9,11},{10,... | collective-permute-start | bytes 56 | tf_op jit(solution)/shard_map/ppermute | solution.py:294
  7.3 1.5 %collective-permute-start.3 = (s32[2,2]{1,0:T(2,128)S(1)}, s32[2,2]{1,0:T(2,128)S(1)}, u32[]{:S(2)}, u32[]{:S(2)}) collective-permute-start(s32[2,2]{1,0:T(2,128)S(1)} %multiply_add_fusion.refs_0_), channel_id=1, source_target_pairs={{0,1},{1,2},{2,3},{3,4},{4,5},{5,6},{6,7},{7,0},{8,9},{9,10},{10,1... | collective-permute-start | bytes 56 | tf_op jit(solution)/shard_map/ppermute | solution.py:294
  8.8 1.0 %collective-permute-start.5 = (s32[2,2]{1,0:T(2,128)S(1)}, s32[2,2]{1,0:T(2,128)S(1)}, u32[]{:S(2)}, u32[]{:S(2)}) collective-permute-start(s32[2,2]{1,0:T(2,128)S(1)} %multiply_add_fusion.refs_0_), channel_id=1, source_target_pairs={{0,3},{1,4},{2,5},{3,6},{4,7},{5,0},{6,1},{7,2},{8,11},{9,12},{10,... | collective-permute-start | bytes 56 | tf_op jit(solution)/shard_map/ppermute | solution.py:294
  9.9 2.7 %collective-permute-start.6 = (s32[2,2]{1,0:T(2,128)S(1)}, s32[2,2]{1,0:T(2,128)S(1)}, u32[]{:S(2)}, u32[]{:S(2)}) collective-permute-start(s32[2,2]{1,0:T(2,128)S(1)} %multiply_add_fusion.refs_0_), channel_id=1, source_target_pairs={{0,4},{1,5},{2,6},{3,7},{4,0},{5,1},{6,2},{7,3},{8,12},{9,13},{10,... | collective-permute-start | bytes 56 | tf_op jit(solution)/shard_map/ppermute | solution.py:294
  12.6 1.7 %collective-permute-done.4.refs_2_.places = s32[2,2]{1,0:T(2,128)S(1)} collective-permute-done((s32[2,2]{1,0:T(2,128)S(1)}, s32[2,2]{1,0:T(2,128)S(1)}, u32[]{:S(2)}, u32[]{:S(2)}) %collective-permute-start.4) | collective-permute-done | bytes 48 | tf_op jit(solution)/shard_map/ppermute | solution.py:294
  14.3 1.0 %collective-permute-done.3.refs_1_ = s32[2,2]{1,0:T(2,128)S(1)} collective-permute-done((s32[2,2]{1,0:T(2,128)S(1)}, s32[2,2]{1,0:T(2,128)S(1)}, u32[]{:S(2)}, u32[]{:S(2)}) %collective-permute-start.3) | collective-permute-done | bytes 48 | tf_op jit(solution)/shard_map/ppermute | solution.py:294
  15.3 0.0 collective-permute-done.5.refs_3_
  15.3 0.0 collective-permute-done.6.refs_4_
  15.3 1.2 %extract.1 = (bf16[2,2,64,256]{3,2,1,0:T(8,128)(2,1)S(1)}, bf16[2,2,64,256]{3,2,1,0:T(8,128)(2,1)S(1)}, bf16[2,2,64,256]{3,2,1,0:T(8,128)(2,1)S(1)}, bf16[2,2,64...) custom-call(s32[2,2]{1,0:T(2,128)S(1)} %multiply_add_fusion.refs_0_,, ...), custom_call_target="tpu_custom_call" | custom-call | flops 67108864 | bytes 4194304 | tf_op jit(solution)/shard_map/extract/pallas_call | solution.py:344
  16.5 3.4 %collective-permute-start.8 = (bf16[2,256,256]{2,1,0:T(8,128)(2,1)S(1)}, bf16[2,256,256]{2,1,0:T(8,128)(2,1)S(1)}, u32[]{:S(2)}, u32[]{:S(2)}) collective-permute-start(bf16[2,256,256]{2,1,0:T(8,128)(2,1)S(1)} %collective-permute-done.7.refs_0_), channel_id=1, source_target_pairs={{0,16},{1,17},{2,18},{3,19},{4,20},{5,21},{6,22},{7,23},{8,24},{9,... | collective-permute-start | bytes 786440 | tf_op jit(solution)/shard_map/ppermute | solution.py:304
  19.9 0.8 collective-permute-start.9
  20.7 1.5 %collective-permute-start.10 = (bf16[2,2,64,256]{3,2,1,0:T(8,128)(2,1)S(1)}, bf16[2,2,64,256]{3,2,1,0:T(8,128)(2,1)S(1)}, u32[]{:S(2)}, u32[]{:S(2)}) collective-permute-start(bf16[2,2,64,256]{3,2,1,0:T(8,128)(2,1)S(1)} %get-tuple-element.127), channel_id=1, source_target_pairs={{0,1},{1,2},{2,3},{3,4},{4,5},{5,6},{6,7},{7,0},{8,9},{9,10},{10,1... | collective-permute-start | bytes 393224 | tf_op jit(solution)/shard_map/ppermute | solution.py:304
  22.2 3.2 %collective-permute-start.11 = (bf16[2,2,64,256]{3,2,1,0:T(8,128)(2,1)S(1)}, bf16[2,2,64,256]{3,2,1,0:T(8,128)(2,1)S(1)}, u32[]{:S(2)}, u32[]{:S(2)}) collective-permute-start(bf16[2,2,64,256]{3,2,1,0:T(8,128)(2,1)S(1)} %get-tuple-element.129), channel_id=1, source_target_pairs={{0,7},{1,0},{2,1},{3,2},{4,3},{5,4},{6,5},{7,6},{8,15},{9,8},{10,9... | collective-permute-start | bytes 393224 | tf_op jit(solution)/shard_map/ppermute | solution.py:304
  25.4 1.2 %collective-permute-start.12 = (bf16[2,2,64,256]{3,2,1,0:T(8,128)(2,1)S(1)}, bf16[2,2,64,256]{3,2,1,0:T(8,128)(2,1)S(1)}, u32[]{:S(2)}, u32[]{:S(2)}) collective-permute-start(bf16[2,2,64,256]{3,2,1,0:T(8,128)(2,1)S(1)} %get-tuple-element.130), channel_id=1, source_target_pairs={{0,6},{1,7},{2,0},{3,1},{4,2},{5,3},{6,4},{7,5},{8,14},{9,15},{10,... | collective-permute-start | bytes 393224 | tf_op jit(solution)/shard_map/ppermute | solution.py:304
  26.7 1.4 %collective-permute-done.9.refs_0_ = bf16[2,2,64,256]{3,2,1,0:T(8,128)(2,1)S(1)} collective-permute-done((bf16[2,2,64,256]{3,2,1,0:T(8,128)(2,1)S(1)}, bf16[2,2,64,256]{3,2,1,0:T(8,128)(2,1)S(1)}, u32[]{:S(2)}, u32[]{:S(2)}) %collective-permute-start.9) | collective-permute-done | bytes 131104 | tf_op jit(solution)/shard_map/ppermute | solution.py:304
  28.1 0.0 collective-permute-start.13
  28.1 2.1 %collective-permute-done.10.refs_1_ = bf16[2,2,64,256]{3,2,1,0:T(8,128)(2,1)S(1)} collective-permute-done((bf16[2,2,64,256]{3,2,1,0:T(8,128)(2,1)S(1)}, bf16[2,2,64,256]{3,2,1,0:T(8,128)(2,1)S(1)}, u32[]{:S(2)}, u32[]{:S(2)}) %collective-permute-start.10) | collective-permute-done | bytes 131104 | tf_op jit(solution)/shard_map/ppermute | solution.py:304
  30.2 4.4 %collective-permute-start.16 = (bf16[2,2,64,256]{3,2,1,0:T(8,128)(2,1)S(1)}, bf16[2,2,64,256]{3,2,1,0:T(8,128)(2,1)S(1)}, u32[]{:S(2)}, u32[]{:S(2)}) collective-permute-start(bf16[2,2,64,256]{3,2,1,0:T(8,128)(2,1)S(1)} %get-tuple-element.134), channel_id=1, source_target_pairs={{0,15},{1,8},{2,9},{3,10},{4,11},{5,12},{6,13},{7,14},{8,7},{9,0},... | collective-permute-start | bytes 393224 | tf_op jit(solution)/shard_map/ppermute | solution.py:304
  34.6 0.0 collective-permute-done.12.refs_4_
  34.6 0.0 collective-permute-start.17
  34.7 0.4 collective-permute-start.15
  35.0 1.1 %copy-done.3 = bf16[768,512]{1,0:T(8,128)(2,1)S(1)} copy-done((bf16[768,512]{1,0:T(8,128)(2,1)S(1)}, bf16[768,512]{1,0:T(8,128)(2,1)}, u32[]{:S(2)}) %copy-start.3) | copy-done | bytes 786456
  36.2 1.0 %start.1 = f32[2,2,256,256]{3,2,1,0:T(8,128)S(1)} custom-call(s32[2,2]{1,0:T(2,128)S(1)} %collective-permute-done.4.refs_2_.places, f32[2,256,256]{2,1,0:T(8,128)S(1)} %copy-done.1, bf16[2,256,256]{2,1,0:T(8,128)(2,1)S(1)} %collective-permute-done.7.refs_0_, bf16[2,256,256]{2,1,0:T(8,128)(2,1)S(1)} %collective-permute-done.8.refs_1_, ...), custom_call_target="tpu_custom_call" | custom-call | flops 1073741824 | bytes 4194304 | tf_op jit(solution)/shard_map/start/pallas_call | solution.py:359
  37.2 0.0 collective-permute-done.13.refs_5_
  37.2 1.8 %collective-permute-done.14.refs_6_ = bf16[2,2,64,256]{3,2,1,0:T(8,128)(2,1)S(1)} collective-permute-done((bf16[2,2,64,256]{3,2,1,0:T(8,128)(2,1)S(1)}, bf16[2,2,64,256]{3,2,1,0:T(8,128)(2,1)S(1)}, u32[]{:S(2)}, u32[]{:S(2)}) %collective-permute-start.14) | collective-permute-done | bytes 131104 | tf_op jit(solution)/shard_map/ppermute | solution.py:304
  39.0 0.0 collective-permute-done.16.refs_8_
  39.0 1.6 %collective-permute-done.17.refs_9_ = bf16[2,2,64,256]{3,2,1,0:T(8,128)(2,1)S(1)} collective-permute-done((bf16[2,2,64,256]{3,2,1,0:T(8,128)(2,1)S(1)}, bf16[2,2,64,256]{3,2,1,0:T(8,128)(2,1)S(1)}, u32[]{:S(2)}, u32[]{:S(2)}) %collective-permute-start.17) | collective-permute-done | bytes 131104 | tf_op jit(solution)/shard_map/ppermute | solution.py:304
  40.5 0.0 collective-permute-done.15.refs_7_
  40.6 2.0 %near.3 = (bf16[2,2,256,256]{3,2,1,0:T(8,128)(2,1)S(1)}, f32[2,256,256]{2,1,0:T(8,128)S(1)}, bf16[2,256,256]{2,1,0:T(8,128)(2,1)S(1)}) custom-call(s32[2,2]{1,0:T(2,128)S(1)} %collective-permute-done.4.refs_2_.places, f32[2,2,256,256]{3,2,1,0:T(8,128)S(1)} %start.1, bf16[512,768]{1,0:T(8,128)(2,1)S(1)} %copy-done.2, bf16[768,512]{1,0:T(8,128)(2,1)S(1)} %copy-done.4, ...), custom_call_target="tpu_custom_call" | custom-call | flops 1073741824 | bytes 4194304 | tf_op jit(solution)/shard_map/near/pallas_call | solution.py:368
  42.5 0.1 collective-permute-start.19
  42.6 4.4 %near.2 = (bf16[2,2,256,256]{3,2,1,0:T(8,128)(2,1)S(1)}, f32[2,256,256]{2,1,0:T(8,128)S(1)}, bf16[2,256,256]{2,1,0:T(8,128)(2,1)S(1)}) custom-call(s32[2,2]{1,0:T(2,128)S(1)} %collective-permute-done.4.refs_2_.places, f32[2,2,256,256]{3,2,1,0:T(8,128)S(1)} %start.1, bf16[512,768]{1,0:T(8,128)(2,1)S(1)} %copy-done.2, bf16[768,512]{1,0:T(8,128)(2,1)S(1)} %copy-done.4, ...), custom_call_target="tpu_custom_call" | custom-call | flops 1073741824 | bytes 4194304 | tf_op jit(solution)/shard_map/near/pallas_call | solution.py:368
  47.0 2.1 %collective-permute-start.18 = (bf16[2,256,256]{2,1,0:T(8,128)(2,1)S(1)}, bf16[2,256,256]{2,1,0:T(8,128)(2,1)S(1)}, u32[]{:S(2)}, u32[]{:S(2)}) collective-permute-start(bf16[2,256,256]{2,1,0:T(8,128)(2,1)S(1)} %get-tuple-element.138), channel_id=1, source_target_pairs={{0,16},{1,17},{2,18},{3,19},{4,20},{5,21},{6,22},{7,23},{8,24},{9,... | collective-permute-start | bytes 786440 | tf_op jit(solution)/shard_map/ppermute | solution.py:304
  49.1 2.7 %collective-permute-done.19.arrived = bf16[2,256,256]{2,1,0:T(8,128)(2,1)S(1)} collective-permute-done((bf16[2,256,256]{2,1,0:T(8,128)(2,1)S(1)}, bf16[2,256,256]{2,1,0:T(8,128)(2,1)S(1)}, u32[]{:S(2)}, u32[]{:S(2)}) %collective-permute-start.19) | collective-permute-done | bytes 262176 | tf_op jit(solution)/shard_map/ppermute | solution.py:304
  51.8 3.9 %far.3 = (bf16[2,256,256]{2,1,0:T(8,128)(2,1)S(1)}, bf16[2,256,256]{2,1,0:T(8,128)(2,1)S(1)}, f32[2,256,256]{2,1,0:T(8,128)S(1)}) custom-call(f32[2,2,256,256]{3,2,1,0:T(8,128)S(1)} %start.1, bf16[512,768]{1,0:T(8,128)(2,1)S(1)} %copy-done.2, bf16[768,512]{1,0:T(8,128)(2,1)S(1)} %copy-done.4, bf16[2,2,256,256]{3,2,1,0:T(8,128)(2,1)S(1)} %get-tuple-element.140.frames, ...), custom_call_target="tpu_custom_call" | custom-call | flops 2147483648 | bytes 4194304 | tf_op jit(solution)/shard_map/far/pallas_call | solution.py:378
  55.7 0.1 collective-permute-start.21
  55.8 0.8 collective-permute-done.18.arrived
  56.6 1.5 %far.2 = (bf16[2,256,256]{2,1,0:T(8,128)(2,1)S(1)}, bf16[2,256,256]{2,1,0:T(8,128)(2,1)S(1)}, f32[2,256,256]{2,1,0:T(8,128)S(1)}) custom-call(f32[2,2,256,256]{3,2,1,0:T(8,128)S(1)} %start.1, bf16[512,768]{1,0:T(8,128)(2,1)S(1)} %copy-done.2, bf16[768,512]{1,0:T(8,128)(2,1)S(1)} %copy-done.4, bf16[2,2,256,256]{3,2,1,0:T(8,128)(2,1)S(1)} %get-tuple-element.136.frames, ...), custom_call_target="tpu_custom_call" | custom-call | flops 2147483648 | bytes 4194304 | tf_op jit(solution)/shard_map/far/pallas_call | solution.py:378
  58.1 0.1 collective-permute-start.20
  58.2 1.1 %probe.3 = (f32[2,64,256]{2,1,0:T(8,128)S(1)}, f32[2,64,256]{2,1,0:T(8,128)S(1)}, bf16[2,2,64,256]{3,2,1,0:T(8,128)(2,1)S(1)}) custom-call(s32[2,2]{1,0:T(2,128)S(1)} %collective-permute-done.4.refs_2_.places, f32[2,256,256]{2,1,0:T(8,128)S(1)} %get-tuple-element.139.refs_0_, f32[2,256,256]{2,1,0:T(8,128)S(1)} %get-tuple-element.143.refs_1_), custom_call_target="tpu_custom_call" | custom-call | flops 67108864 | bytes 4194304 | tf_op jit(solution)/shard_map/probe/pallas_call | solution.py:398
  59.2 0.6 collective-permute-start.22
  59.8 0.0 collective-permute-done.21.refs_3_
  59.8 0.0 collective-permute-done.20.refs_2_
  59.8 0.7 part.1
  60.5 2.0 %collective-permute-start.23 = (bf16[2,2,2,64,256]{4,3,2,1,0:T(8,128)(2,1)S(1)}, bf16[2,2,2,64,256]{4,3,2,1,0:T(8,128)(2,1)S(1)}, u32[]{:S(2)}, u32[]{:S(2)}) collective-permute-start(bf16[2,2,2,64,256]{4,3,2,1,0:T(8,128)(2,1)S(1)} %get-tuple-element.154), channel_id=1, source_target_pairs={{0,6},{1,7},{2,0},{3,1},{4,2},{5,3},{6,4},{7,5},{8,14},{9,15},{10,... | collective-permute-start | bytes 786440 | tf_op jit(solution)/shard_map/ppermute | solution.py:304
  62.5 0.0 collective-permute-start.24
  62.5 2.0 %collective-permute-start.25 = (bf16[2,2,2,64,256]{4,3,2,1,0:T(8,128)(2,1)S(1)}, bf16[2,2,2,64,256]{4,3,2,1,0:T(8,128)(2,1)S(1)}, u32[]{:S(2)}, u32[]{:S(2)}) collective-permute-start(bf16[2,2,2,64,256]{4,3,2,1,0:T(8,128)(2,1)S(1)} %get-tuple-element.156), channel_id=1, source_target_pairs={{0,1},{1,2},{2,3},{3,4},{4,5},{5,6},{6,7},{7,0},{8,9},{9,10},{10,1... | collective-permute-start | bytes 786440 | tf_op jit(solution)/shard_map/ppermute | solution.py:304
  64.5 0.0 collective-permute-start.26
  64.6 0.0 collective-permute-done.22
  64.6 22.7 %while.14 = (s32[]{:T(128)}, f32[2,64,256]{2,1,0:T(8,128)S(1)}, f32[2,64,256]{2,1,0:T(8,128)S(1)}, s32[]{:T(128)}, pred[]{:T(512)}, /*index=5*/bf16[2,2,64,256]{3,2,1,0:T(8,128)(2,1)S(1)}, s32[]{:T(128)}) while((s32[]{:T(128)}, f32[2,64,256]{2,1,0:T(8,128)S(1)}, f32[2,64,256]{2,1,0:T(8,128)S(1)}, s32[]{:T(128)}, pred[]{:T(512)}, ...), condition=%wide.region_1.2_spmd, body=%wide.region_0.1_spmd.sunk | while | flops 458754 | bytes 1966278 | solution.py:427
  64.6 2.9 %collective-permute-start = (bf16[2,64,256]{2,1,0:T(8,128)(2,1)S(1)}, bf16[2,64,256]{2,1,0:T(8,128)(2,1)S(1)}, u32[]{:S(2)}, u32[]{:S(2)}) collective-permute-start(bf16[2,64,256]{2,1,0:T(8,128)(2,1)S(1)} %fusion.5), channel_id=1, source_target_pairs={{0,16},{1,17},{2,18},{3,19},{4,20},{5,21},{6,22},{7,23},{8,24},{9,... | collective-permute-start | bytes 196616 | tf_op jit(solution)/shard_map/while/body/ppermute | solution.py:304
  67.6 1.9 %collective-permute-done = bf16[2,64,256]{2,1,0:T(8,128)(2,1)S(1)} collective-permute-done((bf16[2,64,256]{2,1,0:T(8,128)(2,1)S(1)}, bf16[2,64,256]{2,1,0:T(8,128)(2,1)S(1)}, u32[]{:S(2)}, u32[]{:S(2)}) %collective-permute-start) | collective-permute-done | bytes 65568 | tf_op jit(solution)/shard_map/while/body/ppermute | solution.py:304
  69.5 0.7 collective-permute-start.1
  70.2 12.7 %collective-permute-done.1 = bf16[2,64,256]{2,1,0:T(8,128)(2,1)S(1)} collective-permute-done((bf16[2,64,256]{2,1,0:T(8,128)(2,1)S(1)}, bf16[2,64,256]{2,1,0:T(8,128)(2,1)S(1)}, u32[]{:S(2)}, u32[]{:S(2)}) %collective-permute-start.1) | collective-permute-done | bytes 65568 | tf_op jit(solution)/shard_map/while/body/ppermute | solution.py:411
  82.9 0.8 collective-permute-start.2
  83.7 3.5 %collective-permute-done.2 = bf16[2,64,256]{2,1,0:T(8,128)(2,1)S(1)} collective-permute-done((bf16[2,64,256]{2,1,0:T(8,128)(2,1)S(1)}, bf16[2,64,256]{2,1,0:T(8,128)(2,1)S(1)}, u32[]{:S(2)}, u32[]{:S(2)}) %collective-permute-start.2) | collective-permute-done | bytes 65568 | tf_op jit(solution)/shard_map/while/body/ppermute | solution.py:411
  87.3 0.0 collective-permute-done.25.refs_8_
  87.3 1.2 %collective-permute-start.27 = (bf16[2,64,256]{2,1,0:T(8,128)(2,1)S(1)}, bf16[2,64,256]{2,1,0:T(8,128)(2,1)S(1)}, u32[]{:S(2)}, u32[]{:S(2)}) collective-permute-start(bf16[2,64,256]{2,1,0:T(8,128)(2,1)S(1)} %convert_element_type.65), channel_id=1, source_target_pairs={{0,2},{1,3},{2,0},{3,1},{4,6},{5,7},{6,4},{7,5},{8,10},{9,11},{10,... | collective-permute-start | bytes 196616 | tf_op jit(solution)/shard_map/ppermute | solution.py:411
  88.6 2.7 %deposit.1 = f32[2,64,3072]{2,1,0:T(8,128)} custom-call(s32[2,2]{1,0:T(2,128)S(1)} %multiply_add_fusion.refs_0_, s32[2,2]{1,0:T(2,128)S(1)} %collective-permute-done.3.refs_1_, s32[2,2]{1,0:T(2,128)S(1)} %collective-permute-done.4.refs_2_.places, s32[2,2]{1,0:T(2,128)S(1)} %collective-permute-done.5.refs_3_, s32[2,2]{1,0:T(2,128)S(1)} %collective-permute-done.6.refs_4_, ...), custom_call_target="tpu_custom_call" | custom-call | flops 67108864 | bytes 4194304 | tf_op jit(solution)/shard_map/deposit/pallas_call | solution.py:433
  91.3 0.4 collective-permute-done.27
  91.7 0.7 convert_add_fusion.3
  (24 shorter events, 0.1 us)
Async XLA Ops:
  0.6 5.1 %copy-start.6 = (s32[2,2]{1,0:T(2,128)S(1)}, s32[2,2]{1,0:T(2,128)}, u32[]{:S(2)}) copy-start(s32[2,2]{1,0:T(2,128)} %param.12) | copy-start | bytes 52
  0.6 5.0 %copy-start.5 = (s32[2,2]{1,0:T(2,128)S(1)}, s32[2,2]{1,0:T(2,128)}, u32[]{:S(2)}) copy-start(s32[2,2]{1,0:T(2,128)} %param.13) | copy-start | bytes 52
  0.7 14.6 %copy-start = (f32[1,2,64,3072]{3,2,1,0:T(8,128)S(1)}, f32[1,2,64,3072]{3,2,1,0:T(8,128)}, u32[]{:S(2)}) copy-start(f32[1,2,64,3072]{3,2,1,0:T(8,128)} %param.9) | copy-start | bytes 4718596
  2.6 32.4 %copy-start.1 = (f32[2,256,256]{2,1,0:T(8,128)S(1)}, f32[2,256,256]{2,1,0:T(8,128)}, u32[]{:S(2)}) copy-start(f32[2,256,256]{2,1,0:T(8,128)} %probe.2) | copy-start | bytes 1572868
  2.6 32.4 %copy-start.2 = (bf16[512,768]{1,0:T(8,128)(2,1)S(1)}, bf16[512,768]{1,0:T(8,128)(2,1)}, u32[]{:S(2)}) copy-start(bf16[512,768]{1,0:T(8,128)(2,1)} %constant.46.clone.refs_2_.left) | copy-start | bytes 2359300
  2.6 13.9 %collective-permute-start.7 = (bf16[2,256,256]{2,1,0:T(8,128)(2,1)}, bf16[2,256,256]{2,1,0:T(8,128)(2,1)S(1)}, u32[]{:S(2)}, u32[]{:S(2)}) collective-permute-start(bf16[2,256,256]{2,1,0:T(8,128)(2,1)} %pick.1), channel_id=1, source_target_pairs={{0,2},{1,3},{2,4},{3,5},{4,6},{5,7},{6,0},{7,1},{8,10},{9,11},{10,... | collective-permute-start | bytes 786440 | tf_op jit(solution)/shard_map/ppermute | solution.py:294
  5.7 8.6 %collective-permute-start.4 = (s32[2,2]{1,0:T(2,128)S(1)}, s32[2,2]{1,0:T(2,128)S(1)}, u32[]{:S(2)}, u32[]{:S(2)}) collective-permute-start(s32[2,2]{1,0:T(2,128)S(1)} %multiply_add_fusion.refs_0_), channel_id=1, source_target_pairs={{0,2},{1,3},{2,4},{3,5},{4,6},{5,7},{6,0},{7,1},{8,10},{9,11},{10,... | collective-permute-start | bytes 56 | tf_op jit(solution)/shard_map/ppermute | solution.py:294
  7.3 7.9 %collective-permute-start.3 = (s32[2,2]{1,0:T(2,128)S(1)}, s32[2,2]{1,0:T(2,128)S(1)}, u32[]{:S(2)}, u32[]{:S(2)}) collective-permute-start(s32[2,2]{1,0:T(2,128)S(1)} %multiply_add_fusion.refs_0_), channel_id=1, source_target_pairs={{0,1},{1,2},{2,3},{3,4},{4,5},{5,6},{6,7},{7,0},{8,9},{9,10},{10,1... | collective-permute-start | bytes 56 | tf_op jit(solution)/shard_map/ppermute | solution.py:294
  8.8 6.4 %collective-permute-start.5 = (s32[2,2]{1,0:T(2,128)S(1)}, s32[2,2]{1,0:T(2,128)S(1)}, u32[]{:S(2)}, u32[]{:S(2)}) collective-permute-start(s32[2,2]{1,0:T(2,128)S(1)} %multiply_add_fusion.refs_0_), channel_id=1, source_target_pairs={{0,3},{1,4},{2,5},{3,6},{4,7},{5,0},{6,1},{7,2},{8,11},{9,12},{10,... | collective-permute-start | bytes 56 | tf_op jit(solution)/shard_map/ppermute | solution.py:294
  9.9 5.4 %collective-permute-start.6 = (s32[2,2]{1,0:T(2,128)S(1)}, s32[2,2]{1,0:T(2,128)S(1)}, u32[]{:S(2)}, u32[]{:S(2)}) collective-permute-start(s32[2,2]{1,0:T(2,128)S(1)} %multiply_add_fusion.refs_0_), channel_id=1, source_target_pairs={{0,4},{1,5},{2,6},{3,7},{4,0},{5,1},{6,2},{7,3},{8,12},{9,13},{10,... | collective-permute-start | bytes 56 | tf_op jit(solution)/shard_map/ppermute | solution.py:294
  16.5 18.2 %collective-permute-start.8 = (bf16[2,256,256]{2,1,0:T(8,128)(2,1)S(1)}, bf16[2,256,256]{2,1,0:T(8,128)(2,1)S(1)}, u32[]{:S(2)}, u32[]{:S(2)}) collective-permute-start(bf16[2,256,256]{2,1,0:T(8,128)(2,1)S(1)} %collective-permute-done.7.refs_0_), channel_id=1, source_target_pairs={{0,16},{1,17},{2,18},{3,19},{4,20},{5,21},{6,22},{7,23},{8,24},{9,... | collective-permute-start | bytes 786440 | tf_op jit(solution)/shard_map/ppermute | solution.py:304
  19.9 8.2 %collective-permute-start.9 = (bf16[2,2,64,256]{3,2,1,0:T(8,128)(2,1)S(1)}, bf16[2,2,64,256]{3,2,1,0:T(8,128)(2,1)S(1)}, u32[]{:S(2)}, u32[]{:S(2)}) collective-permute-start(bf16[2,2,64,256]{3,2,1,0:T(8,128)(2,1)S(1)} %get-tuple-element.125), channel_id=1, source_target_pairs={{0,2},{1,3},{2,4},{3,5},{4,6},{5,7},{6,0},{7,1},{8,10},{9,11},{10,... | collective-permute-start | bytes 393224 | tf_op jit(solution)/shard_map/ppermute | solution.py:304
  20.7 9.5 %collective-permute-start.10 = (bf16[2,2,64,256]{3,2,1,0:T(8,128)(2,1)S(1)}, bf16[2,2,64,256]{3,2,1,0:T(8,128)(2,1)S(1)}, u32[]{:S(2)}, u32[]{:S(2)}) collective-permute-start(bf16[2,2,64,256]{3,2,1,0:T(8,128)(2,1)S(1)} %get-tuple-element.127), channel_id=1, source_target_pairs={{0,1},{1,2},{2,3},{3,4},{4,5},{5,6},{6,7},{7,0},{8,9},{9,10},{10,1... | collective-permute-start | bytes 393224 | tf_op jit(solution)/shard_map/ppermute | solution.py:304
  22.2 8.0 %collective-permute-start.11 = (bf16[2,2,64,256]{3,2,1,0:T(8,128)(2,1)S(1)}, bf16[2,2,64,256]{3,2,1,0:T(8,128)(2,1)S(1)}, u32[]{:S(2)}, u32[]{:S(2)}) collective-permute-start(bf16[2,2,64,256]{3,2,1,0:T(8,128)(2,1)S(1)} %get-tuple-element.129), channel_id=1, source_target_pairs={{0,7},{1,0},{2,1},{3,2},{4,3},{5,4},{6,5},{7,6},{8,15},{9,8},{10,9... | collective-permute-start | bytes 393224 | tf_op jit(solution)/shard_map/ppermute | solution.py:304
  25.4 9.2 %collective-permute-start.12 = (bf16[2,2,64,256]{3,2,1,0:T(8,128)(2,1)S(1)}, bf16[2,2,64,256]{3,2,1,0:T(8,128)(2,1)S(1)}, u32[]{:S(2)}, u32[]{:S(2)}) collective-permute-start(bf16[2,2,64,256]{3,2,1,0:T(8,128)(2,1)S(1)} %get-tuple-element.130), channel_id=1, source_target_pairs={{0,6},{1,7},{2,0},{3,1},{4,2},{5,3},{6,4},{7,5},{8,14},{9,15},{10,... | collective-permute-start | bytes 393224 | tf_op jit(solution)/shard_map/ppermute | solution.py:304
  28.1 9.1 %collective-permute-start.13 = (bf16[2,2,64,256]{3,2,1,0:T(8,128)(2,1)S(1)}, bf16[2,2,64,256]{3,2,1,0:T(8,128)(2,1)S(1)}, u32[]{:S(2)}, u32[]{:S(2)}) collective-permute-start(bf16[2,2,64,256]{3,2,1,0:T(8,128)(2,1)S(1)} %get-tuple-element.131), channel_id=1, source_target_pairs={{0,10},{1,11},{2,12},{3,13},{4,14},{5,15},{6,8},{7,9},{8,2},{9,3},... | collective-permute-start | bytes 393224 | tf_op jit(solution)/shard_map/ppermute | solution.py:304
  30.2 8.8 %collective-permute-start.14 = (bf16[2,2,64,256]{3,2,1,0:T(8,128)(2,1)S(1)}, bf16[2,2,64,256]{3,2,1,0:T(8,128)(2,1)S(1)}, u32[]{:S(2)}, u32[]{:S(2)}) collective-permute-start(bf16[2,2,64,256]{3,2,1,0:T(8,128)(2,1)S(1)} %get-tuple-element.132), channel_id=1, source_target_pairs={{0,9},{1,10},{2,11},{3,12},{4,13},{5,14},{6,15},{7,8},{8,1},{9,2},... | collective-permute-start | bytes 393224 | tf_op jit(solution)/shard_map/ppermute | solution.py:304
  30.2 8.8 %collective-permute-start.16 = (bf16[2,2,64,256]{3,2,1,0:T(8,128)(2,1)S(1)}, bf16[2,2,64,256]{3,2,1,0:T(8,128)(2,1)S(1)}, u32[]{:S(2)}, u32[]{:S(2)}) collective-permute-start(bf16[2,2,64,256]{3,2,1,0:T(8,128)(2,1)S(1)} %get-tuple-element.134), channel_id=1, source_target_pairs={{0,15},{1,8},{2,9},{3,10},{4,11},{5,12},{6,13},{7,14},{8,7},{9,0},... | collective-permute-start | bytes 393224 | tf_op jit(solution)/shard_map/ppermute | solution.py:304
  34.6 5.9 %collective-permute-start.17 = (bf16[2,2,64,256]{3,2,1,0:T(8,128)(2,1)S(1)}, bf16[2,2,64,256]{3,2,1,0:T(8,128)(2,1)S(1)}, u32[]{:S(2)}, u32[]{:S(2)}) collective-permute-start(bf16[2,2,64,256]{3,2,1,0:T(8,128)(2,1)S(1)} %get-tuple-element.135), channel_id=1, source_target_pairs={{0,14},{1,15},{2,8},{3,9},{4,10},{5,11},{6,12},{7,13},{8,6},{9,7},... | collective-permute-start | bytes 393224 | tf_op jit(solution)/shard_map/ppermute | solution.py:304
  34.7 5.9 %collective-permute-start.15 = (bf16[2,2,64,256]{3,2,1,0:T(8,128)(2,1)S(1)}, bf16[2,2,64,256]{3,2,1,0:T(8,128)(2,1)S(1)}, u32[]{:S(2)}, u32[]{:S(2)}) collective-permute-start(bf16[2,2,64,256]{3,2,1,0:T(8,128)(2,1)S(1)} %get-tuple-element.133), channel_id=1, source_target_pairs={{0,8},{1,9},{2,10},{3,11},{4,12},{5,13},{6,14},{7,15},{8,0},{9,1},... | collective-permute-start | bytes 393224 | tf_op jit(solution)/shard_map/ppermute | solution.py:304
  35.0 1.1 %copy-start.3 = (bf16[768,512]{1,0:T(8,128)(2,1)S(1)}, bf16[768,512]{1,0:T(8,128)(2,1)}, u32[]{:S(2)}) copy-start(bf16[768,512]{1,0:T(8,128)(2,1)} %constant.47.clone.refs_3_.right) | copy-start | bytes 2359300
  36.2 4.4 %copy-start.4 = (bf16[768,512]{1,0:T(8,128)(2,1)S(1)}, bf16[768,512]{1,0:T(8,128)(2,1)}, u32[]{:S(2)}) copy-start(bf16[768,512]{1,0:T(8,128)(2,1)} %constant.47.clone.refs_3_.right) | copy-start | bytes 2359300
  42.5 9.2 %collective-permute-start.19 = (bf16[2,256,256]{2,1,0:T(8,128)(2,1)S(1)}, bf16[2,256,256]{2,1,0:T(8,128)(2,1)S(1)}, u32[]{:S(2)}, u32[]{:S(2)}) collective-permute-start(bf16[2,256,256]{2,1,0:T(8,128)(2,1)S(1)} %get-tuple-element.142), channel_id=1, source_target_pairs={{0,16},{1,17},{2,18},{3,19},{4,20},{5,21},{6,22},{7,23},{8,24},{9,... | collective-permute-start | bytes 786440 | tf_op jit(solution)/shard_map/ppermute | solution.py:304
  47.0 9.6 %collective-permute-start.18 = (bf16[2,256,256]{2,1,0:T(8,128)(2,1)S(1)}, bf16[2,256,256]{2,1,0:T(8,128)(2,1)S(1)}, u32[]{:S(2)}, u32[]{:S(2)}) collective-permute-start(bf16[2,256,256]{2,1,0:T(8,128)(2,1)S(1)} %get-tuple-element.138), channel_id=1, source_target_pairs={{0,16},{1,17},{2,18},{3,19},{4,20},{5,21},{6,22},{7,23},{8,24},{9,... | collective-permute-start | bytes 786440 | tf_op jit(solution)/shard_map/ppermute | solution.py:304
  55.7 4.1 %collective-permute-start.21 = (bf16[2,256,256]{2,1,0:T(8,128)(2,1)S(1)}, bf16[2,256,256]{2,1,0:T(8,128)(2,1)S(1)}, u32[]{:S(2)}, u32[]{:S(2)}) collective-permute-start(bf16[2,256,256]{2,1,0:T(8,128)(2,1)S(1)} %get-tuple-element.148), channel_id=1, source_target_pairs={{0,8},{1,9},{2,10},{3,11},{4,12},{5,13},{6,14},{7,15},{8,0},{9,1},... | collective-permute-start | bytes 786440 | tf_op jit(solution)/shard_map/ppermute | solution.py:304
  58.1 1.7 %collective-permute-start.20 = (bf16[2,256,256]{2,1,0:T(8,128)(2,1)S(1)}, bf16[2,256,256]{2,1,0:T(8,128)(2,1)S(1)}, u32[]{:S(2)}, u32[]{:S(2)}) collective-permute-start(bf16[2,256,256]{2,1,0:T(8,128)(2,1)S(1)} %get-tuple-element.147), channel_id=1, source_target_pairs={{0,8},{1,9},{2,10},{3,11},{4,12},{5,13},{6,14},{7,15},{8,0},{9,1},... | collective-permute-start | bytes 786440 | tf_op jit(solution)/shard_map/ppermute | solution.py:304
  59.2 5.4 %collective-permute-start.22 = (bf16[2,2,64,256]{3,2,1,0:T(8,128)(2,1)S(1)}, bf16[2,2,64,256]{3,2,1,0:T(8,128)(2,1)S(1)}, u32[]{:S(2)}, u32[]{:S(2)}) collective-permute-start(bf16[2,2,64,256]{3,2,1,0:T(8,128)(2,1)S(1)} %get-tuple-element.152), channel_id=1, source_target_pairs={{0,8},{1,9},{2,10},{3,11},{4,12},{5,13},{6,14},{7,15},{8,0},{9,1},... | collective-permute-start | bytes 393224 | tf_op jit(solution)/shard_map/ppermute | solution.py:304
  60.5 26.8 %collective-permute-start.23 = (bf16[2,2,2,64,256]{4,3,2,1,0:T(8,128)(2,1)S(1)}, bf16[2,2,2,64,256]{4,3,2,1,0:T(8,128)(2,1)S(1)}, u32[]{:S(2)}, u32[]{:S(2)}) collective-permute-start(bf16[2,2,2,64,256]{4,3,2,1,0:T(8,128)(2,1)S(1)} %get-tuple-element.154), channel_id=1, source_target_pairs={{0,6},{1,7},{2,0},{3,1},{4,2},{5,3},{6,4},{7,5},{8,14},{9,15},{10,... | collective-permute-start | bytes 786440 | tf_op jit(solution)/shard_map/ppermute | solution.py:304
  62.5 24.8 %collective-permute-start.24 = (bf16[2,2,2,64,256]{4,3,2,1,0:T(8,128)(2,1)S(1)}, bf16[2,2,2,64,256]{4,3,2,1,0:T(8,128)(2,1)S(1)}, u32[]{:S(2)}, u32[]{:S(2)}) collective-permute-start(bf16[2,2,2,64,256]{4,3,2,1,0:T(8,128)(2,1)S(1)} %get-tuple-element.155), channel_id=1, source_target_pairs={{0,7},{1,0},{2,1},{3,2},{4,3},{5,4},{6,5},{7,6},{8,15},{9,8},{10,9... | collective-permute-start | bytes 786440 | tf_op jit(solution)/shard_map/ppermute | solution.py:304
  62.5 24.8 %collective-permute-start.25 = (bf16[2,2,2,64,256]{4,3,2,1,0:T(8,128)(2,1)S(1)}, bf16[2,2,2,64,256]{4,3,2,1,0:T(8,128)(2,1)S(1)}, u32[]{:S(2)}, u32[]{:S(2)}) collective-permute-start(bf16[2,2,2,64,256]{4,3,2,1,0:T(8,128)(2,1)S(1)} %get-tuple-element.156), channel_id=1, source_target_pairs={{0,1},{1,2},{2,3},{3,4},{4,5},{5,6},{6,7},{7,0},{8,9},{9,10},{10,1... | collective-permute-start | bytes 786440 | tf_op jit(solution)/shard_map/ppermute | solution.py:304
  64.5 22.8 %collective-permute-start.26 = (bf16[2,2,2,64,256]{4,3,2,1,0:T(8,128)(2,1)S(1)}, bf16[2,2,2,64,256]{4,3,2,1,0:T(8,128)(2,1)S(1)}, u32[]{:S(2)}, u32[]{:S(2)}) collective-permute-start(bf16[2,2,2,64,256]{4,3,2,1,0:T(8,128)(2,1)S(1)} %get-tuple-element.157), channel_id=1, source_target_pairs={{0,2},{1,3},{2,4},{3,5},{4,6},{5,7},{6,0},{7,1},{8,10},{9,11},{10,... | collective-permute-start | bytes 786440 | tf_op jit(solution)/shard_map/ppermute | solution.py:304
  64.6 4.8 %collective-permute-start = (bf16[2,64,256]{2,1,0:T(8,128)(2,1)S(1)}, bf16[2,64,256]{2,1,0:T(8,128)(2,1)S(1)}, u32[]{:S(2)}, u32[]{:S(2)}) collective-permute-start(bf16[2,64,256]{2,1,0:T(8,128)(2,1)S(1)} %fusion.5), channel_id=1, source_target_pairs={{0,16},{1,17},{2,18},{3,19},{4,20},{5,21},{6,22},{7,23},{8,24},{9,... | collective-permute-start | bytes 196616 | tf_op jit(solution)/shard_map/while/body/ppermute | solution.py:304
  69.5 13.4 %collective-permute-start.1 = (bf16[2,64,256]{2,1,0:T(8,128)(2,1)S(1)}, bf16[2,64,256]{2,1,0:T(8,128)(2,1)S(1)}, u32[]{:S(2)}, u32[]{:S(2)}) collective-permute-start(bf16[2,64,256]{2,1,0:T(8,128)(2,1)S(1)} %get-tuple-element.218), channel_id=1, source_target_pairs={{0,4},{1,5},{2,6},{3,7},{4,0},{5,1},{6,2},{7,3},{8,12},{9,13},{10,... | collective-permute-start | bytes 196616 | tf_op jit(solution)/shard_map/while/body/ppermute | solution.py:411
  82.9 4.3 %collective-permute-start.2 = (bf16[2,64,256]{2,1,0:T(8,128)(2,1)S(1)}, bf16[2,64,256]{2,1,0:T(8,128)(2,1)S(1)}, u32[]{:S(2)}, u32[]{:S(2)}) collective-permute-start(bf16[2,64,256]{2,1,0:T(8,128)(2,1)S(1)} %add_convert_fusion.2), channel_id=1, source_target_pairs={{0,1},{1,0},{2,3},{3,2},{4,5},{5,4},{6,7},{7,6},{8,9},{9,8},{10,11... | collective-permute-start | bytes 196616 | tf_op jit(solution)/shard_map/while/body/ppermute | solution.py:411
  87.3 4.3 %collective-permute-start.27 = (bf16[2,64,256]{2,1,0:T(8,128)(2,1)S(1)}, bf16[2,64,256]{2,1,0:T(8,128)(2,1)S(1)}, u32[]{:S(2)}, u32[]{:S(2)}) collective-permute-start(bf16[2,64,256]{2,1,0:T(8,128)(2,1)S(1)} %convert_element_type.65), channel_id=1, source_target_pairs={{0,2},{1,3},{2,0},{3,1},{4,6},{5,7},{6,4},{7,5},{8,10},{9,11},{10,... | collective-permute-start | bytes 196616 | tf_op jit(solution)/shard_map/ppermute | solution.py:411

commit v7 on v4

--- a/solution.py
+++ b/solution.py
@@ -413,7 +413,7 @@
         near, away, given = held
         away = across((away + given[1].astype(f32)).astype(bf16), 2, 0, lower).astype(f32)
         total = jnp.where(half == 0, near + given[0].astype(f32), away)
-        for span in spans[:-1]:
+        for span in spans[:-2]:
             total = scan_round(total, span)
         return total, away, given
 
@@ -426,7 +426,7 @@
         0, once, probe_rounds, (near, away, across(probe_sent, 1, 0))
     )
     probe_grad, returned = lax.optimization_barrier((probe_grad, returned))
-    probe_grad = scan_round(probe_grad, spans[-1])
+    probe_grad = scan_round(probe_grad, spans[-2])
     object_grad = call(
         functools.partial(deposit_kernel, reach),
         shape(transmission.shape[1:], f32),
@@ -434,6 +434,8 @@
         1 << 26,
         "deposit",
     )(*places, *returned)
+    probe_grad, object_grad = lax.optimization_barrier((probe_grad, object_grad))
+    probe_grad = scan_round(probe_grad, spans[-1])
     return object_grad[None], probe_grad
 
 

time: 88.7 us -> 91.7 us (1.034)
  starting transfers between devices: 37.6 us -> 42.4 us
  waiting for transfers between devices: 27.7 us -> 26 us
    ppermute x3, waiting for transfers between devices: 12.8 us -> 8.87 us  [scan_round(): lax.ppermute(rounded, 'scan', route).astype(f32)]
    ppermute x3, starting transfers between devices: 2.72 us -> 5.78 us  [scan_round(): lax.ppermute(rounded, 'scan', route).astype(f32)]
    ppermute x20, waiting for transfers between devices: 12.2 us -> 14.5 us  [across(): return lax.ppermute(value, ('depth', 'scan'), route)]
    ppermute x20, starting transfers between devices: 24.9 us -> 26.7 us  [across(): return lax.ppermute(value, ('depth', 'scan'), route)]
  transfers between devices with their start and end apart: 28 -> 28, of which waited for: 12 -> 11; matrix products, arithmetic and copies ran while one was open for 0% -> 0% of each run, Pallas kernels for 19% -> 18%
where the time goes in v7:
time: 91.7 us; the launch traced here: 91.5 us
  starting transfers between devices  42.4 us (46%)
  waiting for transfers between devices  26 us (28%)
  Pallas kernels  20.3 us (22%)
  local copies, waits for them, and re-layouts  1.16 us (1%)
    ppermute x20, starting transfers between devices, across(): return lax.ppermute(value, ('depth', 'scan'), route)  26.7 us
    ppermute x20, waiting for transfers between devices, across(): return lax.ppermute(value, ('depth', 'scan'), route)  14.5 us
    ppermute x5, starting transfers between devices, along_scan(): lax.ppermute(value, 'scan', [(i, (i + by) % regions) for i in range(regio...  9.99 us
    ppermute x3, waiting for transfers between devices, scan_round(): lax.ppermute(rounded, 'scan', route).astype(f32)  8.87 us
    pallas_call x2, Pallas kernels, local(): call(functools.partial(near_kernel, home, turn, turn == count - 1, width)...  6.35 us
    ppermute x3, starting transfers between devices, scan_round(): lax.ppermute(rounded, 'scan', route).astype(f32)  5.78 us
    pallas_call x2, Pallas kernels, local(): call(functools.partial(far_kernel, turn, turn == count - 1), [shape(wave,...  5.46 us
    pallas_call x1, Pallas kernels, local(): call(functools.partial(deposit_kernel, reach), shape(transmission.shape[1...  2.68 us
  transfers between devices with their start and end apart: 28, of which 11 were waited for; matrix products, arithmetic and copies ran while one was open for 0% of the time, Pallas kernels for 18%

profile of v7, /device:TPU:0, one launch (start us, length us, event | category | flops | bytes accessed | tf_op | source)
XLA Modules:
  0.0 91.5 jit_solution(6233451193044790450)
XLA Ops:
  0.7 1.9 %pick.1 = bf16[2,256,256]{2,1,0:T(8,128)(2,1)} custom-call(f32[2,2,2,256,256]{4,3,2,1,0:T(8,128)} %waves.1), custom_call_target="tpu_custom_call" | custom-call | flops 1048576 | bytes 4194304 | tf_op jit(solution)/shard_map/pick/pallas_call | solution.py:327
  2.6 0.0 copy-start.1
  2.6 0.0 copy-start.2
  2.6 3.1 %collective-permute-start.3 = (bf16[2,256,256]{2,1,0:T(8,128)(2,1)}, bf16[2,256,256]{2,1,0:T(8,128)(2,1)S(1)}, u32[]{:S(2)}, u32[]{:S(2)}) collective-permute-start(bf16[2,256,256]{2,1,0:T(8,128)(2,1)} %pick.1), channel_id=1, source_target_pairs={{0,2},{1,3},{2,4},{3,5},{4,6},{5,7},{6,0},{7,1},{8,10},{9,11},{10,... | collective-permute-start | bytes 786440 | tf_op jit(solution)/shard_map/ppermute | solution.py:293
  5.7 1.6 %collective-permute-start.2 = (s32[2,2]{1,0:T(2,128)S(1)}, s32[2,2]{1,0:T(2,128)S(1)}, u32[]{:S(2)}, u32[]{:S(2)}) collective-permute-start(s32[2,2]{1,0:T(2,128)S(1)} %multiply_add_fusion.refs_0_), channel_id=1, source_target_pairs={{0,2},{1,3},{2,4},{3,5},{4,6},{5,7},{6,0},{7,1},{8,10},{9,11},{10,... | collective-permute-start | bytes 56 | tf_op jit(solution)/shard_map/ppermute | solution.py:293
  7.3 1.5 %collective-permute-start.4 = (s32[2,2]{1,0:T(2,128)S(1)}, s32[2,2]{1,0:T(2,128)S(1)}, u32[]{:S(2)}, u32[]{:S(2)}) collective-permute-start(s32[2,2]{1,0:T(2,128)S(1)} %multiply_add_fusion.refs_0_), channel_id=1, source_target_pairs={{0,1},{1,2},{2,3},{3,4},{4,5},{5,6},{6,7},{7,0},{8,9},{9,10},{10,1... | collective-permute-start | bytes 56 | tf_op jit(solution)/shard_map/ppermute | solution.py:293
  8.8 1.0 %collective-permute-start.5 = (s32[2,2]{1,0:T(2,128)S(1)}, s32[2,2]{1,0:T(2,128)S(1)}, u32[]{:S(2)}, u32[]{:S(2)}) collective-permute-start(s32[2,2]{1,0:T(2,128)S(1)} %multiply_add_fusion.refs_0_), channel_id=1, source_target_pairs={{0,3},{1,4},{2,5},{3,6},{4,7},{5,0},{6,1},{7,2},{8,11},{9,12},{10,... | collective-permute-start | bytes 56 | tf_op jit(solution)/shard_map/ppermute | solution.py:293
  9.9 2.7 %collective-permute-start.6 = (s32[2,2]{1,0:T(2,128)S(1)}, s32[2,2]{1,0:T(2,128)S(1)}, u32[]{:S(2)}, u32[]{:S(2)}) collective-permute-start(s32[2,2]{1,0:T(2,128)S(1)} %multiply_add_fusion.refs_0_), channel_id=1, source_target_pairs={{0,4},{1,5},{2,6},{3,7},{4,0},{5,1},{6,2},{7,3},{8,12},{9,13},{10,... | collective-permute-start | bytes 56 | tf_op jit(solution)/shard_map/ppermute | solution.py:293
  12.6 1.7 %collective-permute-done.2.refs_2_.places = s32[2,2]{1,0:T(2,128)S(1)} collective-permute-done((s32[2,2]{1,0:T(2,128)S(1)}, s32[2,2]{1,0:T(2,128)S(1)}, u32[]{:S(2)}, u32[]{:S(2)}) %collective-permute-start.2) | collective-permute-done | bytes 48 | tf_op jit(solution)/shard_map/ppermute | solution.py:293
  14.3 1.0 %collective-permute-done.4.refs_1_ = s32[2,2]{1,0:T(2,128)S(1)} collective-permute-done((s32[2,2]{1,0:T(2,128)S(1)}, s32[2,2]{1,0:T(2,128)S(1)}, u32[]{:S(2)}, u32[]{:S(2)}) %collective-permute-start.4) | collective-permute-done | bytes 48 | tf_op jit(solution)/shard_map/ppermute | solution.py:293
  15.3 0.0 collective-permute-done.5.refs_3_
  15.3 0.0 collective-permute-done.6.refs_4_
  15.3 1.2 %extract.1 = (bf16[2,2,64,256]{3,2,1,0:T(8,128)(2,1)S(1)}, bf16[2,2,64,256]{3,2,1,0:T(8,128)(2,1)S(1)}, bf16[2,2,64,256]{3,2,1,0:T(8,128)(2,1)S(1)}, bf16[2,2,64...) custom-call(s32[2,2]{1,0:T(2,128)S(1)} %multiply_add_fusion.refs_0_,, ...), custom_call_target="tpu_custom_call" | custom-call | flops 67108864 | bytes 4194304 | tf_op jit(solution)/shard_map/extract/pallas_call | solution.py:343
  16.5 0.0 collective-permute-done.3.refs_0_
  16.5 3.4 %collective-permute-start.7 = (bf16[2,256,256]{2,1,0:T(8,128)(2,1)S(1)}, bf16[2,256,256]{2,1,0:T(8,128)(2,1)S(1)}, u32[]{:S(2)}, u32[]{:S(2)}) collective-permute-start(bf16[2,256,256]{2,1,0:T(8,128)(2,1)S(1)} %collective-permute-done.3.refs_0_), channel_id=1, source_target_pairs={{0,16},{1,17},{2,18},{3,19},{4,20},{5,21},{6,22},{7,23},{8,24},{9,... | collective-permute-start | bytes 786440 | tf_op jit(solution)/shard_map/ppermute | solution.py:303
  19.9 0.8 collective-permute-start.8
  20.7 3.8 %collective-permute-start.10 = (bf16[2,2,64,256]{3,2,1,0:T(8,128)(2,1)S(1)}, bf16[2,2,64,256]{3,2,1,0:T(8,128)(2,1)S(1)}, u32[]{:S(2)}, u32[]{:S(2)}) collective-permute-start(bf16[2,2,64,256]{3,2,1,0:T(8,128)(2,1)S(1)} %get-tuple-element.131), channel_id=1, source_target_pairs={{0,7},{1,0},{2,1},{3,2},{4,3},{5,4},{6,5},{7,6},{8,15},{9,8},{10,9... | collective-permute-start | bytes 393224 | tf_op jit(solution)/shard_map/ppermute | solution.py:303
  24.5 0.3 collective-permute-start.11
  24.8 0.0 collective-permute-start.12
  24.8 3.3 %collective-permute-done.8.refs_0_ = bf16[2,2,64,256]{3,2,1,0:T(8,128)(2,1)S(1)} collective-permute-done((bf16[2,2,64,256]{3,2,1,0:T(8,128)(2,1)S(1)}, bf16[2,2,64,256]{3,2,1,0:T(8,128)(2,1)S(1)}, u32[]{:S(2)}, u32[]{:S(2)}) %collective-permute-start.8) | collective-permute-done | bytes 131104 | tf_op jit(solution)/shard_map/ppermute | solution.py:303
  28.2 0.0 collective-permute-start.13
  28.2 0.0 collective-permute-done.10.refs_3_
  28.2 4.4 %collective-permute-start.15 = (bf16[2,2,64,256]{3,2,1,0:T(8,128)(2,1)S(1)}, bf16[2,2,64,256]{3,2,1,0:T(8,128)(2,1)S(1)}, u32[]{:S(2)}, u32[]{:S(2)}) collective-permute-start(bf16[2,2,64,256]{3,2,1,0:T(8,128)(2,1)S(1)} %get-tuple-element.136), channel_id=1, source_target_pairs={{0,15},{1,8},{2,9},{3,10},{4,11},{5,12},{6,13},{7,14},{8,7},{9,0},... | collective-permute-start | bytes 393224 | tf_op jit(solution)/shard_map/ppermute | solution.py:303
  32.6 0.0 collective-permute-done.11.refs_4_
  32.6 0.0 collective-permute-start.16
  32.7 0.0 collective-permute-done.12.refs_5_
  32.7 1.5 %collective-permute-start.9 = (bf16[2,2,64,256]{3,2,1,0:T(8,128)(2,1)S(1)}, bf16[2,2,64,256]{3,2,1,0:T(8,128)(2,1)S(1)}, u32[]{:S(2)}, u32[]{:S(2)}) collective-permute-start(bf16[2,2,64,256]{3,2,1,0:T(8,128)(2,1)S(1)} %get-tuple-element.129), channel_id=1, source_target_pairs={{0,1},{1,2},{2,3},{3,4},{4,5},{5,6},{6,7},{7,0},{8,9},{9,10},{10,1... | collective-permute-start | bytes 393224 | tf_op jit(solution)/shard_map/ppermute | solution.py:303
  34.2 1.1 %collective-permute-start.14 = (bf16[2,2,64,256]{3,2,1,0:T(8,128)(2,1)S(1)}, bf16[2,2,64,256]{3,2,1,0:T(8,128)(2,1)S(1)}, u32[]{:S(2)}, u32[]{:S(2)}) collective-permute-start(bf16[2,2,64,256]{3,2,1,0:T(8,128)(2,1)S(1)} %get-tuple-element.135), channel_id=1, source_target_pairs={{0,8},{1,9},{2,10},{3,11},{4,12},{5,13},{6,14},{7,15},{8,0},{9,1},... | collective-permute-start | bytes 393224 | tf_op jit(solution)/shard_map/ppermute | solution.py:303
  35.2 1.1 %copy-done.3 = bf16[768,512]{1,0:T(8,128)(2,1)S(1)} copy-done((bf16[768,512]{1,0:T(8,128)(2,1)S(1)}, bf16[768,512]{1,0:T(8,128)(2,1)}, u32[]{:S(2)}) %copy-start.3) | copy-done | bytes 786456
  36.4 1.0 %start.1 = f32[2,2,256,256]{3,2,1,0:T(8,128)S(1)} custom-call(s32[2,2]{1,0:T(2,128)S(1)} %collective-permute-done.2.refs_2_.places, f32[2,256,256]{2,1,0:T(8,128)S(1)} %copy-done.1, bf16[2,256,256]{2,1,0:T(8,128)(2,1)S(1)} %collective-permute-done.3.refs_0_, bf16[2,256,256]{2,1,0:T(8,128)(2,1)S(1)} %collective-permute-done.7.refs_1_, ...), custom_call_target="tpu_custom_call" | custom-call | flops 1073741824 | bytes 4194304 | tf_op jit(solution)/shard_map/start/pallas_call | solution.py:358
  37.4 0.0 collective-permute-done.13.refs_6_
  37.4 1.6 %collective-permute-done.16.refs_9_ = bf16[2,2,64,256]{3,2,1,0:T(8,128)(2,1)S(1)} collective-permute-done((bf16[2,2,64,256]{3,2,1,0:T(8,128)(2,1)S(1)}, bf16[2,2,64,256]{3,2,1,0:T(8,128)(2,1)S(1)}, u32[]{:S(2)}, u32[]{:S(2)}) %collective-permute-start.16) | collective-permute-done | bytes 131104 | tf_op jit(solution)/shard_map/ppermute | solution.py:303
  39.0 1.4 %collective-permute-done.9.refs_1_ = bf16[2,2,64,256]{3,2,1,0:T(8,128)(2,1)S(1)} collective-permute-done((bf16[2,2,64,256]{3,2,1,0:T(8,128)(2,1)S(1)}, bf16[2,2,64,256]{3,2,1,0:T(8,128)(2,1)S(1)}, u32[]{:S(2)}, u32[]{:S(2)}) %collective-permute-start.9) | collective-permute-done | bytes 131104 | tf_op jit(solution)/shard_map/ppermute | solution.py:303
  40.4 2.0 %near.3 = (bf16[2,2,256,256]{3,2,1,0:T(8,128)(2,1)S(1)}, f32[2,256,256]{2,1,0:T(8,128)S(1)}, bf16[2,256,256]{2,1,0:T(8,128)(2,1)S(1)}) custom-call(s32[2,2]{1,0:T(2,128)S(1)} %collective-permute-done.2.refs_2_.places, f32[2,2,256,256]{3,2,1,0:T(8,128)S(1)} %start.1, bf16[512,768]{1,0:T(8,128)(2,1)S(1)} %copy-done.2, bf16[768,512]{1,0:T(8,128)(2,1)S(1)} %copy-done.4, ...), custom_call_target="tpu_custom_call" | custom-call | flops 1073741824 | bytes 4194304 | tf_op jit(solution)/shard_map/near/pallas_call | solution.py:367
  42.3 0.6 collective-permute-start.18
  43.0 4.4 %near.2 = (bf16[2,2,256,256]{3,2,1,0:T(8,128)(2,1)S(1)}, f32[2,256,256]{2,1,0:T(8,128)S(1)}, bf16[2,256,256]{2,1,0:T(8,128)(2,1)S(1)}) custom-call(s32[2,2]{1,0:T(2,128)S(1)} %collective-permute-done.2.refs_2_.places, f32[2,2,256,256]{3,2,1,0:T(8,128)S(1)} %start.1, bf16[512,768]{1,0:T(8,128)(2,1)S(1)} %copy-done.2, bf16[768,512]{1,0:T(8,128)(2,1)S(1)} %copy-done.4, ...), custom_call_target="tpu_custom_call" | custom-call | flops 1073741824 | bytes 4194304 | tf_op jit(solution)/shard_map/near/pallas_call | solution.py:367
  47.3 1.5 %collective-permute-start.17 = (bf16[2,256,256]{2,1,0:T(8,128)(2,1)S(1)}, bf16[2,256,256]{2,1,0:T(8,128)(2,1)S(1)}, u32[]{:S(2)}, u32[]{:S(2)}) collective-permute-start(bf16[2,256,256]{2,1,0:T(8,128)(2,1)S(1)} %get-tuple-element.140), channel_id=1, source_target_pairs={{0,16},{1,17},{2,18},{3,19},{4,20},{5,21},{6,22},{7,23},{8,24},{9,... | collective-permute-start | bytes 786440 | tf_op jit(solution)/shard_map/ppermute | solution.py:303
  48.9 2.5 %collective-permute-done.18.arrived = bf16[2,256,256]{2,1,0:T(8,128)(2,1)S(1)} collective-permute-done((bf16[2,256,256]{2,1,0:T(8,128)(2,1)S(1)}, bf16[2,256,256]{2,1,0:T(8,128)(2,1)S(1)}, u32[]{:S(2)}, u32[]{:S(2)}) %collective-permute-start.18) | collective-permute-done | bytes 262176 | tf_op jit(solution)/shard_map/ppermute | solution.py:303
  51.3 3.9 %far.3 = (bf16[2,256,256]{2,1,0:T(8,128)(2,1)S(1)}, bf16[2,256,256]{2,1,0:T(8,128)(2,1)S(1)}, f32[2,256,256]{2,1,0:T(8,128)S(1)}) custom-call(f32[2,2,256,256]{3,2,1,0:T(8,128)S(1)} %start.1, bf16[512,768]{1,0:T(8,128)(2,1)S(1)} %copy-done.2, bf16[768,512]{1,0:T(8,128)(2,1)S(1)} %copy-done.4, bf16[2,2,256,256]{3,2,1,0:T(8,128)(2,1)S(1)} %get-tuple-element.142.frames, ...), custom_call_target="tpu_custom_call" | custom-call | flops 2147483648 | bytes 4194304 | tf_op jit(solution)/shard_map/far/pallas_call | solution.py:377
  55.3 0.7 collective-permute-start.20
  56.0 1.0 %collective-permute-done.17.arrived = bf16[2,256,256]{2,1,0:T(8,128)(2,1)S(1)} collective-permute-done((bf16[2,256,256]{2,1,0:T(8,128)(2,1)S(1)}, bf16[2,256,256]{2,1,0:T(8,128)(2,1)S(1)}, u32[]{:S(2)}, u32[]{:S(2)}) %collective-permute-start.17) | collective-permute-done | bytes 262176 | tf_op jit(solution)/shard_map/ppermute | solution.py:303
  56.9 1.5 %far.2 = (bf16[2,256,256]{2,1,0:T(8,128)(2,1)S(1)}, bf16[2,256,256]{2,1,0:T(8,128)(2,1)S(1)}, f32[2,256,256]{2,1,0:T(8,128)S(1)}) custom-call(f32[2,2,256,256]{3,2,1,0:T(8,128)S(1)} %start.1, bf16[512,768]{1,0:T(8,128)(2,1)S(1)} %copy-done.2, bf16[768,512]{1,0:T(8,128)(2,1)S(1)} %copy-done.4, bf16[2,2,256,256]{3,2,1,0:T(8,128)(2,1)S(1)} %get-tuple-element.138.frames, ...), custom_call_target="tpu_custom_call" | custom-call | flops 2147483648 | bytes 4194304 | tf_op jit(solution)/shard_map/far/pallas_call | solution.py:377
  58.5 0.2 collective-permute-start.19
  58.7 1.0 %probe.3 = (f32[2,64,256]{2,1,0:T(8,128)S(1)}, f32[2,64,256]{2,1,0:T(8,128)S(1)}, bf16[2,2,64,256]{3,2,1,0:T(8,128)(2,1)S(1)}) custom-call(s32[2,2]{1,0:T(2,128)S(1)} %collective-permute-done.2.refs_2_.places, f32[2,256,256]{2,1,0:T(8,128)S(1)} %get-tuple-element.141.refs_0_, f32[2,256,256]{2,1,0:T(8,128)S(1)} %get-tuple-element.145.refs_1_), custom_call_target="tpu_custom_call" | custom-call | flops 67108864 | bytes 4194304 | tf_op jit(solution)/shard_map/probe/pallas_call | solution.py:397
  59.7 0.5 collective-permute-start.21
  60.2 0.7 part.1
  60.9 2.4 %collective-permute-start.22 = (bf16[2,2,2,64,256]{4,3,2,1,0:T(8,128)(2,1)S(1)}, bf16[2,2,2,64,256]{4,3,2,1,0:T(8,128)(2,1)S(1)}, u32[]{:S(2)}, u32[]{:S(2)}) collective-permute-start(bf16[2,2,2,64,256]{4,3,2,1,0:T(8,128)(2,1)S(1)} %get-tuple-element.156), channel_id=1, source_target_pairs={{0,6},{1,7},{2,0},{3,1},{4,2},{5,3},{6,4},{7,5},{8,14},{9,15},{10,... | collective-permute-start | bytes 786440 | tf_op jit(solution)/shard_map/ppermute | solution.py:303
  63.3 1.0 %collective-permute-start.23 = (bf16[2,2,2,64,256]{4,3,2,1,0:T(8,128)(2,1)S(1)}, bf16[2,2,2,64,256]{4,3,2,1,0:T(8,128)(2,1)S(1)}, u32[]{:S(2)}, u32[]{:S(2)}) collective-permute-start(bf16[2,2,2,64,256]{4,3,2,1,0:T(8,128)(2,1)S(1)} %get-tuple-element.157), channel_id=1, source_target_pairs={{0,7},{1,0},{2,1},{3,2},{4,3},{5,4},{6,5},{7,6},{8,15},{9,8},{10,9... | collective-permute-start | bytes 786440 | tf_op jit(solution)/shard_map/ppermute | solution.py:303
  64.2 1.1 %collective-permute-start.24 = (bf16[2,2,2,64,256]{4,3,2,1,0:T(8,128)(2,1)S(1)}, bf16[2,2,2,64,256]{4,3,2,1,0:T(8,128)(2,1)S(1)}, u32[]{:S(2)}, u32[]{:S(2)}) collective-permute-start(bf16[2,2,2,64,256]{4,3,2,1,0:T(8,128)(2,1)S(1)} %get-tuple-element.158), channel_id=1, source_target_pairs={{0,1},{1,2},{2,3},{3,4},{4,5},{5,6},{6,7},{7,0},{8,9},{9,10},{10,1... | collective-permute-start | bytes 786440 | tf_op jit(solution)/shard_map/ppermute | solution.py:303
  65.3 0.9 collective-permute-start.25
  66.2 12.1 %while.14 = (s32[]{:T(128)}, f32[2,64,256]{2,1,0:T(8,128)S(1)}, f32[2,64,256]{2,1,0:T(8,128)S(1)}, s32[]{:T(128)}, pred[]{:T(512)}, /*index=5*/bf16[2,2,64,256]{3,2,1,0:T(8,128)(2,1)S(1)}, s32[]{:T(128)}) while((s32[]{:T(128)}, f32[2,64,256]{2,1,0:T(8,128)S(1)}, f32[2,64,256]{2,1,0:T(8,128)S(1)}, s32[]{:T(128)}, pred[]{:T(512)}, ...), condition=%wide.region_1.2_spmd, body=%wide.region_0.1_spmd.sunk | while | flops 327682 | bytes 1507486 | solution.py:425
  66.2 2.5 %collective-permute-start = (bf16[2,64,256]{2,1,0:T(8,128)(2,1)S(1)}, bf16[2,64,256]{2,1,0:T(8,128)(2,1)S(1)}, u32[]{:S(2)}, u32[]{:S(2)}) collective-permute-start(bf16[2,64,256]{2,1,0:T(8,128)(2,1)S(1)} %fusion.5), channel_id=1, source_target_pairs={{0,16},{1,17},{2,18},{3,19},{4,20},{5,21},{6,22},{7,23},{8,24},{9,... | collective-permute-start | bytes 196616 | tf_op jit(solution)/shard_map/while/body/ppermute | solution.py:303
  68.7 1.9 %collective-permute-done = bf16[2,64,256]{2,1,0:T(8,128)(2,1)S(1)} collective-permute-done((bf16[2,64,256]{2,1,0:T(8,128)(2,1)S(1)}, bf16[2,64,256]{2,1,0:T(8,128)(2,1)S(1)}, u32[]{:S(2)}, u32[]{:S(2)}) %collective-permute-start) | collective-permute-done | bytes 65568 | tf_op jit(solution)/shard_map/while/body/ppermute | solution.py:303
  70.6 1.5 %collective-permute-start.1 = (bf16[2,64,256]{2,1,0:T(8,128)(2,1)S(1)}, bf16[2,64,256]{2,1,0:T(8,128)(2,1)S(1)}, u32[]{:S(2)}, u32[]{:S(2)}) collective-permute-start(bf16[2,64,256]{2,1,0:T(8,128)(2,1)S(1)} %get-tuple-element.222), channel_id=1, source_target_pairs={{0,1},{1,0},{2,3},{3,2},{4,5},{5,4},{6,7},{7,6},{8,9},{9,8},{10,11... | collective-permute-start | bytes 196616 | tf_op jit(solution)/shard_map/while/body/ppermute | solution.py:410
  72.1 6.1 %collective-permute-done.1 = bf16[2,64,256]{2,1,0:T(8,128)(2,1)S(1)} collective-permute-done((bf16[2,64,256]{2,1,0:T(8,128)(2,1)S(1)}, bf16[2,64,256]{2,1,0:T(8,128)(2,1)S(1)}, u32[]{:S(2)}, u32[]{:S(2)}) %collective-permute-start.1) | collective-permute-done | bytes 65568 | tf_op jit(solution)/shard_map/while/body/ppermute | solution.py:410
  78.3 0.0 collective-permute-done.22.refs_5_
  78.3 0.0 collective-permute-done.24.refs_8_
  78.3 2.8 %collective-permute-done.25.refs_9_ = bf16[2,2,2,64,256]{4,3,2,1,0:T(8,128)(2,1)S(1)} collective-permute-done((bf16[2,2,2,64,256]{4,3,2,1,0:T(8,128)(2,1)S(1)}, bf16[2,2,2,64,256]{4,3,2,1,0:T(8,128)(2,1)S(1)}, u32[]{:S(2)}, u32[]{:S(2)}) %collective-permute-start.25) | collective-permute-done | bytes 262176 | tf_op jit(solution)/shard_map/ppermute | solution.py:303
  81.2 1.7 %collective-permute-start.26 = (bf16[2,64,256]{2,1,0:T(8,128)(2,1)S(1)}, bf16[2,64,256]{2,1,0:T(8,128)(2,1)S(1)}, u32[]{:S(2)}, u32[]{:S(2)}) collective-permute-start(bf16[2,64,256]{2,1,0:T(8,128)(2,1)S(1)} %convert_element_type.59), channel_id=1, source_target_pairs={{0,2},{1,3},{2,0},{3,1},{4,6},{5,7},{6,4},{7,5},{8,10},{9,11},{10,... | collective-permute-start | bytes 196616 | tf_op jit(solution)/shard_map/ppermute | solution.py:410
  82.9 2.7 %deposit.1 = f32[2,64,3072]{2,1,0:T(8,128)} custom-call(s32[2,2]{1,0:T(2,128)S(1)} %multiply_add_fusion.refs_0_, s32[2,2]{1,0:T(2,128)S(1)} %collective-permute-done.4.refs_1_, s32[2,2]{1,0:T(2,128)S(1)} %collective-permute-done.2.refs_2_.places, s32[2,2]{1,0:T(2,128)S(1)} %collective-permute-done.5.refs_3_, s32[2,2]{1,0:T(2,128)S(1)} %collective-permute-done.6.refs_4_, ...), custom_call_target="tpu_custom_call" | custom-call | flops 67108864 | bytes 4194304 | tf_op jit(solution)/shard_map/deposit/pallas_call | solution.py:430
  85.6 0.0 collective-permute-done.26
  85.6 2.5 %collective-permute-start.27 = (bf16[2,64,256]{2,1,0:T(8,128)(2,1)S(1)}, bf16[2,64,256]{2,1,0:T(8,128)(2,1)S(1)}, u32[]{:S(2)}, u32[]{:S(2)}) collective-permute-start(bf16[2,64,256]{2,1,0:T(8,128)(2,1)S(1)} %convert_add_fusion.4), channel_id=1, source_target_pairs={{0,4},{1,5},{2,6},{3,7},{4,0},{5,1},{6,2},{7,3},{8,12},{9,13},{10,... | collective-permute-start | bytes 196616 | tf_op jit(solution)/shard_map/ppermute | solution.py:410
  88.1 2.7 %collective-permute-done.27 = bf16[2,64,256]{2,1,0:T(8,128)(2,1)S(1)} collective-permute-done((bf16[2,64,256]{2,1,0:T(8,128)(2,1)S(1)}, bf16[2,64,256]{2,1,0:T(8,128)(2,1)S(1)}, u32[]{:S(2)}, u32[]{:S(2)}) %collective-permute-start.27) | collective-permute-done | bytes 65568 | tf_op jit(solution)/shard_map/ppermute | solution.py:410
  90.8 0.7 convert_add_fusion.3
  (24 shorter events, 0.1 us)
Async XLA Ops:
  0.6 5.1 %copy-start.6 = (s32[2,2]{1,0:T(2,128)S(1)}, s32[2,2]{1,0:T(2,128)}, u32[]{:S(2)}) copy-start(s32[2,2]{1,0:T(2,128)} %param.12) | copy-start | bytes 52
  0.6 5.0 %copy-start.5 = (s32[2,2]{1,0:T(2,128)S(1)}, s32[2,2]{1,0:T(2,128)}, u32[]{:S(2)}) copy-start(s32[2,2]{1,0:T(2,128)} %param.13) | copy-start | bytes 52
  0.7 14.6 %copy-start = (f32[1,2,64,3072]{3,2,1,0:T(8,128)S(1)}, f32[1,2,64,3072]{3,2,1,0:T(8,128)}, u32[]{:S(2)}) copy-start(f32[1,2,64,3072]{3,2,1,0:T(8,128)} %param.9) | copy-start | bytes 4718596
  2.6 32.7 %copy-start.1 = (f32[2,256,256]{2,1,0:T(8,128)S(1)}, f32[2,256,256]{2,1,0:T(8,128)}, u32[]{:S(2)}) copy-start(f32[2,256,256]{2,1,0:T(8,128)} %probe.2) | copy-start | bytes 1572868
  2.6 32.6 %copy-start.2 = (bf16[512,768]{1,0:T(8,128)(2,1)S(1)}, bf16[512,768]{1,0:T(8,128)(2,1)}, u32[]{:S(2)}) copy-start(bf16[512,768]{1,0:T(8,128)(2,1)} %constant.46.clone.refs_2_.left) | copy-start | bytes 2359300
  2.6 13.9 %collective-permute-start.3 = (bf16[2,256,256]{2,1,0:T(8,128)(2,1)}, bf16[2,256,256]{2,1,0:T(8,128)(2,1)S(1)}, u32[]{:S(2)}, u32[]{:S(2)}) collective-permute-start(bf16[2,256,256]{2,1,0:T(8,128)(2,1)} %pick.1), channel_id=1, source_target_pairs={{0,2},{1,3},{2,4},{3,5},{4,6},{5,7},{6,0},{7,1},{8,10},{9,11},{10,... | collective-permute-start | bytes 786440 | tf_op jit(solution)/shard_map/ppermute | solution.py:293
  5.7 8.6 %collective-permute-start.2 = (s32[2,2]{1,0:T(2,128)S(1)}, s32[2,2]{1,0:T(2,128)S(1)}, u32[]{:S(2)}, u32[]{:S(2)}) collective-permute-start(s32[2,2]{1,0:T(2,128)S(1)} %multiply_add_fusion.refs_0_), channel_id=1, source_target_pairs={{0,2},{1,3},{2,4},{3,5},{4,6},{5,7},{6,0},{7,1},{8,10},{9,11},{10,... | collective-permute-start | bytes 56 | tf_op jit(solution)/shard_map/ppermute | solution.py:293
  7.3 7.9 %collective-permute-start.4 = (s32[2,2]{1,0:T(2,128)S(1)}, s32[2,2]{1,0:T(2,128)S(1)}, u32[]{:S(2)}, u32[]{:S(2)}) collective-permute-start(s32[2,2]{1,0:T(2,128)S(1)} %multiply_add_fusion.refs_0_), channel_id=1, source_target_pairs={{0,1},{1,2},{2,3},{3,4},{4,5},{5,6},{6,7},{7,0},{8,9},{9,10},{10,1... | collective-permute-start | bytes 56 | tf_op jit(solution)/shard_map/ppermute | solution.py:293
  8.8 6.4 %collective-permute-start.5 = (s32[2,2]{1,0:T(2,128)S(1)}, s32[2,2]{1,0:T(2,128)S(1)}, u32[]{:S(2)}, u32[]{:S(2)}) collective-permute-start(s32[2,2]{1,0:T(2,128)S(1)} %multiply_add_fusion.refs_0_), channel_id=1, source_target_pairs={{0,3},{1,4},{2,5},{3,6},{4,7},{5,0},{6,1},{7,2},{8,11},{9,12},{10,... | collective-permute-start | bytes 56 | tf_op jit(solution)/shard_map/ppermute | solution.py:293
  9.9 5.4 %collective-permute-start.6 = (s32[2,2]{1,0:T(2,128)S(1)}, s32[2,2]{1,0:T(2,128)S(1)}, u32[]{:S(2)}, u32[]{:S(2)}) collective-permute-start(s32[2,2]{1,0:T(2,128)S(1)} %multiply_add_fusion.refs_0_), channel_id=1, source_target_pairs={{0,4},{1,5},{2,6},{3,7},{4,0},{5,1},{6,2},{7,3},{8,12},{9,13},{10,... | collective-permute-start | bytes 56 | tf_op jit(solution)/shard_map/ppermute | solution.py:293
  16.5 17.7 %collective-permute-start.7 = (bf16[2,256,256]{2,1,0:T(8,128)(2,1)S(1)}, bf16[2,256,256]{2,1,0:T(8,128)(2,1)S(1)}, u32[]{:S(2)}, u32[]{:S(2)}) collective-permute-start(bf16[2,256,256]{2,1,0:T(8,128)(2,1)S(1)} %collective-permute-done.3.refs_0_), channel_id=1, source_target_pairs={{0,16},{1,17},{2,18},{3,19},{4,20},{5,21},{6,22},{7,23},{8,24},{9,... | collective-permute-start | bytes 786440 | tf_op jit(solution)/shard_map/ppermute | solution.py:303
  19.9 8.3 %collective-permute-start.8 = (bf16[2,2,64,256]{3,2,1,0:T(8,128)(2,1)S(1)}, bf16[2,2,64,256]{3,2,1,0:T(8,128)(2,1)S(1)}, u32[]{:S(2)}, u32[]{:S(2)}) collective-permute-start(bf16[2,2,64,256]{3,2,1,0:T(8,128)(2,1)S(1)} %get-tuple-element.127), channel_id=1, source_target_pairs={{0,2},{1,3},{2,4},{3,5},{4,6},{5,7},{6,0},{7,1},{8,10},{9,11},{10,... | collective-permute-start | bytes 393224 | tf_op jit(solution)/shard_map/ppermute | solution.py:303
  20.7 7.5 %collective-permute-start.10 = (bf16[2,2,64,256]{3,2,1,0:T(8,128)(2,1)S(1)}, bf16[2,2,64,256]{3,2,1,0:T(8,128)(2,1)S(1)}, u32[]{:S(2)}, u32[]{:S(2)}) collective-permute-start(bf16[2,2,64,256]{3,2,1,0:T(8,128)(2,1)S(1)} %get-tuple-element.131), channel_id=1, source_target_pairs={{0,7},{1,0},{2,1},{3,2},{4,3},{5,4},{6,5},{7,6},{8,15},{9,8},{10,9... | collective-permute-start | bytes 393224 | tf_op jit(solution)/shard_map/ppermute | solution.py:303
  24.5 8.1 %collective-permute-start.11 = (bf16[2,2,64,256]{3,2,1,0:T(8,128)(2,1)S(1)}, bf16[2,2,64,256]{3,2,1,0:T(8,128)(2,1)S(1)}, u32[]{:S(2)}, u32[]{:S(2)}) collective-permute-start(bf16[2,2,64,256]{3,2,1,0:T(8,128)(2,1)S(1)} %get-tuple-element.132), channel_id=1, source_target_pairs={{0,6},{1,7},{2,0},{3,1},{4,2},{5,3},{6,4},{7,5},{8,14},{9,15},{10,... | collective-permute-start | bytes 393224 | tf_op jit(solution)/shard_map/ppermute | solution.py:303
  24.8 7.8 %collective-permute-start.12 = (bf16[2,2,64,256]{3,2,1,0:T(8,128)(2,1)S(1)}, bf16[2,2,64,256]{3,2,1,0:T(8,128)(2,1)S(1)}, u32[]{:S(2)}, u32[]{:S(2)}) collective-permute-start(bf16[2,2,64,256]{3,2,1,0:T(8,128)(2,1)S(1)} %get-tuple-element.133), channel_id=1, source_target_pairs={{0,10},{1,11},{2,12},{3,13},{4,14},{5,15},{6,8},{7,9},{8,2},{9,3},... | collective-permute-start | bytes 393224 | tf_op jit(solution)/shard_map/ppermute | solution.py:303
  28.2 9.2 %collective-permute-start.13 = (bf16[2,2,64,256]{3,2,1,0:T(8,128)(2,1)S(1)}, bf16[2,2,64,256]{3,2,1,0:T(8,128)(2,1)S(1)}, u32[]{:S(2)}, u32[]{:S(2)}) collective-permute-start(bf16[2,2,64,256]{3,2,1,0:T(8,128)(2,1)S(1)} %get-tuple-element.134), channel_id=1, source_target_pairs={{0,9},{1,10},{2,11},{3,12},{4,13},{5,14},{6,15},{7,8},{8,1},{9,2},... | collective-permute-start | bytes 393224 | tf_op jit(solution)/shard_map/ppermute | solution.py:303
  28.2 9.2 %collective-permute-start.15 = (bf16[2,2,64,256]{3,2,1,0:T(8,128)(2,1)S(1)}, bf16[2,2,64,256]{3,2,1,0:T(8,128)(2,1)S(1)}, u32[]{:S(2)}, u32[]{:S(2)}) collective-permute-start(bf16[2,2,64,256]{3,2,1,0:T(8,128)(2,1)S(1)} %get-tuple-element.136), channel_id=1, source_target_pairs={{0,15},{1,8},{2,9},{3,10},{4,11},{5,12},{6,13},{7,14},{8,7},{9,0},... | collective-permute-start | bytes 393224 | tf_op jit(solution)/shard_map/ppermute | solution.py:303
  32.6 6.4 %collective-permute-start.16 = (bf16[2,2,64,256]{3,2,1,0:T(8,128)(2,1)S(1)}, bf16[2,2,64,256]{3,2,1,0:T(8,128)(2,1)S(1)}, u32[]{:S(2)}, u32[]{:S(2)}) collective-permute-start(bf16[2,2,64,256]{3,2,1,0:T(8,128)(2,1)S(1)} %get-tuple-element.137), channel_id=1, source_target_pairs={{0,14},{1,15},{2,8},{3,9},{4,10},{5,11},{6,12},{7,13},{8,6},{9,7},... | collective-permute-start | bytes 393224 | tf_op jit(solution)/shard_map/ppermute | solution.py:303
  32.7 7.7 %collective-permute-start.9 = (bf16[2,2,64,256]{3,2,1,0:T(8,128)(2,1)S(1)}, bf16[2,2,64,256]{3,2,1,0:T(8,128)(2,1)S(1)}, u32[]{:S(2)}, u32[]{:S(2)}) collective-permute-start(bf16[2,2,64,256]{3,2,1,0:T(8,128)(2,1)S(1)} %get-tuple-element.129), channel_id=1, source_target_pairs={{0,1},{1,2},{2,3},{3,4},{4,5},{5,6},{6,7},{7,0},{8,9},{9,10},{10,1... | collective-permute-start | bytes 393224 | tf_op jit(solution)/shard_map/ppermute | solution.py:303
  34.2 6.2 %collective-permute-start.14 = (bf16[2,2,64,256]{3,2,1,0:T(8,128)(2,1)S(1)}, bf16[2,2,64,256]{3,2,1,0:T(8,128)(2,1)S(1)}, u32[]{:S(2)}, u32[]{:S(2)}) collective-permute-start(bf16[2,2,64,256]{3,2,1,0:T(8,128)(2,1)S(1)} %get-tuple-element.135), channel_id=1, source_target_pairs={{0,8},{1,9},{2,10},{3,11},{4,12},{5,13},{6,14},{7,15},{8,0},{9,1},... | collective-permute-start | bytes 393224 | tf_op jit(solution)/shard_map/ppermute | solution.py:303
  35.2 1.1 %copy-start.3 = (bf16[768,512]{1,0:T(8,128)(2,1)S(1)}, bf16[768,512]{1,0:T(8,128)(2,1)}, u32[]{:S(2)}) copy-start(bf16[768,512]{1,0:T(8,128)(2,1)} %constant.47.clone.refs_3_.right) | copy-start | bytes 2359300
  36.4 4.0 %copy-start.4 = (bf16[768,512]{1,0:T(8,128)(2,1)S(1)}, bf16[768,512]{1,0:T(8,128)(2,1)}, u32[]{:S(2)}) copy-start(bf16[768,512]{1,0:T(8,128)(2,1)} %constant.47.clone.refs_3_.right) | copy-start | bytes 2359300
  42.3 9.0 %collective-permute-start.18 = (bf16[2,256,256]{2,1,0:T(8,128)(2,1)S(1)}, bf16[2,256,256]{2,1,0:T(8,128)(2,1)S(1)}, u32[]{:S(2)}, u32[]{:S(2)}) collective-permute-start(bf16[2,256,256]{2,1,0:T(8,128)(2,1)S(1)} %get-tuple-element.144), channel_id=1, source_target_pairs={{0,16},{1,17},{2,18},{3,19},{4,20},{5,21},{6,22},{7,23},{8,24},{9,... | collective-permute-start | bytes 786440 | tf_op jit(solution)/shard_map/ppermute | solution.py:303
  47.3 9.6 %collective-permute-start.17 = (bf16[2,256,256]{2,1,0:T(8,128)(2,1)S(1)}, bf16[2,256,256]{2,1,0:T(8,128)(2,1)S(1)}, u32[]{:S(2)}, u32[]{:S(2)}) collective-permute-start(bf16[2,256,256]{2,1,0:T(8,128)(2,1)S(1)} %get-tuple-element.140), channel_id=1, source_target_pairs={{0,16},{1,17},{2,18},{3,19},{4,20},{5,21},{6,22},{7,23},{8,24},{9,... | collective-permute-start | bytes 786440 | tf_op jit(solution)/shard_map/ppermute | solution.py:303
  55.3 4.9 %collective-permute-start.20 = (bf16[2,256,256]{2,1,0:T(8,128)(2,1)S(1)}, bf16[2,256,256]{2,1,0:T(8,128)(2,1)S(1)}, u32[]{:S(2)}, u32[]{:S(2)}) collective-permute-start(bf16[2,256,256]{2,1,0:T(8,128)(2,1)S(1)} %get-tuple-element.150), channel_id=1, source_target_pairs={{0,8},{1,9},{2,10},{3,11},{4,12},{5,13},{6,14},{7,15},{8,0},{9,1},... | collective-permute-start | bytes 786440 | tf_op jit(solution)/shard_map/ppermute | solution.py:303
  58.5 1.7 %collective-permute-start.19 = (bf16[2,256,256]{2,1,0:T(8,128)(2,1)S(1)}, bf16[2,256,256]{2,1,0:T(8,128)(2,1)S(1)}, u32[]{:S(2)}, u32[]{:S(2)}) collective-permute-start(bf16[2,256,256]{2,1,0:T(8,128)(2,1)S(1)} %get-tuple-element.149), channel_id=1, source_target_pairs={{0,8},{1,9},{2,10},{3,11},{4,12},{5,13},{6,14},{7,15},{8,0},{9,1},... | collective-permute-start | bytes 786440 | tf_op jit(solution)/shard_map/ppermute | solution.py:303
  59.7 6.5 %collective-permute-start.21 = (bf16[2,2,64,256]{3,2,1,0:T(8,128)(2,1)S(1)}, bf16[2,2,64,256]{3,2,1,0:T(8,128)(2,1)S(1)}, u32[]{:S(2)}, u32[]{:S(2)}) collective-permute-start(bf16[2,2,64,256]{3,2,1,0:T(8,128)(2,1)S(1)} %get-tuple-element.154), channel_id=1, source_target_pairs={{0,8},{1,9},{2,10},{3,11},{4,12},{5,13},{6,14},{7,15},{8,0},{9,1},... | collective-permute-start | bytes 393224 | tf_op jit(solution)/shard_map/ppermute | solution.py:303
  60.9 17.4 %collective-permute-start.22 = (bf16[2,2,2,64,256]{4,3,2,1,0:T(8,128)(2,1)S(1)}, bf16[2,2,2,64,256]{4,3,2,1,0:T(8,128)(2,1)S(1)}, u32[]{:S(2)}, u32[]{:S(2)}) collective-permute-start(bf16[2,2,2,64,256]{4,3,2,1,0:T(8,128)(2,1)S(1)} %get-tuple-element.156), channel_id=1, source_target_pairs={{0,6},{1,7},{2,0},{3,1},{4,2},{5,3},{6,4},{7,5},{8,14},{9,15},{10,... | collective-permute-start | bytes 786440 | tf_op jit(solution)/shard_map/ppermute | solution.py:303
  63.3 15.0 %collective-permute-start.23 = (bf16[2,2,2,64,256]{4,3,2,1,0:T(8,128)(2,1)S(1)}, bf16[2,2,2,64,256]{4,3,2,1,0:T(8,128)(2,1)S(1)}, u32[]{:S(2)}, u32[]{:S(2)}) collective-permute-start(bf16[2,2,2,64,256]{4,3,2,1,0:T(8,128)(2,1)S(1)} %get-tuple-element.157), channel_id=1, source_target_pairs={{0,7},{1,0},{2,1},{3,2},{4,3},{5,4},{6,5},{7,6},{8,15},{9,8},{10,9... | collective-permute-start | bytes 786440 | tf_op jit(solution)/shard_map/ppermute | solution.py:303
  64.2 14.1 %collective-permute-start.24 = (bf16[2,2,2,64,256]{4,3,2,1,0:T(8,128)(2,1)S(1)}, bf16[2,2,2,64,256]{4,3,2,1,0:T(8,128)(2,1)S(1)}, u32[]{:S(2)}, u32[]{:S(2)}) collective-permute-start(bf16[2,2,2,64,256]{4,3,2,1,0:T(8,128)(2,1)S(1)} %get-tuple-element.158), channel_id=1, source_target_pairs={{0,1},{1,2},{2,3},{3,4},{4,5},{5,6},{6,7},{7,0},{8,9},{9,10},{10,1... | collective-permute-start | bytes 786440 | tf_op jit(solution)/shard_map/ppermute | solution.py:303
  65.3 15.9 %collective-permute-start.25 = (bf16[2,2,2,64,256]{4,3,2,1,0:T(8,128)(2,1)S(1)}, bf16[2,2,2,64,256]{4,3,2,1,0:T(8,128)(2,1)S(1)}, u32[]{:S(2)}, u32[]{:S(2)}) collective-permute-start(bf16[2,2,2,64,256]{4,3,2,1,0:T(8,128)(2,1)S(1)} %get-tuple-element.159), channel_id=1, source_target_pairs={{0,2},{1,3},{2,4},{3,5},{4,6},{5,7},{6,0},{7,1},{8,10},{9,11},{10,... | collective-permute-start | bytes 786440 | tf_op jit(solution)/shard_map/ppermute | solution.py:303
  66.2 4.4 %collective-permute-start = (bf16[2,64,256]{2,1,0:T(8,128)(2,1)S(1)}, bf16[2,64,256]{2,1,0:T(8,128)(2,1)S(1)}, u32[]{:S(2)}, u32[]{:S(2)}) collective-permute-start(bf16[2,64,256]{2,1,0:T(8,128)(2,1)S(1)} %fusion.5), channel_id=1, source_target_pairs={{0,16},{1,17},{2,18},{3,19},{4,20},{5,21},{6,22},{7,23},{8,24},{9,... | collective-permute-start | bytes 196616 | tf_op jit(solution)/shard_map/while/body/ppermute | solution.py:303
  70.6 7.7 %collective-permute-start.1 = (bf16[2,64,256]{2,1,0:T(8,128)(2,1)S(1)}, bf16[2,64,256]{2,1,0:T(8,128)(2,1)S(1)}, u32[]{:S(2)}, u32[]{:S(2)}) collective-permute-start(bf16[2,64,256]{2,1,0:T(8,128)(2,1)S(1)} %get-tuple-element.222), channel_id=1, source_target_pairs={{0,1},{1,0},{2,3},{3,2},{4,5},{5,4},{6,7},{7,6},{8,9},{9,8},{10,11... | collective-permute-start | bytes 196616 | tf_op jit(solution)/shard_map/while/body/ppermute | solution.py:410
  81.2 4.4 %collective-permute-start.26 = (bf16[2,64,256]{2,1,0:T(8,128)(2,1)S(1)}, bf16[2,64,256]{2,1,0:T(8,128)(2,1)S(1)}, u32[]{:S(2)}, u32[]{:S(2)}) collective-permute-start(bf16[2,64,256]{2,1,0:T(8,128)(2,1)S(1)} %convert_element_type.59), channel_id=1, source_target_pairs={{0,2},{1,3},{2,0},{3,1},{4,6},{5,7},{6,4},{7,5},{8,10},{9,11},{10,... | collective-permute-start | bytes 196616 | tf_op jit(solution)/shard_map/ppermute | solution.py:410
  85.6 5.2 %collective-permute-start.27 = (bf16[2,64,256]{2,1,0:T(8,128)(2,1)S(1)}, bf16[2,64,256]{2,1,0:T(8,128)(2,1)S(1)}, u32[]{:S(2)}, u32[]{:S(2)}) collective-permute-start(bf16[2,64,256]{2,1,0:T(8,128)(2,1)S(1)} %convert_add_fusion.4), channel_id=1, source_target_pairs={{0,4},{1,5},{2,6},{3,7},{4,0},{5,1},{6,2},{7,3},{8,12},{9,13},{10,... | collective-permute-start | bytes 196616 | tf_op jit(solution)/shard_map/ppermute | solution.py:410

commit v8 on v4

--- a/solution.py
+++ b/solution.py
@@ -351,8 +351,10 @@
     adjoint, pieces[0, home] = lax.optimization_barrier((adjoint, pieces[0, home]))
     adjoints = [adjoint, across(adjoint, 2, 0, lower)]
     for flip, step in far_first:
-        if (flip, step) == (1, home):
-            pieces[1, home], pieces[0, 0] = lax.optimization_barrier((pieces[1, home], pieces[0, 0]))
+        if flip == 1 and step in (home, home + 1):
+            pieces[flip, step], pieces[0, 0] = lax.optimization_barrier(
+                (pieces[flip, step], pieces[0, 0])
+            )
         pieces[flip, step] = across(pieces[flip, step], flip, home - step)
 
     start = call(

time: 88.7 us -> 88.4 us (level)
  waiting for transfers between devices: 27.7 us -> 25.5 us
  starting transfers between devices: 37.6 us -> 39.5 us
    ppermute x3, waiting for transfers between devices: 12.8 us -> 10.5 us  [scan_round(): lax.ppermute(rounded, 'scan', route).astype(f32)]
    ppermute x3, starting transfers between devices: 2.72 us -> 4.49 us  [scan_round(): lax.ppermute(rounded, 'scan', route).astype(f32)]
where the time goes in v8:
time: 88.4 us; the launch traced here: 88.2 us
  starting transfers between devices  39.5 us (45%)
  waiting for transfers between devices  25.5 us (29%)
  Pallas kernels  20.3 us (23%)
  local copies, waits for them, and re-layouts  1.16 us (1%)
    ppermute x20, starting transfers between devices, across(): return lax.ppermute(value, ('depth', 'scan'), route)  25.1 us
    ppermute x20, waiting for transfers between devices, across(): return lax.ppermute(value, ('depth', 'scan'), route)  12.4 us
    ppermute x3, waiting for transfers between devices, scan_round(): lax.ppermute(rounded, 'scan', route).astype(f32)  10.5 us
    ppermute x5, starting transfers between devices, along_scan(): lax.ppermute(value, 'scan', [(i, (i + by) % regions) for i in range(regio...  9.99 us
    pallas_call x2, Pallas kernels, local(): call(functools.partial(near_kernel, home, turn, turn == count - 1, width)...  6.36 us
    pallas_call x2, Pallas kernels, local(): call(functools.partial(far_kernel, turn, turn == count - 1), [shape(wave,...  5.47 us
    ppermute x3, starting transfers between devices, scan_round(): lax.ppermute(rounded, 'scan', route).astype(f32)  4.49 us
    pallas_call x1, Pallas kernels, local(): call(functools.partial(deposit_kernel, reach), shape(transmission.shape[1...  2.69 us
  transfers between devices with their start and end apart: 28, of which 12 were waited for; matrix products, arithmetic and copies ran while one was open for 0% of the time, Pallas kernels for 19%

profile of v8, /device:TPU:0, one launch (start us, length us, event | category | flops | bytes accessed | tf_op | source)
XLA Modules:
  0.0 88.2 jit_solution(13954045250622808887)
XLA Ops:
  0.7 1.9 %pick.1 = bf16[2,256,256]{2,1,0:T(8,128)(2,1)} custom-call(f32[2,2,2,256,256]{4,3,2,1,0:T(8,128)} %waves.1), custom_call_target="tpu_custom_call" | custom-call | flops 1048576 | bytes 4194304 | tf_op jit(solution)/shard_map/pick/pallas_call | solution.py:327
  2.6 0.0 copy-start.1
  2.6 0.0 copy-start.2
  2.6 3.1 %collective-permute-start.7 = (bf16[2,256,256]{2,1,0:T(8,128)(2,1)}, bf16[2,256,256]{2,1,0:T(8,128)(2,1)S(1)}, u32[]{:S(2)}, u32[]{:S(2)}) collective-permute-start(bf16[2,256,256]{2,1,0:T(8,128)(2,1)} %pick.1), channel_id=1, source_target_pairs={{0,2},{1,3},{2,4},{3,5},{4,6},{5,7},{6,0},{7,1},{8,10},{9,11},{10,... | collective-permute-start | bytes 786440 | tf_op jit(solution)/shard_map/ppermute | solution.py:293
  5.7 1.6 %collective-permute-start.4 = (s32[2,2]{1,0:T(2,128)S(1)}, s32[2,2]{1,0:T(2,128)S(1)}, u32[]{:S(2)}, u32[]{:S(2)}) collective-permute-start(s32[2,2]{1,0:T(2,128)S(1)} %multiply_add_fusion.refs_0_), channel_id=1, source_target_pairs={{0,2},{1,3},{2,4},{3,5},{4,6},{5,7},{6,0},{7,1},{8,10},{9,11},{10,... | collective-permute-start | bytes 56 | tf_op jit(solution)/shard_map/ppermute | solution.py:293
  7.3 1.5 %collective-permute-start.3 = (s32[2,2]{1,0:T(2,128)S(1)}, s32[2,2]{1,0:T(2,128)S(1)}, u32[]{:S(2)}, u32[]{:S(2)}) collective-permute-start(s32[2,2]{1,0:T(2,128)S(1)} %multiply_add_fusion.refs_0_), channel_id=1, source_target_pairs={{0,1},{1,2},{2,3},{3,4},{4,5},{5,6},{6,7},{7,0},{8,9},{9,10},{10,1... | collective-permute-start | bytes 56 | tf_op jit(solution)/shard_map/ppermute | solution.py:293
  8.8 1.0 %collective-permute-start.5 = (s32[2,2]{1,0:T(2,128)S(1)}, s32[2,2]{1,0:T(2,128)S(1)}, u32[]{:S(2)}, u32[]{:S(2)}) collective-permute-start(s32[2,2]{1,0:T(2,128)S(1)} %multiply_add_fusion.refs_0_), channel_id=1, source_target_pairs={{0,3},{1,4},{2,5},{3,6},{4,7},{5,0},{6,1},{7,2},{8,11},{9,12},{10,... | collective-permute-start | bytes 56 | tf_op jit(solution)/shard_map/ppermute | solution.py:293
  9.9 2.7 %collective-permute-start.6 = (s32[2,2]{1,0:T(2,128)S(1)}, s32[2,2]{1,0:T(2,128)S(1)}, u32[]{:S(2)}, u32[]{:S(2)}) collective-permute-start(s32[2,2]{1,0:T(2,128)S(1)} %multiply_add_fusion.refs_0_), channel_id=1, source_target_pairs={{0,4},{1,5},{2,6},{3,7},{4,0},{5,1},{6,2},{7,3},{8,12},{9,13},{10,... | collective-permute-start | bytes 56 | tf_op jit(solution)/shard_map/ppermute | solution.py:293
  12.6 1.7 %collective-permute-done.4.refs_2_.places = s32[2,2]{1,0:T(2,128)S(1)} collective-permute-done((s32[2,2]{1,0:T(2,128)S(1)}, s32[2,2]{1,0:T(2,128)S(1)}, u32[]{:S(2)}, u32[]{:S(2)}) %collective-permute-start.4) | collective-permute-done | bytes 48 | tf_op jit(solution)/shard_map/ppermute | solution.py:293
  14.3 1.0 %collective-permute-done.3.refs_1_ = s32[2,2]{1,0:T(2,128)S(1)} collective-permute-done((s32[2,2]{1,0:T(2,128)S(1)}, s32[2,2]{1,0:T(2,128)S(1)}, u32[]{:S(2)}, u32[]{:S(2)}) %collective-permute-start.3) | collective-permute-done | bytes 48 | tf_op jit(solution)/shard_map/ppermute | solution.py:293
  15.3 0.0 collective-permute-done.5.refs_3_
  15.3 0.0 collective-permute-done.6.refs_4_
  15.3 1.2 %extract.1 = (bf16[2,2,64,256]{3,2,1,0:T(8,128)(2,1)S(1)}, bf16[2,2,64,256]{3,2,1,0:T(8,128)(2,1)S(1)}, bf16[2,2,64,256]{3,2,1,0:T(8,128)(2,1)S(1)}, bf16[2,2,64...) custom-call(s32[2,2]{1,0:T(2,128)S(1)} %multiply_add_fusion.refs_0_,, ...), custom_call_target="tpu_custom_call" | custom-call | flops 67108864 | bytes 4194304 | tf_op jit(solution)/shard_map/extract/pallas_call | solution.py:343
  16.5 0.0 collective-permute-done.7.refs_0_
  16.5 3.4 %collective-permute-start.8 = (bf16[2,256,256]{2,1,0:T(8,128)(2,1)S(1)}, bf16[2,256,256]{2,1,0:T(8,128)(2,1)S(1)}, u32[]{:S(2)}, u32[]{:S(2)}) collective-permute-start(bf16[2,256,256]{2,1,0:T(8,128)(2,1)S(1)} %collective-permute-done.7.refs_0_), channel_id=1, source_target_pairs={{0,16},{1,17},{2,18},{3,19},{4,20},{5,21},{6,22},{7,23},{8,24},{9,... | collective-permute-start | bytes 786440 | tf_op jit(solution)/shard_map/ppermute | solution.py:303
  19.9 0.8 collective-permute-start.9
  20.7 1.5 %collective-permute-start.10 = (bf16[2,2,64,256]{3,2,1,0:T(8,128)(2,1)S(1)}, bf16[2,2,64,256]{3,2,1,0:T(8,128)(2,1)S(1)}, u32[]{:S(2)}, u32[]{:S(2)}) collective-permute-start(bf16[2,2,64,256]{3,2,1,0:T(8,128)(2,1)S(1)} %get-tuple-element.131), channel_id=1, source_target_pairs={{0,1},{1,2},{2,3},{3,4},{4,5},{5,6},{6,7},{7,0},{8,9},{9,10},{10,1... | collective-permute-start | bytes 393224 | tf_op jit(solution)/shard_map/ppermute | solution.py:303
  22.2 3.2 %collective-permute-start.11 = (bf16[2,2,64,256]{3,2,1,0:T(8,128)(2,1)S(1)}, bf16[2,2,64,256]{3,2,1,0:T(8,128)(2,1)S(1)}, u32[]{:S(2)}, u32[]{:S(2)}) collective-permute-start(bf16[2,2,64,256]{3,2,1,0:T(8,128)(2,1)S(1)} %get-tuple-element.133), channel_id=1, source_target_pairs={{0,7},{1,0},{2,1},{3,2},{4,3},{5,4},{6,5},{7,6},{8,15},{9,8},{10,9... | collective-permute-start | bytes 393224 | tf_op jit(solution)/shard_map/ppermute | solution.py:303
  25.4 1.2 %collective-permute-start.12 = (bf16[2,2,64,256]{3,2,1,0:T(8,128)(2,1)S(1)}, bf16[2,2,64,256]{3,2,1,0:T(8,128)(2,1)S(1)}, u32[]{:S(2)}, u32[]{:S(2)}) collective-permute-start(bf16[2,2,64,256]{3,2,1,0:T(8,128)(2,1)S(1)} %get-tuple-element.134), channel_id=1, source_target_pairs={{0,6},{1,7},{2,0},{3,1},{4,2},{5,3},{6,4},{7,5},{8,14},{9,15},{10,... | collective-permute-start | bytes 393224 | tf_op jit(solution)/shard_map/ppermute | solution.py:303
  26.7 1.4 %collective-permute-done.9.refs_0_ = bf16[2,2,64,256]{3,2,1,0:T(8,128)(2,1)S(1)} collective-permute-done((bf16[2,2,64,256]{3,2,1,0:T(8,128)(2,1)S(1)}, bf16[2,2,64,256]{3,2,1,0:T(8,128)(2,1)S(1)}, u32[]{:S(2)}, u32[]{:S(2)}) %collective-permute-start.9) | collective-permute-done | bytes 131104 | tf_op jit(solution)/shard_map/ppermute | solution.py:303
  28.1 0.0 collective-permute-start.13
  28.1 2.1 %collective-permute-done.10.refs_1_ = bf16[2,2,64,256]{3,2,1,0:T(8,128)(2,1)S(1)} collective-permute-done((bf16[2,2,64,256]{3,2,1,0:T(8,128)(2,1)S(1)}, bf16[2,2,64,256]{3,2,1,0:T(8,128)(2,1)S(1)}, u32[]{:S(2)}, u32[]{:S(2)}) %collective-permute-start.10) | collective-permute-done | bytes 131104 | tf_op jit(solution)/shard_map/ppermute | solution.py:303
  30.2 0.0 collective-permute-start.14
  30.2 0.0 collective-permute-done.11.refs_3_
  30.2 1.5 %collective-permute-start.17 = (bf16[2,2,64,256]{3,2,1,0:T(8,128)(2,1)S(1)}, bf16[2,2,64,256]{3,2,1,0:T(8,128)(2,1)S(1)}, u32[]{:S(2)}, u32[]{:S(2)}) collective-permute-start(bf16[2,2,64,256]{3,2,1,0:T(8,128)(2,1)S(1)} %get-tuple-element.139), channel_id=1, source_target_pairs={{0,14},{1,15},{2,8},{3,9},{4,10},{5,11},{6,12},{7,13},{8,6},{9,7},... | collective-permute-start | bytes 393224 | tf_op jit(solution)/shard_map/ppermute | solution.py:303
  31.7 0.0 collective-permute-done.12.refs_4_
  31.7 1.2 %collective-permute-start.15 = (bf16[2,2,64,256]{3,2,1,0:T(8,128)(2,1)S(1)}, bf16[2,2,64,256]{3,2,1,0:T(8,128)(2,1)S(1)}, u32[]{:S(2)}, u32[]{:S(2)}) collective-permute-start(bf16[2,2,64,256]{3,2,1,0:T(8,128)(2,1)S(1)} %get-tuple-element.137), channel_id=1, source_target_pairs={{0,8},{1,9},{2,10},{3,11},{4,12},{5,13},{6,14},{7,15},{8,0},{9,1},... | collective-permute-start | bytes 393224 | tf_op jit(solution)/shard_map/ppermute | solution.py:303
  32.9 0.0 collective-permute-done.8.refs_1_
  32.9 1.9 %collective-permute-start.16 = (bf16[2,2,64,256]{3,2,1,0:T(8,128)(2,1)S(1)}, bf16[2,2,64,256]{3,2,1,0:T(8,128)(2,1)S(1)}, u32[]{:S(2)}, u32[]{:S(2)}) collective-permute-start(bf16[2,2,64,256]{3,2,1,0:T(8,128)(2,1)S(1)} %get-tuple-element.138), channel_id=1, source_target_pairs={{0,15},{1,8},{2,9},{3,10},{4,11},{5,12},{6,13},{7,14},{8,7},{9,0},... | collective-permute-start | bytes 393224 | tf_op jit(solution)/shard_map/ppermute | solution.py:303
  34.9 1.1 %copy-done.3 = bf16[768,512]{1,0:T(8,128)(2,1)S(1)} copy-done((bf16[768,512]{1,0:T(8,128)(2,1)S(1)}, bf16[768,512]{1,0:T(8,128)(2,1)}, u32[]{:S(2)}) %copy-start.3) | copy-done | bytes 786456
  36.0 1.0 %start.1 = f32[2,2,256,256]{3,2,1,0:T(8,128)S(1)} custom-call(s32[2,2]{1,0:T(2,128)S(1)} %collective-permute-done.4.refs_2_.places, f32[2,256,256]{2,1,0:T(8,128)S(1)} %copy-done.1, bf16[2,256,256]{2,1,0:T(8,128)(2,1)S(1)} %collective-permute-done.7.refs_0_, bf16[2,256,256]{2,1,0:T(8,128)(2,1)S(1)} %collective-permute-done.8.refs_1_, ...), custom_call_target="tpu_custom_call" | custom-call | flops 1073741824 | bytes 4194304 | tf_op jit(solution)/shard_map/start/pallas_call | solution.py:360
  37.0 0.0 collective-permute-done.13.refs_5_
  37.0 2.1 %collective-permute-done.14.refs_6_ = bf16[2,2,64,256]{3,2,1,0:T(8,128)(2,1)S(1)} collective-permute-done((bf16[2,2,64,256]{3,2,1,0:T(8,128)(2,1)S(1)}, bf16[2,2,64,256]{3,2,1,0:T(8,128)(2,1)S(1)}, u32[]{:S(2)}, u32[]{:S(2)}) %collective-permute-start.14) | collective-permute-done | bytes 131104 | tf_op jit(solution)/shard_map/ppermute | solution.py:303
  39.2 0.0 collective-permute-done.17.refs_9_
  39.2 1.4 %collective-permute-done.16.refs_8_ = bf16[2,2,64,256]{3,2,1,0:T(8,128)(2,1)S(1)} collective-permute-done((bf16[2,2,64,256]{3,2,1,0:T(8,128)(2,1)S(1)}, bf16[2,2,64,256]{3,2,1,0:T(8,128)(2,1)S(1)}, u32[]{:S(2)}, u32[]{:S(2)}) %collective-permute-start.16) | collective-permute-done | bytes 131104 | tf_op jit(solution)/shard_map/ppermute | solution.py:303
  40.5 2.0 %near.3 = (bf16[2,2,256,256]{3,2,1,0:T(8,128)(2,1)S(1)}, f32[2,256,256]{2,1,0:T(8,128)S(1)}, bf16[2,256,256]{2,1,0:T(8,128)(2,1)S(1)}) custom-call(s32[2,2]{1,0:T(2,128)S(1)} %collective-permute-done.4.refs_2_.places, f32[2,2,256,256]{3,2,1,0:T(8,128)S(1)} %start.1, bf16[512,768]{1,0:T(8,128)(2,1)S(1)} %copy-done.2, bf16[768,512]{1,0:T(8,128)(2,1)S(1)} %copy-done.4, ...), custom_call_target="tpu_custom_call" | custom-call | flops 1073741824 | bytes 4194304 | tf_op jit(solution)/shard_map/near/pallas_call | solution.py:369
  42.5 0.1 collective-permute-start.19
  42.6 4.4 %near.2 = (bf16[2,2,256,256]{3,2,1,0:T(8,128)(2,1)S(1)}, f32[2,256,256]{2,1,0:T(8,128)S(1)}, bf16[2,256,256]{2,1,0:T(8,128)(2,1)S(1)}) custom-call(s32[2,2]{1,0:T(2,128)S(1)} %collective-permute-done.4.refs_2_.places, f32[2,2,256,256]{3,2,1,0:T(8,128)S(1)} %start.1, bf16[512,768]{1,0:T(8,128)(2,1)S(1)} %copy-done.2, bf16[768,512]{1,0:T(8,128)(2,1)S(1)} %copy-done.4, ...), custom_call_target="tpu_custom_call" | custom-call | flops 1073741824 | bytes 4194304 | tf_op jit(solution)/shard_map/near/pallas_call | solution.py:369
  47.0 2.1 %collective-permute-start.18 = (bf16[2,256,256]{2,1,0:T(8,128)(2,1)S(1)}, bf16[2,256,256]{2,1,0:T(8,128)(2,1)S(1)}, u32[]{:S(2)}, u32[]{:S(2)}) collective-permute-start(bf16[2,256,256]{2,1,0:T(8,128)(2,1)S(1)} %get-tuple-element.142), channel_id=1, source_target_pairs={{0,16},{1,17},{2,18},{3,19},{4,20},{5,21},{6,22},{7,23},{8,24},{9,... | collective-permute-start | bytes 786440 | tf_op jit(solution)/shard_map/ppermute | solution.py:303
  49.1 2.7 %collective-permute-done.19.arrived = bf16[2,256,256]{2,1,0:T(8,128)(2,1)S(1)} collective-permute-done((bf16[2,256,256]{2,1,0:T(8,128)(2,1)S(1)}, bf16[2,256,256]{2,1,0:T(8,128)(2,1)S(1)}, u32[]{:S(2)}, u32[]{:S(2)}) %collective-permute-start.19) | collective-permute-done | bytes 262176 | tf_op jit(solution)/shard_map/ppermute | solution.py:303
  51.7 3.9 %far.3 = (bf16[2,256,256]{2,1,0:T(8,128)(2,1)S(1)}, bf16[2,256,256]{2,1,0:T(8,128)(2,1)S(1)}, f32[2,256,256]{2,1,0:T(8,128)S(1)}) custom-call(f32[2,2,256,256]{3,2,1,0:T(8,128)S(1)} %start.1, bf16[512,768]{1,0:T(8,128)(2,1)S(1)} %copy-done.2, bf16[768,512]{1,0:T(8,128)(2,1)S(1)} %copy-done.4, bf16[2,2,256,256]{3,2,1,0:T(8,128)(2,1)S(1)} %get-tuple-element.144.frames, ...), custom_call_target="tpu_custom_call" | custom-call | flops 2147483648 | bytes 4194304 | tf_op jit(solution)/shard_map/far/pallas_call | solution.py:379
  55.7 0.1 collective-permute-start.21
  55.8 0.8 collective-permute-done.18.arrived
  56.5 1.5 %far.2 = (bf16[2,256,256]{2,1,0:T(8,128)(2,1)S(1)}, bf16[2,256,256]{2,1,0:T(8,128)(2,1)S(1)}, f32[2,256,256]{2,1,0:T(8,128)S(1)}) custom-call(f32[2,2,256,256]{3,2,1,0:T(8,128)S(1)} %start.1, bf16[512,768]{1,0:T(8,128)(2,1)S(1)} %copy-done.2, bf16[768,512]{1,0:T(8,128)(2,1)S(1)} %copy-done.4, bf16[2,2,256,256]{3,2,1,0:T(8,128)(2,1)S(1)} %get-tuple-element.140.frames, ...), custom_call_target="tpu_custom_call" | custom-call | flops 2147483648 | bytes 4194304 | tf_op jit(solution)/shard_map/far/pallas_call | solution.py:379
  58.1 0.1 collective-permute-start.20
  58.1 1.1 %probe.3 = (f32[2,64,256]{2,1,0:T(8,128)S(1)}, f32[2,64,256]{2,1,0:T(8,128)S(1)}, bf16[2,2,64,256]{3,2,1,0:T(8,128)(2,1)S(1)}) custom-call(s32[2,2]{1,0:T(2,128)S(1)} %collective-permute-done.4.refs_2_.places, f32[2,256,256]{2,1,0:T(8,128)S(1)} %get-tuple-element.143.refs_0_, f32[2,256,256]{2,1,0:T(8,128)S(1)} %get-tuple-element.147.refs_1_), custom_call_target="tpu_custom_call" | custom-call | flops 67108864 | bytes 4194304 | tf_op jit(solution)/shard_map/probe/pallas_call | solution.py:399
  59.2 0.6 collective-permute-start.22
  59.8 0.7 part.1
  60.5 0.1 collective-permute-start.23
  60.6 2.8 %collective-permute-start.24 = (bf16[2,2,2,64,256]{4,3,2,1,0:T(8,128)(2,1)S(1)}, bf16[2,2,2,64,256]{4,3,2,1,0:T(8,128)(2,1)S(1)}, u32[]{:S(2)}, u32[]{:S(2)}) collective-permute-start(bf16[2,2,2,64,256]{4,3,2,1,0:T(8,128)(2,1)S(1)} %get-tuple-element.159), channel_id=1, source_target_pairs={{0,7},{1,0},{2,1},{3,2},{4,3},{5,4},{6,5},{7,6},{8,15},{9,8},{10,9... | collective-permute-start | bytes 786440 | tf_op jit(solution)/shard_map/ppermute | solution.py:303
  63.4 0.5 collective-permute-start.25
  63.9 1.5 %collective-permute-start.26 = (bf16[2,2,2,64,256]{4,3,2,1,0:T(8,128)(2,1)S(1)}, bf16[2,2,2,64,256]{4,3,2,1,0:T(8,128)(2,1)S(1)}, u32[]{:S(2)}, u32[]{:S(2)}) collective-permute-start(bf16[2,2,2,64,256]{4,3,2,1,0:T(8,128)(2,1)S(1)} %get-tuple-element.161), channel_id=1, source_target_pairs={{0,2},{1,3},{2,4},{3,5},{4,6},{5,7},{6,0},{7,1},{8,10},{9,11},{10,... | collective-permute-start | bytes 786440 | tf_op jit(solution)/shard_map/ppermute | solution.py:303
  65.3 16.2 %while.14 = (s32[]{:T(128)}, f32[2,64,256]{2,1,0:T(8,128)S(1)}, f32[2,64,256]{2,1,0:T(8,128)S(1)}, s32[]{:T(128)}, pred[]{:T(512)}, /*index=5*/bf16[2,2,64,256]{3,2,1,0:T(8,128)(2,1)S(1)}, s32[]{:T(128)}) while((s32[]{:T(128)}, f32[2,64,256]{2,1,0:T(8,128)S(1)}, f32[2,64,256]{2,1,0:T(8,128)S(1)}, s32[]{:T(128)}, pred[]{:T(512)}, ...), condition=%wide.region_1.2_spmd, body=%wide.region_0.1_spmd.sunk | while | flops 458754 | bytes 1966278 | solution.py:427
  65.3 2.5 %collective-permute-start = (bf16[2,64,256]{2,1,0:T(8,128)(2,1)S(1)}, bf16[2,64,256]{2,1,0:T(8,128)(2,1)S(1)}, u32[]{:S(2)}, u32[]{:S(2)}) collective-permute-start(bf16[2,64,256]{2,1,0:T(8,128)(2,1)S(1)} %fusion.5), channel_id=1, source_target_pairs={{0,16},{1,17},{2,18},{3,19},{4,20},{5,21},{6,22},{7,23},{8,24},{9,... | collective-permute-start | bytes 196616 | tf_op jit(solution)/shard_map/while/body/ppermute | solution.py:303
  67.8 1.9 %collective-permute-done = bf16[2,64,256]{2,1,0:T(8,128)(2,1)S(1)} collective-permute-done((bf16[2,64,256]{2,1,0:T(8,128)(2,1)S(1)}, bf16[2,64,256]{2,1,0:T(8,128)(2,1)S(1)}, u32[]{:S(2)}, u32[]{:S(2)}) %collective-permute-start) | collective-permute-done | bytes 65568 | tf_op jit(solution)/shard_map/while/body/ppermute | solution.py:303
  69.7 1.5 %collective-permute-start.1 = (bf16[2,64,256]{2,1,0:T(8,128)(2,1)S(1)}, bf16[2,64,256]{2,1,0:T(8,128)(2,1)S(1)}, u32[]{:S(2)}, u32[]{:S(2)}) collective-permute-start(bf16[2,64,256]{2,1,0:T(8,128)(2,1)S(1)} %get-tuple-element.222), channel_id=1, source_target_pairs={{0,1},{1,0},{2,3},{3,2},{4,5},{5,4},{6,7},{7,6},{8,9},{9,8},{10,11... | collective-permute-start | bytes 196616 | tf_op jit(solution)/shard_map/while/body/ppermute | solution.py:412
  71.3 5.9 %collective-permute-done.1 = bf16[2,64,256]{2,1,0:T(8,128)(2,1)S(1)} collective-permute-done((bf16[2,64,256]{2,1,0:T(8,128)(2,1)S(1)}, bf16[2,64,256]{2,1,0:T(8,128)(2,1)S(1)}, u32[]{:S(2)}, u32[]{:S(2)}) %collective-permute-start.1) | collective-permute-done | bytes 65568 | tf_op jit(solution)/shard_map/while/body/ppermute | solution.py:412
  77.1 0.8 collective-permute-start.2
  77.9 3.5 %collective-permute-done.2 = bf16[2,64,256]{2,1,0:T(8,128)(2,1)S(1)} collective-permute-done((bf16[2,64,256]{2,1,0:T(8,128)(2,1)S(1)}, bf16[2,64,256]{2,1,0:T(8,128)(2,1)S(1)}, u32[]{:S(2)}, u32[]{:S(2)}) %collective-permute-start.2) | collective-permute-done | bytes 65568 | tf_op jit(solution)/shard_map/while/body/ppermute | solution.py:412
  81.5 0.0 collective-permute-done.24.refs_6_
  81.6 2.2 %collective-permute-start.27 = (bf16[2,64,256]{2,1,0:T(8,128)(2,1)S(1)}, bf16[2,64,256]{2,1,0:T(8,128)(2,1)S(1)}, u32[]{:S(2)}, u32[]{:S(2)}) collective-permute-start(bf16[2,64,256]{2,1,0:T(8,128)(2,1)S(1)} %convert_element_type.65), channel_id=1, source_target_pairs={{0,4},{1,5},{2,6},{3,7},{4,0},{5,1},{6,2},{7,3},{8,12},{9,13},{10,... | collective-permute-start | bytes 196616 | tf_op jit(solution)/shard_map/ppermute | solution.py:412
  83.7 2.7 %deposit.1 = f32[2,64,3072]{2,1,0:T(8,128)} custom-call(s32[2,2]{1,0:T(2,128)S(1)} %multiply_add_fusion.refs_0_, s32[2,2]{1,0:T(2,128)S(1)} %collective-permute-done.3.refs_1_, s32[2,2]{1,0:T(2,128)S(1)} %collective-permute-done.4.refs_2_.places, s32[2,2]{1,0:T(2,128)S(1)} %collective-permute-done.5.refs_3_, s32[2,2]{1,0:T(2,128)S(1)} %collective-permute-done.6.refs_4_, ...), custom_call_target="tpu_custom_call" | custom-call | flops 67108864 | bytes 4194304 | tf_op jit(solution)/shard_map/deposit/pallas_call | solution.py:432
  86.4 1.1 %collective-permute-done.27 = bf16[2,64,256]{2,1,0:T(8,128)(2,1)S(1)} collective-permute-done((bf16[2,64,256]{2,1,0:T(8,128)(2,1)S(1)}, bf16[2,64,256]{2,1,0:T(8,128)(2,1)S(1)}, u32[]{:S(2)}, u32[]{:S(2)}) %collective-permute-start.27) | collective-permute-done | bytes 65568 | tf_op jit(solution)/shard_map/ppermute | solution.py:412
  87.5 0.7 convert_add_fusion.3
  (24 shorter events, 0.1 us)
Async XLA Ops:
  0.6 5.1 %copy-start.6 = (s32[2,2]{1,0:T(2,128)S(1)}, s32[2,2]{1,0:T(2,128)}, u32[]{:S(2)}) copy-start(s32[2,2]{1,0:T(2,128)} %param.12) | copy-start | bytes 52
  0.6 5.0 %copy-start.5 = (s32[2,2]{1,0:T(2,128)S(1)}, s32[2,2]{1,0:T(2,128)}, u32[]{:S(2)}) copy-start(s32[2,2]{1,0:T(2,128)} %param.13) | copy-start | bytes 52
  0.7 14.6 %copy-start = (f32[1,2,64,3072]{3,2,1,0:T(8,128)S(1)}, f32[1,2,64,3072]{3,2,1,0:T(8,128)}, u32[]{:S(2)}) copy-start(f32[1,2,64,3072]{3,2,1,0:T(8,128)} %param.9) | copy-start | bytes 4718596
  2.6 32.3 %copy-start.1 = (f32[2,256,256]{2,1,0:T(8,128)S(1)}, f32[2,256,256]{2,1,0:T(8,128)}, u32[]{:S(2)}) copy-start(f32[2,256,256]{2,1,0:T(8,128)} %probe.2) | copy-start | bytes 1572868
  2.6 32.3 %copy-start.2 = (bf16[512,768]{1,0:T(8,128)(2,1)S(1)}, bf16[512,768]{1,0:T(8,128)(2,1)}, u32[]{:S(2)}) copy-start(bf16[512,768]{1,0:T(8,128)(2,1)} %constant.46.clone.refs_2_.left) | copy-start | bytes 2359300
  2.6 13.9 %collective-permute-start.7 = (bf16[2,256,256]{2,1,0:T(8,128)(2,1)}, bf16[2,256,256]{2,1,0:T(8,128)(2,1)S(1)}, u32[]{:S(2)}, u32[]{:S(2)}) collective-permute-start(bf16[2,256,256]{2,1,0:T(8,128)(2,1)} %pick.1), channel_id=1, source_target_pairs={{0,2},{1,3},{2,4},{3,5},{4,6},{5,7},{6,0},{7,1},{8,10},{9,11},{10,... | collective-permute-start | bytes 786440 | tf_op jit(solution)/shard_map/ppermute | solution.py:293
  5.7 8.6 %collective-permute-start.4 = (s32[2,2]{1,0:T(2,128)S(1)}, s32[2,2]{1,0:T(2,128)S(1)}, u32[]{:S(2)}, u32[]{:S(2)}) collective-permute-start(s32[2,2]{1,0:T(2,128)S(1)} %multiply_add_fusion.refs_0_), channel_id=1, source_target_pairs={{0,2},{1,3},{2,4},{3,5},{4,6},{5,7},{6,0},{7,1},{8,10},{9,11},{10,... | collective-permute-start | bytes 56 | tf_op jit(solution)/shard_map/ppermute | solution.py:293
  7.3 7.9 %collective-permute-start.3 = (s32[2,2]{1,0:T(2,128)S(1)}, s32[2,2]{1,0:T(2,128)S(1)}, u32[]{:S(2)}, u32[]{:S(2)}) collective-permute-start(s32[2,2]{1,0:T(2,128)S(1)} %multiply_add_fusion.refs_0_), channel_id=1, source_target_pairs={{0,1},{1,2},{2,3},{3,4},{4,5},{5,6},{6,7},{7,0},{8,9},{9,10},{10,1... | collective-permute-start | bytes 56 | tf_op jit(solution)/shard_map/ppermute | solution.py:293
  8.8 6.4 %collective-permute-start.5 = (s32[2,2]{1,0:T(2,128)S(1)}, s32[2,2]{1,0:T(2,128)S(1)}, u32[]{:S(2)}, u32[]{:S(2)}) collective-permute-start(s32[2,2]{1,0:T(2,128)S(1)} %multiply_add_fusion.refs_0_), channel_id=1, source_target_pairs={{0,3},{1,4},{2,5},{3,6},{4,7},{5,0},{6,1},{7,2},{8,11},{9,12},{10,... | collective-permute-start | bytes 56 | tf_op jit(solution)/shard_map/ppermute | solution.py:293
  9.9 5.4 %collective-permute-start.6 = (s32[2,2]{1,0:T(2,128)S(1)}, s32[2,2]{1,0:T(2,128)S(1)}, u32[]{:S(2)}, u32[]{:S(2)}) collective-permute-start(s32[2,2]{1,0:T(2,128)S(1)} %multiply_add_fusion.refs_0_), channel_id=1, source_target_pairs={{0,4},{1,5},{2,6},{3,7},{4,0},{5,1},{6,2},{7,3},{8,12},{9,13},{10,... | collective-permute-start | bytes 56 | tf_op jit(solution)/shard_map/ppermute | solution.py:293
  16.5 16.5 %collective-permute-start.8 = (bf16[2,256,256]{2,1,0:T(8,128)(2,1)S(1)}, bf16[2,256,256]{2,1,0:T(8,128)(2,1)S(1)}, u32[]{:S(2)}, u32[]{:S(2)}) collective-permute-start(bf16[2,256,256]{2,1,0:T(8,128)(2,1)S(1)} %collective-permute-done.7.refs_0_), channel_id=1, source_target_pairs={{0,16},{1,17},{2,18},{3,19},{4,20},{5,21},{6,22},{7,23},{8,24},{9,... | collective-permute-start | bytes 786440 | tf_op jit(solution)/shard_map/ppermute | solution.py:303
  19.9 8.2 %collective-permute-start.9 = (bf16[2,2,64,256]{3,2,1,0:T(8,128)(2,1)S(1)}, bf16[2,2,64,256]{3,2,1,0:T(8,128)(2,1)S(1)}, u32[]{:S(2)}, u32[]{:S(2)}) collective-permute-start(bf16[2,2,64,256]{3,2,1,0:T(8,128)(2,1)S(1)} %get-tuple-element.128), channel_id=1, source_target_pairs={{0,2},{1,3},{2,4},{3,5},{4,6},{5,7},{6,0},{7,1},{8,10},{9,11},{10,... | collective-permute-start | bytes 393224 | tf_op jit(solution)/shard_map/ppermute | solution.py:303
  20.7 9.5 %collective-permute-start.10 = (bf16[2,2,64,256]{3,2,1,0:T(8,128)(2,1)S(1)}, bf16[2,2,64,256]{3,2,1,0:T(8,128)(2,1)S(1)}, u32[]{:S(2)}, u32[]{:S(2)}) collective-permute-start(bf16[2,2,64,256]{3,2,1,0:T(8,128)(2,1)S(1)} %get-tuple-element.131), channel_id=1, source_target_pairs={{0,1},{1,2},{2,3},{3,4},{4,5},{5,6},{6,7},{7,0},{8,9},{9,10},{10,1... | collective-permute-start | bytes 393224 | tf_op jit(solution)/shard_map/ppermute | solution.py:303
  22.2 8.0 %collective-permute-start.11 = (bf16[2,2,64,256]{3,2,1,0:T(8,128)(2,1)S(1)}, bf16[2,2,64,256]{3,2,1,0:T(8,128)(2,1)S(1)}, u32[]{:S(2)}, u32[]{:S(2)}) collective-permute-start(bf16[2,2,64,256]{3,2,1,0:T(8,128)(2,1)S(1)} %get-tuple-element.133), channel_id=1, source_target_pairs={{0,7},{1,0},{2,1},{3,2},{4,3},{5,4},{6,5},{7,6},{8,15},{9,8},{10,9... | collective-permute-start | bytes 393224 | tf_op jit(solution)/shard_map/ppermute | solution.py:303
  25.4 6.3 %collective-permute-start.12 = (bf16[2,2,64,256]{3,2,1,0:T(8,128)(2,1)S(1)}, bf16[2,2,64,256]{3,2,1,0:T(8,128)(2,1)S(1)}, u32[]{:S(2)}, u32[]{:S(2)}) collective-permute-start(bf16[2,2,64,256]{3,2,1,0:T(8,128)(2,1)S(1)} %get-tuple-element.134), channel_id=1, source_target_pairs={{0,6},{1,7},{2,0},{3,1},{4,2},{5,3},{6,4},{7,5},{8,14},{9,15},{10,... | collective-permute-start | bytes 393224 | tf_op jit(solution)/shard_map/ppermute | solution.py:303
  28.1 8.9 %collective-permute-start.13 = (bf16[2,2,64,256]{3,2,1,0:T(8,128)(2,1)S(1)}, bf16[2,2,64,256]{3,2,1,0:T(8,128)(2,1)S(1)}, u32[]{:S(2)}, u32[]{:S(2)}) collective-permute-start(bf16[2,2,64,256]{3,2,1,0:T(8,128)(2,1)S(1)} %get-tuple-element.135), channel_id=1, source_target_pairs={{0,10},{1,11},{2,12},{3,13},{4,14},{5,15},{6,8},{7,9},{8,2},{9,3},... | collective-permute-start | bytes 393224 | tf_op jit(solution)/shard_map/ppermute | solution.py:303
  30.2 9.0 %collective-permute-start.14 = (bf16[2,2,64,256]{3,2,1,0:T(8,128)(2,1)S(1)}, bf16[2,2,64,256]{3,2,1,0:T(8,128)(2,1)S(1)}, u32[]{:S(2)}, u32[]{:S(2)}) collective-permute-start(bf16[2,2,64,256]{3,2,1,0:T(8,128)(2,1)S(1)} %get-tuple-element.136), channel_id=1, source_target_pairs={{0,9},{1,10},{2,11},{3,12},{4,13},{5,14},{6,15},{7,8},{8,1},{9,2},... | collective-permute-start | bytes 393224 | tf_op jit(solution)/shard_map/ppermute | solution.py:303
  30.2 9.0 %collective-permute-start.17 = (bf16[2,2,64,256]{3,2,1,0:T(8,128)(2,1)S(1)}, bf16[2,2,64,256]{3,2,1,0:T(8,128)(2,1)S(1)}, u32[]{:S(2)}, u32[]{:S(2)}) collective-permute-start(bf16[2,2,64,256]{3,2,1,0:T(8,128)(2,1)S(1)} %get-tuple-element.139), channel_id=1, source_target_pairs={{0,14},{1,15},{2,8},{3,9},{4,10},{5,11},{6,12},{7,13},{8,6},{9,7},... | collective-permute-start | bytes 393224 | tf_op jit(solution)/shard_map/ppermute | solution.py:303
  31.7 7.5 %collective-permute-start.15 = (bf16[2,2,64,256]{3,2,1,0:T(8,128)(2,1)S(1)}, bf16[2,2,64,256]{3,2,1,0:T(8,128)(2,1)S(1)}, u32[]{:S(2)}, u32[]{:S(2)}) collective-permute-start(bf16[2,2,64,256]{3,2,1,0:T(8,128)(2,1)S(1)} %get-tuple-element.137), channel_id=1, source_target_pairs={{0,8},{1,9},{2,10},{3,11},{4,12},{5,13},{6,14},{7,15},{8,0},{9,1},... | collective-permute-start | bytes 393224 | tf_op jit(solution)/shard_map/ppermute | solution.py:303
  32.9 7.6 %collective-permute-start.16 = (bf16[2,2,64,256]{3,2,1,0:T(8,128)(2,1)S(1)}, bf16[2,2,64,256]{3,2,1,0:T(8,128)(2,1)S(1)}, u32[]{:S(2)}, u32[]{:S(2)}) collective-permute-start(bf16[2,2,64,256]{3,2,1,0:T(8,128)(2,1)S(1)} %get-tuple-element.138), channel_id=1, source_target_pairs={{0,15},{1,8},{2,9},{3,10},{4,11},{5,12},{6,13},{7,14},{8,7},{9,0},... | collective-permute-start | bytes 393224 | tf_op jit(solution)/shard_map/ppermute | solution.py:303
  34.9 1.1 %copy-start.3 = (bf16[768,512]{1,0:T(8,128)(2,1)S(1)}, bf16[768,512]{1,0:T(8,128)(2,1)}, u32[]{:S(2)}) copy-start(bf16[768,512]{1,0:T(8,128)(2,1)} %constant.47.clone.refs_3_.right) | copy-start | bytes 2359300
  36.0 4.5 %copy-start.4 = (bf16[768,512]{1,0:T(8,128)(2,1)S(1)}, bf16[768,512]{1,0:T(8,128)(2,1)}, u32[]{:S(2)}) copy-start(bf16[768,512]{1,0:T(8,128)(2,1)} %constant.47.clone.refs_3_.right) | copy-start | bytes 2359300
  42.5 9.2 %collective-permute-start.19 = (bf16[2,256,256]{2,1,0:T(8,128)(2,1)S(1)}, bf16[2,256,256]{2,1,0:T(8,128)(2,1)S(1)}, u32[]{:S(2)}, u32[]{:S(2)}) collective-permute-start(bf16[2,256,256]{2,1,0:T(8,128)(2,1)S(1)} %get-tuple-element.146), channel_id=1, source_target_pairs={{0,16},{1,17},{2,18},{3,19},{4,20},{5,21},{6,22},{7,23},{8,24},{9,... | collective-permute-start | bytes 786440 | tf_op jit(solution)/shard_map/ppermute | solution.py:303
  47.0 9.6 %collective-permute-start.18 = (bf16[2,256,256]{2,1,0:T(8,128)(2,1)S(1)}, bf16[2,256,256]{2,1,0:T(8,128)(2,1)S(1)}, u32[]{:S(2)}, u32[]{:S(2)}) collective-permute-start(bf16[2,256,256]{2,1,0:T(8,128)(2,1)S(1)} %get-tuple-element.142), channel_id=1, source_target_pairs={{0,16},{1,17},{2,18},{3,19},{4,20},{5,21},{6,22},{7,23},{8,24},{9,... | collective-permute-start | bytes 786440 | tf_op jit(solution)/shard_map/ppermute | solution.py:303
  55.7 4.1 %collective-permute-start.21 = (bf16[2,256,256]{2,1,0:T(8,128)(2,1)S(1)}, bf16[2,256,256]{2,1,0:T(8,128)(2,1)S(1)}, u32[]{:S(2)}, u32[]{:S(2)}) collective-permute-start(bf16[2,256,256]{2,1,0:T(8,128)(2,1)S(1)} %get-tuple-element.152), channel_id=1, source_target_pairs={{0,8},{1,9},{2,10},{3,11},{4,12},{5,13},{6,14},{7,15},{8,0},{9,1},... | collective-permute-start | bytes 786440 | tf_op jit(solution)/shard_map/ppermute | solution.py:303
  58.1 1.7 %collective-permute-start.20 = (bf16[2,256,256]{2,1,0:T(8,128)(2,1)S(1)}, bf16[2,256,256]{2,1,0:T(8,128)(2,1)S(1)}, u32[]{:S(2)}, u32[]{:S(2)}) collective-permute-start(bf16[2,256,256]{2,1,0:T(8,128)(2,1)S(1)} %get-tuple-element.151), channel_id=1, source_target_pairs={{0,8},{1,9},{2,10},{3,11},{4,12},{5,13},{6,14},{7,15},{8,0},{9,1},... | collective-permute-start | bytes 786440 | tf_op jit(solution)/shard_map/ppermute | solution.py:303
  59.2 6.1 %collective-permute-start.22 = (bf16[2,2,64,256]{3,2,1,0:T(8,128)(2,1)S(1)}, bf16[2,2,64,256]{3,2,1,0:T(8,128)(2,1)S(1)}, u32[]{:S(2)}, u32[]{:S(2)}) collective-permute-start(bf16[2,2,64,256]{3,2,1,0:T(8,128)(2,1)S(1)} %get-tuple-element.156), channel_id=1, source_target_pairs={{0,8},{1,9},{2,10},{3,11},{4,12},{5,13},{6,14},{7,15},{8,0},{9,1},... | collective-permute-start | bytes 393224 | tf_op jit(solution)/shard_map/ppermute | solution.py:303
  60.5 21.0 %collective-permute-start.23 = (bf16[2,2,2,64,256]{4,3,2,1,0:T(8,128)(2,1)S(1)}, bf16[2,2,2,64,256]{4,3,2,1,0:T(8,128)(2,1)S(1)}, u32[]{:S(2)}, u32[]{:S(2)}) collective-permute-start(bf16[2,2,2,64,256]{4,3,2,1,0:T(8,128)(2,1)S(1)} %get-tuple-element.158), channel_id=1, source_target_pairs={{0,6},{1,7},{2,0},{3,1},{4,2},{5,3},{6,4},{7,5},{8,14},{9,15},{10,... | collective-permute-start | bytes 786440 | tf_op jit(solution)/shard_map/ppermute | solution.py:303
  60.6 21.0 %collective-permute-start.24 = (bf16[2,2,2,64,256]{4,3,2,1,0:T(8,128)(2,1)S(1)}, bf16[2,2,2,64,256]{4,3,2,1,0:T(8,128)(2,1)S(1)}, u32[]{:S(2)}, u32[]{:S(2)}) collective-permute-start(bf16[2,2,2,64,256]{4,3,2,1,0:T(8,128)(2,1)S(1)} %get-tuple-element.159), channel_id=1, source_target_pairs={{0,7},{1,0},{2,1},{3,2},{4,3},{5,4},{6,5},{7,6},{8,15},{9,8},{10,9... | collective-permute-start | bytes 786440 | tf_op jit(solution)/shard_map/ppermute | solution.py:303
  63.4 18.2 %collective-permute-start.25 = (bf16[2,2,2,64,256]{4,3,2,1,0:T(8,128)(2,1)S(1)}, bf16[2,2,2,64,256]{4,3,2,1,0:T(8,128)(2,1)S(1)}, u32[]{:S(2)}, u32[]{:S(2)}) collective-permute-start(bf16[2,2,2,64,256]{4,3,2,1,0:T(8,128)(2,1)S(1)} %get-tuple-element.160), channel_id=1, source_target_pairs={{0,1},{1,2},{2,3},{3,4},{4,5},{5,6},{6,7},{7,0},{8,9},{9,10},{10,1... | collective-permute-start | bytes 786440 | tf_op jit(solution)/shard_map/ppermute | solution.py:303
  63.9 17.7 %collective-permute-start.26 = (bf16[2,2,2,64,256]{4,3,2,1,0:T(8,128)(2,1)S(1)}, bf16[2,2,2,64,256]{4,3,2,1,0:T(8,128)(2,1)S(1)}, u32[]{:S(2)}, u32[]{:S(2)}) collective-permute-start(bf16[2,2,2,64,256]{4,3,2,1,0:T(8,128)(2,1)S(1)} %get-tuple-element.161), channel_id=1, source_target_pairs={{0,2},{1,3},{2,4},{3,5},{4,6},{5,7},{6,0},{7,1},{8,10},{9,11},{10,... | collective-permute-start | bytes 786440 | tf_op jit(solution)/shard_map/ppermute | solution.py:303
  65.3 4.4 %collective-permute-start = (bf16[2,64,256]{2,1,0:T(8,128)(2,1)S(1)}, bf16[2,64,256]{2,1,0:T(8,128)(2,1)S(1)}, u32[]{:S(2)}, u32[]{:S(2)}) collective-permute-start(bf16[2,64,256]{2,1,0:T(8,128)(2,1)S(1)} %fusion.5), channel_id=1, source_target_pairs={{0,16},{1,17},{2,18},{3,19},{4,20},{5,21},{6,22},{7,23},{8,24},{9,... | collective-permute-start | bytes 196616 | tf_op jit(solution)/shard_map/while/body/ppermute | solution.py:303
  69.7 7.4 %collective-permute-start.1 = (bf16[2,64,256]{2,1,0:T(8,128)(2,1)S(1)}, bf16[2,64,256]{2,1,0:T(8,128)(2,1)S(1)}, u32[]{:S(2)}, u32[]{:S(2)}) collective-permute-start(bf16[2,64,256]{2,1,0:T(8,128)(2,1)S(1)} %get-tuple-element.222), channel_id=1, source_target_pairs={{0,1},{1,0},{2,3},{3,2},{4,5},{5,4},{6,7},{7,6},{8,9},{9,8},{10,11... | collective-permute-start | bytes 196616 | tf_op jit(solution)/shard_map/while/body/ppermute | solution.py:412
  77.1 4.3 %collective-permute-start.2 = (bf16[2,64,256]{2,1,0:T(8,128)(2,1)S(1)}, bf16[2,64,256]{2,1,0:T(8,128)(2,1)S(1)}, u32[]{:S(2)}, u32[]{:S(2)}) collective-permute-start(bf16[2,64,256]{2,1,0:T(8,128)(2,1)S(1)} %add_convert_fusion.2), channel_id=1, source_target_pairs={{0,2},{1,3},{2,0},{3,1},{4,6},{5,7},{6,4},{7,5},{8,10},{9,11},{10,... | collective-permute-start | bytes 196616 | tf_op jit(solution)/shard_map/while/body/ppermute | solution.py:412
  81.6 5.9 %collective-permute-start.27 = (bf16[2,64,256]{2,1,0:T(8,128)(2,1)S(1)}, bf16[2,64,256]{2,1,0:T(8,128)(2,1)S(1)}, u32[]{:S(2)}, u32[]{:S(2)}) collective-permute-start(bf16[2,64,256]{2,1,0:T(8,128)(2,1)S(1)} %convert_element_type.65), channel_id=1, source_target_pairs={{0,4},{1,5},{2,6},{3,7},{4,0},{5,1},{6,2},{7,3},{8,12},{9,13},{10,... | collective-permute-start | bytes 196616 | tf_op jit(solution)/shard_map/ppermute | solution.py:412
